TPU v7x, 32 devices: a whole 2x2x4 slice. The times are simulated.
32 devices in a mesh: batch: 4 (over x, core), seq: 8 (over z, y).
Axes of the slice: x: 2, y: 2, z: 4, core: 2. Of those that a mesh axis runs over, the one named last changes fastest.
Arguments:
- tokens: bfloat16 [16, 1024, 768], P('batch', 'seq'), may hold values from -6 to 6
- ln1_gain: float32 [768], replicated, may hold values from 0.5 to 1.5
- ln1_bias: float32 [768], replicated, may hold values from -1.8 to 1.8
- qkv_weight: bfloat16 [768, 896], replicated, may hold values from -0.3125 to 0.3125
- qkv_bias: float32 [896], replicated, may hold values from -1.8 to 1.8
- out_weight: bfloat16 [768, 768], replicated, may hold values from -0.875 to 0.875
- ln2_gain: float32 [768], replicated, may hold values from 0.5 to 1.5
- ln2_bias: float32 [768], replicated, may hold values from -1.8 to 1.8
- fc1_weight: bfloat16 [768, 3072], replicated, may hold values from -0.21875 to 0.21875
- fc1_bias: float32 [3072], replicated, may hold values from -1.8 to 1.8
- fc2_weight: bfloat16 [3072, 768], replicated, may hold values from -0.109375 to 0.109375
- out_bias: float32 [768], replicated, may hold values from -1.8 to 1.8
- output_grad: bfloat16 [16, 1024, 768], P('batch', 'seq'), may hold values from -6 to 6
- key_value_grad: bfloat16 [16, 1024, 128], P('batch', 'seq'), may hold values from -6 to 6
Outputs:
- output: bfloat16 [16, 1024, 768], P('batch', 'seq')
- key_value: bfloat16 [16, 1024, 128], P('batch', 'seq')
- tokens_grad: bfloat16 [16, 1024, 768], P('batch', 'seq')
- ln1_gain_grad: float32 [768], replicated
- ln1_bias_grad: float32 [768], replicated
- qkv_weight_grad: float32 [768, 896], P('seq')
- qkv_bias_grad: float32 [896], replicated
- out_weight_grad: float32 [768, 768], P('seq')
- ln2_gain_grad: float32 [768], replicated
- ln2_bias_grad: float32 [768], replicated
- fc1_weight_grad: float32 [768, 3072], P('seq')
- fc1_bias_grad: float32 [3072], replicated
- fc2_weight_grad: float32 [3072, 768], P('seq')
- out_bias_grad: float32 [768], replicated
All inputs are finite; a program needn't handle non-finite values.
Results may differ from a plain program's by a relative error of at most 0.015.
Values may be sent and summed in bfloat16 or wider, within the bound.
No kernel may reach another device: no remote copies, remote signals or barrier semaphores. Data moves between devices by JAX's collectives and lax.ppermute only.
A program may use at most 128 MiB of HBM per device.

v0:
```python
import functools
import math

import jax
import jax.numpy as jnp
from jax import lax
from jax.experimental import pallas as pl
from jax.experimental.pallas import tpu as pltpu
from jax.sharding import PartitionSpec as P

D = 768
HEADS = 12
HEAD_DIM = 64
ROT = 16
PAIRS = HEADS // 2
SCALE = 1.0 / math.sqrt(HEAD_DIM)
NORM_EPS = 1e-05
MASKED = -1e30
F32 = jnp.float32
BF16 = jnp.bfloat16
VMEM_BYTES = 56 * 1024 * 1024


def dot(a, b):
    return lax.dot_general(a, b, (((1,), (0,)), ((), ())), preferred_element_type=F32)


def dot_nt(a, b):
    return lax.dot_general(a, b, (((1,), (1,)), ((), ())), preferred_element_type=F32)


def dot_tn(a, b):
    return lax.dot_general(a, b, (((0,), (0,)), ((), ())), preferred_element_type=F32)


def params():
    return pltpu.CompilerParams(vmem_limit_bytes=VMEM_BYTES)


def flipped(block, axis, bits):
    return lax.ppermute(block, axis, [(i, i ^ bits) for i in range(lax.axis_size(axis))])


def along(block, distance):
    size = lax.axis_size("seq")
    return lax.ppermute(block, "seq", [(i, (i + 2 * distance) % size) for i in range(size)])


def to_owner(block, distance):
    size = lax.axis_size("seq")
    half = size // 4
    route = []
    for b in range(lax.axis_size("batch")):
        for i in range(size):
            j = i ^ (2 * distance)
            if (j // 2) // half == b % 2:
                route.append((b * size + i, b * size + j))
    return lax.ppermute(block, ("batch", "seq"), route)


def after(values, *others):
    return lax.optimization_barrier((tuple(values), others))[0]


def tree_sum(parts):
    parts = [p.astype(F32) for p in parts]
    while len(parts) > 1:
        parts = [sum(parts[i : i + 2][1:], parts[i]) for i in range(0, len(parts), 2)]
    return parts[0]


def take(block, index, axis):
    return lax.dynamic_index_in_dim(block, index, axis, keepdims=False)


def normalize(rows):
    centre = jnp.mean(rows, axis=-1, keepdims=True)
    centred = rows - centre
    spread = jnp.mean(centred * centred, axis=-1, keepdims=True)
    inverse = lax.rsqrt(spread + NORM_EPS)
    return centred * inverse, inverse


def rotary_tables(first, count):
    lane = jnp.arange(128) % HEAD_DIM
    half = ROT // 2
    freqs = 10000.0 ** (-(lane % half).astype(F32) / half)
    places = (first + jnp.arange(count)).astype(F32) * 0.25
    angles = places[:, None] * freqs[None, :]
    cosine, sine = jnp.cos(angles), jnp.sin(angles)
    return jnp.stack(
        [
            jnp.where(lane < ROT, cosine, 1.0),
            jnp.where((lane >= half) & (lane < ROT), sine, 0.0),
            jnp.where(lane < half, -sine, 0.0),
        ]
    )


def turn(values, tables, sign):
    moved = pltpu.roll(values, ROT // 2, 1) * tables[1] + pltpu.roll(values, 128 - ROT // 2, 1) * tables[2]
    return values * tables[0] + (moved if sign > 0 else -moved)


def repeated(tables_ref, count):
    return [jnp.concatenate([tables_ref[i]] * count, axis=0) for i in range(3)]


def key_tables(tables):
    low = lax.broadcasted_iota(jnp.int32, (1, 128), 1) < HEAD_DIM
    return [jnp.where(low, tables[0], 1.0), jnp.where(low, tables[1], 0.0), jnp.where(low, tables[2], 0.0)]

VMEM = pl.BlockSpec(memory_space=pltpu.VMEM)
SMEM = pl.BlockSpec(memory_space=pltpu.SMEM)
SHAPE = jax.ShapeDtypeStruct


def cost(share):
    return pl.CostEstimate(flops=int(share * 3e9), bytes_accessed=0, transcendentals=0)


def wide(ref):
    return ref[...].reshape(1, -1)


def add_split(place, items):
    def kernel(place_ref, *refs):
        sources, results = refs[: 2 * len(items)], refs[2 * len(items) :]
        for n, (_, _, which) in enumerate(items):
            a, b = sources[2 * n], sources[2 * n + 1]
            own = place_ref[which]
            for m in range(a.shape[0]):
                for result, at in ((results[2 * n], 1 - own), (results[2 * n + 1], own)):
                    result[m] = (a[m, at].astype(F32) + b[m, at].astype(F32)).astype(BF16)

    shapes = []
    for a, _, _ in items:
        shapes += [SHAPE((a.shape[0],) + a.shape[2:], BF16)] * 2
    arrays = [v for item in items for v in item[:2]]
    return pl.pallas_call(
        kernel,
        in_specs=[SMEM] + [VMEM] * len(arrays),
        out_specs=[VMEM] * len(shapes),
        out_shape=shapes,
        compiler_params=params(),
        cost_estimate=cost(1.2),
        name="add_split",
    )(place, *arrays)


def add_cut(place, items):
    def kernel(place_ref, *refs):
        sources, results = refs[: 2 * len(items)], refs[2 * len(items) :]
        start = 0
        for n, (first, _) in enumerate(items):
            a, b = sources[2 * n], sources[2 * n + 1]
            count = first.shape[0]
            for i in range(count):
                at = lax.rem(place_ref[3] ^ i, count)
                results[start + i][...] = (a[at].astype(F32) + b[at].astype(F32)).astype(BF16)
            start += count

    shapes = []
    for a, _ in items:
        shapes += [SHAPE(a.shape[1:], BF16)] * a.shape[0]
    arrays = [v for item in items for v in item]
    return pl.pallas_call(
        kernel,
        in_specs=[SMEM] + [VMEM] * len(arrays),
        out_specs=[VMEM] * len(shapes),
        out_shape=shapes,
        compiler_params=params(),
        cost_estimate=cost(0.8),
        name="add_cut",
    )(place, *arrays)


def sum_split(place, parts):
    def kernel(place_ref, *refs):
        sources, results = refs[:-2], refs[-2:]
        y = place_ref[2]
        for result, at in ((results[0], 1 - y), (results[1], y)):
            result[...] = tree_sum([ref[at] for ref in sources]).astype(BF16)

    return pl.pallas_call(
        kernel,
        in_specs=[SMEM] + [VMEM] * len(parts),
        out_specs=[VMEM] * 2,
        out_shape=[SHAPE(parts[0].shape[1:], BF16)] * 2,
        compiler_params=params(),
        cost_estimate=cost(1.6),
        name="sum_split",
    )(place, *parts)


def project_kernel(copies, x_ref, gain_ref, bias_ref, weight_ref, add_ref, tables_ref, q_ref, kv_ref):
    normed, _ = normalize(x_ref[...].astype(F32))
    first_in = (normed * wide(gain_ref) + wide(bias_ref)).astype(BF16)
    tables = repeated(tables_ref, copies)
    bias = wide(add_ref)
    for p in (PAIRS,) + tuple(range(PAIRS)):
        columns = slice(p * 128, (p + 1) * 128)
        part = dot(first_in, weight_ref[:, columns]) + bias[:, columns]
        if p < PAIRS:
            q_ref[:, columns] = (turn(part, tables, 1) * SCALE).astype(BF16)
        else:
            kv_ref[...] = turn(part, key_tables(tables), 1).astype(BF16)


def project(x, gain, bias, weight, add, tables):
    rows = x.shape[0]
    return pl.pallas_call(
        functools.partial(project_kernel, rows // tables.shape[1]),
        in_specs=[VMEM] * 6,
        out_specs=[VMEM] * 2,
        out_shape=[SHAPE((rows, D), BF16), SHAPE((rows, 128), BF16)],
        compiler_params=params(),
        cost_estimate=cost(2),
        name="project",
    )(x, gain, bias, weight, add, tables)


def gelu_parts(h):
    t = pl.reciprocal(1.0 + (0.3275911 / math.sqrt(2.0)) * jnp.abs(h))
    e = jnp.exp(-0.5 * h * h)
    poly = 0.5 * 1.061405429
    for coefficient in (-1.453152027, 1.421413741, -0.284496736, 0.254829592):
        poly = poly * t + 0.5 * coefficient
    tail = poly * t * e
    cdf = jnp.where(h >= 0.0, 1.0 - tail, tail)
    return h * cdf, cdf + h * e * (1.0 / math.sqrt(2.0 * math.pi))


def forward_kernel(
    place_ref,
    x_ref,
    xx_ref,
    g_ref,
    gg_ref,
    gain_ref,
    bias_ref,
    w1_ref,
    b1_ref,
    w2_ref,
    own_ref,
    other_ref,
    slope_ref,
    in_t_ref,
    *refs,
):
    grad_refs, (in_scr, g_scr, acc_scr) = refs[:-3], refs[-3:]
    step, steps = pl.program_id(0), pl.num_programs(0)
    rows = x_ref.shape[0]

    @pl.when(step == 0)
    def _():
        for i, (tokens, grads) in enumerate(((x_ref, g_ref), (xx_ref, gg_ref))):
            at = slice(i * rows, (i + 1) * rows)
            normed, _ = normalize(tokens[...].astype(F32))
            second_in = normed * wide(gain_ref) + wide(bias_ref)
            in_scr[at] = second_in.astype(BF16)
            in_t_ref[:, at] = second_in.T.astype(BF16)
            g_scr[at] = grads[...]

    w2 = w2_ref[...]
    act, slope = gelu_parts(dot(in_scr[...], w1_ref[...]) + b1_ref[...])
    act = act.astype(BF16)
    slope_ref[...] = slope.astype(BF16)
    grad = dot_tn(act, g_scr[...]).astype(BF16)
    if len(grad_refs) == 1:
        grad_refs[0][...] = grad
    for i in range(len(grad_refs) if len(grad_refs) > 1 else 0):

        @pl.when(step == steps - 1 - i)
        def _(i=i):
            grad_refs[i][...] = grad

    mlp = dot(act, w2)

    @pl.when(step == 0)
    def _():
        acc_scr[...] = mlp

    @pl.when((step > 0) & (step < steps - 1))
    def _():
        acc_scr[...] += mlp

    @pl.when(step == steps - 1)
    def _():
        total = acc_scr[...] + mlp
        own_ref[...] = total[:rows]
        other_ref[...] = total[rows:].astype(BF16)


CHUNK = 512


def feed_forward(place, depth, x, xx, g, gg, gain, bias, w1, b1, w2):
    rows = x.shape[0]
    half = w1.shape[1] // 2
    pieces = depth // 2
    aligned = half % (pieces * 256) == 0
    chunk = half // pieces if aligned else CHUNK
    steps = half // chunk
    whole = lambda a: pl.BlockSpec(a.shape, lambda i, place: (0,) * a.ndim)
    fixed = lambda *shape: pl.BlockSpec(shape, lambda i, place: (0, 0))
    if aligned:
        piece = lambda i, place: (place[3] ^ (steps - 1 - i)) % steps
        grad_specs = [fixed(chunk, D)] * pieces
        grad_shapes = [SHAPE((chunk, D), BF16)] * pieces
    else:
        piece = lambda i, place: i
        grad_specs = [pl.BlockSpec((chunk, D), lambda i, place: (i, 0))]
        grad_shapes = [SHAPE((half, D), BF16)]
    at = lambda i, place: place[0] * steps + piece(i, place)
    spec = pltpu.PrefetchScalarGridSpec(
        num_scalar_prefetch=1,
        grid=(steps,),
        in_specs=[
            whole(x),
            whole(xx),
            whole(g),
            whole(gg),
            whole(gain),
            whole(bias),
            pl.BlockSpec((D, chunk), lambda i, place: (0, at(i, place))),
            pl.BlockSpec((1, chunk), lambda i, place: (0, at(i, place))),
            pl.BlockSpec((chunk, D), lambda i, place: (at(i, place), 0)),
        ],
        out_specs=[
            fixed(rows, D),
            fixed(rows, D),
            pl.BlockSpec((2 * rows, chunk), lambda i, place: (0, piece(i, place))),
            fixed(D, 2 * rows),
        ]
        + grad_specs,
        scratch_shapes=[
            pltpu.VMEM((2 * rows, D), BF16),
            pltpu.VMEM((2 * rows, D), BF16),
            pltpu.VMEM((2 * rows, D), F32),
        ],
    )
    result = pl.pallas_call(
        forward_kernel,
        grid_spec=spec,
        out_shape=[
            SHAPE((rows, D), F32),
            SHAPE((rows, D), BF16),
            SHAPE((2 * rows, half), BF16),
            SHAPE((D, 2 * rows), BF16),
        ]
        + grad_shapes,
        compiler_params=params(),
        cost_estimate=cost(8),
        name="feed_forward",
    )(place, x, xx, g, gg, gain, bias, w1, b1, w2)
    grads = result[4:]
    if not aligned:
        cut = grads[0].reshape(pieces, -1, D)
        grads = [take(cut, (place[3] ^ i) % pieces, 0) for i in range(pieces)]
    return result[:4], grads


def backward_kernel(
    place_ref,
    g_ref,
    gg_ref,
    slope_ref,
    in_theirs_ref,
    in_mine_ref,
    w1_ref,
    w2_ref,
    wo_ref,
    own_ref,
    other_ref,
    attn_grad_ref,
    theirs_ref,
    mine_ref,
    b1_grad_ref,
    g_scr,
    acc_scr,
):
    step, steps = pl.program_id(0), pl.num_programs(0)
    rows = g_ref.shape[0]

    @pl.when(step == 0)
    def _():
        g_scr[:rows] = g_ref[...]
        g_scr[rows:] = gg_ref[...]
        attn_grad_ref[...] = dot_nt(g_ref[...], wo_ref[...]).astype(BF16)

    w1 = w1_ref[...]
    pre = dot_nt(g_scr[...], w2_ref[...]) * slope_ref[...].astype(F32)
    pre16 = pre.astype(BF16)
    b1_grad_ref[...] = jnp.sum(pre, axis=0, keepdims=True)
    for source, result in ((in_theirs_ref, theirs_ref), (in_mine_ref, mine_ref)):
        left = source[...].reshape(-1, 2 * rows)
        result[...] = dot(left, pre16).astype(BF16).reshape(result.shape)
    back = dot_nt(pre16, w1)

    @pl.when(step == 0)
    def _():
        acc_scr[...] = back

    @pl.when((step > 0) & (step < steps - 1))
    def _():
        acc_scr[...] += back

    @pl.when(step == steps - 1)
    def _():
        total = acc_scr[...] + back
        own_ref[...] = total[:rows]
        other_ref[...] = total[rows:].astype(BF16)


def feed_backward(place, count, g, gg, slope, in_t, w1, w2, wo):
    rows = g.shape[0]
    half = w1.shape[1] // 2
    steps = half // CHUNK
    per = D // count // 2
    in_t = in_t.reshape(count, 2, per, 2 * rows)
    whole = lambda a: pl.BlockSpec(a.shape, lambda i, place: (0,) * a.ndim)
    fixed = lambda *shape: pl.BlockSpec(shape, lambda i, place: (0, 0))
    at = lambda i, place: place[0] * steps + i
    cut = pl.BlockSpec((count, per, CHUNK), lambda i, place: (0, 0, i))
    spec = pltpu.PrefetchScalarGridSpec(
        num_scalar_prefetch=1,
        grid=(steps,),
        in_specs=[
            whole(g),
            whole(gg),
            pl.BlockSpec((2 * rows, CHUNK), lambda i, place: (0, i)),
            pl.BlockSpec((count, None, per, 2 * rows), lambda i, place: (0, 1 - place[1], 0, 0)),
            pl.BlockSpec((count, None, per, 2 * rows), lambda i, place: (0, place[1], 0, 0)),
            pl.BlockSpec((D, CHUNK), lambda i, place: (0, at(i, place))),
            pl.BlockSpec((CHUNK, D), lambda i, place: (at(i, place), 0)),
            whole(wo),
        ],
        out_specs=[
            fixed(rows, D),
            fixed(rows, D),
            fixed(rows, D),
            cut,
            cut,
            pl.BlockSpec((1, CHUNK), lambda i, place: (0, i)),
        ],
        scratch_shapes=[pltpu.VMEM((2 * rows, D), BF16), pltpu.VMEM((2 * rows, D), F32)],
    )
    return pl.pallas_call(
        backward_kernel,
        grid_spec=spec,
        out_shape=[
            SHAPE((rows, D), F32),
            SHAPE((rows, D), BF16),
            SHAPE((rows, D), BF16),
            SHAPE((count, per, half), BF16),
            SHAPE((count, per, half), BF16),
            SHAPE((1, half), F32),
        ],
        compiler_params=params(),
        cost_estimate=cost(6.4),
        name="feed_backward",
    )(place, g, gg, slope, in_t, in_t, w1, w2, wo)


def present(slot, y, z):
    back = slot // 2
    return (back <= z) & ((slot % 2 == 0) | (back >= 1) | (y == 1))


def whole_kernel(span, depth, place_ref, *refs):
    even_ref, odd_ref, q_ref, do_ref, out_ref, dq_ref, even_out_ref, odd_out_ref = refs
    y, z = place_ref[2], place_ref[3]
    rows = PAIRS * span
    low = lax.broadcasted_iota(jnp.int32, (1, 128), 1) < HEAD_DIM

    def stacked(ref):
        return jnp.concatenate([ref[:, p * 128 : (p + 1) * 128] for p in range(PAIRS)], axis=0)

    blocks = [ref[k] for k in range(depth) for ref in (even_ref, odd_ref)]
    kv = jnp.concatenate(blocks, axis=0)
    swapped = pltpu.roll(kv.astype(F32), HEAD_DIM, 1).astype(BF16)
    zero, one = jnp.zeros_like(kv), jnp.ones_like(kv)
    keys = (jnp.where(low, kv, zero), jnp.where(low, zero, swapped))
    values = (jnp.where(low, swapped, zero), jnp.where(low, zero, kv))
    summing = (jnp.where(low, swapped, one), jnp.where(low, one, kv))
    slot = lax.broadcasted_iota(jnp.int32, (1, (2 * depth - 1) * span), 1) // span + 1
    absent = jnp.where(present(slot, y, z), 0.0, MASKED)
    token = lax.broadcasted_iota(jnp.int32, (rows, span), 0) % span
    seen = lax.broadcasted_iota(jnp.int32, (rows, span), 1) <= token
    q = stacked(q_ref)
    do = stacked(do_ref)
    do32 = do.astype(F32)

    expd, mixed = [], []
    for h in range(2):
        scores = dot_nt(q, keys[h])
        scores = jnp.concatenate([jnp.where(seen, scores[:, :span], MASKED), scores[:, span:] + absent], axis=1)
        top = jnp.max(scores, axis=1, keepdims=True)
        expd.append(jnp.exp(scores - top).astype(BF16))
        mixed.append(dot(expd[h], summing[h]))
    total = jnp.where(low, pltpu.roll(mixed[0], HEAD_DIM, 1), pltpu.roll(mixed[1], HEAD_DIM, 1))
    inverse = 1.0 / total
    out = jnp.where(low, mixed[0], mixed[1]) * inverse
    for p in range(PAIRS):
        out_ref[:, p * 128 : (p + 1) * 128] = out[p * span : (p + 1) * span].astype(BF16)
    product = do32 * out
    do_t = (do32 * inverse).T.astype(BF16)
    q_t = (q.astype(F32) * inverse).T.astype(BF16)
    dq = dk = dv = 0.0
    for h in range(2):
        head = slice(h * HEAD_DIM, (h + 1) * HEAD_DIM)
        delta = jnp.sum(jnp.where(low == (h == 0), product, 0.0), axis=1, keepdims=True)
        dprob = dot_nt(do, values[h])
        dscore = (expd[h].astype(F32) * (dprob - delta)).astype(BF16)
        dq = dq + dot(dscore, keys[h])
        dk = dk + dot(q_t[head], dscore)
        dv = dv + dot(do_t[head], expd[h])
    dq = dq * inverse
    for p in range(PAIRS):
        dq_ref[:, p * 128 : (p + 1) * 128] = dq[p * span : (p + 1) * span]
    both = jnp.concatenate([dk, dv], axis=0).T.astype(BF16)
    for k in range(depth):
        even_out_ref[k] = both[2 * k * span : (2 * k + 1) * span]
        odd_out_ref[k] = both[(2 * k + 1) * span : (2 * k + 2) * span]


def loop_kernel(groups, span, block, count, place_ref, *refs):
    even_ref, odd_ref, q_ref, do_ref, out_ref, dq_ref, even_out_ref, odd_out_ref = refs[:8]
    kv_scr, e_ref, kv_t_ref, max_ref, acc_ref, ext_ref = refs[8:]
    depth = count // 2
    rows = groups * span
    per = block // span
    y, z = place_ref[2], place_ref[3]
    used = (2 * (z + 1) + per - 1) // per
    group, group_count = pl.program_id(1), pl.num_programs(1)
    low = lax.broadcasted_iota(jnp.int32, (1, 128), 1) < HEAD_DIM
    lanes = lax.broadcasted_iota(jnp.int32, (rows, 128), 1)

    def stacked(ref):
        return jnp.concatenate([ref[:, p * 128 : (p + 1) * 128] for p in range(groups)], axis=0)

    @pl.when(group == 0)
    def _():
        for i in range(count):
            kv_scr[i * span : (i + 1) * span] = (odd_ref if i % 2 else even_ref)[i // 2]

    q = stacked(q_ref)
    do = stacked(do_ref)

    def load(b):
        kv = kv_scr[pl.ds(pl.multiple_of(b * block, block), block)]
        swapped = pltpu.roll(kv.astype(F32), HEAD_DIM, 1).astype(BF16)
        return kv, swapped, jnp.zeros_like(kv)

    def absent(b):
        row = lax.broadcasted_iota(jnp.int32, (block, 128), 0) + b * block
        lane = lax.broadcasted_iota(jnp.int32, (block, 128), 1)
        mask = jnp.where(present(row // span, y, z), 0.0, MASKED)
        return jnp.where(lane < 2, -1.0, jnp.where(lane == 2, mask, 0.0)).astype(BF16)

    def key_tiles(b):
        kv, swapped, zero = load(b)
        ext = absent(b)
        return [
            jnp.concatenate([jnp.where(low, kv, zero), ext], axis=1),
            jnp.concatenate([jnp.where(low, zero, swapped), ext], axis=1),
        ]

    def value_tiles(b):
        kv, swapped, zero = load(b)
        ext = absent(b)
        return [
            jnp.concatenate([jnp.where(low, swapped, zero), ext], axis=1),
            jnp.concatenate([jnp.where(low, zero, kv), ext], axis=1),
        ]

    def seen():
        token = lax.broadcasted_iota(jnp.int32, (rows, block), 0) % span
        key = lax.broadcasted_iota(jnp.int32, (rows, block), 1)
        return (key <= token) | (key >= span)

    def extended(values):
        high = values.astype(BF16).astype(F32)
        rest = jnp.where(lanes == 1, values - high, jnp.where(lanes == 2, 1.0, 0.0))
        return jnp.where(lanes == 0, high, rest).astype(BF16)

    def over_blocks(step):
        step(0, True)

        def body(b, carry):
            step(b, False)
            return carry

        lax.fori_loop(1, used, body, 0)

    plain = jnp.concatenate([q, jnp.where(lanes == 2, 1.0, 0.0).astype(BF16)], axis=1)

    def maxima(b, diagonal):
        keys = key_tiles(b)
        for h in range(2):
            scores = dot_nt(plain, keys[h])
            if diagonal:
                scores = jnp.where(seen(), scores, MASKED)
            top = functools.reduce(jnp.maximum, [scores[:, i : i + 128] for i in range(0, block, 128)])
            max_ref[h] = top if diagonal else jnp.maximum(max_ref[h], top)

    over_blocks(maxima)
    for h in range(2):
        top = jnp.max(max_ref[h], axis=1, keepdims=True)
        ext_ref[h] = jnp.concatenate([q, extended(jnp.broadcast_to(top, (rows, 128)))], axis=1)

    def forward(b, diagonal):
        keys = key_tiles(b)
        kv, swapped, _ = load(b)
        one = jnp.ones_like(kv)
        values = (jnp.where(low, swapped, one), jnp.where(low, one, kv))
        for h in range(2):
            expd = jnp.exp(dot_nt(ext_ref[h], keys[h]))
            if diagonal:
                expd = jnp.where(seen(), expd, 0.0)
            expd = expd.astype(BF16)
            e_ref[b, h] = expd
            mixed = dot(expd, values[h])
            acc_ref[h] = mixed if diagonal else acc_ref[h] + mixed

    over_blocks(forward)
    first, second = acc_ref[0], acc_ref[1]
    total = jnp.where(low, pltpu.roll(first, HEAD_DIM, 1), pltpu.roll(second, HEAD_DIM, 1))
    inverse = 1.0 / total
    out = jnp.where(low, first, second) * inverse
    for p in range(groups):
        out_ref[:, p * 128 : (p + 1) * 128] = out[p * span : (p + 1) * span].astype(BF16)
    do32 = do.astype(F32)
    product = do32 * out
    high = product.astype(BF16)
    rest = (product - high.astype(F32)).astype(BF16)
    place = lax.broadcasted_iota(jnp.int32, (128, 128), 0)
    for h in range(2):
        ones = jnp.where((place < HEAD_DIM) == (h == 0), 1.0, 0.0).astype(BF16)
        delta = dot(high, ones) + dot(rest, ones)
        ext_ref[h] = jnp.concatenate([do, extended(delta)], axis=1)
    do_t = (do32 * inverse).T.astype(BF16)
    q_t = (q.astype(F32) * inverse).T.astype(BF16)

    def backward(b, start):
        values = value_tiles(b)
        kv, swapped, zero = load(b)
        keys = (jnp.where(low, kv, zero), jnp.where(low, zero, swapped))
        dq = dk = dv = 0.0
        for h in range(2):
            expd = e_ref[b, h]
            head = slice(h * HEAD_DIM, (h + 1) * HEAD_DIM)
            dscore = (expd.astype(F32) * dot_nt(ext_ref[h], values[h])).astype(BF16)
            dq = dq + dot(dscore, keys[h])
            dk = dk + dot(q_t[head], dscore)
            dv = dv + dot(do_t[head], expd)
        acc_ref[0] = dq if start else acc_ref[0] + dq
        both = jnp.concatenate([dk, dv], axis=0)
        kv_t_ref[b] = jnp.where(group == 0, both, kv_t_ref[b] + both)

    over_blocks(backward)
    dq = acc_ref[0] * inverse
    for p in range(groups):
        dq_ref[:, p * 128 : (p + 1) * 128] = dq[p * span : (p + 1) * span]

    @pl.when(group == group_count - 1)
    def _():
        for b in range(count // per):
            used_block = jnp.where(b < used, kv_t_ref[b], 0.0).T.astype(BF16)
            for i in range(per):
                slot = b * per + i
                result = odd_out_ref if slot % 2 else even_out_ref
                result[slot // 2] = used_block[i * span : (i + 1) * span]


def attention(place, evens, odds, q, do):
    depth = evens.shape[0]
    count = 2 * depth
    seqs, span, _ = q.shape
    single = count * span <= 1024
    groups = PAIRS if single else 2
    wide_spec = pl.BlockSpec((None, span, groups * 128), lambda s, i: (s, 0, i))
    pieces = pl.BlockSpec((depth, None, span, 128), lambda s, i: (0, s, 0, 0))
    if single:
        kernel, scratch = functools.partial(whole_kernel, span, depth), []
    else:
        block = max(512, span)
        blocks = count * span // block
        rows = groups * span
        kernel = functools.partial(loop_kernel, groups, span, block, count)
        scratch = [
            pltpu.VMEM((count * span, 128), BF16),
            pltpu.VMEM((blocks, 2, rows, block), BF16),
            pltpu.VMEM((blocks, 128, block), F32),
            pltpu.VMEM((2, rows, 128), F32),
            pltpu.VMEM((2, rows, 128), F32),
            pltpu.VMEM((2, rows, 256), BF16),
        ]
    return pl.pallas_call(
        kernel,
        grid=(seqs, PAIRS // groups),
        in_specs=[SMEM, pieces, pieces, wide_spec, wide_spec],
        out_specs=[wide_spec] * 2 + [pieces] * 2,
        out_shape=[SHAPE((seqs, span, D), BF16), SHAPE((seqs, span, D), F32)]
        + [SHAPE((depth, seqs, span, 128), BF16)] * 2,
        scratch_shapes=scratch,
        compiler_params=params(),
        cost_estimate=cost(10),
        name="attention",
    )(place, evens, odds, q, do)


def mix_kernel(
    copies,
    calls,
    place_ref,
    *refs,
):
    outs, dqs, refs = refs[:calls], refs[calls : 2 * calls], refs[2 * calls :]
    (
        x_ref,
        g_ref,
        mlp_ref,
        mlp2_ref,
        gain_ref,
        bias_ref,
        add_ref,
        wo_ref,
        wqkv_ref,
        tables_ref,
        output_ref,
        send_ref,
        keep_ref,
        first_ref,
        small_ref,
    ) = refs
    half = D // 2
    x = x_ref[...].astype(F32)
    g = g_ref[...]
    attn = jnp.concatenate([r[...] for r in outs], axis=0)
    normed, _ = normalize(x)
    first_in = normed * wide(gain_ref) + wide(bias_ref)
    tables = repeated(tables_ref, copies)
    parts = []
    for p in range(PAIRS):
        dq = jnp.concatenate([r[:, p * 128 : (p + 1) * 128] for r in dqs], axis=0)
        parts.append(turn(dq * SCALE, tables, -1).astype(BF16))
    grad = jnp.concatenate(parts, axis=1)
    attn_t = attn.astype(F32).T.astype(BF16)
    first_t = first_in.T.astype(BF16)
    own = place_ref[0] == 0
    for i, (left, right) in enumerate(((attn_t, g), (first_t, grad))):
        lower, upper = right[:, :half], right[:, half:]
        send_ref[i] = dot(left, jnp.where(own, upper, lower)).astype(BF16)
        keep_ref[i] = dot(left, jnp.where(own, lower, upper)).astype(BF16)
    small_ref[...] = jnp.zeros_like(small_ref)
    small_ref[0:1] = jnp.sum(grad.astype(F32), axis=0, keepdims=True)
    small_ref[1:2] = jnp.sum(g.astype(F32), axis=0, keepdims=True)
    mlp = mlp_ref[...] + mlp2_ref[...].astype(F32)
    output_ref[...] = (x + (mlp + dot(attn, wo_ref[...])) + wide(add_ref)).astype(BF16)
    first_ref[...] = dot_nt(grad, wqkv_ref[:, :D])


def mix(place, outs, dqs, x, g, mlp, mlp2, gain, bias, add, wo, wqkv, tables):
    rows = x.shape[0]
    calls = len(outs)
    return pl.pallas_call(
        functools.partial(mix_kernel, rows // tables.shape[1], calls),
        in_specs=[SMEM] + [VMEM] * (2 * calls + 10),
        out_specs=[VMEM] * 5,
        out_shape=[
            SHAPE((rows, D), BF16),
            SHAPE((2, D, D // 2), BF16),
            SHAPE((2, D, D // 2), BF16),
            SHAPE((rows, D), F32),
            SHAPE((8, D), F32),
        ],
        compiler_params=params(),
        cost_estimate=cost(3.2),
        name="mix",
    )(place, *outs, *dqs, x, g, mlp, mlp2, gain, bias, add, wo, wqkv, tables)


def finish_kernel(copies, groups, *refs):
    sums = []
    for group in groups:
        total = refs[0][...].astype(F32)
        for ref in refs[1:group]:
            total += ref[...].astype(F32)
        sums.append(total)
        refs = refs[group:]
    (
        extra_ref,
        x_ref,
        g_ref,
        first_ref,
        back_ref,
        back2_ref,
        gain_ref,
        bias_ref,
        gain2_ref,
        wqkv_ref,
        tables_ref,
        tokens_ref,
        weight_ref,
        small_ref,
    ) = refs
    total = jnp.concatenate(sums, axis=0) + extra_ref[...].astype(F32)
    tables = repeated(tables_ref, copies)
    grad = turn(total, key_tables(tables), -1).astype(BF16)
    x = x_ref[...].astype(F32)
    normed, inverse = normalize(x)
    gain = wide(gain_ref)
    first_in = normed * gain + wide(bias_ref)
    weight_ref[...] = dot(first_in.T.astype(BF16), grad).astype(BF16)
    first_grad = first_ref[...] + dot_nt(grad, wqkv_ref[:, D:])
    second_grad = back_ref[...] + back2_ref[...].astype(F32)
    small_ref[...] = jnp.zeros_like(small_ref)
    for i, rows in enumerate((first_grad * normed, first_grad, second_grad * normed, second_grad)):
        small_ref[i : i + 1] = jnp.sum(rows, axis=0, keepdims=True)
    small_ref[4:5, :128] = jnp.sum(grad.astype(F32), axis=0, keepdims=True)
    normed_grad = first_grad * gain + second_grad * wide(gain2_ref)
    mean = jnp.mean(normed_grad, axis=-1, keepdims=True)
    along_rows = jnp.mean(normed_grad * normed, axis=-1, keepdims=True)
    tokens_ref[...] = (g_ref[...].astype(F32) + inverse * (normed_grad - mean - normed * along_rows)).astype(BF16)


def finish(kv_parts, extra, x, g, first, back, back2, gain, bias, gain2, wqkv, tables):
    rows = x.shape[0]
    groups = [len(parts) for parts in kv_parts]
    arrays = [v for parts in kv_parts for v in parts]
    return pl.pallas_call(
        functools.partial(finish_kernel, rows // tables.shape[1], groups),
        in_specs=[VMEM] * (len(arrays) + 11),
        out_specs=[VMEM] * 3,
        out_shape=[SHAPE((rows, D), BF16), SHAPE((D, 128), BF16), SHAPE((8, D), F32)],
        compiler_params=params(),
        cost_estimate=cost(2.4),
        name="finish",
    )(*arrays, extra, x, g, first, back, back2, gain, bias, gain2, wqkv, tables)


def local(
    tokens,
    ln1_gain,
    ln1_bias,
    qkv_weight,
    qkv_bias,
    out_weight,
    ln2_gain,
    ln2_bias,
    fc1_weight,
    fc1_bias,
    fc2_weight,
    out_bias,
    output_grad,
    key_value_grad,
):
    seqs, span, _ = tokens.shape
    rows = seqs * span
    ff = fc1_weight.shape[1]
    count = lax.axis_size("seq")
    batches = lax.axis_size("batch")
    depth = count // 2
    half_depth = depth // 2
    per1, per2 = D // count, ff // count
    own = lax.axis_index("seq").astype(jnp.int32)
    batch = lax.axis_index("batch").astype(jnp.int32)
    y, z = own & 1, own >> 1
    core, xs = batch & 1, batch >> 1
    place = jnp.stack([core, xs, y, z])
    x = tokens.reshape(rows, D)
    g = output_grad.reshape(rows, D)
    over_core = lambda v: flipped(v, "batch", 1)
    over_x = lambda v: flipped(v, "batch", 2)
    over_y = lambda v: flipped(v, "seq", 1)
    flat = lambda v: v.reshape(rows, -1)

    def pair(mine, other, index, axis):
        first = jnp.where(index == 0, mine, other)
        second = jnp.where(index == 0, other, mine)
        return jnp.concatenate([first, second], axis=axis)

    def summed(*parts):
        return tree_sum(parts).astype(BF16)

    x_other, g_other = over_core(x), over_core(g)
    tables = rotary_tables(own * span, span)
    q, kv = project(x, ln1_gain, ln1_bias, qkv_weight, qkv_bias, tables)
    kv3 = kv.reshape(seqs, span, 128)
    evens = [kv3] + [along(kv3, k) for k in range(1, depth)]

    x_fed, g_fed = after((x, g), kv)
    (mlp, mlp_other, slope, in_t), grads2 = feed_forward(
        place, depth, x_fed, x_other, g_fed, g_other, ln2_gain, ln2_bias, fc1_weight, fc1_bias.reshape(1, -1), fc2_weight
    )
    parts2 = [grads2[0]] + [to_owner(grads2[i % half_depth], i) for i in range(1, depth)]
    mlp_come = over_core(mlp_other)
    evens = [kv3] + list(after(evens[1:], slope))
    evens = jnp.stack(evens)
    odds = over_y(evens)
    back, back_other, attn_grad, theirs1, mine1, b1_grad = feed_backward(
        place, count, g, g_other, slope, in_t, fc1_weight, fc2_weight, out_weight
    )
    come1 = over_x(theirs1)
    back_come = over_core(back_other)

    q3, do3 = q.reshape(seqs, span, D), attn_grad.reshape(seqs, span, D)
    out, dq, even, odd = attention(place, evens, odds, q3, do3)
    odd = over_y(odd)

    cut = lambda v: v.reshape(depth, 2, per1 // 2, ff // 2)
    mine1, come1 = after((mine1, come1), out)
    theirs1, mine1 = add_split(place, [(cut(mine1), cut(come1), 2)])
    come1 = over_y(theirs1)

    g_mix, mlp_come = after((g, mlp_come), theirs1)
    output, send, keep, first, small_mix = mix(
        place, [flat(out)], [flat(dq)], x, g_mix, mlp, mlp_come, ln1_gain, ln1_bias, out_bias, out_weight, qkv_weight, tables
    )
    come = over_core(send)
    even, odd = after((even, odd), send)
    kv_sums = [summed(even[k], odd[k]) for k in range(depth)]
    got = [along(kv_sums[k], -k) for k in range(1, depth)]

    parts2 = after(parts2, *kv_sums)
    theirs2, mine2 = sum_split(place, [v.reshape(2, per2, D) for v in parts2])
    come2 = over_y(theirs2)

    mine1, come1 = after((mine1, come1), theirs2)
    cuts1 = add_cut(place, [(mine1, come1)])
    parts1 = [cuts1[0]] + [flipped(cuts1[i], "seq", 2 * i) for i in range(1, depth)]

    keep, come = after((keep, come), cuts1[0])
    cut_o = lambda v: v[0].reshape(depth, 2, per1, D // 2)
    cut_q = lambda v: v[1].reshape(count, 2, per1 // 2, D // 2)
    theirs_o, mine_o, theirs_q, mine_q = add_split(
        place, [(cut_o(keep), cut_o(come), 2), (cut_q(keep), cut_q(come), 1)]
    )
    come_o, come_q = over_y(theirs_o), over_x(theirs_q)

    mine2, come2 = after((mine2, come2), theirs_o)
    sum2 = summed(mine2, come2)
    other2 = over_x(sum2)

    got = after(got, sum2)
    kv_parts = [[v.reshape(-1, 128) for v in (kv_sums[0], *got)]]
    tokens_grad, kv_weight, small = finish(
        kv_parts, flat(key_value_grad), x, g, first, back, back_come, ln1_gain, ln1_bias, ln2_gain, qkv_weight, tables
    )

    b1_half = b1_grad.reshape(-1, 128)
    empty = jnp.zeros_like(b1_half)
    vector = jnp.concatenate(
        [
            jnp.where(core == 0, b1_half, empty),
            jnp.where(core == 0, empty, b1_half),
            small_mix[:2].reshape(-1, 128),
            small[:4].reshape(-1, 128),
            small[4:5, :128],
        ]
    )
    lines = vector.shape[0]

    def packed(weight, vector):
        high = vector.astype(BF16)
        rest = (vector - high.astype(F32)).astype(BF16)
        return jnp.concatenate([weight.astype(BF16), high, rest])

    def unpacked(message):
        message = message.astype(F32)
        return jnp.concatenate([message[:per1], message[per1 : per1 + lines] + message[per1 + lines :]])

    shards = kv_weight.reshape(depth, 2, per1, 128)
    vector16 = packed(kv_weight[:0], vector)
    late_send = jnp.concatenate([take(shards, 1 - y, 1).reshape(-1, 128), vector16])
    late_keep = jnp.concatenate([take(shards, y, 1).reshape(-1, 128), vector16])
    late_come = over_y(late_send)

    mine_o, come_o, mine_q, come_q = after((mine_o, come_o, mine_q, come_q), late_send)
    cuts_o = add_cut(place, [(mine_o, come_o)])
    parts_o = [cuts_o[0]] + [flipped(cuts_o[i], "seq", 2 * i) for i in range(1, depth)]
    cut_q = lambda v: v.reshape(depth, 2, per1 // 2, D // 2)
    theirs_q, mine_q = add_split(place, [(cut_q(mine_q), cut_q(come_q), 2)])
    come_q = over_y(theirs_q)

    late_keep, late_come = after((late_keep, late_come), theirs_q, cuts_o[0])
    unpack = lambda v, at: v[at : at + lines].astype(F32) + v[at + lines :].astype(F32)
    shards = late_keep[: depth * per1].astype(F32) + late_come[: depth * per1].astype(F32)
    shards = shards.reshape(depth, per1, 128)
    vector = unpack(late_keep, depth * per1) + unpack(late_come, depth * per1)
    messages = [packed(take(shards, z ^ i, 0), vector) for i in range(depth)]
    got = [flipped(messages[i], "seq", 2 * i) for i in range(1, depth)]

    sum2, other2 = after((sum2, other2), *messages)
    sum2 = summed(sum2, other2)
    other2 = over_core(sum2)
    parts1 = after(parts1, sum2)
    sum1 = summed(*parts1)
    other1 = over_x(sum1)

    got = after(got, sum1)
    total = tree_sum([unpacked(v) for v in [messages[0], *got]])
    message = packed(total[:per1], total[per1:])
    got = [flipped(message, "batch", i) for i in range(1, batches)]

    parts_o = after(parts_o, message)
    sum_o = summed(*parts_o)
    other_o = over_x(sum_o)
    mine_q, come_q = after((mine_q, come_q), sum_o)
    cuts_q = add_cut(place, [(mine_q, come_q)])
    parts_q = [cuts_q[0]] + [flipped(cuts_q[i], "seq", 2 * i) for i in range(1, depth)]

    sum1, other1 = after((sum1, other1), cuts_q[0])
    sum1 = pair(sum1, other1, xs, 0)
    other1 = over_core(sum1)
    sum_o, other_o = after((sum_o, other_o), sum1)
    sum_o = summed(sum_o, other_o)
    other_o = over_core(sum_o)
    owner = z // half_depth == core
    (other2,) = after((other2,), sum_o)
    fc2_grad = jnp.where(owner, sum2, other2).astype(F32)
    parts_q = after(parts_q, fc2_grad)
    sum_q = summed(*parts_q)
    other_q = over_x(sum_q)
    got = after(got, sum_q)
    total = tree_sum([unpacked(v) for v in [message, *got]])
    (other1,) = after((other1,), total)
    fc1_grad = pair(sum1, other1, core, 1).astype(F32)
    sum_q, other_q = after((sum_q, other_q), fc1_grad)
    sum_q = pair(sum_q, other_q, xs, 0)
    other_q = over_core(sum_q)
    (other_o,) = after((other_o,), sum_q)
    out_grad = pair(sum_o, other_o, core, 1).astype(F32)
    q_grad = pair(sum_q, other_q, core, 1).astype(F32)

    vector = total[per1:]
    b1_lines, d_lines = ff // 128, D // 128
    row = lambda i: vector[b1_lines + i * d_lines : b1_lines + (i + 1) * d_lines].reshape(-1)
    return (
        output.reshape(tokens.shape),
        kv3,
        tokens_grad.reshape(tokens.shape),
        row(2),
        row(3),
        jnp.concatenate([q_grad, total[:per1]], axis=1),
        jnp.concatenate([row(0), vector[-1]]),
        out_grad,
        row(4),
        row(5),
        fc1_grad,
        vector[:b1_lines].reshape(-1),
        fc2_grad,
        row(1),
    )


def solution(mesh):
    part = P("batch", "seq", None)
    whole = P()
    split = P("seq", None)
    return jax.shard_map(
        local,
        mesh=mesh,
        in_specs=(part,) + (whole,) * 11 + (part, part),
        out_specs=(
            part, part, part, whole, whole, split, whole, split, whole, whole, split, whole, split, whole,
        ),
        check_vma=False,
    )
```

profile of v0, /device:TPU:0, one launch (start us, length us, event | category | flops | bytes accessed | tf_op | source)
XLA Modules:
  0.0 207.5 jit_solution(4108334539235507347)
XLA Ops:
  2.3 4.7 %project.1 = (bf16[512,768]{1,0:T(8,128)(2,1)}, bf16[512,128]{1,0:T(8,128)(2,1)}) custom-call(bf16[512,768]{1,0:T(8,128)(2,1)} %bitcast.97, f32[768]{0:T(1024)} %refs_10_.3, f32[768]{0:T(1024)} %refs_11_.1, bf16[768,896]{1,0:T(8,128)(2,1)} %refs_13_.1, f32[896]{0:T(1024)} %add_ref.1, f32[3,128,128]{2,1,0:T(8,128)} %pad_maximum_fusion.3.tables_ref.refs_11_.refs_14_), custom_call_target="tpu_custom_call" | custom-call | flops 6000000000 | tf_op jit(solution)/shard_map/project/pallas_call | solution.py:212
  7.0 3.0 %collective-permute-start = (bf16[4,128,128]{2,1,0:T(8,128)(2,1)}, bf16[4,128,128]{2,1,0:T(8,128)(2,1)S(1)}, u32[]{:S(2)}, u32[]{:S(2)}) collective-permute-start(bf16[4,128,128]{2,1,0:T(8,128)(2,1)} %bitcast.85), channel_id=1, source_target_pairs={{0,2},{1,3},{2,4},{3,5},{4,6},{5,7},{6,0},{7,1},{8,10},{9,11},{10,... | collective-permute-start | bytes 393224 | tf_op jit(solution)/shard_map/ppermute | solution.py:46
  10.0 2.6 %collective-permute-start.1 = (bf16[4,128,128]{2,1,0:T(8,128)(2,1)}, bf16[4,128,128]{2,1,0:T(8,128)(2,1)S(1)}, u32[]{:S(2)}, u32[]{:S(2)}) collective-permute-start(bf16[4,128,128]{2,1,0:T(8,128)(2,1)} %bitcast.86), channel_id=1, source_target_pairs={{0,4},{1,5},{2,6},{3,7},{4,0},{5,1},{6,2},{7,3},{8,12},{9,13},{10,... | collective-permute-start | bytes 393224 | tf_op jit(solution)/shard_map/ppermute | solution.py:46
  12.5 1.3 collective-permute-start.2
  15.6 22.2 %feed_forward.1 = (f32[512,768]{1,0:T(8,128)}, bf16[512,768]{1,0:T(8,128)(2,1)}, bf16[1024,1536]{1,0:T(8,128)(2,1)}, bf16[768,1024]{1,0:T(8,128)(2,1)}, bf16[768...) custom-call(s32[4]{0:T(128)} %pad_add_fusion.place_ref, bf16[512,768]{1,0:T(8,128)(2,1)} %bitcast.98, ...), custom_call_target="tpu_custom_call" | custom-call | flops 24000000000 | tf_op jit(solution)/shard_map/feed_forward/pallas_call | solution.py:343
  37.9 2.5 %collective-permute-start.12 = (bf16[768,768]{1,0:T(8,128)(2,1)}, bf16[768,768]{1,0:T(8,128)(2,1)}, u32[]{:S(2)}, u32[]{:S(2)}) collective-permute-start(bf16[768,768]{1,0:T(8,128)(2,1)} %get-tuple-element.151), channel_id=1, source_target_pairs={{0,2},{1,3},{2,0},{3,1},{12,14},{13,15},{14,12},{15,13},{16,18},{1... | collective-permute-start | bytes 3538952 | tf_op jit(solution)/shard_map/ppermute | solution.py:58
  40.4 1.5 collective-permute-start.14
  42.0 1.6 collective-permute-start.5
  44.7 15.5 %feed_backward.1 = (f32[512,768]{1,0:T(8,128)}, bf16[512,768]{1,0:T(8,128)(2,1)}, bf16[512,768]{1,0:T(8,128)(2,1)}, bf16[8,48,1536]{2,1,0:T(8,128)(2,1)}, bf16[8...) custom-call(s32[4]{0:T(128)} %pad_add_fusion.place_ref, bf16[512,768]{1,0:T(8,128)(2,1)} %bitcast.103, ...), custom_call_target="tpu_custom_call" | custom-call | flops 19200000000 | tf_op jit(solution)/shard_map/feed_backward/pallas_call | solution.py:449
  60.2 1.6 collective-permute-start.7
  61.8 1.3 collective-permute-start.13
  63.1 23.9 %attention.1 = (bf16[4,128,768]{2,1,0:T(8,128)(2,1)}, f32[4,128,768]{2,1,0:T(8,128)}, bf16[4,4,128,128]{3,2,1,0:T(8,128)(2,1)}, bf16[4,4,128,128]{3,2,1,0:T(8,128)(2,1)}) custom-call(s32[4]{0:T(128)} %pad_add_fusion.place_ref, bf16[4,4,128,128]{3,2,1,0:T(8,128)(2,1)} %copy-done.3, bf16[4,4,128,128]{3,2,1,0:T(8,128)(2,1)} %copy-done.17, ...), custom_call_target="tpu_custom_call" | custom-call | flops 30000001024 | tf_op jit(solution)/shard_map/attention/pallas_call | solution.py:700
  87.0 1.4 collective-permute-done.7
  89.4 2.9 %add_split.3 = (bf16[4,48,1536]{2,1,0:T(8,128)(2,1)}, bf16[4,48,1536]{2,1,0:T(8,128)(2,1)}) custom-call(s32[4]{0:T(128)} %pad_add_fusion.place_ref, bf16[4,2,48,1536]{3,2,1,0:T(8,128)(2,1)} %bitcast.115, bf16[4,2,48,1536]{3,2,1,0:T(8,128)(2,1)} %bitcast.95), custom_call_target="tpu_custom_call" | custom-call | flops 3600000000 | tf_op jit(solution)/shard_map/add_split/pallas_call | solution.py:140
  93.2 8.7 %mix.1 = (bf16[512,768]{1,0:T(8,128)(2,1)}, bf16[2,768,384]{2,1,0:T(8,128)(2,1)}, bf16[2,768,384]{2,1,0:T(8,128)(2,1)}, f32[512,768]{1,0:T(8,128)}, f32[8,768]{1,0:T(8,128)}) custom-call(s32[4]{0:T(128)} %pad_add_fusion.place_ref, bf16[512,768]{1,0:T(8,128)(2,1)} %bitcast.119, f32[512,768]{1,0:T(8,128)} %bitcast.114, bf16[512,768]{1,0:T(8,128)(2,1)} %bitcast.99, ...), custom_call_target="tpu_custom_call" | custom-call | flops 9600000000 | tf_op jit(solution)/shard_map/mix/pallas_call | solution.py:768
  102.0 3.4 %collective-permute-start.16 = (bf16[2,768,384]{2,1,0:T(8,128)(2,1)}, bf16[2,768,384]{2,1,0:T(8,128)(2,1)S(1)}, u32[]{:S(2)}, u32[]{:S(2)}) collective-permute-start(bf16[2,768,384]{2,1,0:T(8,128)(2,1)} %get-tuple-element.147), channel_id=1, source_target_pairs={{0,8},{8,0},{16,24},{24,16},{1,9},{9,1},{17,25},{25,17},{2,10},{10... | collective-permute-start | bytes 3538952 | tf_op jit(solution)/shard_map/ppermute | solution.py:41
  107.1 1.7 collective-permute-start.9
  108.8 1.4 collective-permute-start.10
  110.9 3.9 %sum_split.1 = (bf16[384,768]{1,0:T(8,128)(2,1)}, bf16[384,768]{1,0:T(8,128)(2,1)}) custom-call(s32[4]{0:T(128)} %pad_add_fusion.place_ref, bf16[2,384,768]{2,1,0:T(8,128)(2,1)} %bitcast.24.refs_0_, bf16[2,384,768]{2,1,0:T(8,128)(2,1)} %bitcast.25.refs_1_, bf16[2,384,768]{2,1,0:T(8,128)(2,1)} %bitcast.26.refs_2_, bf16[2,384,768]{2,1,0:T(8,128)(2,1)} %bitcast.27.refs_3_), custom_call_target="tpu_custom_call" | custom-call | flops 4800000000 | tf_op jit(solution)/shard_map/sum_split/pallas_call | solution.py:185
  114.8 6.3 %collective-permute-done.17.refs_1_ = bf16[4,48,1536]{2,1,0:T(8,128)(2,1)} collective-permute-done((bf16[4,48,1536]{2,1,0:T(8,128)(2,1)}, bf16[4,48,1536]{2,1,0:T(8,128)(2,1)}, u32[]{:S(2)}, u32[]{:S(2)}) %collective-permute-start.17) | collective-permute-done | bytes 589856 | tf_op jit(solution)/shard_map/ppermute | solution.py:41
  121.1 1.5 collective-permute-start.11
  122.7 2.3 %add_cut.3 = (bf16[48,1536]{1,0:T(8,128)(2,1)}, bf16[48,1536]{1,0:T(8,128)(2,1)}, bf16[48,1536]{1,0:T(8,128)(2,1)}, bf16[48,1536]{1,0:T(8,128)(2,1)}) custom-call(s32[4]{0:T(128)} %pad_add_fusion.place_ref, bf16[4,48,1536]{2,1,0:T(8,128)(2,1)} %get-tuple-element.160.refs_0_, bf16[4,48,1536]{2,1,0:T(8,128)(2,1)} %collective-permute-done.17.refs_1_), custom_call_target="tpu_custom_call" | custom-call | flops 2400000000 | tf_op jit(solution)/shard_map/add_cut/pallas_call | solution.py:167
  125.8 1.1 fusion.26
  126.9 1.1 fusion.25
  128.1 2.7 %add_split.4 = (bf16[4,96,384]{2,1,0:T(8,128)(2,1)}, bf16[4,96,384]{2,1,0:T(8,128)(2,1)}, bf16[8,48,384]{2,1,0:T(8,128)(2,1)}, bf16[8,48,384]{2,1,0:T(8,128)(2,1)}) custom-call(s32[4]{0:T(128)} %pad_add_fusion.place_ref, bf16[4,2,96,384]{3,2,1,0:T(8,128)(2,1)} %bitcast.77, bf16[4,2,96,384]{3,2,1,0:T(8,128)(2,1)} %bitcast.79, ...), custom_call_target="tpu_custom_call" | custom-call | flops 3600000000 | tf_op jit(solution)/shard_map/add_split/pallas_call | solution.py:140
  130.8 8.4 %collective-permute-done.15 = bf16[384,768]{1,0:T(8,128)(2,1)S(1)} collective-permute-done((bf16[384,768]{1,0:T(8,128)(2,1)S(1)}, bf16[384,768]{1,0:T(8,128)(2,1)S(1)}, u32[]{:S(2)}, u32[]{:S(2)}) %collective-permute-start.15) | collective-permute-done | bytes 589856 | tf_op jit(solution)/shard_map/ppermute | solution.py:41
  139.6 2.6 %collective-permute-start.26 = (bf16[48,1536]{1,0:T(8,128)(2,1)}, bf16[48,1536]{1,0:T(8,128)(2,1)S(1)}, u32[]{:S(2)}, u32[]{:S(2)}) collective-permute-start(bf16[48,1536]{1,0:T(8,128)(2,1)} %get-tuple-element.191), channel_id=1, source_target_pairs={{0,4},{1,5},{2,6},{3,7},{4,0},{5,1},{6,2},{7,3},{8,12},{9,13},{10,... | collective-permute-start | bytes 442376 | tf_op jit(solution)/shard_map/ppermute | solution.py:41
  142.3 1.5 collective-permute-start.27
  144.7 6.3 %finish.1 = (bf16[512,768]{1,0:T(8,128)(2,1)}, bf16[768,128]{1,0:T(8,128)(2,1)}, f32[8,768]{1,0:T(8,128)}) custom-call(bf16[512,128]{1,0:T(8,128)(2,1)} %bitcast.84, bf16[512,128]{1,0:T(8,128)(2,1)} %bitcast.108, bf16[512,128]{1,0:T(8,128)(2,1)} %bitcast.109, bf16[512,128]{1,0:T(8,128)(2,1)} %bitcast.110, bf16[512,128]{1,0:T(8,128)(2,1)} %bitcast.107, ...), custom_call_target="tpu_custom_call" | custom-call | flops 7200000000 | tf_op jit(solution)/shard_map/finish/pallas_call | solution.py:833
  155.1 4.8 %collective-permute-done.20.refs_1_ = bf16[4,96,384]{2,1,0:T(8,128)(2,1)S(1)} collective-permute-done((bf16[4,96,384]{2,1,0:T(8,128)(2,1)S(1)}, bf16[4,96,384]{2,1,0:T(8,128)(2,1)S(1)}, u32[]{:S(2)}, u32[]{:S(2)}) %collective-permute-start.20) | collective-permute-done | bytes 294944 | tf_op jit(solution)/shard_map/ppermute | solution.py:41
  159.9 2.3 %collective-permute-done.21 = bf16[8,48,384]{2,1,0:T(8,128)(2,1)S(1)} collective-permute-done((bf16[8,48,384]{2,1,0:T(8,128)(2,1)S(1)}, bf16[8,48,384]{2,1,0:T(8,128)(2,1)S(1)}, u32[]{:S(2)}, u32[]{:S(2)}) %collective-permute-start.21) | collective-permute-done | bytes 294944 | tf_op jit(solution)/shard_map/ppermute | solution.py:41
  162.2 1.8 collective-permute-start.19
  164.1 1.8 add_split.5
  165.9 1.8 add_cut.4
  167.9 4.7 %collective-permute-done.28 = bf16[384,768]{1,0:T(8,128)(2,1)S(1)} collective-permute-done((bf16[384,768]{1,0:T(8,128)(2,1)S(1)}, bf16[384,768]{1,0:T(8,128)(2,1)S(1)}, u32[]{:S(2)}, u32[]{:S(2)}) %collective-permute-start.28) | collective-permute-done | bytes 589856 | tf_op jit(solution)/shard_map/ppermute | solution.py:41
  173.3 1.9 collective-permute-start.24
  175.2 1.3 collective-permute-start.32
  176.4 1.2 collective-permute-start.33
  177.7 1.2 collective-permute-start.34
  179.0 3.9 %collective-permute-start.35 = (bf16[96,384]{1,0:T(8,128)(2,1)S(1)}, bf16[96,384]{1,0:T(8,128)(2,1)S(1)}, u32[]{:S(2)}, u32[]{:S(2)}) collective-permute-start(bf16[96,384]{1,0:T(8,128)(2,1)S(1)} %copy-done.27), channel_id=1, source_target_pairs={{0,6},{1,7},{2,4},{3,5},{4,2},{5,3},{6,0},{7,1},{8,14},{9,15},{10,... | collective-permute-start | bytes 221192 | tf_op jit(solution)/shard_map/ppermute | solution.py:41
  185.3 1.4 collective-permute-start.41
  187.5 1.7 add_cut.5
  189.2 2.3 %collective-permute-done.41 = bf16[48,1536]{1,0:T(8,128)(2,1)S(1)} collective-permute-done((bf16[48,1536]{1,0:T(8,128)(2,1)S(1)}, bf16[48,1536]{1,0:T(8,128)(2,1)S(1)}, u32[]{:S(2)}, u32[]{:S(2)}) %collective-permute-start.41) | collective-permute-done | bytes 147488 | tf_op jit(solution)/shard_map/ppermute | solution.py:41
  192.3 2.6 %collective-permute-start.37 = (bf16[48,384]{1,0:T(8,128)(2,1)S(1)}, bf16[48,384]{1,0:T(8,128)(2,1)S(1)}, u32[]{:S(2)}, u32[]{:S(2)}) collective-permute-start(bf16[48,384]{1,0:T(8,128)(2,1)S(1)} %copy-done.31), channel_id=1, source_target_pairs={{0,4},{1,5},{2,6},{3,7},{4,0},{5,1},{6,2},{7,3},{8,12},{9,13},{10,... | collective-permute-start | bytes 110600 | tf_op jit(solution)/shard_map/ppermute | solution.py:41
  194.9 1.2 collective-permute-start.38
  197.2 1.1 collective-permute-start.43
  198.4 2.3 %collective-permute-done.38 = bf16[48,384]{1,0:T(8,128)(2,1)S(1)} collective-permute-done((bf16[48,384]{1,0:T(8,128)(2,1)S(1)}, bf16[48,384]{1,0:T(8,128)(2,1)S(1)}, u32[]{:S(2)}, u32[]{:S(2)}) %collective-permute-start.38) | collective-permute-done | bytes 36896 | tf_op jit(solution)/shard_map/ppermute | solution.py:41
  203.6 1.1 maximum_convert_fusion
  (197 shorter events, 26.7 us)
Async XLA Ops:
  0.6 13.8 %collective-permute-start.3 = (bf16[512,768]{1,0:T(8,128)(2,1)}, bf16[512,768]{1,0:T(8,128)(2,1)S(1)}, u32[]{:S(2)}, u32[]{:S(2)}) collective-permute-start(bf16[512,768]{1,0:T(8,128)(2,1)} %bitcast.96), channel_id=1, source_target_pairs={{0,8},{8,0},{16,24},{24,16},{1,9},{9,1},{17,25},{25,17},{2,10},{10... | collective-permute-start | bytes 2359304 | tf_op jit(solution)/shard_map/ppermute | solution.py:41
  1.2 13.3 %collective-permute-start.4 = (bf16[512,768]{1,0:T(8,128)(2,1)}, bf16[512,768]{1,0:T(8,128)(2,1)S(1)}, u32[]{:S(2)}, u32[]{:S(2)}) collective-permute-start(bf16[512,768]{1,0:T(8,128)(2,1)} %bitcast.101), channel_id=1, source_target_pairs={{0,8},{8,0},{16,24},{24,16},{1,9},{9,1},{17,25},{25,17},{2,10},{10... | collective-permute-start | bytes 2359304 | tf_op jit(solution)/shard_map/ppermute | solution.py:41
  7.0 34.9 %collective-permute-start = (bf16[4,128,128]{2,1,0:T(8,128)(2,1)}, bf16[4,128,128]{2,1,0:T(8,128)(2,1)S(1)}, u32[]{:S(2)}, u32[]{:S(2)}) collective-permute-start(bf16[4,128,128]{2,1,0:T(8,128)(2,1)} %bitcast.85), channel_id=1, source_target_pairs={{0,2},{1,3},{2,4},{3,5},{4,6},{5,7},{6,0},{7,1},{8,10},{9,11},{10,... | collective-permute-start | bytes 393224 | tf_op jit(solution)/shard_map/ppermute | solution.py:46
  10.0 31.9 %collective-permute-start.1 = (bf16[4,128,128]{2,1,0:T(8,128)(2,1)}, bf16[4,128,128]{2,1,0:T(8,128)(2,1)S(1)}, u32[]{:S(2)}, u32[]{:S(2)}) collective-permute-start(bf16[4,128,128]{2,1,0:T(8,128)(2,1)} %bitcast.86), channel_id=1, source_target_pairs={{0,4},{1,5},{2,6},{3,7},{4,0},{5,1},{6,2},{7,3},{8,12},{9,13},{10,... | collective-permute-start | bytes 393224 | tf_op jit(solution)/shard_map/ppermute | solution.py:46
  12.5 29.3 %collective-permute-start.2 = (bf16[4,128,128]{2,1,0:T(8,128)(2,1)}, bf16[4,128,128]{2,1,0:T(8,128)(2,1)S(1)}, u32[]{:S(2)}, u32[]{:S(2)}) collective-permute-start(bf16[4,128,128]{2,1,0:T(8,128)(2,1)} %bitcast.87), channel_id=1, source_target_pairs={{0,6},{1,7},{2,0},{3,1},{4,2},{5,3},{6,4},{7,5},{8,14},{9,15},{10,... | collective-permute-start | bytes 393224 | tf_op jit(solution)/shard_map/ppermute | solution.py:46
  15.6 26.3 %copy-start.6 = (bf16[512,128]{1,0:T(8,128)(2,1)S(1)}, bf16[512,128]{1,0:T(8,128)(2,1)}, u32[]{:S(2)}) copy-start(bf16[512,128]{1,0:T(8,128)(2,1)} %get-tuple-element.123) | copy-start | bytes 393220
  37.9 69.2 %collective-permute-start.12 = (bf16[768,768]{1,0:T(8,128)(2,1)}, bf16[768,768]{1,0:T(8,128)(2,1)}, u32[]{:S(2)}, u32[]{:S(2)}) collective-permute-start(bf16[768,768]{1,0:T(8,128)(2,1)} %get-tuple-element.151), channel_id=1, source_target_pairs={{0,2},{1,3},{2,0},{3,1},{12,14},{13,15},{14,12},{15,13},{16,18},{1... | collective-permute-start | bytes 3538952 | tf_op jit(solution)/shard_map/ppermute | solution.py:58
  40.4 68.4 %collective-permute-start.14 = (bf16[768,768]{1,0:T(8,128)(2,1)}, bf16[768,768]{1,0:T(8,128)(2,1)}, u32[]{:S(2)}, u32[]{:S(2)}) collective-permute-start(bf16[768,768]{1,0:T(8,128)(2,1)} %get-tuple-element.151), channel_id=1, source_target_pairs={{4,2},{5,3},{6,0},{7,1},{8,14},{9,15},{10,12},{11,13},{20,18},{21,... | collective-permute-start | bytes 3538952 | tf_op jit(solution)/shard_map/ppermute | solution.py:58
  42.0 18.2 %copy-start.3 = (bf16[4,4,128,128]{3,2,1,0:T(8,128)(2,1)}, bf16[4,4,128,128]{3,2,1,0:T(8,128)(2,1)S(1)}, u32[]{:S(2)}) copy-start(bf16[4,4,128,128]{3,2,1,0:T(8,128)(2,1)S(1)} %pad_maximum_fusion.refs_0_) | copy-start | bytes 1572868
  42.0 19.8 %collective-permute-start.5 = (bf16[4,4,128,128]{3,2,1,0:T(8,128)(2,1)S(1)}, bf16[4,4,128,128]{3,2,1,0:T(8,128)(2,1)S(1)}, u32[]{:S(2)}, u32[]{:S(2)}) collective-permute-start(bf16[4,4,128,128]{3,2,1,0:T(8,128)(2,1)S(1)} %pad_maximum_fusion.refs_0_), channel_id=1, source_target_pairs={{0,1},{1,0},{2,3},{3,2},{4,5},{5,4},{6,7},{7,6},{8,9},{9,8},{10,11... | collective-permute-start | bytes 1572872 | tf_op jit(solution)/shard_map/ppermute | solution.py:41
  43.6 48.8 %collective-permute-start.6 = (bf16[512,768]{1,0:T(8,128)(2,1)}, bf16[512,768]{1,0:T(8,128)(2,1)S(1)}, u32[]{:S(2)}, u32[]{:S(2)}) collective-permute-start(bf16[512,768]{1,0:T(8,128)(2,1)} %get-tuple-element.135), channel_id=1, source_target_pairs={{0,8},{8,0},{16,24},{24,16},{1,9},{9,1},{17,25},{25,17},{2,10},{10... | collective-permute-start | bytes 2359304 | tf_op jit(solution)/shard_map/ppermute | solution.py:41
  60.2 28.2 %collective-permute-start.7 = (bf16[8,48,1536]{2,1,0:T(8,128)(2,1)}, bf16[8,48,1536]{2,1,0:T(8,128)(2,1)S(1)}, u32[]{:S(2)}, u32[]{:S(2)}) collective-permute-start(bf16[8,48,1536]{2,1,0:T(8,128)(2,1)} %get-tuple-element.137), channel_id=1, source_target_pairs={{0,16},{8,24},{16,0},{24,8},{1,17},{9,25},{17,1},{25,9},{2,18},{10... | collective-permute-start | bytes 3538952 | tf_op jit(solution)/shard_map/ppermute | solution.py:41
  61.8 45.3 %collective-permute-start.13 = (bf16[768,768]{1,0:T(8,128)(2,1)}, bf16[768,768]{1,0:T(8,128)(2,1)}, u32[]{:S(2)}, u32[]{:S(2)}) collective-permute-start(bf16[768,768]{1,0:T(8,128)(2,1)} %get-tuple-element.152), channel_id=1, source_target_pairs={{4,0},{5,1},{6,2},{7,3},{8,12},{9,13},{10,14},{11,15},{20,16},{21,... | collective-permute-start | bytes 3538952 | tf_op jit(solution)/shard_map/ppermute | solution.py:58
  88.4 17.1 %collective-permute-start.8 = (bf16[4,4,128,128]{3,2,1,0:T(8,128)(2,1)}, bf16[4,4,128,128]{3,2,1,0:T(8,128)(2,1)S(1)}, u32[]{:S(2)}, u32[]{:S(2)}) collective-permute-start(bf16[4,4,128,128]{3,2,1,0:T(8,128)(2,1)} %get-tuple-element.146), channel_id=1, source_target_pairs={{0,1},{1,0},{2,3},{3,2},{4,5},{5,4},{6,7},{7,6},{8,9},{9,8},{10,11... | collective-permute-start | bytes 1572872 | tf_op jit(solution)/shard_map/ppermute | solution.py:41
  102.0 23.0 %collective-permute-start.16 = (bf16[2,768,384]{2,1,0:T(8,128)(2,1)}, bf16[2,768,384]{2,1,0:T(8,128)(2,1)S(1)}, u32[]{:S(2)}, u32[]{:S(2)}) collective-permute-start(bf16[2,768,384]{2,1,0:T(8,128)(2,1)} %get-tuple-element.147), channel_id=1, source_target_pairs={{0,8},{8,0},{16,24},{24,16},{1,9},{9,1},{17,25},{25,17},{2,10},{10... | collective-permute-start | bytes 3538952 | tf_op jit(solution)/shard_map/ppermute | solution.py:41
  105.4 15.7 %collective-permute-start.17 = (bf16[4,48,1536]{2,1,0:T(8,128)(2,1)}, bf16[4,48,1536]{2,1,0:T(8,128)(2,1)}, u32[]{:S(2)}, u32[]{:S(2)}) collective-permute-start(bf16[4,48,1536]{2,1,0:T(8,128)(2,1)} %get-tuple-element.140), channel_id=1, source_target_pairs={{0,1},{1,0},{2,3},{3,2},{4,5},{5,4},{6,7},{7,6},{8,9},{9,8},{10,11... | collective-permute-start | bytes 1769480 | tf_op jit(solution)/shard_map/ppermute | solution.py:41
  107.1 36.7 %collective-permute-start.18 = (bf16[512,768]{1,0:T(8,128)(2,1)S(1)}, bf16[512,768]{1,0:T(8,128)(2,1)S(1)}, u32[]{:S(2)}, u32[]{:S(2)}) collective-permute-start(bf16[512,768]{1,0:T(8,128)(2,1)S(1)} %copy-done.11), channel_id=1, source_target_pairs={{0,8},{8,0},{16,24},{24,16},{1,9},{9,1},{17,25},{25,17},{2,10},{10... | collective-permute-start | bytes 2359304 | tf_op jit(solution)/shard_map/ppermute | solution.py:41
  107.1 32.5 %collective-permute-start.9 = (bf16[4,128,128]{2,1,0:T(8,128)(2,1)S(1)}, bf16[4,128,128]{2,1,0:T(8,128)(2,1)S(1)}, u32[]{:S(2)}, u32[]{:S(2)}) collective-permute-start(bf16[4,128,128]{2,1,0:T(8,128)(2,1)S(1)} %get-tuple-element.246), channel_id=1, source_target_pairs={{0,6},{1,7},{2,0},{3,1},{4,2},{5,3},{6,4},{7,5},{8,14},{9,15},{10,... | collective-permute-start | bytes 393224 | tf_op jit(solution)/shard_map/ppermute | solution.py:46
  108.8 33.5 %collective-permute-start.10 = (bf16[4,128,128]{2,1,0:T(8,128)(2,1)S(1)}, bf16[4,128,128]{2,1,0:T(8,128)(2,1)S(1)}, u32[]{:S(2)}, u32[]{:S(2)}) collective-permute-start(bf16[4,128,128]{2,1,0:T(8,128)(2,1)S(1)} %get-tuple-element.245), channel_id=1, source_target_pairs={{0,4},{1,5},{2,6},{3,7},{4,0},{5,1},{6,2},{7,3},{8,12},{9,13},{10,... | collective-permute-start | bytes 393224 | tf_op jit(solution)/shard_map/ppermute | solution.py:46
  121.1 22.7 %collective-permute-start.11 = (bf16[4,128,128]{2,1,0:T(8,128)(2,1)S(1)}, bf16[4,128,128]{2,1,0:T(8,128)(2,1)S(1)}, u32[]{:S(2)}, u32[]{:S(2)}) collective-permute-start(bf16[4,128,128]{2,1,0:T(8,128)(2,1)S(1)} %get-tuple-element.244), channel_id=1, source_target_pairs={{0,2},{1,3},{2,4},{3,5},{4,6},{5,7},{6,0},{7,1},{8,10},{9,11},{10,... | collective-permute-start | bytes 393224 | tf_op jit(solution)/shard_map/ppermute | solution.py:46
  124.9 14.2 %collective-permute-start.15 = (bf16[384,768]{1,0:T(8,128)(2,1)S(1)}, bf16[384,768]{1,0:T(8,128)(2,1)S(1)}, u32[]{:S(2)}, u32[]{:S(2)}) collective-permute-start(bf16[384,768]{1,0:T(8,128)(2,1)S(1)} %copy-done.16), channel_id=1, source_target_pairs={{0,1},{1,0},{2,3},{3,2},{4,5},{5,4},{6,7},{7,6},{8,9},{9,8},{10,11... | collective-permute-start | bytes 1769480 | tf_op jit(solution)/shard_map/ppermute | solution.py:41
  139.2 34.1 %collective-permute-start.25 = (bf16[48,1536]{1,0:T(8,128)(2,1)}, bf16[48,1536]{1,0:T(8,128)(2,1)S(1)}, u32[]{:S(2)}, u32[]{:S(2)}) collective-permute-start(bf16[48,1536]{1,0:T(8,128)(2,1)} %get-tuple-element.190), channel_id=1, source_target_pairs={{0,2},{1,3},{2,0},{3,1},{4,6},{5,7},{6,4},{7,5},{8,10},{9,11},{10,... | collective-permute-start | bytes 442376 | tf_op jit(solution)/shard_map/ppermute | solution.py:41
  139.6 35.5 %collective-permute-start.26 = (bf16[48,1536]{1,0:T(8,128)(2,1)}, bf16[48,1536]{1,0:T(8,128)(2,1)S(1)}, u32[]{:S(2)}, u32[]{:S(2)}) collective-permute-start(bf16[48,1536]{1,0:T(8,128)(2,1)} %get-tuple-element.191), channel_id=1, source_target_pairs={{0,4},{1,5},{2,6},{3,7},{4,0},{5,1},{6,2},{7,3},{8,12},{9,13},{10,... | collective-permute-start | bytes 442376 | tf_op jit(solution)/shard_map/ppermute | solution.py:41
  142.3 34.2 %collective-permute-start.27 = (bf16[48,1536]{1,0:T(8,128)(2,1)}, bf16[48,1536]{1,0:T(8,128)(2,1)S(1)}, u32[]{:S(2)}, u32[]{:S(2)}) collective-permute-start(bf16[48,1536]{1,0:T(8,128)(2,1)} %get-tuple-element.192), channel_id=1, source_target_pairs={{0,6},{1,7},{2,4},{3,5},{4,2},{5,3},{6,0},{7,1},{8,14},{9,15},{10,... | collective-permute-start | bytes 442376 | tf_op jit(solution)/shard_map/ppermute | solution.py:41
  152.4 7.5 %collective-permute-start.20 = (bf16[4,96,384]{2,1,0:T(8,128)(2,1)S(1)}, bf16[4,96,384]{2,1,0:T(8,128)(2,1)S(1)}, u32[]{:S(2)}, u32[]{:S(2)}) collective-permute-start(bf16[4,96,384]{2,1,0:T(8,128)(2,1)S(1)} %copy-done.19), channel_id=1, source_target_pairs={{0,1},{1,0},{2,3},{3,2},{4,5},{5,4},{6,7},{7,6},{8,9},{9,8},{10,11... | collective-permute-start | bytes 884744 | tf_op jit(solution)/shard_map/ppermute | solution.py:41
  153.2 9.0 %collective-permute-start.21 = (bf16[8,48,384]{2,1,0:T(8,128)(2,1)S(1)}, bf16[8,48,384]{2,1,0:T(8,128)(2,1)S(1)}, u32[]{:S(2)}, u32[]{:S(2)}) collective-permute-start(bf16[8,48,384]{2,1,0:T(8,128)(2,1)S(1)} %copy-done.18), channel_id=1, source_target_pairs={{0,16},{8,24},{16,0},{24,8},{1,17},{9,25},{17,1},{25,9},{2,18},{10... | collective-permute-start | bytes 884744 | tf_op jit(solution)/shard_map/ppermute | solution.py:41
  159.9 12.7 %collective-permute-start.28 = (bf16[384,768]{1,0:T(8,128)(2,1)S(1)}, bf16[384,768]{1,0:T(8,128)(2,1)S(1)}, u32[]{:S(2)}, u32[]{:S(2)}) collective-permute-start(bf16[384,768]{1,0:T(8,128)(2,1)S(1)} %add_convert_fusion.1), channel_id=1, source_target_pairs={{0,16},{8,24},{16,0},{24,8},{1,17},{9,25},{17,1},{25,9},{2,18},{10... | collective-permute-start | bytes 1769480 | tf_op jit(solution)/shard_map/ppermute | solution.py:41
  162.2 5.4 %collective-permute-start.19 = (bf16[506,128]{1,0:T(8,128)(2,1)S(1)}, bf16[506,128]{1,0:T(8,128)(2,1)S(1)}, u32[]{:S(2)}, u32[]{:S(2)}) collective-permute-start(bf16[506,128]{1,0:T(8,128)(2,1)S(1)} %get-tuple-element.276), channel_id=1, source_target_pairs={{0,1},{1,0},{2,3},{3,2},{4,5},{5,4},{6,7},{7,6},{8,9},{9,8},{10,11... | collective-permute-start | bytes 388616 | tf_op jit(solution)/shard_map/ppermute | solution.py:41
  167.8 9.9 %collective-permute-start.22 = (bf16[218,128]{1,0:T(8,128)(2,1)S(1)}, bf16[218,128]{1,0:T(8,128)(2,1)S(1)}, u32[]{:S(2)}, u32[]{:S(2)}) collective-permute-start(bf16[218,128]{1,0:T(8,128)(2,1)S(1)} %get-tuple-element.273), channel_id=1, source_target_pairs={{0,2},{1,3},{2,0},{3,1},{4,6},{5,7},{6,4},{7,5},{8,10},{9,11},{10,... | collective-permute-start | bytes 167432 | tf_op jit(solution)/shard_map/ppermute | solution.py:41
  172.6 6.3 %collective-permute-start.23 = (bf16[218,128]{1,0:T(8,128)(2,1)S(1)}, bf16[218,128]{1,0:T(8,128)(2,1)S(1)}, u32[]{:S(2)}, u32[]{:S(2)}) collective-permute-start(bf16[218,128]{1,0:T(8,128)(2,1)S(1)} %get-tuple-element.274), channel_id=1, source_target_pairs={{0,4},{1,5},{2,6},{3,7},{4,0},{5,1},{6,2},{7,3},{8,12},{9,13},{10,... | collective-permute-start | bytes 167432 | tf_op jit(solution)/shard_map/ppermute | solution.py:41
  173.3 9.6 %collective-permute-start.24 = (bf16[218,128]{1,0:T(8,128)(2,1)S(1)}, bf16[218,128]{1,0:T(8,128)(2,1)S(1)}, u32[]{:S(2)}, u32[]{:S(2)}) collective-permute-start(bf16[218,128]{1,0:T(8,128)(2,1)S(1)} %get-tuple-element.275), channel_id=1, source_target_pairs={{0,6},{1,7},{2,4},{3,5},{4,2},{5,3},{6,0},{7,1},{8,14},{9,15},{10,... | collective-permute-start | bytes 167432 | tf_op jit(solution)/shard_map/ppermute | solution.py:41
  175.2 11.5 %collective-permute-start.32 = (bf16[4,48,384]{2,1,0:T(8,128)(2,1)S(1)}, bf16[4,48,384]{2,1,0:T(8,128)(2,1)S(1)}, u32[]{:S(2)}, u32[]{:S(2)}) collective-permute-start(bf16[4,48,384]{2,1,0:T(8,128)(2,1)S(1)} %copy-done.22), channel_id=1, source_target_pairs={{0,1},{1,0},{2,3},{3,2},{4,5},{5,4},{6,7},{7,6},{8,9},{9,8},{10,11... | collective-permute-start | bytes 442376 | tf_op jit(solution)/shard_map/ppermute | solution.py:41
  176.4 6.8 %collective-permute-start.33 = (bf16[96,384]{1,0:T(8,128)(2,1)S(1)}, bf16[96,384]{1,0:T(8,128)(2,1)S(1)}, u32[]{:S(2)}, u32[]{:S(2)}) collective-permute-start(bf16[96,384]{1,0:T(8,128)(2,1)S(1)} %copy-done.29), channel_id=1, source_target_pairs={{0,2},{1,3},{2,0},{3,1},{4,6},{5,7},{6,4},{7,5},{8,10},{9,11},{10,... | collective-permute-start | bytes 221192 | tf_op jit(solution)/shard_map/ppermute | solution.py:41
  177.7 6.6 %collective-permute-start.34 = (bf16[96,384]{1,0:T(8,128)(2,1)S(1)}, bf16[96,384]{1,0:T(8,128)(2,1)S(1)}, u32[]{:S(2)}, u32[]{:S(2)}) collective-permute-start(bf16[96,384]{1,0:T(8,128)(2,1)S(1)} %copy-done.28), channel_id=1, source_target_pairs={{0,4},{1,5},{2,6},{3,7},{4,0},{5,1},{6,2},{7,3},{8,12},{9,13},{10,... | collective-permute-start | bytes 221192 | tf_op jit(solution)/shard_map/ppermute | solution.py:41
  179.0 6.3 %collective-permute-start.35 = (bf16[96,384]{1,0:T(8,128)(2,1)S(1)}, bf16[96,384]{1,0:T(8,128)(2,1)S(1)}, u32[]{:S(2)}, u32[]{:S(2)}) collective-permute-start(bf16[96,384]{1,0:T(8,128)(2,1)S(1)} %copy-done.27), channel_id=1, source_target_pairs={{0,6},{1,7},{2,4},{3,5},{4,2},{5,3},{6,0},{7,1},{8,14},{9,15},{10,... | collective-permute-start | bytes 221192 | tf_op jit(solution)/shard_map/ppermute | solution.py:41
  183.1 17.7 %collective-permute-start.29 = (bf16[218,128]{1,0:T(8,128)(2,1)S(1)}, bf16[218,128]{1,0:T(8,128)(2,1)S(1)}, u32[]{:S(2)}, u32[]{:S(2)}) collective-permute-start(bf16[218,128]{1,0:T(8,128)(2,1)S(1)} %get-tuple-element.270), channel_id=1, source_target_pairs={{0,8},{8,0},{16,24},{24,16},{1,9},{9,1},{17,25},{25,17},{2,10},{10... | collective-permute-start | bytes 167432 | tf_op jit(solution)/shard_map/ppermute | solution.py:41
  183.2 17.6 %collective-permute-start.30 = (bf16[218,128]{1,0:T(8,128)(2,1)S(1)}, bf16[218,128]{1,0:T(8,128)(2,1)S(1)}, u32[]{:S(2)}, u32[]{:S(2)}) collective-permute-start(bf16[218,128]{1,0:T(8,128)(2,1)S(1)} %get-tuple-element.270), channel_id=1, source_target_pairs={{0,16},{8,24},{16,0},{24,8},{1,17},{9,25},{17,1},{25,9},{2,18},{10... | collective-permute-start | bytes 167432 | tf_op jit(solution)/shard_map/ppermute | solution.py:41
  184.3 10.6 %collective-permute-start.39 = (bf16[384,768]{1,0:T(8,128)(2,1)S(1)}, bf16[384,768]{1,0:T(8,128)(2,1)S(1)}, u32[]{:S(2)}, u32[]{:S(2)}) collective-permute-start(bf16[384,768]{1,0:T(8,128)(2,1)S(1)} %add_convert_fusion), channel_id=1, source_target_pairs={{0,8},{8,0},{16,24},{24,16},{1,9},{9,1},{17,25},{25,17},{2,10},{10... | collective-permute-start | bytes 1769480 | tf_op jit(solution)/shard_map/ppermute | solution.py:41
  185.3 6.2 %collective-permute-start.41 = (bf16[48,1536]{1,0:T(8,128)(2,1)S(1)}, bf16[48,1536]{1,0:T(8,128)(2,1)S(1)}, u32[]{:S(2)}, u32[]{:S(2)}) collective-permute-start(bf16[48,1536]{1,0:T(8,128)(2,1)S(1)} %add_convert_fusion.2), channel_id=1, source_target_pairs={{0,16},{8,24},{16,0},{24,8},{1,17},{9,25},{17,1},{25,9},{2,18},{10... | collective-permute-start | bytes 442376 | tf_op jit(solution)/shard_map/ppermute | solution.py:41
  186.7 5.5 %collective-permute-start.40 = (bf16[96,384]{1,0:T(8,128)(2,1)S(1)}, bf16[96,384]{1,0:T(8,128)(2,1)S(1)}, u32[]{:S(2)}, u32[]{:S(2)}) collective-permute-start(bf16[96,384]{1,0:T(8,128)(2,1)S(1)} %add_convert_fusion.8), channel_id=1, source_target_pairs={{0,16},{8,24},{16,0},{24,8},{1,17},{9,25},{17,1},{25,9},{2,18},{10... | collective-permute-start | bytes 221192 | tf_op jit(solution)/shard_map/ppermute | solution.py:41
  191.5 5.8 %collective-permute-start.36 = (bf16[48,384]{1,0:T(8,128)(2,1)}, bf16[48,384]{1,0:T(8,128)(2,1)S(1)}, u32[]{:S(2)}, u32[]{:S(2)}) collective-permute-start(bf16[48,384]{1,0:T(8,128)(2,1)} %get-tuple-element.213), channel_id=1, source_target_pairs={{0,2},{1,3},{2,0},{3,1},{4,6},{5,7},{6,4},{7,5},{8,10},{9,11},{10,... | collective-permute-start | bytes 110600 | tf_op jit(solution)/shard_map/ppermute | solution.py:41
  192.3 5.0 %collective-permute-start.37 = (bf16[48,384]{1,0:T(8,128)(2,1)S(1)}, bf16[48,384]{1,0:T(8,128)(2,1)S(1)}, u32[]{:S(2)}, u32[]{:S(2)}) collective-permute-start(bf16[48,384]{1,0:T(8,128)(2,1)S(1)} %copy-done.31), channel_id=1, source_target_pairs={{0,4},{1,5},{2,6},{3,7},{4,0},{5,1},{6,2},{7,3},{8,12},{9,13},{10,... | collective-permute-start | bytes 110600 | tf_op jit(solution)/shard_map/ppermute | solution.py:41
  194.9 5.8 %collective-permute-start.38 = (bf16[48,384]{1,0:T(8,128)(2,1)S(1)}, bf16[48,384]{1,0:T(8,128)(2,1)S(1)}, u32[]{:S(2)}, u32[]{:S(2)}) collective-permute-start(bf16[48,384]{1,0:T(8,128)(2,1)S(1)} %copy-done.30), channel_id=1, source_target_pairs={{0,6},{1,7},{2,4},{3,5},{4,2},{5,3},{6,0},{7,1},{8,14},{9,15},{10,... | collective-permute-start | bytes 110600 | tf_op jit(solution)/shard_map/ppermute | solution.py:41
  197.2 3.8 %collective-permute-start.31 = (bf16[218,128]{1,0:T(8,128)(2,1)S(1)}, bf16[218,128]{1,0:T(8,128)(2,1)S(1)}, u32[]{:S(2)}, u32[]{:S(2)}) collective-permute-start(bf16[218,128]{1,0:T(8,128)(2,1)S(1)} %get-tuple-element.270), channel_id=1, source_target_pairs={{0,24},{8,16},{16,8},{24,0},{1,25},{9,17},{17,9},{25,1},{2,26},{10... | collective-permute-start | bytes 167432 | tf_op jit(solution)/shard_map/ppermute | solution.py:41
  197.2 6.3 %collective-permute-start.43 = (bf16[96,1536]{1,0:T(8,128)(2,1)S(1)}, bf16[96,1536]{1,0:T(8,128)(2,1)S(1)}, u32[]{:S(2)}, u32[]{:S(2)}) collective-permute-start(bf16[96,1536]{1,0:T(8,128)(2,1)S(1)} %pad_maximum_fusion.2), channel_id=1, source_target_pairs={{0,8},{8,0},{16,24},{24,16},{1,9},{9,1},{17,25},{25,17},{2,10},{10... | collective-permute-start | bytes 884744 | tf_op jit(solution)/shard_map/ppermute | solution.py:41
  200.7 4.8 %collective-permute-start.45 = (bf16[96,384]{1,0:T(8,128)(2,1)S(1)}, bf16[96,384]{1,0:T(8,128)(2,1)S(1)}, u32[]{:S(2)}, u32[]{:S(2)}) collective-permute-start(bf16[96,384]{1,0:T(8,128)(2,1)S(1)} %add_convert_fusion.7), channel_id=1, source_target_pairs={{0,8},{8,0},{16,24},{24,16},{1,9},{9,1},{17,25},{25,17},{2,10},{10... | collective-permute-start | bytes 221192 | tf_op jit(solution)/shard_map/ppermute | solution.py:41
  201.1 4.2 %collective-permute-start.42 = (bf16[48,384]{1,0:T(8,128)(2,1)S(1)}, bf16[48,384]{1,0:T(8,128)(2,1)S(1)}, u32[]{:S(2)}, u32[]{:S(2)}) collective-permute-start(bf16[48,384]{1,0:T(8,128)(2,1)S(1)} %add_convert_fusion.9), channel_id=1, source_target_pairs={{0,16},{8,24},{16,0},{24,8},{1,17},{9,25},{17,1},{25,9},{2,18},{10... | collective-permute-start | bytes 110600 | tf_op jit(solution)/shard_map/ppermute | solution.py:41
  205.4 1.3 collective-permute-start.44
  (31 other events, 149.0 us)
where the time goes:
time: 208 us
  Pallas kernels  98.4 us (47%)
  starting transfers between devices  54.5 us (26%)
  waiting for transfers between devices  34.9 us (17%)
  local copies, waits for them, and re-layouts  10.5 us (5%)
  other arithmetic  7.84 us (4%)
    ppermute x37, starting transfers between devices, flipped(): lax.ppermute(block, axis, [(i, i ^ bits) for i in range(lax.axis_size(axi...  37.7 us
    ppermute x37, waiting for transfers between devices, flipped(): lax.ppermute(block, axis, [(i, i ^ bits) for i in range(lax.axis_size(axi...  34.9 us
    pallas_call x1, Pallas kernels, attention(): pl.pallas_call(kernel, grid=(seqs, PAIRS // groups), in_specs=[SMEM, piec...  23.9 us
    pallas_call x1, Pallas kernels, feed_forward(): pl.pallas_call(forward_kernel, grid_spec=spec, out_shape=[SHAPE((rows, D)...  22.2 us
    pallas_call x1, Pallas kernels, feed_backward(): pl.pallas_call(backward_kernel, grid_spec=spec, out_shape=[SHAPE((rows, D...  15.5 us
    ppermute x6, starting transfers between devices, along(): lax.ppermute(block, 'seq', [(i, (i + 2 * distance) % size) for i in range...  11.5 us
    pallas_call x1, Pallas kernels, mix(): pl.pallas_call(functools.partial(mix_kernel, rows // tables.shape[1], cal...  8.7 us
    pallas_call x3, Pallas kernels, add_split(): pl.pallas_call(kernel, in_specs=[SMEM] + [VMEM] * len(arrays), out_specs=...  7.48 us
  transfers between devices with their start and end apart: 46, of which 12 were waited for; matrix products, arithmetic and copies ran while one was open for 7% of the time, Pallas kernels for 47%

commit v1 on v0

--- a/solution.py
+++ b/solution.py
@@ -46,14 +46,13 @@
     return lax.ppermute(block, "seq", [(i, (i + 2 * distance) % size) for i in range(size)])
 
 
-def to_owner(block, distance):
+def to_owner(block):
     size = lax.axis_size("seq")
-    half = size // 4
     route = []
     for b in range(lax.axis_size("batch")):
         for i in range(size):
-            j = i ^ (2 * distance)
-            if (j // 2) // half == b % 2:
+            j = i ^ (size // 2)
+            if j // (size // 2) == b % 2:
                 route.append((b * size + i, b * size + j))
     return lax.ppermute(block, ("batch", "seq"), route)
 
@@ -128,7 +127,7 @@
         sources, results = refs[: 2 * len(items)], refs[2 * len(items) :]
         for n, (_, _, which) in enumerate(items):
             a, b = sources[2 * n], sources[2 * n + 1]
-            own = place_ref[which]
+            own = place_ref[which] if which < 3 else lax.rem(lax.shift_right_logical(place_ref[3], which - 3), 2)
             for m in range(a.shape[0]):
                 for result, at in ((results[2 * n], 1 - own), (results[2 * n + 1], own)):
                     result[m] = (a[m, at].astype(F32) + b[m, at].astype(F32)).astype(BF16)
@@ -146,51 +145,6 @@
         cost_estimate=cost(1.2),
         name="add_split",
     )(place, *arrays)
-
-
-def add_cut(place, items):
-    def kernel(place_ref, *refs):
-        sources, results = refs[: 2 * len(items)], refs[2 * len(items) :]
-        start = 0
-        for n, (first, _) in enumerate(items):
-            a, b = sources[2 * n], sources[2 * n + 1]
-            count = first.shape[0]
-            for i in range(count):
-                at = lax.rem(place_ref[3] ^ i, count)
-                results[start + i][...] = (a[at].astype(F32) + b[at].astype(F32)).astype(BF16)
-            start += count
-
-    shapes = []
-    for a, _ in items:
-        shapes += [SHAPE(a.shape[1:], BF16)] * a.shape[0]
-    arrays = [v for item in items for v in item]
-    return pl.pallas_call(
-        kernel,
-        in_specs=[SMEM] + [VMEM] * len(arrays),
-        out_specs=[VMEM] * len(shapes),
-        out_shape=shapes,
-        compiler_params=params(),
-        cost_estimate=cost(0.8),
-        name="add_cut",
-    )(place, *arrays)
-
-
-def sum_split(place, parts):
-    def kernel(place_ref, *refs):
-        sources, results = refs[:-2], refs[-2:]
-        y = place_ref[2]
-        for result, at in ((results[0], 1 - y), (results[1], y)):
-            result[...] = tree_sum([ref[at] for ref in sources]).astype(BF16)
-
-    return pl.pallas_call(
-        kernel,
-        in_specs=[SMEM] + [VMEM] * len(parts),
-        out_specs=[VMEM] * 2,
-        out_shape=[SHAPE(parts[0].shape[1:], BF16)] * 2,
-        compiler_params=params(),
-        cost_estimate=cost(1.6),
-        name="sum_split",
-    )(place, *parts)
 
 
 def project_kernel(copies, x_ref, gain_ref, bias_ref, weight_ref, add_ref, tables_ref, q_ref, kv_ref):
@@ -271,7 +225,7 @@
         grad_refs[0][...] = grad
     for i in range(len(grad_refs) if len(grad_refs) > 1 else 0):
 
-        @pl.when(step == steps - 1 - i)
+        @pl.when(step == i)
         def _(i=i):
             grad_refs[i][...] = grad
 
@@ -288,7 +242,7 @@
     @pl.when(step == steps - 1)
     def _():
         total = acc_scr[...] + mlp
-        own_ref[...] = total[:rows]
+        own_ref[...] = total[:rows].astype(BF16)
         other_ref[...] = total[rows:].astype(BF16)
 
 
@@ -299,13 +253,13 @@
     rows = x.shape[0]
     half = w1.shape[1] // 2
     pieces = depth // 2
-    aligned = half % (pieces * 256) == 0
+    aligned = pieces == 2 and half % 512 == 0
     chunk = half // pieces if aligned else CHUNK
     steps = half // chunk
     whole = lambda a: pl.BlockSpec(a.shape, lambda i, place: (0,) * a.ndim)
     fixed = lambda *shape: pl.BlockSpec(shape, lambda i, place: (0, 0))
     if aligned:
-        piece = lambda i, place: (place[3] ^ (steps - 1 - i)) % steps
+        piece = lambda i, place: (place[3] ^ (1 - i)) & 1
         grad_specs = [fixed(chunk, D)] * pieces
         grad_shapes = [SHAPE((chunk, D), BF16)] * pieces
     else:
@@ -344,7 +298,7 @@
         forward_kernel,
         grid_spec=spec,
         out_shape=[
-            SHAPE((rows, D), F32),
+            SHAPE((rows, D), BF16),
             SHAPE((rows, D), BF16),
             SHAPE((2 * rows, half), BF16),
             SHAPE((D, 2 * rows), BF16),
@@ -356,8 +310,9 @@
     )(place, x, xx, g, gg, gain, bias, w1, b1, w2)
     grads = result[4:]
     if not aligned:
-        cut = grads[0].reshape(pieces, -1, D)
-        grads = [take(cut, (place[3] ^ i) % pieces, 0) for i in range(pieces)]
+        cut = grads[0].reshape(pieces // 2, 2, -1, D)
+        low = place[3] & 1
+        grads = [take(cut, 1 - low, 1), take(cut, low, 1)]
     return result[:4], grads
 
 
@@ -409,7 +364,7 @@
     @pl.when(step == steps - 1)
     def _():
         total = acc_scr[...] + back
-        own_ref[...] = total[:rows]
+        own_ref[...] = total[:rows].astype(BF16)
         other_ref[...] = total[rows:].astype(BF16)
 
 
@@ -450,7 +405,7 @@
         backward_kernel,
         grid_spec=spec,
         out_shape=[
-            SHAPE((rows, D), F32),
+            SHAPE((rows, D), BF16),
             SHAPE((rows, D), BF16),
             SHAPE((rows, D), BF16),
             SHAPE((count, per, half), BF16),
@@ -518,7 +473,7 @@
         dv = dv + dot(do_t[head], expd[h])
     dq = dq * inverse
     for p in range(PAIRS):
-        dq_ref[:, p * 128 : (p + 1) * 128] = dq[p * span : (p + 1) * span]
+        dq_ref[:, p * 128 : (p + 1) * 128] = dq[p * span : (p + 1) * span].astype(BF16)
     both = jnp.concatenate([dk, dv], axis=0).T.astype(BF16)
     for k in range(depth):
         even_out_ref[k] = both[2 * k * span : (2 * k + 1) * span]
@@ -662,7 +617,7 @@
     over_blocks(backward)
     dq = acc_ref[0] * inverse
     for p in range(groups):
-        dq_ref[:, p * 128 : (p + 1) * 128] = dq[p * span : (p + 1) * span]
+        dq_ref[:, p * 128 : (p + 1) * 128] = dq[p * span : (p + 1) * span].astype(BF16)
 
     @pl.when(group == group_count - 1)
     def _():
@@ -702,7 +657,7 @@
         grid=(seqs, PAIRS // groups),
         in_specs=[SMEM, pieces, pieces, wide_spec, wide_spec],
         out_specs=[wide_spec] * 2 + [pieces] * 2,
-        out_shape=[SHAPE((seqs, span, D), BF16), SHAPE((seqs, span, D), F32)]
+        out_shape=[SHAPE((seqs, span, D), BF16), SHAPE((seqs, span, D), BF16)]
         + [SHAPE((depth, seqs, span, 128), BF16)] * 2,
         scratch_shapes=scratch,
         compiler_params=params(),
@@ -711,85 +666,99 @@
     )(place, evens, odds, q, do)
 
 
-def mix_kernel(
+def weights_kernel(
+    copies, place_ref, dq_ref, attn_ref, g_ref, x_ref, gain_ref, bias_ref, tables_ref, send_ref, keep_ref, grad_ref, small_ref
+):
+    half = D // 2
+    own = place_ref[0] == 0
+
+    def products(left, right):
+        lower, upper = right[:, :half], right[:, half:]
+        send_ref[0] = dot(left, jnp.where(own, upper, lower)).astype(BF16)
+        keep_ref[0] = dot(left, jnp.where(own, lower, upper)).astype(BF16)
+
+    @pl.when(pl.program_id(0) == 0)
+    def _():
+        g = g_ref[...]
+        small_ref[1:2] = jnp.sum(g.astype(F32), axis=0, keepdims=True)
+        products(attn_ref[...].astype(F32).T.astype(BF16), g)
+
+    @pl.when(pl.program_id(0) == 1)
+    def _():
+        tables = repeated(tables_ref, copies)
+        for p in range(PAIRS):
+            columns = slice(p * 128, (p + 1) * 128)
+            grad_ref[:, columns] = turn(dq_ref[:, columns].astype(F32) * SCALE, tables, -1).astype(BF16)
+        grad = grad_ref[...]
+        small_ref[0:1] = jnp.sum(grad.astype(F32), axis=0, keepdims=True)
+        normed, _ = normalize(x_ref[...].astype(F32))
+        first_in = normed * wide(gain_ref) + wide(bias_ref)
+        products(first_in.T.astype(BF16), grad)
+
+
+def weights(place, dq, attn, g, x, gain, bias, tables):
+    rows = x.shape[0]
+    whole = lambda a: pl.BlockSpec(a.shape, lambda i: (0,) * a.ndim)
+    fixed = lambda *shape: pl.BlockSpec(shape, lambda i: (0, 0))
+    part = pl.BlockSpec((1, D, D // 2), lambda i: (i, 0, 0))
+    arrays = (dq, attn, g, x, gain, bias, tables)
+    return pl.pallas_call(
+        functools.partial(weights_kernel, rows // tables.shape[1]),
+        grid=(2,),
+        in_specs=[SMEM] + [whole(a) for a in arrays],
+        out_specs=[part, part, fixed(rows, D), fixed(8, D)],
+        out_shape=[
+            SHAPE((2, D, D // 2), BF16),
+            SHAPE((2, D, D // 2), BF16),
+            SHAPE((rows, D), BF16),
+            SHAPE((8, D), F32),
+        ],
+        compiler_params=params(),
+        cost_estimate=cost(2.4),
+        name="weights",
+    )(place, *arrays)
+
+
+def mix_kernel(x_ref, mlp_ref, mlp2_ref, attn_ref, grad_ref, add_ref, wo_ref, wq_ref, output_ref, first_ref):
+    first_ref[...] = dot_nt(grad_ref[...], wq_ref[...]).astype(BF16)
+    mlp = mlp_ref[...].astype(F32) + mlp2_ref[...].astype(F32)
+    x = x_ref[...].astype(F32)
+    output_ref[...] = (x + (mlp + dot(attn_ref[...], wo_ref[...])) + wide(add_ref)).astype(BF16)
+
+
+def mix(x, mlp, mlp2, attn, grad, add, wo, wqkv):
+    rows = x.shape[0]
+    row = pl.BlockSpec((rows // 2, D), lambda i: (i, 0))
+    square = pl.BlockSpec((D, D), lambda i: (0, 0))
+    return pl.pallas_call(
+        mix_kernel,
+        grid=(2,),
+        in_specs=[row] * 5 + [pl.BlockSpec((D,), lambda i: (0,)), square, square],
+        out_specs=[row] * 2,
+        out_shape=[SHAPE((rows, D), BF16)] * 2,
+        compiler_params=params(),
+        cost_estimate=cost(2.4),
+        name="mix",
+    )(x, mlp, mlp2, attn, grad, add, wo, wqkv)
+
+
+def two_terms(values):
+    high = values.astype(BF16)
+    return high, (values - high.astype(F32)).astype(BF16)
+
+
+def message_lines(ff):
+    return -(-(ff // 128 + 6 * (D // 128) + 1) // 16) * 16
+
+
+def finish_kernel(
     copies,
-    calls,
+    count,
+    lines,
     place_ref,
     *refs,
 ):
-    outs, dqs, refs = refs[:calls], refs[calls : 2 * calls], refs[2 * calls :]
-    (
-        x_ref,
-        g_ref,
-        mlp_ref,
-        mlp2_ref,
-        gain_ref,
-        bias_ref,
-        add_ref,
-        wo_ref,
-        wqkv_ref,
-        tables_ref,
-        output_ref,
-        send_ref,
-        keep_ref,
-        first_ref,
-        small_ref,
-    ) = refs
-    half = D // 2
-    x = x_ref[...].astype(F32)
-    g = g_ref[...]
-    attn = jnp.concatenate([r[...] for r in outs], axis=0)
-    normed, _ = normalize(x)
-    first_in = normed * wide(gain_ref) + wide(bias_ref)
-    tables = repeated(tables_ref, copies)
-    parts = []
-    for p in range(PAIRS):
-        dq = jnp.concatenate([r[:, p * 128 : (p + 1) * 128] for r in dqs], axis=0)
-        parts.append(turn(dq * SCALE, tables, -1).astype(BF16))
-    grad = jnp.concatenate(parts, axis=1)
-    attn_t = attn.astype(F32).T.astype(BF16)
-    first_t = first_in.T.astype(BF16)
-    own = place_ref[0] == 0
-    for i, (left, right) in enumerate(((attn_t, g), (first_t, grad))):
-        lower, upper = right[:, :half], right[:, half:]
-        send_ref[i] = dot(left, jnp.where(own, upper, lower)).astype(BF16)
-        keep_ref[i] = dot(left, jnp.where(own, lower, upper)).astype(BF16)
-    small_ref[...] = jnp.zeros_like(small_ref)
-    small_ref[0:1] = jnp.sum(grad.astype(F32), axis=0, keepdims=True)
-    small_ref[1:2] = jnp.sum(g.astype(F32), axis=0, keepdims=True)
-    mlp = mlp_ref[...] + mlp2_ref[...].astype(F32)
-    output_ref[...] = (x + (mlp + dot(attn, wo_ref[...])) + wide(add_ref)).astype(BF16)
-    first_ref[...] = dot_nt(grad, wqkv_ref[:, :D])
-
-
-def mix(place, outs, dqs, x, g, mlp, mlp2, gain, bias, add, wo, wqkv, tables):
-    rows = x.shape[0]
-    calls = len(outs)
-    return pl.pallas_call(
-        functools.partial(mix_kernel, rows // tables.shape[1], calls),
-        in_specs=[SMEM] + [VMEM] * (2 * calls + 10),
-        out_specs=[VMEM] * 5,
-        out_shape=[
-            SHAPE((rows, D), BF16),
-            SHAPE((2, D, D // 2), BF16),
-            SHAPE((2, D, D // 2), BF16),
-            SHAPE((rows, D), F32),
-            SHAPE((8, D), F32),
-        ],
-        compiler_params=params(),
-        cost_estimate=cost(3.2),
-        name="mix",
-    )(place, *outs, *dqs, x, g, mlp, mlp2, gain, bias, add, wo, wqkv, tables)
-
-
-def finish_kernel(copies, groups, *refs):
-    sums = []
-    for group in groups:
-        total = refs[0][...].astype(F32)
-        for ref in refs[1:group]:
-            total += ref[...].astype(F32)
-        sums.append(total)
-        refs = refs[group:]
+    kv_refs, refs = refs[:count], refs[count:]
     (
         extra_ref,
         x_ref,
@@ -800,45 +769,124 @@
         gain_ref,
         bias_ref,
         gain2_ref,
-        wqkv_ref,
+        wkv_ref,
         tables_ref,
+        b1_ref,
+        early_ref,
         tokens_ref,
-        weight_ref,
-        small_ref,
+        message_ref,
+        vector_scr,
     ) = refs
-    total = jnp.concatenate(sums, axis=0) + extra_ref[...].astype(F32)
+    total = extra_ref[...].astype(F32)
+    for ref in kv_refs:
+        total += ref[...].astype(F32)
     tables = repeated(tables_ref, copies)
     grad = turn(total, key_tables(tables), -1).astype(BF16)
     x = x_ref[...].astype(F32)
     normed, inverse = normalize(x)
     gain = wide(gain_ref)
     first_in = normed * gain + wide(bias_ref)
-    weight_ref[...] = dot(first_in.T.astype(BF16), grad).astype(BF16)
-    first_grad = first_ref[...] + dot_nt(grad, wqkv_ref[:, D:])
-    second_grad = back_ref[...] + back2_ref[...].astype(F32)
-    small_ref[...] = jnp.zeros_like(small_ref)
-    for i, rows in enumerate((first_grad * normed, first_grad, second_grad * normed, second_grad)):
-        small_ref[i : i + 1] = jnp.sum(rows, axis=0, keepdims=True)
-    small_ref[4:5, :128] = jnp.sum(grad.astype(F32), axis=0, keepdims=True)
+    first_grad = first_ref[...].astype(F32) + dot_nt(grad, wkv_ref[...])
+    second_grad = back_ref[...].astype(F32) + back2_ref[...].astype(F32)
+
+    vector_scr[...] = jnp.zeros_like(vector_scr)
+    b1 = b1_ref[...]
+    b1_lines = b1.shape[1] // 128
+    for i in range(b1_lines):
+        vector_scr[pl.ds(place_ref[0] * b1_lines + i, 1)] = b1[:, i * 128 : (i + 1) * 128]
+    at = 2 * b1_lines
+    sums = [early_ref[0:1], early_ref[1:2]]
+    for rows in (first_grad * normed, first_grad, second_grad * normed, second_grad):
+        sums.append(jnp.sum(rows, axis=0, keepdims=True))
+    sums.append(jnp.sum(grad.astype(F32), axis=0, keepdims=True))
+    for row in sums:
+        for i in range(row.shape[1] // 128):
+            vector_scr[at : at + 1] = row[:, i * 128 : (i + 1) * 128]
+            at += 1
+    high, rest = two_terms(vector_scr[...])
+    weight = dot(first_in.T.astype(BF16), grad).astype(BF16)
+    places = message_ref.shape[0]
+    per = weight.shape[0] // places
+    for i in range(places):
+        message_ref[i, :lines] = high
+        message_ref[i, lines : 2 * lines] = rest
+        message_ref[i, 2 * lines :] = weight[i * per : (i + 1) * per]
+
     normed_grad = first_grad * gain + second_grad * wide(gain2_ref)
     mean = jnp.mean(normed_grad, axis=-1, keepdims=True)
     along_rows = jnp.mean(normed_grad * normed, axis=-1, keepdims=True)
     tokens_ref[...] = (g_ref[...].astype(F32) + inverse * (normed_grad - mean - normed * along_rows)).astype(BF16)
 
 
-def finish(kv_parts, extra, x, g, first, back, back2, gain, bias, gain2, wqkv, tables):
+def finish(place, places, ff, kv_parts, extra, x, g, first, back, back2, gain, bias, gain2, wqkv, tables, b1, early):
     rows = x.shape[0]
-    groups = [len(parts) for parts in kv_parts]
-    arrays = [v for parts in kv_parts for v in parts]
+    lines = message_lines(ff)
+    whole = lambda a: pl.BlockSpec(a.shape, lambda i: (0,) * a.ndim)
+    before = (*kv_parts, extra, x, g, first, back, back2, gain, bias, gain2)
+    after_it = (tables, b1, early)
     return pl.pallas_call(
-        functools.partial(finish_kernel, rows // tables.shape[1], groups),
-        in_specs=[VMEM] * (len(arrays) + 11),
-        out_specs=[VMEM] * 3,
-        out_shape=[SHAPE((rows, D), BF16), SHAPE((D, 128), BF16), SHAPE((8, D), F32)],
+        functools.partial(finish_kernel, rows // tables.shape[1], len(kv_parts), lines),
+        grid=(1,),
+        in_specs=[SMEM]
+        + [whole(a) for a in before]
+        + [pl.BlockSpec((D, 128), lambda i: (0, D // 128))]
+        + [whole(a) for a in after_it],
+        out_specs=[
+            pl.BlockSpec((rows, D), lambda i: (0, 0)),
+            pl.BlockSpec((places, 2 * lines + D // places, 128), lambda i: (0, 0, 0)),
+        ],
+        out_shape=[SHAPE((rows, D), BF16), SHAPE((places, 2 * lines + D // places, 128), BF16)],
+        scratch_shapes=[pltpu.VMEM((lines, 128), F32)],
         compiler_params=params(),
         cost_estimate=cost(2.4),
         name="finish",
-    )(*arrays, extra, x, g, first, back, back2, gain, bias, gain2, wqkv, tables)
+    )(place, *before, wqkv, *after_it)
+
+
+def gather_sums(messages, lines):
+    rows = messages.shape[1]
+
+    def kernel(refs, result):
+        total = tree_sum([refs[i] for i in range(messages.shape[0])])
+        high, rest = two_terms(total[:lines] + total[lines : 2 * lines])
+        result[:lines] = high
+        result[lines : 2 * lines] = rest
+        result[2 * lines :] = total[2 * lines :].astype(BF16)
+
+    return pl.pallas_call(
+        kernel,
+        in_specs=[VMEM],
+        out_specs=VMEM,
+        out_shape=SHAPE((rows, 128), BF16),
+        compiler_params=params(),
+        cost_estimate=cost(0.6),
+        name="gather_sums",
+    )(messages)
+
+
+def last_sums(messages, lines, widths):
+    rows = messages[0].shape[0] - 2 * lines
+
+    def kernel(*refs):
+        sources, results = refs[: len(messages)], refs[len(messages) :]
+        total = tree_sum([ref[...] for ref in sources])
+        vector = total[:lines] + total[lines : 2 * lines]
+        at = 0
+        for result, width in zip(results[:-1], widths):
+            for i in range(width // 128):
+                result[i * 128 : (i + 1) * 128] = vector[at + i]
+            at += width // 128
+        results[-1][...] = total[2 * lines :]
+
+    return pl.pallas_call(
+        kernel,
+        in_specs=[VMEM] * len(messages),
+        out_specs=[VMEM] * (len(widths) + 1),
+        out_shape=[SHAPE((width,), F32) for width in widths] + [SHAPE((rows, 128), F32)],
+        compiler_params=params(),
+        cost_estimate=cost(0.6),
+        name="last_sums",
+    )(*messages)
 
 
 def local(
@@ -875,6 +923,8 @@
     over_core = lambda v: flipped(v, "batch", 1)
     over_x = lambda v: flipped(v, "batch", 2)
     over_y = lambda v: flipped(v, "seq", 1)
+    over_z = lambda v, bit: flipped(v, "seq", 2 << bit)
+    z_bits = depth.bit_length() - 1
     flat = lambda v: v.reshape(rows, -1)
 
     def pair(mine, other, index, axis):
@@ -895,7 +945,8 @@
     (mlp, mlp_other, slope, in_t), grads2 = feed_forward(
         place, depth, x_fed, x_other, g_fed, g_other, ln2_gain, ln2_bias, fc1_weight, fc1_bias.reshape(1, -1), fc2_weight
     )
-    parts2 = [grads2[0]] + [to_owner(grads2[i % half_depth], i) for i in range(1, depth)]
+    theirs2, mine2 = grads2
+    come2 = over_z(theirs2, 0)
     mlp_come = over_core(mlp_other)
     evens = [kv3] + list(after(evens[1:], slope))
     evens = jnp.stack(evens)
@@ -910,149 +961,125 @@
     out, dq, even, odd = attention(place, evens, odds, q3, do3)
     odd = over_y(odd)
 
-    cut = lambda v: v.reshape(depth, 2, per1 // 2, ff // 2)
-    mine1, come1 = after((mine1, come1), out)
-    theirs1, mine1 = add_split(place, [(cut(mine1), cut(come1), 2)])
-    come1 = over_y(theirs1)
-
-    g_mix, mlp_come = after((g, mlp_come), theirs1)
-    output, send, keep, first, small_mix = mix(
-        place, [flat(out)], [flat(dq)], x, g_mix, mlp, mlp_come, ln1_gain, ln1_bias, out_bias, out_weight, qkv_weight, tables
-    )
-    come = over_core(send)
-    even, odd = after((even, odd), send)
+    def halved(a, parts, height):
+        return a.reshape(parts, 2, height, a.shape[-1])
+
+    g_weights, x_weights, come1, mlp_come, back_come = after((g, x, come1, mlp_come, back_come), out)
+    send, keep, q_rows, early = weights(place, flat(dq), flat(out), g_weights, x_weights, ln1_gain, ln1_bias, tables)
+    come3 = over_core(send)
+
+    mine2, come2 = after((mine2, come2), send)
+    height = per2 // 2
+    view = lambda v: halved(v, half_depth, height)
+    theirs2, mine2 = add_split(place, [(view(mine2), view(come2), 1)])
+    come2 = over_x(theirs2)
+
+    even, odd = after((even, odd), theirs2)
     kv_sums = [summed(even[k], odd[k]) for k in range(depth)]
     got = [along(kv_sums[k], -k) for k in range(1, depth)]
 
-    parts2 = after(parts2, *kv_sums)
-    theirs2, mine2 = sum_split(place, [v.reshape(2, per2, D) for v in parts2])
+    mine1, come1 = after((mine1, come1), *kv_sums)
+    view = lambda v: halved(v, depth, per1 // 2)
+    theirs1, mine1 = add_split(place, [(view(mine1), view(come1), 2)])
+    come1 = over_y(theirs1)
+
+    x_mix, mlp_come = after((x, mlp_come), theirs1)
+    output, first = mix(x_mix, mlp, mlp_come, flat(out), q_rows, out_bias, out_weight, qkv_weight)
+
+    keep, come3 = after((keep, come3), first)
+    view = lambda v: halved(v, 2 * depth, per1)
+    theirs3, mine3 = add_split(place, [(view(keep), view(come3), 2)])
+    come3 = over_y(theirs3)
+
+    mine2, come2 = after((mine2, come2), theirs3)
+    view = lambda v: halved(v, half_depth // 2, height)
+    theirs2, mine2 = add_split(place, [(view(mine2), view(come2), 2)])
     come2 = over_y(theirs2)
 
-    mine1, come1 = after((mine1, come1), theirs2)
-    cuts1 = add_cut(place, [(mine1, come1)])
-    parts1 = [cuts1[0]] + [flipped(cuts1[i], "seq", 2 * i) for i in range(1, depth)]
-
-    keep, come = after((keep, come), cuts1[0])
-    cut_o = lambda v: v[0].reshape(depth, 2, per1, D // 2)
-    cut_q = lambda v: v[1].reshape(count, 2, per1 // 2, D // 2)
-    theirs_o, mine_o, theirs_q, mine_q = add_split(
-        place, [(cut_o(keep), cut_o(come), 2), (cut_q(keep), cut_q(come), 1)]
+    got = after(got, theirs2)
+    lines = message_lines(ff)
+    tokens_grad, messages = finish(
+        place, count, ff, [flat(v) for v in (kv_sums[0], *got)], flat(key_value_grad), x, g, first, back, back_come,
+        ln1_gain, ln1_bias, ln2_gain, qkv_weight, tables, b1_grad, early,
     )
-    come_o, come_q = over_y(theirs_o), over_x(theirs_q)
-
-    mine2, come2 = after((mine2, come2), theirs_o)
-    sum2 = summed(mine2, come2)
+    messages = lax.all_to_all(messages, "seq", 0, 0, tiled=True)
+
+    mine3, come3 = after((mine3, come3), tokens_grad)
+    view = lambda v: halved(v, depth, per1)
+    theirs3, mine3 = add_split(place, [(view(mine3), view(come3), 3)])
+    come3 = over_z(theirs3, 0)
+    mine1, come1 = after((mine1, come1), theirs3)
+    view = lambda v: halved(v, depth // 2, per1 // 2)
+    theirs1, mine1 = add_split(place, [(view(mine1), view(come1), 3)])
+    come1 = over_z(theirs1, 0)
+    mine2, come2 = after((mine2, come2), theirs1)
+    for bit in range(1, z_bits - 1):
+        view = lambda v: halved(v, half_depth >> (bit + 1), height)
+        theirs2, mine2 = add_split(place, [(view(mine2), view(come2), 3 + bit)])
+        come2 = over_z(theirs2, bit)
+    sum2 = summed(mine2, come2).reshape(height, D)
+    come2 = to_owner(sum2)
+
+    (messages,) = after((messages,), sum2)
+    message = gather_sums(messages, lines)
+    got = [flipped(message, "batch", i) for i in range(1, batches)]
+
+    mine3, come3 = after((mine3, come3), message)
+    for bit in range(1, z_bits):
+        view = lambda v: halved(v, 2 * (depth >> (bit + 1)), per1)
+        theirs3, mine3 = add_split(place, [(view(mine3), view(come3), 3 + bit)])
+        come3 = over_z(theirs3, bit)
+    mine1, come1 = after((mine1, come1), theirs3)
+    for bit in range(1, z_bits):
+        view = lambda v: halved(v, depth >> (bit + 1), per1 // 2)
+        theirs1, mine1 = add_split(place, [(view(mine1), view(come1), 3 + bit)])
+        come1 = over_z(theirs1, bit)
+
+    sum2, come2 = after((sum2, come2), theirs1)
+    sum2 = summed(sum2, come2)
     other2 = over_x(sum2)
-
     got = after(got, sum2)
-    kv_parts = [[v.reshape(-1, 128) for v in (kv_sums[0], *got)]]
-    tokens_grad, kv_weight, small = finish(
-        kv_parts, flat(key_value_grad), x, g, first, back, back_come, ln1_gain, ln1_bias, ln2_gain, qkv_weight, tables
-    )
-
-    b1_half = b1_grad.reshape(-1, 128)
-    empty = jnp.zeros_like(b1_half)
-    vector = jnp.concatenate(
-        [
-            jnp.where(core == 0, b1_half, empty),
-            jnp.where(core == 0, empty, b1_half),
-            small_mix[:2].reshape(-1, 128),
-            small[:4].reshape(-1, 128),
-            small[4:5, :128],
-        ]
-    )
-    lines = vector.shape[0]
-
-    def packed(weight, vector):
-        high = vector.astype(BF16)
-        rest = (vector - high.astype(F32)).astype(BF16)
-        return jnp.concatenate([weight.astype(BF16), high, rest])
-
-    def unpacked(message):
-        message = message.astype(F32)
-        return jnp.concatenate([message[:per1], message[per1 : per1 + lines] + message[per1 + lines :]])
-
-    shards = kv_weight.reshape(depth, 2, per1, 128)
-    vector16 = packed(kv_weight[:0], vector)
-    late_send = jnp.concatenate([take(shards, 1 - y, 1).reshape(-1, 128), vector16])
-    late_keep = jnp.concatenate([take(shards, y, 1).reshape(-1, 128), vector16])
-    late_come = over_y(late_send)
-
-    mine_o, come_o, mine_q, come_q = after((mine_o, come_o, mine_q, come_q), late_send)
-    cuts_o = add_cut(place, [(mine_o, come_o)])
-    parts_o = [cuts_o[0]] + [flipped(cuts_o[i], "seq", 2 * i) for i in range(1, depth)]
-    cut_q = lambda v: v.reshape(depth, 2, per1 // 2, D // 2)
-    theirs_q, mine_q = add_split(place, [(cut_q(mine_q), cut_q(come_q), 2)])
-    come_q = over_y(theirs_q)
-
-    late_keep, late_come = after((late_keep, late_come), theirs_q, cuts_o[0])
-    unpack = lambda v, at: v[at : at + lines].astype(F32) + v[at + lines :].astype(F32)
-    shards = late_keep[: depth * per1].astype(F32) + late_come[: depth * per1].astype(F32)
-    shards = shards.reshape(depth, per1, 128)
-    vector = unpack(late_keep, depth * per1) + unpack(late_come, depth * per1)
-    messages = [packed(take(shards, z ^ i, 0), vector) for i in range(depth)]
-    got = [flipped(messages[i], "seq", 2 * i) for i in range(1, depth)]
-
-    sum2, other2 = after((sum2, other2), *messages)
-    sum2 = summed(sum2, other2)
+    widths = (ff,) + (D,) * 6 + (128,)
+    b1_sum, q_sum, out_sum, gain1, bias1, gain2, bias2, kv_bias, kv_sum = last_sums([message, *got], lines, widths)
+    mine3, come3 = after((mine3, come3), kv_sum)
+    sum3 = summed(mine3, come3)
+    other3 = over_x(sum3)
+    mine1, come1 = after((mine1, come1), sum3)
+    sum1 = summed(mine1, come1).reshape(per1 // 2, -1)
+    other1 = over_x(sum1)
+
+    sum2, other2 = after((sum2, other2), sum1)
+    sum2 = pair(sum2, other2, xs, 0)
     other2 = over_core(sum2)
-    parts1 = after(parts1, sum2)
-    sum1 = summed(*parts1)
-    other1 = over_x(sum1)
-
-    got = after(got, sum1)
-    total = tree_sum([unpacked(v) for v in [messages[0], *got]])
-    message = packed(total[:per1], total[per1:])
-    got = [flipped(message, "batch", i) for i in range(1, batches)]
-
-    parts_o = after(parts_o, message)
-    sum_o = summed(*parts_o)
-    other_o = over_x(sum_o)
-    mine_q, come_q = after((mine_q, come_q), sum_o)
-    cuts_q = add_cut(place, [(mine_q, come_q)])
-    parts_q = [cuts_q[0]] + [flipped(cuts_q[i], "seq", 2 * i) for i in range(1, depth)]
-
-    sum1, other1 = after((sum1, other1), cuts_q[0])
+    sum3, other3 = after((sum3, other3), sum2)
+    sum3 = summed(sum3, other3)
+    other3 = over_core(sum3)
+    sum1, other1 = after((sum1, other1), sum3)
     sum1 = pair(sum1, other1, xs, 0)
     other1 = over_core(sum1)
-    sum_o, other_o = after((sum_o, other_o), sum1)
-    sum_o = summed(sum_o, other_o)
-    other_o = over_core(sum_o)
-    owner = z // half_depth == core
-    (other2,) = after((other2,), sum_o)
+
+    owner = (z >> (z_bits - 1)) == core
+    (other2,) = after((other2,), sum1)
     fc2_grad = jnp.where(owner, sum2, other2).astype(F32)
-    parts_q = after(parts_q, fc2_grad)
-    sum_q = summed(*parts_q)
-    other_q = over_x(sum_q)
-    got = after(got, sum_q)
-    total = tree_sum([unpacked(v) for v in [message, *got]])
-    (other1,) = after((other1,), total)
+    (other3,) = after((other3,), fc2_grad)
+    both3 = pair(sum3, other3, core, 2).astype(F32)
+    (other1,) = after((other1,), both3)
     fc1_grad = pair(sum1, other1, core, 1).astype(F32)
-    sum_q, other_q = after((sum_q, other_q), fc1_grad)
-    sum_q = pair(sum_q, other_q, xs, 0)
-    other_q = over_core(sum_q)
-    (other_o,) = after((other_o,), sum_q)
-    out_grad = pair(sum_o, other_o, core, 1).astype(F32)
-    q_grad = pair(sum_q, other_q, core, 1).astype(F32)
-
-    vector = total[per1:]
-    b1_lines, d_lines = ff // 128, D // 128
-    row = lambda i: vector[b1_lines + i * d_lines : b1_lines + (i + 1) * d_lines].reshape(-1)
     return (
         output.reshape(tokens.shape),
         kv3,
         tokens_grad.reshape(tokens.shape),
-        row(2),
-        row(3),
-        jnp.concatenate([q_grad, total[:per1]], axis=1),
-        jnp.concatenate([row(0), vector[-1]]),
-        out_grad,
-        row(4),
-        row(5),
+        gain1,
+        bias1,
+        jnp.concatenate([both3[1], kv_sum], axis=1),
+        jnp.concatenate([q_sum, kv_bias]),
+        both3[0],
+        gain2,
+        bias2,
         fc1_grad,
-        vector[:b1_lines].reshape(-1),
+        b1_sum,
         fc2_grad,
-        row(1),
+        out_sum,
     )
 
 

time: 208 us -> 185 us (0.89)
  starting transfers between devices: 54.5 us -> 37.1 us
  waiting for transfers between devices: 34.9 us -> 23.6 us
  Pallas kernels: 98.4 us -> 107 us
  local copies, waits for them, and re-layouts: 10.5 us -> 8.26 us
    ppermute x37 -> x26, starting transfers between devices: 37.7 us -> 20.5 us  [flipped(): lax.ppermute(block, axis, [(i, i ^ bits) for i in range(lax.axis_size(axi...]
    pallas_call x3 -> x8, Pallas kernels: 7.48 us -> 19 us  [add_split(): pl.pallas_call(kernel, in_specs=[SMEM] + [VMEM] * len(arrays), out_specs=...]
    ppermute x37 -> x26, waiting for transfers between devices: 34.9 us -> 23.6 us  [flipped(): lax.ppermute(block, axis, [(i, i ^ bits) for i in range(lax.axis_size(axi...]
    all_to_all x0 -> x1, starting transfers between devices: none -> 5.61 us  [local(): messages = lax.all_to_all(messages, 'seq', 0, 0, tiled=True)]
    slice x16 -> x0, local copies, waits for them, and re-layouts: 4.49 us -> none  [the longest x2 2.27 us: local(): cut_q = lambda v: v[1].reshape(count, 2, per1 // 2, D // 2)]
    ppermute x3 -> x1, starting transfers between devices: 5.28 us -> 1.29 us  [to_owner(): return lax.ppermute(block, ('batch', 'seq'), route)]
    unnamed x64 -> x60, local copies, waits for them, and re-layouts: 3.56 us -> 7.51 us
    pallas_call x5 -> x4, Pallas kernels: 18.3 us -> 16.3 us  [the longest x1 7.84 us: weights(): pl.pallas_call(functools.partial(weights_kernel, rows // tables.shape[1])...]
  transfers between devices with their start and end apart: 46 -> 34, of which waited for: 12 -> 7; matrix products, arithmetic and copies ran while one was open for 7% -> 4% of each run, Pallas kernels for 47% -> 58%
where the time goes in v1:
time: 185 us
  Pallas kernels  107 us (58%)
  starting transfers between devices  37.1 us (20%)
  waiting for transfers between devices  23.6 us (13%)
  local copies, waits for them, and re-layouts  8.26 us (4%)
  other arithmetic  7.34 us (4%)
    pallas_call x1, Pallas kernels, attention(): pl.pallas_call(kernel, grid=(seqs, PAIRS // groups), in_specs=[SMEM, piec...  24.1 us
    ppermute x26, waiting for transfers between devices, flipped(): lax.ppermute(block, axis, [(i, i ^ bits) for i in range(lax.axis_size(axi...  23.6 us
    pallas_call x1, Pallas kernels, feed_forward(): pl.pallas_call(forward_kernel, grid_spec=spec, out_shape=[SHAPE((rows, D)...  22 us
    ppermute x26, starting transfers between devices, flipped(): lax.ppermute(block, axis, [(i, i ^ bits) for i in range(lax.axis_size(axi...  20.5 us
    pallas_call x8, Pallas kernels, add_split(): pl.pallas_call(kernel, in_specs=[SMEM] + [VMEM] * len(arrays), out_specs=...  19 us
    pallas_call x1, Pallas kernels, feed_backward(): pl.pallas_call(backward_kernel, grid_spec=spec, out_shape=[SHAPE((rows, D...  15.4 us
    ppermute x6, starting transfers between devices, along(): lax.ppermute(block, 'seq', [(i, (i + 2 * distance) % size) for i in range...  9.78 us
    pallas_call x1, Pallas kernels, weights(): pl.pallas_call(functools.partial(weights_kernel, rows // tables.shape[1])...  7.84 us
  transfers between devices with their start and end apart: 34, of which 7 were waited for; matrix products, arithmetic and copies ran while one was open for 4% of the time, Pallas kernels for 58%

profile of v1, /device:TPU:0, one launch (start us, length us, event | category | flops | bytes accessed | tf_op | source)
XLA Modules:
  0.0 184.6 jit_solution(12413927204556627702)
XLA Ops:
  2.3 4.7 %project.1 = (bf16[512,768]{1,0:T(8,128)(2,1)}, bf16[512,128]{1,0:T(8,128)(2,1)}) custom-call(bf16[512,768]{1,0:T(8,128)(2,1)} %bitcast.67, f32[768]{0:T(1024)} %refs_10_.1, f32[768]{0:T(1024)} %refs_11_.1, bf16[768,896]{1,0:T(8,128)(2,1)} %refs_13_.1, f32[896]{0:T(1024)} %add_ref.2, f32[3,128,128]{2,1,0:T(8,128)} %pad_maximum_fusion.4.tables_ref.refs_14_), custom_call_target="tpu_custom_call" | custom-call | flops 6000000000 | tf_op jit(solution)/shard_map/project/pallas_call | solution.py:166
  7.0 3.0 %collective-permute-start.5 = (bf16[4,128,128]{2,1,0:T(8,128)(2,1)}, bf16[4,128,128]{2,1,0:T(8,128)(2,1)S(1)}, u32[]{:S(2)}, u32[]{:S(2)}) collective-permute-start(bf16[4,128,128]{2,1,0:T(8,128)(2,1)} %bitcast.55), channel_id=1, source_target_pairs={{0,2},{1,3},{2,4},{3,5},{4,6},{5,7},{6,0},{7,1},{8,10},{9,11},{10,... | collective-permute-start | bytes 393224 | tf_op jit(solution)/shard_map/ppermute | solution.py:46
  10.0 2.6 %collective-permute-start.6 = (bf16[4,128,128]{2,1,0:T(8,128)(2,1)}, bf16[4,128,128]{2,1,0:T(8,128)(2,1)S(1)}, u32[]{:S(2)}, u32[]{:S(2)}) collective-permute-start(bf16[4,128,128]{2,1,0:T(8,128)(2,1)} %bitcast.56), channel_id=1, source_target_pairs={{0,4},{1,5},{2,6},{3,7},{4,0},{5,1},{6,2},{7,3},{8,12},{9,13},{10,... | collective-permute-start | bytes 393224 | tf_op jit(solution)/shard_map/ppermute | solution.py:46
  12.6 1.3 collective-permute-start.7
  14.5 0.9 copy-done.13
  15.6 22.0 %feed_forward.1 = (bf16[512,768]{1,0:T(8,128)(2,1)}, bf16[512,768]{1,0:T(8,128)(2,1)}, bf16[1024,1536]{1,0:T(8,128)(2,1)}, bf16[768,1024]{1,0:T(8,128)(2,1)}, bf...) custom-call(s32[4]{0:T(128)} %pad_add_fusion.place_ref, bf16[512,768]{1,0:T(8,128)(2,1)} %bitcast.68, ...), custom_call_target="tpu_custom_call" | custom-call | flops 24000000000 | tf_op jit(solution)/shard_map/feed_forward/pallas_call | solution.py:297
  37.8 1.6 collective-permute-start.8
  39.4 15.4 %feed_backward.1 = (bf16[512,768]{1,0:T(8,128)(2,1)}, bf16[512,768]{1,0:T(8,128)(2,1)}, bf16[512,768]{1,0:T(8,128)(2,1)}, bf16[8,48,1536]{2,1,0:T(8,128)(2,1)}, ...) custom-call(s32[4]{0:T(128)} %pad_add_fusion.place_ref, bf16[512,768]{1,0:T(8,128)(2,1)} %bitcast.74, ...), custom_call_target="tpu_custom_call" | custom-call | flops 19200000000 | tf_op jit(solution)/shard_map/feed_backward/pallas_call | solution.py:404
  54.8 1.6 collective-permute-start.2
  58.4 24.1 %attention.1 = (bf16[4,128,768]{2,1,0:T(8,128)(2,1)}, bf16[4,128,768]{2,1,0:T(8,128)(2,1)}, bf16[4,4,128,128]{3,2,1,0:T(8,128)(2,1)}, bf16[4,4,128,128]{3,2,1,0:T(8,128)(2,1)}) custom-call(s32[4]{0:T(128)} %pad_add_fusion.place_ref, bf16[4,4,128,128]{3,2,1,0:T(8,128)(2,1)} %copy-done.1, bf16[4,4,128,128]{3,2,1,0:T(8,128)(2,1)} %copy-done.21, ...), custom_call_target="tpu_custom_call" | custom-call | flops 30000001024 | tf_op jit(solution)/shard_map/attention/pallas_call | solution.py:655
  83.0 7.8 %weights.1 = (bf16[2,768,384]{2,1,0:T(8,128)(2,1)}, bf16[2,768,384]{2,1,0:T(8,128)(2,1)}, bf16[512,768]{1,0:T(8,128)(2,1)}, f32[8,768]{1,0:T(8,128)}) custom-call(s32[4]{0:T(128)} %pad_add_fusion.place_ref, bf16[512,768]{1,0:T(8,128)(2,1)} %bitcast.98, bf16[512,768]{1,0:T(8,128)(2,1)} %bitcast.95, bf16[512,768]{1,0:T(8,128)(2,1)} %bitcast.75, ...), custom_call_target="tpu_custom_call" | custom-call | flops 7200000000 | tf_op jit(solution)/shard_map/weights/pallas_call | solution.py:705
  91.0 1.0 copy-done.11
  92.0 2.9 %add_split.8 = (bf16[2,192,768]{2,1,0:T(8,128)(2,1)}, bf16[2,192,768]{2,1,0:T(8,128)(2,1)}) custom-call(s32[4]{0:T(128)} %pad_add_fusion.place_ref, bf16[2,2,192,768]{3,2,1,0:T(8,128)(2,1)} %bitcast.90, bf16[2,2,192,768]{3,2,1,0:T(8,128)(2,1)} %bitcast.65), custom_call_target="tpu_custom_call" | custom-call | flops 3600000000 | tf_op jit(solution)/shard_map/add_split/pallas_call | solution.py:139
  97.0 1.1 collective-permute-start.11
  98.2 1.7 collective-permute-start.12
  99.9 2.9 %add_split.9 = (bf16[4,48,1536]{2,1,0:T(8,128)(2,1)}, bf16[4,48,1536]{2,1,0:T(8,128)(2,1)}) custom-call(s32[4]{0:T(128)} %pad_add_fusion.place_ref, bf16[4,2,48,1536]{3,2,1,0:T(8,128)(2,1)} %bitcast.89, bf16[4,2,48,1536]{3,2,1,0:T(8,128)(2,1)} %bitcast.63), custom_call_target="tpu_custom_call" | custom-call | flops 3600000000 | tf_op jit(solution)/shard_map/add_split/pallas_call | solution.py:139
  102.7 5.2 %mix.1 = (bf16[512,768]{1,0:T(8,128)(2,1)}, bf16[512,768]{1,0:T(8,128)(2,1)}) custom-call(bf16[512,768]{1,0:T(8,128)(2,1)} %bitcast.70, bf16[512,768]{1,0:T(8,128)(2,1)} %get-tuple-element.153.mlp_ref, bf16[512,768]{1,0:T(8,128)(2,1)} %copy-done.14, bf16[512,768]{1,0:T(8,128)(2,1)} %bitcast.96, bf16[512,768]{1,0:T(8,128)(2,1)} %get-tuple-element.155.grad_ref, ...), custom_call_target="tpu_custom_call" | custom-call | flops 7200000000 | tf_op jit(solution)/shard_map/mix/pallas_call | solution.py:733
  109.0 2.9 %add_split.10 = (bf16[8,96,384]{2,1,0:T(8,128)(2,1)}, bf16[8,96,384]{2,1,0:T(8,128)(2,1)}) custom-call(s32[4]{0:T(128)} %pad_add_fusion.place_ref, bf16[8,2,96,384]{3,2,1,0:T(8,128)(2,1)} %bitcast.91, bf16[8,2,96,384]{3,2,1,0:T(8,128)(2,1)} %bitcast.64), custom_call_target="tpu_custom_call" | custom-call | flops 3600000000 | tf_op jit(solution)/shard_map/add_split/pallas_call | solution.py:139
  111.9 1.1 collective-permute-start.18
  113.0 2.2 %add_split.11 = (bf16[1,192,768]{2,1,0:T(8,128)(2,1)}, bf16[1,192,768]{2,1,0:T(8,128)(2,1)}) custom-call(s32[4]{0:T(128)} %pad_add_fusion.place_ref, bf16[1,2,192,768]{3,2,1,0:T(8,128)(2,1)} %bitcast.100, bf16[1,2,192,768]{3,2,1,0:T(8,128)(2,1)} %bitcast.78), custom_call_target="tpu_custom_call" | custom-call | flops 3600000000 | tf_op jit(solution)/shard_map/add_split/pallas_call | solution.py:139
  115.2 1.0 collective-permute-start.16
  116.9 5.7 %finish.1 = (bf16[512,768]{1,0:T(8,128)(2,1)}, bf16[8,224,128]{2,1,0:T(8,128)(2,1)}) custom-call(s32[4]{0:T(128)} %pad_add_fusion.place_ref, bf16[512,128]{1,0:T(8,128)(2,1)} %bitcast.54, bf16[512,128]{1,0:T(8,128)(2,1)} %bitcast.83, bf16[512,128]{1,0:T(8,128)(2,1)} %bitcast.84, bf16[512,128]{1,0:T(8,128)(2,1)} %bitcast.85, bf16[512,128]{1,0:T(8,128)(2,1)} %bitcast.82, ...), custom_call_target="tpu_custom_call" | custom-call | flops 7200000000 | tf_op jit(solution)/shard_map/finish/pallas_call | solution.py:827
  122.5 5.6 %all-to-all-start = ((bf16[8,224,128]{2,1,0:T(8,128)(2,1)}), bf16[8,224,128]{2,1,0:T(8,128)(2,1)S(1)}, u32[]{:S(2)}, u32[]{:S(2)}) async-start(bf16[8,224,128]{2,1,0:T(8,128)(2,1)} %get-tuple-element.174), calls=%async_computation | async-start | bytes 917504 | tf_op jit(solution)/shard_map/all_to_all | solution.py:1005
  128.1 12.5 %collective-permute-done.18 = bf16[8,96,384]{2,1,0:T(8,128)(2,1)S(1)} collective-permute-done((bf16[8,96,384]{2,1,0:T(8,128)(2,1)}, bf16[8,96,384]{2,1,0:T(8,128)(2,1)S(1)}, u32[]{:S(2)}, u32[]{:S(2)}) %collective-permute-start.18) | collective-permute-done | bytes 589856 | tf_op jit(solution)/shard_map/ppermute | solution.py:41
  140.6 0.8 copy-done.20
  141.4 2.2 %add_split.12 = (bf16[4,96,384]{2,1,0:T(8,128)(2,1)}, bf16[4,96,384]{2,1,0:T(8,128)(2,1)}) custom-call(s32[4]{0:T(128)} %pad_add_fusion.place_ref, bf16[4,2,96,384]{3,2,1,0:T(8,128)(2,1)} %bitcast.101, bf16[4,2,96,384]{3,2,1,0:T(8,128)(2,1)} %bitcast.79), custom_call_target="tpu_custom_call" | custom-call | flops 3600000000 | tf_op jit(solution)/shard_map/add_split/pallas_call | solution.py:139
  143.6 1.8 collective-permute-start.24
  145.4 0.8 copy-done.18
  146.2 2.2 %add_split.13 = (bf16[2,48,1536]{2,1,0:T(8,128)(2,1)}, bf16[2,48,1536]{2,1,0:T(8,128)(2,1)}) custom-call(s32[4]{0:T(128)} %pad_add_fusion.place_ref, bf16[2,2,48,1536]{3,2,1,0:T(8,128)(2,1)} %bitcast.99, bf16[2,2,48,1536]{3,2,1,0:T(8,128)(2,1)} %bitcast.77), custom_call_target="tpu_custom_call" | custom-call | flops 3600000000 | tf_op jit(solution)/shard_map/add_split/pallas_call | solution.py:139
  148.8 1.3 collective-permute-start.22
  150.9 1.7 gather_sums.1.refs_0_
  153.3 1.2 collective-permute-start.21
  154.5 1.8 add_split.14
  156.3 1.8 collective-permute-done.23
  158.0 1.9 %collective-permute-start.25 = (bf16[2,96,384]{2,1,0:T(8,128)(2,1)}, bf16[2,96,384]{2,1,0:T(8,128)(2,1)S(1)}, u32[]{:S(2)}, u32[]{:S(2)}) collective-permute-start(bf16[2,96,384]{2,1,0:T(8,128)(2,1)} %get-tuple-element.191), channel_id=1, source_target_pairs={{0,4},{1,5},{2,6},{3,7},{4,0},{5,1},{6,2},{7,3},{8,12},{9,13},{10,... | collective-permute-start | bytes 442376 | tf_op jit(solution)/shard_map/ppermute | solution.py:41
  159.9 1.8 add_split.15
  161.8 1.0 collective-permute-start.28
  162.9 2.5 %collective-permute-start.27 = (bf16[192,768]{1,0:T(8,128)(2,1)S(1)}, bf16[192,768]{1,0:T(8,128)(2,1)S(1)}, u32[]{:S(2)}, u32[]{:S(2)}) collective-permute-start(bf16[192,768]{1,0:T(8,128)(2,1)S(1)} %add_convert_fusion), channel_id=1, source_target_pairs={{0,16},{8,24},{16,0},{24,8},{1,17},{9,25},{17,1},{25,9},{2,18},{10... | collective-permute-start | bytes 884744 | tf_op jit(solution)/shard_map/ppermute | solution.py:41
  166.7 1.6 last_sums.1
  168.3 1.3 pad_maximum_fusion.5
  169.5 2.7 %collective-permute-done.25 = bf16[2,96,384]{2,1,0:T(8,128)(2,1)S(1)} collective-permute-done((bf16[2,96,384]{2,1,0:T(8,128)(2,1)}, bf16[2,96,384]{2,1,0:T(8,128)(2,1)S(1)}, u32[]{:S(2)}, u32[]{:S(2)}) %collective-permute-start.25) | collective-permute-done | bytes 147488 | tf_op jit(solution)/shard_map/ppermute | solution.py:41
  172.3 1.0 collective-permute-start.26
  173.3 0.9 collective-permute-done.28
  174.2 1.1 collective-permute-start.31
  175.5 3.4 %collective-permute-done.26 = bf16[2,96,384]{2,1,0:T(8,128)(2,1)S(1)} collective-permute-done((bf16[2,96,384]{2,1,0:T(8,128)(2,1)S(1)}, bf16[2,96,384]{2,1,0:T(8,128)(2,1)S(1)}, u32[]{:S(2)}, u32[]{:S(2)}) %collective-permute-start.26) | collective-permute-done | bytes 147488 | tf_op jit(solution)/shard_map/ppermute | solution.py:41
  179.0 1.5 collective-permute-done.31
  180.6 1.1 select_convert_fusion
  183.5 1.1 maximum_convert_fusion
  (122 shorter events, 14.3 us)
Async XLA Ops:
  0.6 13.9 %collective-permute-start = (bf16[512,768]{1,0:T(8,128)(2,1)}, bf16[512,768]{1,0:T(8,128)(2,1)S(1)}, u32[]{:S(2)}, u32[]{:S(2)}) collective-permute-start(bf16[512,768]{1,0:T(8,128)(2,1)} %bitcast.72), channel_id=1, source_target_pairs={{0,8},{8,0},{16,24},{24,16},{1,9},{9,1},{17,25},{25,17},{2,10},{10... | collective-permute-start | bytes 2359304 | tf_op jit(solution)/shard_map/ppermute | solution.py:41
  1.2 13.3 %collective-permute-start.1 = (bf16[512,768]{1,0:T(8,128)(2,1)}, bf16[512,768]{1,0:T(8,128)(2,1)S(1)}, u32[]{:S(2)}, u32[]{:S(2)}) collective-permute-start(bf16[512,768]{1,0:T(8,128)(2,1)} %bitcast.66), channel_id=1, source_target_pairs={{0,8},{8,0},{16,24},{24,16},{1,9},{9,1},{17,25},{25,17},{2,10},{10... | collective-permute-start | bytes 2359304 | tf_op jit(solution)/shard_map/ppermute | solution.py:41
  7.0 30.7 %collective-permute-start.5 = (bf16[4,128,128]{2,1,0:T(8,128)(2,1)}, bf16[4,128,128]{2,1,0:T(8,128)(2,1)S(1)}, u32[]{:S(2)}, u32[]{:S(2)}) collective-permute-start(bf16[4,128,128]{2,1,0:T(8,128)(2,1)} %bitcast.55), channel_id=1, source_target_pairs={{0,2},{1,3},{2,4},{3,5},{4,6},{5,7},{6,0},{7,1},{8,10},{9,11},{10,... | collective-permute-start | bytes 393224 | tf_op jit(solution)/shard_map/ppermute | solution.py:46
  10.0 27.7 %collective-permute-start.6 = (bf16[4,128,128]{2,1,0:T(8,128)(2,1)}, bf16[4,128,128]{2,1,0:T(8,128)(2,1)S(1)}, u32[]{:S(2)}, u32[]{:S(2)}) collective-permute-start(bf16[4,128,128]{2,1,0:T(8,128)(2,1)} %bitcast.56), channel_id=1, source_target_pairs={{0,4},{1,5},{2,6},{3,7},{4,0},{5,1},{6,2},{7,3},{8,12},{9,13},{10,... | collective-permute-start | bytes 393224 | tf_op jit(solution)/shard_map/ppermute | solution.py:46
  12.6 25.1 %collective-permute-start.7 = (bf16[4,128,128]{2,1,0:T(8,128)(2,1)}, bf16[4,128,128]{2,1,0:T(8,128)(2,1)S(1)}, u32[]{:S(2)}, u32[]{:S(2)}) collective-permute-start(bf16[4,128,128]{2,1,0:T(8,128)(2,1)} %bitcast.57), channel_id=1, source_target_pairs={{0,6},{1,7},{2,0},{3,1},{4,2},{5,3},{6,4},{7,5},{8,14},{9,15},{10,... | collective-permute-start | bytes 393224 | tf_op jit(solution)/shard_map/ppermute | solution.py:46
  15.6 22.1 %copy-start.6 = (bf16[512,128]{1,0:T(8,128)(2,1)S(1)}, bf16[512,128]{1,0:T(8,128)(2,1)}, u32[]{:S(2)}) copy-start(bf16[512,128]{1,0:T(8,128)(2,1)} %get-tuple-element.119) | copy-start | bytes 393220
  37.8 17.0 %copy-start.1 = (bf16[4,4,128,128]{3,2,1,0:T(8,128)(2,1)}, bf16[4,4,128,128]{3,2,1,0:T(8,128)(2,1)S(1)}, u32[]{:S(2)}) copy-start(bf16[4,4,128,128]{3,2,1,0:T(8,128)(2,1)S(1)} %pad_maximum_fusion.1.refs_0_) | copy-start | bytes 1572868
  37.8 19.8 %collective-permute-start.8 = (bf16[4,4,128,128]{3,2,1,0:T(8,128)(2,1)S(1)}, bf16[4,4,128,128]{3,2,1,0:T(8,128)(2,1)S(1)}, u32[]{:S(2)}, u32[]{:S(2)}) collective-permute-start(bf16[4,4,128,128]{3,2,1,0:T(8,128)(2,1)S(1)} %pad_maximum_fusion.1.refs_0_), channel_id=1, source_target_pairs={{0,1},{1,0},{2,3},{3,2},{4,5},{5,4},{6,7},{7,6},{8,9},{9,8},{10,11... | collective-permute-start | bytes 1572872 | tf_op jit(solution)/shard_map/ppermute | solution.py:41
  39.4 17.0 %copy-start.16 = (bf16[512,768]{1,0:T(8,128)(2,1)S(1)}, bf16[512,768]{1,0:T(8,128)(2,1)}, u32[]{:S(2)}) copy-start(bf16[512,768]{1,0:T(8,128)(2,1)} %get-tuple-element.125) | copy-start | bytes 2359300
  39.4 17.5 %copy-start.9 = (bf16[768,768]{1,0:T(8,128)(2,1)S(1)}, bf16[768,768]{1,0:T(8,128)(2,1)}, u32[]{:S(2)}) copy-start(bf16[768,768]{1,0:T(8,128)(2,1)} %get-tuple-element.139) | copy-start | bytes 3538948
  54.8 28.1 %collective-permute-start.2 = (bf16[8,48,1536]{2,1,0:T(8,128)(2,1)}, bf16[8,48,1536]{2,1,0:T(8,128)(2,1)S(1)}, u32[]{:S(2)}, u32[]{:S(2)}) collective-permute-start(bf16[8,48,1536]{2,1,0:T(8,128)(2,1)} %get-tuple-element.124), channel_id=1, source_target_pairs={{0,16},{8,24},{16,0},{24,8},{1,17},{9,25},{17,1},{25,9},{2,18},{10... | collective-permute-start | bytes 3538952 | tf_op jit(solution)/shard_map/ppermute | solution.py:41
  56.4 26.6 %collective-permute-start.3 = (bf16[512,768]{1,0:T(8,128)(2,1)S(1)}, bf16[512,768]{1,0:T(8,128)(2,1)S(1)}, u32[]{:S(2)}, u32[]{:S(2)}) collective-permute-start(bf16[512,768]{1,0:T(8,128)(2,1)S(1)} %copy-done.16), channel_id=1, source_target_pairs={{0,8},{8,0},{16,24},{24,16},{1,9},{9,1},{17,25},{25,17},{2,10},{10... | collective-permute-start | bytes 2359304 | tf_op jit(solution)/shard_map/ppermute | solution.py:41
  56.4 26.6 %collective-permute-start.4 = (bf16[512,768]{1,0:T(8,128)(2,1)}, bf16[512,768]{1,0:T(8,128)(2,1)S(1)}, u32[]{:S(2)}, u32[]{:S(2)}) collective-permute-start(bf16[512,768]{1,0:T(8,128)(2,1)} %get-tuple-element.126), channel_id=1, source_target_pairs={{0,8},{8,0},{16,24},{24,16},{1,9},{9,1},{17,25},{25,17},{2,10},{10... | collective-permute-start | bytes 2359304 | tf_op jit(solution)/shard_map/ppermute | solution.py:41
  56.9 34.0 %collective-permute-start.10 = (bf16[768,768]{1,0:T(8,128)(2,1)S(1)}, bf16[768,768]{1,0:T(8,128)(2,1)S(1)}, u32[]{:S(2)}, u32[]{:S(2)}) collective-permute-start(bf16[768,768]{1,0:T(8,128)(2,1)S(1)} %copy-done.9), channel_id=1, source_target_pairs={{0,2},{1,3},{2,0},{3,1},{4,6},{5,7},{6,4},{7,5},{8,10},{9,11},{10,... | collective-permute-start | bytes 3538952 | tf_op jit(solution)/shard_map/ppermute | solution.py:41
  82.4 13.7 %collective-permute-start.9 = (bf16[4,4,128,128]{3,2,1,0:T(8,128)(2,1)}, bf16[4,4,128,128]{3,2,1,0:T(8,128)(2,1)S(1)}, u32[]{:S(2)}, u32[]{:S(2)}) collective-permute-start(bf16[4,4,128,128]{3,2,1,0:T(8,128)(2,1)} %get-tuple-element.137), channel_id=1, source_target_pairs={{0,1},{1,0},{2,3},{3,2},{4,5},{5,4},{6,7},{7,6},{8,9},{9,8},{10,11... | collective-permute-start | bytes 1572872 | tf_op jit(solution)/shard_map/ppermute | solution.py:41
  83.0 7.9 %copy-start.14 = (bf16[512,768]{1,0:T(8,128)(2,1)}, bf16[512,768]{1,0:T(8,128)(2,1)S(1)}, u32[]{:S(2)}) copy-start(bf16[512,768]{1,0:T(8,128)(2,1)S(1)} %collective-permute-done.3.mlp2_ref) | copy-start | bytes 2359300
  83.0 7.9 %copy-start.12 = (bf16[512,768]{1,0:T(8,128)(2,1)}, bf16[512,768]{1,0:T(8,128)(2,1)S(1)}, u32[]{:S(2)}) copy-start(bf16[512,768]{1,0:T(8,128)(2,1)S(1)} %collective-permute-done.4.refs_9_) | copy-start | bytes 2359300
  83.0 7.9 %copy-start.8 = (bf16[8,48,1536]{2,1,0:T(8,128)(2,1)}, bf16[8,48,1536]{2,1,0:T(8,128)(2,1)S(1)}, u32[]{:S(2)}) copy-start(bf16[8,48,1536]{2,1,0:T(8,128)(2,1)S(1)} %collective-permute-done.2) | copy-start | bytes 3538948
  90.9 17.1 %collective-permute-start.15 = (bf16[2,768,384]{2,1,0:T(8,128)(2,1)}, bf16[2,768,384]{2,1,0:T(8,128)(2,1)S(1)}, u32[]{:S(2)}, u32[]{:S(2)}) collective-permute-start(bf16[2,768,384]{2,1,0:T(8,128)(2,1)} %get-tuple-element.143), channel_id=1, source_target_pairs={{0,8},{8,0},{16,24},{24,16},{1,9},{9,1},{17,25},{25,17},{2,10},{10... | collective-permute-start | bytes 3538952 | tf_op jit(solution)/shard_map/ppermute | solution.py:41
  92.0 4.2 %copy-start = (bf16[4,4,128,128]{3,2,1,0:T(8,128)(2,1)S(1)}, bf16[4,4,128,128]{3,2,1,0:T(8,128)(2,1)}, u32[]{:S(2)}) copy-start(bf16[4,4,128,128]{3,2,1,0:T(8,128)(2,1)} %get-tuple-element.147) | copy-start | bytes 1572868
  94.9 17.0 %collective-permute-start.14 = (bf16[2,192,768]{2,1,0:T(8,128)(2,1)}, bf16[2,192,768]{2,1,0:T(8,128)(2,1)S(1)}, u32[]{:S(2)}, u32[]{:S(2)}) collective-permute-start(bf16[2,192,768]{2,1,0:T(8,128)(2,1)} %get-tuple-element.146), channel_id=1, source_target_pairs={{0,16},{8,24},{16,0},{24,8},{1,17},{9,25},{17,1},{25,9},{2,18},{10... | collective-permute-start | bytes 1769480 | tf_op jit(solution)/shard_map/ppermute | solution.py:41
  97.0 18.2 %collective-permute-start.11 = (bf16[4,128,128]{2,1,0:T(8,128)(2,1)S(1)}, bf16[4,128,128]{2,1,0:T(8,128)(2,1)S(1)}, u32[]{:S(2)}, u32[]{:S(2)}) collective-permute-start(bf16[4,128,128]{2,1,0:T(8,128)(2,1)S(1)} %get-tuple-element.227), channel_id=1, source_target_pairs={{0,6},{1,7},{2,0},{3,1},{4,2},{5,3},{6,4},{7,5},{8,14},{9,15},{10,... | collective-permute-start | bytes 393224 | tf_op jit(solution)/shard_map/ppermute | solution.py:46
  98.2 18.0 %collective-permute-start.12 = (bf16[4,128,128]{2,1,0:T(8,128)(2,1)S(1)}, bf16[4,128,128]{2,1,0:T(8,128)(2,1)S(1)}, u32[]{:S(2)}, u32[]{:S(2)}) collective-permute-start(bf16[4,128,128]{2,1,0:T(8,128)(2,1)S(1)} %get-tuple-element.226), channel_id=1, source_target_pairs={{0,4},{1,5},{2,6},{3,7},{4,0},{5,1},{6,2},{7,3},{8,12},{9,13},{10,... | collective-permute-start | bytes 393224 | tf_op jit(solution)/shard_map/ppermute | solution.py:46
  99.9 16.3 %collective-permute-start.13 = (bf16[4,128,128]{2,1,0:T(8,128)(2,1)S(1)}, bf16[4,128,128]{2,1,0:T(8,128)(2,1)S(1)}, u32[]{:S(2)}, u32[]{:S(2)}) collective-permute-start(bf16[4,128,128]{2,1,0:T(8,128)(2,1)S(1)} %get-tuple-element.225), channel_id=1, source_target_pairs={{0,2},{1,3},{2,4},{3,5},{4,6},{5,7},{6,0},{7,1},{8,10},{9,11},{10,... | collective-permute-start | bytes 393224 | tf_op jit(solution)/shard_map/ppermute | solution.py:46
  102.7 5.2 %copy-start.17 = (bf16[4,48,1536]{2,1,0:T(8,128)(2,1)S(1)}, bf16[4,48,1536]{2,1,0:T(8,128)(2,1)}, u32[]{:S(2)}) copy-start(bf16[4,48,1536]{2,1,0:T(8,128)(2,1)} %get-tuple-element.151) | copy-start | bytes 1769476
  108.0 37.4 %collective-permute-start.17 = (bf16[4,48,1536]{2,1,0:T(8,128)(2,1)S(1)}, bf16[4,48,1536]{2,1,0:T(8,128)(2,1)S(1)}, u32[]{:S(2)}, u32[]{:S(2)}) collective-permute-start(bf16[4,48,1536]{2,1,0:T(8,128)(2,1)S(1)} %copy-done.17), channel_id=1, source_target_pairs={{0,1},{1,0},{2,3},{3,2},{4,5},{5,4},{6,7},{7,6},{8,9},{9,8},{10,11... | collective-permute-start | bytes 1769480 | tf_op jit(solution)/shard_map/ppermute | solution.py:41
  111.9 28.7 %collective-permute-start.18 = (bf16[8,96,384]{2,1,0:T(8,128)(2,1)}, bf16[8,96,384]{2,1,0:T(8,128)(2,1)S(1)}, u32[]{:S(2)}, u32[]{:S(2)}) collective-permute-start(bf16[8,96,384]{2,1,0:T(8,128)(2,1)} %get-tuple-element.162), channel_id=1, source_target_pairs={{0,1},{1,0},{2,3},{3,2},{4,5},{5,4},{6,7},{7,6},{8,9},{9,8},{10,11... | collective-permute-start | bytes 1769480 | tf_op jit(solution)/shard_map/ppermute | solution.py:41
  115.2 33.5 %collective-permute-start.16 = (bf16[1,192,768]{2,1,0:T(8,128)(2,1)}, bf16[1,192,768]{2,1,0:T(8,128)(2,1)S(1)}, u32[]{:S(2)}, u32[]{:S(2)}) collective-permute-start(bf16[1,192,768]{2,1,0:T(8,128)(2,1)} %get-tuple-element.165), channel_id=1, source_target_pairs={{0,1},{1,0},{2,3},{3,2},{4,5},{5,4},{6,7},{7,6},{8,9},{9,8},{10,11... | collective-permute-start | bytes 884744 | tf_op jit(solution)/shard_map/ppermute | solution.py:41
  122.5 27.6 %all-to-all-start = ((bf16[8,224,128]{2,1,0:T(8,128)(2,1)}), bf16[8,224,128]{2,1,0:T(8,128)(2,1)S(1)}, u32[]{:S(2)}, u32[]{:S(2)}) async-start(bf16[8,224,128]{2,1,0:T(8,128)(2,1)} %get-tuple-element.174), calls=%async_computation | async-start | bytes 917504 | tf_op jit(solution)/shard_map/all_to_all | solution.py:1005
  143.6 9.6 %collective-permute-start.24 = (bf16[4,96,384]{2,1,0:T(8,128)(2,1)}, bf16[4,96,384]{2,1,0:T(8,128)(2,1)S(1)}, u32[]{:S(2)}, u32[]{:S(2)}) collective-permute-start(bf16[4,96,384]{2,1,0:T(8,128)(2,1)} %get-tuple-element.180), channel_id=1, source_target_pairs={{0,2},{1,3},{2,0},{3,1},{4,6},{5,7},{6,4},{7,5},{8,10},{9,11},{10,... | collective-permute-start | bytes 884744 | tf_op jit(solution)/shard_map/ppermute | solution.py:41
  146.2 2.5 %copy-start.3 = (bf16[1,192,768]{2,1,0:T(8,128)(2,1)S(1)}, bf16[1,192,768]{2,1,0:T(8,128)(2,1)}, u32[]{:S(2)}) copy-start(bf16[1,192,768]{2,1,0:T(8,128)(2,1)} %get-tuple-element.184) | copy-start | bytes 884740
  148.5 9.6 %collective-permute-start.23 = (bf16[2,48,1536]{2,1,0:T(8,128)(2,1)}, bf16[2,48,1536]{2,1,0:T(8,128)(2,1)S(1)}, u32[]{:S(2)}, u32[]{:S(2)}) collective-permute-start(bf16[2,48,1536]{2,1,0:T(8,128)(2,1)} %get-tuple-element.183), channel_id=1, source_target_pairs={{0,2},{1,3},{2,0},{3,1},{4,6},{5,7},{6,4},{7,5},{8,10},{9,11},{10,... | collective-permute-start | bytes 884744 | tf_op jit(solution)/shard_map/ppermute | solution.py:41
  148.8 12.9 %collective-permute-start.22 = (bf16[192,768]{1,0:T(8,128)(2,1)S(1)}, bf16[192,768]{1,0:T(8,128)(2,1)S(1)}, u32[]{:S(2)}, u32[]{:S(2)}) collective-permute-start(bf16[192,768]{1,0:T(8,128)(2,1)S(1)} %fusion), channel_id=1, source_target_pairs={{4,0},{5,1},{6,2},{7,3},{8,12},{9,13},{10,14},{11,15},{20,16},{21,... | collective-permute-start | bytes 884744 | tf_op jit(solution)/shard_map/ppermute | solution.py:57
  152.6 10.3 %collective-permute-start.19 = (bf16[224,128]{1,0:T(8,128)(2,1)}, bf16[224,128]{1,0:T(8,128)(2,1)S(1)}, u32[]{:S(2)}, u32[]{:S(2)}) collective-permute-start(bf16[224,128]{1,0:T(8,128)(2,1)} %gather_sums.1.refs_0_), channel_id=1, source_target_pairs={{0,8},{8,0},{16,24},{24,16},{1,9},{9,1},{17,25},{25,17},{2,10},{10... | collective-permute-start | bytes 172040 | tf_op jit(solution)/shard_map/ppermute | solution.py:41
  152.6 12.9 %collective-permute-start.20 = (bf16[224,128]{1,0:T(8,128)(2,1)}, bf16[224,128]{1,0:T(8,128)(2,1)S(1)}, u32[]{:S(2)}, u32[]{:S(2)}) collective-permute-start(bf16[224,128]{1,0:T(8,128)(2,1)} %gather_sums.1.refs_0_), channel_id=1, source_target_pairs={{0,16},{8,24},{16,0},{24,8},{1,17},{9,25},{17,1},{25,9},{2,18},{10... | collective-permute-start | bytes 172040 | tf_op jit(solution)/shard_map/ppermute | solution.py:41
  153.3 12.2 %collective-permute-start.21 = (bf16[224,128]{1,0:T(8,128)(2,1)}, bf16[224,128]{1,0:T(8,128)(2,1)S(1)}, u32[]{:S(2)}, u32[]{:S(2)}) collective-permute-start(bf16[224,128]{1,0:T(8,128)(2,1)} %gather_sums.1.refs_0_), channel_id=1, source_target_pairs={{0,24},{8,16},{16,8},{24,0},{1,25},{9,17},{17,9},{25,1},{2,26},{10... | collective-permute-start | bytes 172040 | tf_op jit(solution)/shard_map/ppermute | solution.py:41
  158.0 1.9 %copy-start.22 = (bf16[2,48,1536]{2,1,0:T(8,128)(2,1)}, bf16[2,48,1536]{2,1,0:T(8,128)(2,1)S(1)}, u32[]{:S(2)}) copy-start(bf16[2,48,1536]{2,1,0:T(8,128)(2,1)S(1)} %collective-permute-done.23) | copy-start | bytes 884740
  158.0 14.2 %collective-permute-start.25 = (bf16[2,96,384]{2,1,0:T(8,128)(2,1)}, bf16[2,96,384]{2,1,0:T(8,128)(2,1)S(1)}, u32[]{:S(2)}, u32[]{:S(2)}) collective-permute-start(bf16[2,96,384]{2,1,0:T(8,128)(2,1)} %get-tuple-element.191), channel_id=1, source_target_pairs={{0,4},{1,5},{2,6},{3,7},{4,0},{5,1},{6,2},{7,3},{8,12},{9,13},{10,... | collective-permute-start | bytes 442376 | tf_op jit(solution)/shard_map/ppermute | solution.py:41
  161.8 12.4 %collective-permute-start.28 = (bf16[1,48,1536]{2,1,0:T(8,128)(2,1)}, bf16[1,48,1536]{2,1,0:T(8,128)(2,1)S(1)}, u32[]{:S(2)}, u32[]{:S(2)}) collective-permute-start(bf16[1,48,1536]{2,1,0:T(8,128)(2,1)} %get-tuple-element.194), channel_id=1, source_target_pairs={{0,4},{1,5},{2,6},{3,7},{4,0},{5,1},{6,2},{7,3},{8,12},{9,13},{10,... | collective-permute-start | bytes 442376 | tf_op jit(solution)/shard_map/ppermute | solution.py:41
  162.9 9.4 %copy-start.4 = (bf16[2,96,384]{2,1,0:T(8,128)(2,1)S(1)}, bf16[2,96,384]{2,1,0:T(8,128)(2,1)}, u32[]{:S(2)}) copy-start(bf16[2,96,384]{2,1,0:T(8,128)(2,1)} %get-tuple-element.204) | copy-start | bytes 442372
  162.9 11.3 %copy-start.5 = (bf16[1,48,1536]{2,1,0:T(8,128)(2,1)S(1)}, bf16[1,48,1536]{2,1,0:T(8,128)(2,1)}, u32[]{:S(2)}) copy-start(bf16[1,48,1536]{2,1,0:T(8,128)(2,1)} %get-tuple-element.207) | copy-start | bytes 442372
  162.9 2.6 %copy-start.27 = (bf16[224,128]{1,0:T(8,128)(2,1)}, bf16[224,128]{1,0:T(8,128)(2,1)S(1)}, u32[]{:S(2)}) copy-start(bf16[224,128]{1,0:T(8,128)(2,1)S(1)} %collective-permute-done.19.refs_1_) | copy-start | bytes 172036
  162.9 12.4 %collective-permute-start.27 = (bf16[192,768]{1,0:T(8,128)(2,1)S(1)}, bf16[192,768]{1,0:T(8,128)(2,1)S(1)}, u32[]{:S(2)}, u32[]{:S(2)}) collective-permute-start(bf16[192,768]{1,0:T(8,128)(2,1)S(1)} %add_convert_fusion), channel_id=1, source_target_pairs={{0,16},{8,24},{16,0},{24,8},{1,17},{9,25},{17,1},{25,9},{2,18},{10... | collective-permute-start | bytes 884744 | tf_op jit(solution)/shard_map/ppermute | solution.py:41
  172.3 6.6 %collective-permute-start.26 = (bf16[2,96,384]{2,1,0:T(8,128)(2,1)S(1)}, bf16[2,96,384]{2,1,0:T(8,128)(2,1)S(1)}, u32[]{:S(2)}, u32[]{:S(2)}) collective-permute-start(bf16[2,96,384]{2,1,0:T(8,128)(2,1)S(1)} %add_convert_fusion.4), channel_id=1, source_target_pairs={{0,16},{8,24},{16,0},{24,8},{1,17},{9,25},{17,1},{25,9},{2,18},{10... | collective-permute-start | bytes 442376 | tf_op jit(solution)/shard_map/ppermute | solution.py:41
  174.2 6.3 %collective-permute-start.31 = (bf16[48,1536]{1,0:T(8,128)(2,1)S(1)}, bf16[48,1536]{1,0:T(8,128)(2,1)S(1)}, u32[]{:S(2)}, u32[]{:S(2)}) collective-permute-start(bf16[48,1536]{1,0:T(8,128)(2,1)S(1)} %fusion.1), channel_id=1, source_target_pairs={{0,16},{8,24},{16,0},{24,8},{1,17},{9,25},{17,1},{25,9},{2,18},{10... | collective-permute-start | bytes 442376 | tf_op jit(solution)/shard_map/ppermute | solution.py:41
  175.4 5.2 %collective-permute-start.30 = (bf16[384,768]{1,0:T(8,128)(2,1)S(1)}, bf16[384,768]{1,0:T(8,128)(2,1)S(1)}, u32[]{:S(2)}, u32[]{:S(2)}) collective-permute-start(bf16[384,768]{1,0:T(8,128)(2,1)S(1)} %pad_maximum_fusion), channel_id=1, source_target_pairs={{0,8},{8,0},{16,24},{24,16},{1,9},{9,1},{17,25},{25,17},{2,10},{10... | collective-permute-start | bytes 1769480 | tf_op jit(solution)/shard_map/ppermute | solution.py:41
  178.9 2.8 %collective-permute-start.29 = (bf16[2,96,384]{2,1,0:T(8,128)(2,1)S(1)}, bf16[2,96,384]{2,1,0:T(8,128)(2,1)S(1)}, u32[]{:S(2)}, u32[]{:S(2)}) collective-permute-start(bf16[2,96,384]{2,1,0:T(8,128)(2,1)S(1)} %add_convert_fusion.2), channel_id=1, source_target_pairs={{0,8},{8,0},{16,24},{24,16},{1,9},{9,1},{17,25},{25,17},{2,10},{10... | collective-permute-start | bytes 442376 | tf_op jit(solution)/shard_map/ppermute | solution.py:41
  180.5 2.8 %collective-permute-start.32 = (bf16[96,1536]{1,0:T(8,128)(2,1)S(1)}, bf16[96,1536]{1,0:T(8,128)(2,1)S(1)}, u32[]{:S(2)}, u32[]{:S(2)}) collective-permute-start(bf16[96,1536]{1,0:T(8,128)(2,1)S(1)} %pad_maximum_fusion.3), channel_id=1, source_target_pairs={{0,8},{8,0},{16,24},{24,16},{1,9},{9,1},{17,25},{25,17},{2,10},{10... | collective-permute-start | bytes 884744 | tf_op jit(solution)/shard_map/ppermute | solution.py:41
  (16 other events, 13.9 us)

commit v2 on v1

--- a/solution.py
+++ b/solution.py
@@ -147,31 +147,64 @@
     )(place, *arrays)
 
 
-def project_kernel(copies, x_ref, gain_ref, bias_ref, weight_ref, add_ref, tables_ref, q_ref, kv_ref):
+def keys_kernel(copies, x_ref, gain_ref, bias_ref, weight_ref, add_ref, tables_ref, kv_ref, first_ref):
     normed, _ = normalize(x_ref[...].astype(F32))
     first_in = (normed * wide(gain_ref) + wide(bias_ref)).astype(BF16)
+    first_ref[...] = first_in
+    part = dot(first_in, weight_ref[...]) + wide(add_ref)[:, D:]
+    kv_ref[...] = turn(part, key_tables(repeated(tables_ref, copies)), 1).astype(BF16)
+
+
+def queries_kernel(copies, first_ref, weight_ref, add_ref, tables_ref, q_ref):
+    first_in = first_ref[...]
     tables = repeated(tables_ref, copies)
     bias = wide(add_ref)
-    for p in (PAIRS,) + tuple(range(PAIRS)):
+    for p in range(PAIRS):
         columns = slice(p * 128, (p + 1) * 128)
         part = dot(first_in, weight_ref[:, columns]) + bias[:, columns]
-        if p < PAIRS:
-            q_ref[:, columns] = (turn(part, tables, 1) * SCALE).astype(BF16)
-        else:
-            kv_ref[...] = turn(part, key_tables(tables), 1).astype(BF16)
-
-
-def project(x, gain, bias, weight, add, tables):
+        q_ref[:, columns] = (turn(part, tables, 1) * SCALE).astype(BF16)
+
+
+def project_keys(x, gain, bias, weight, add, tables):
     rows = x.shape[0]
+    whole = lambda a: pl.BlockSpec(a.shape, lambda i: (0,) * a.ndim)
     return pl.pallas_call(
-        functools.partial(project_kernel, rows // tables.shape[1]),
-        in_specs=[VMEM] * 6,
-        out_specs=[VMEM] * 2,
-        out_shape=[SHAPE((rows, D), BF16), SHAPE((rows, 128), BF16)],
+        functools.partial(keys_kernel, rows // tables.shape[1]),
+        grid=(1,),
+        in_specs=[
+            whole(x),
+            whole(gain),
+            whole(bias),
+            pl.BlockSpec((D, 128), lambda i: (0, D // 128)),
+            whole(add),
+            whole(tables),
+        ],
+        out_specs=[pl.BlockSpec((rows, 128), lambda i: (0, 0)), pl.BlockSpec((rows, D), lambda i: (0, 0))],
+        out_shape=[SHAPE((rows, 128), BF16), SHAPE((rows, D), BF16)],
+        compiler_params=params(),
+        cost_estimate=cost(1),
+        name="project_keys",
+    )(x, gain, bias, weight, add, tables)
+
+
+def project_queries(first_in, weight, add, tables):
+    rows = first_in.shape[0]
+    whole = lambda a: pl.BlockSpec(a.shape, lambda i: (0,) * a.ndim)
+    return pl.pallas_call(
+        functools.partial(queries_kernel, rows // tables.shape[1]),
+        grid=(1,),
+        in_specs=[
+            whole(first_in),
+            pl.BlockSpec((D, D), lambda i: (0, 0)),
+            whole(add),
+            whole(tables),
+        ],
+        out_specs=pl.BlockSpec((rows, D), lambda i: (0, 0)),
+        out_shape=SHAPE((rows, D), BF16),
         compiler_params=params(),
         cost_estimate=cost(2),
-        name="project",
-    )(x, gain, bias, weight, add, tables)
+        name="project_queries",
+    )(first_in, weight, add, tables)
 
 
 def gelu_parts(h):
@@ -185,7 +218,7 @@
     return h * cdf, cdf + h * e * (1.0 / math.sqrt(2.0 * math.pi))
 
 
-def forward_kernel(
+def feed_kernel(
     place_ref,
     x_ref,
     xx_ref,
@@ -196,13 +229,18 @@
     w1_ref,
     b1_ref,
     w2_ref,
-    own_ref,
-    other_ref,
-    slope_ref,
-    in_t_ref,
+    wo_ref,
+    mlp_ref,
+    mlp2_ref,
+    back_ref,
+    back2_ref,
+    attn_grad_ref,
+    b1_grad_ref,
+    theirs1_ref,
+    mine1_ref,
     *refs,
 ):
-    grad_refs, (in_scr, g_scr, acc_scr) = refs[:-3], refs[-3:]
+    grad_refs, (in_scr, in_t_scr, g_scr, mlp_scr, back_scr) = refs[:-5], refs[-5:]
     step, steps = pl.program_id(0), pl.num_programs(0)
     rows = x_ref.shape[0]
 
@@ -213,14 +251,20 @@
             normed, _ = normalize(tokens[...].astype(F32))
             second_in = normed * wide(gain_ref) + wide(bias_ref)
             in_scr[at] = second_in.astype(BF16)
-            in_t_ref[:, at] = second_in.T.astype(BF16)
+            in_t_scr[:, :, :, at] = second_in.T.astype(BF16).reshape(in_t_scr.shape[:3] + (rows,))
             g_scr[at] = grads[...]
-
+        attn_grad_ref[...] = dot_nt(g_ref[...], wo_ref[...]).astype(BF16)
+
+    g = g_scr[...]
+    w1 = w1_ref[...]
     w2 = w2_ref[...]
-    act, slope = gelu_parts(dot(in_scr[...], w1_ref[...]) + b1_ref[...])
+    act, slope = gelu_parts(dot(in_scr[...], w1) + b1_ref[...])
     act = act.astype(BF16)
-    slope_ref[...] = slope.astype(BF16)
-    grad = dot_tn(act, g_scr[...]).astype(BF16)
+    pre = dot_nt(g, w2) * slope
+    pre16 = pre.astype(BF16)
+    b1_grad_ref[...] = jnp.sum(pre, axis=0, keepdims=True)
+    mlp = dot(act, w2)
+    grad = dot_tn(act, g).astype(BF16)
     if len(grad_refs) == 1:
         grad_refs[0][...] = grad
     for i in range(len(grad_refs) if len(grad_refs) > 1 else 0):
@@ -229,34 +273,44 @@
         def _(i=i):
             grad_refs[i][...] = grad
 
-    mlp = dot(act, w2)
+    back = dot_nt(pre16, w1)
+    own = place_ref[1]
+    for result, at in ((theirs1_ref, 1 - own), (mine1_ref, own)):
+        left = in_t_scr[:, pl.ds(at, 1)].reshape(D // 2, 2 * rows)
+        result[...] = dot(left, pre16).astype(BF16).reshape(result.shape)
 
     @pl.when(step == 0)
     def _():
-        acc_scr[...] = mlp
+        mlp_scr[...] = mlp
+        back_scr[...] = back
 
     @pl.when((step > 0) & (step < steps - 1))
     def _():
-        acc_scr[...] += mlp
+        mlp_scr[...] += mlp
+        back_scr[...] += back
 
     @pl.when(step == steps - 1)
     def _():
-        total = acc_scr[...] + mlp
-        own_ref[...] = total[:rows].astype(BF16)
-        other_ref[...] = total[rows:].astype(BF16)
+        for scr, last, own_ref, other_ref in ((mlp_scr, mlp, mlp_ref, mlp2_ref), (back_scr, back, back_ref, back2_ref)):
+            total = (scr[...] + last).astype(BF16)
+            own_ref[...] = total[:rows]
+            other_ref[...] = total[rows:]
 
 
 CHUNK = 512
 
 
-def feed_forward(place, depth, x, xx, g, gg, gain, bias, w1, b1, w2):
+def feed(place, count, x, xx, g, gg, gain, bias, w1, b1, w2, wo):
     rows = x.shape[0]
     half = w1.shape[1] // 2
+    depth = count // 2
+    per = D // count // 2
     pieces = depth // 2
     aligned = pieces == 2 and half % 512 == 0
     chunk = half // pieces if aligned else CHUNK
     steps = half // chunk
-    whole = lambda a: pl.BlockSpec(a.shape, lambda i, place: (0,) * a.ndim)
+    single = pl.Buffered(1)
+    whole = lambda a: pl.BlockSpec(a.shape, lambda i, place: (0,) * a.ndim, pipeline_mode=single)
     fixed = lambda *shape: pl.BlockSpec(shape, lambda i, place: (0, 0))
     if aligned:
         piece = lambda i, place: (place[3] ^ (1 - i)) & 1
@@ -267,6 +321,7 @@
         grad_specs = [pl.BlockSpec((chunk, D), lambda i, place: (i, 0))]
         grad_shapes = [SHAPE((half, D), BF16)]
     at = lambda i, place: place[0] * steps + piece(i, place)
+    cut = pl.BlockSpec((count, per, chunk), lambda i, place: (0, 0, piece(i, place)))
     spec = pltpu.PrefetchScalarGridSpec(
         num_scalar_prefetch=1,
         grid=(steps,),
@@ -280,142 +335,35 @@
             pl.BlockSpec((D, chunk), lambda i, place: (0, at(i, place))),
             pl.BlockSpec((1, chunk), lambda i, place: (0, at(i, place))),
             pl.BlockSpec((chunk, D), lambda i, place: (at(i, place), 0)),
+            whole(wo),
         ],
-        out_specs=[
-            fixed(rows, D),
-            fixed(rows, D),
-            pl.BlockSpec((2 * rows, chunk), lambda i, place: (0, piece(i, place))),
-            fixed(D, 2 * rows),
-        ]
+        out_specs=[fixed(rows, D)] * 5
+        + [pl.BlockSpec((1, chunk), lambda i, place: (0, piece(i, place))), cut, cut]
         + grad_specs,
         scratch_shapes=[
             pltpu.VMEM((2 * rows, D), BF16),
+            pltpu.VMEM((count, 2, per, 2 * rows), BF16),
             pltpu.VMEM((2 * rows, D), BF16),
+            pltpu.VMEM((2 * rows, D), F32),
             pltpu.VMEM((2 * rows, D), F32),
         ],
     )
     result = pl.pallas_call(
-        forward_kernel,
+        feed_kernel,
         grid_spec=spec,
-        out_shape=[
-            SHAPE((rows, D), BF16),
-            SHAPE((rows, D), BF16),
-            SHAPE((2 * rows, half), BF16),
-            SHAPE((D, 2 * rows), BF16),
-        ]
+        out_shape=[SHAPE((rows, D), BF16)] * 5
+        + [SHAPE((1, half), F32), SHAPE((count, per, half), BF16), SHAPE((count, per, half), BF16)]
         + grad_shapes,
         compiler_params=params(),
-        cost_estimate=cost(8),
+        cost_estimate=cost(12),
         name="feed_forward",
-    )(place, x, xx, g, gg, gain, bias, w1, b1, w2)
-    grads = result[4:]
+    )(place, x, xx, g, gg, gain, bias, w1, b1, w2, wo)
+    grads = result[8:]
     if not aligned:
         cut = grads[0].reshape(pieces // 2, 2, -1, D)
         low = place[3] & 1
         grads = [take(cut, 1 - low, 1), take(cut, low, 1)]
-    return result[:4], grads
-
-
-def backward_kernel(
-    place_ref,
-    g_ref,
-    gg_ref,
-    slope_ref,
-    in_theirs_ref,
-    in_mine_ref,
-    w1_ref,
-    w2_ref,
-    wo_ref,
-    own_ref,
-    other_ref,
-    attn_grad_ref,
-    theirs_ref,
-    mine_ref,
-    b1_grad_ref,
-    g_scr,
-    acc_scr,
-):
-    step, steps = pl.program_id(0), pl.num_programs(0)
-    rows = g_ref.shape[0]
-
-    @pl.when(step == 0)
-    def _():
-        g_scr[:rows] = g_ref[...]
-        g_scr[rows:] = gg_ref[...]
-        attn_grad_ref[...] = dot_nt(g_ref[...], wo_ref[...]).astype(BF16)
-
-    w1 = w1_ref[...]
-    pre = dot_nt(g_scr[...], w2_ref[...]) * slope_ref[...].astype(F32)
-    pre16 = pre.astype(BF16)
-    b1_grad_ref[...] = jnp.sum(pre, axis=0, keepdims=True)
-    for source, result in ((in_theirs_ref, theirs_ref), (in_mine_ref, mine_ref)):
-        left = source[...].reshape(-1, 2 * rows)
-        result[...] = dot(left, pre16).astype(BF16).reshape(result.shape)
-    back = dot_nt(pre16, w1)
-
-    @pl.when(step == 0)
-    def _():
-        acc_scr[...] = back
-
-    @pl.when((step > 0) & (step < steps - 1))
-    def _():
-        acc_scr[...] += back
-
-    @pl.when(step == steps - 1)
-    def _():
-        total = acc_scr[...] + back
-        own_ref[...] = total[:rows].astype(BF16)
-        other_ref[...] = total[rows:].astype(BF16)
-
-
-def feed_backward(place, count, g, gg, slope, in_t, w1, w2, wo):
-    rows = g.shape[0]
-    half = w1.shape[1] // 2
-    steps = half // CHUNK
-    per = D // count // 2
-    in_t = in_t.reshape(count, 2, per, 2 * rows)
-    whole = lambda a: pl.BlockSpec(a.shape, lambda i, place: (0,) * a.ndim)
-    fixed = lambda *shape: pl.BlockSpec(shape, lambda i, place: (0, 0))
-    at = lambda i, place: place[0] * steps + i
-    cut = pl.BlockSpec((count, per, CHUNK), lambda i, place: (0, 0, i))
-    spec = pltpu.PrefetchScalarGridSpec(
-        num_scalar_prefetch=1,
-        grid=(steps,),
-        in_specs=[
-            whole(g),
-            whole(gg),
-            pl.BlockSpec((2 * rows, CHUNK), lambda i, place: (0, i)),
-            pl.BlockSpec((count, None, per, 2 * rows), lambda i, place: (0, 1 - place[1], 0, 0)),
-            pl.BlockSpec((count, None, per, 2 * rows), lambda i, place: (0, place[1], 0, 0)),
-            pl.BlockSpec((D, CHUNK), lambda i, place: (0, at(i, place))),
-            pl.BlockSpec((CHUNK, D), lambda i, place: (at(i, place), 0)),
-            whole(wo),
-        ],
-        out_specs=[
-            fixed(rows, D),
-            fixed(rows, D),
-            fixed(rows, D),
-            cut,
-            cut,
-            pl.BlockSpec((1, CHUNK), lambda i, place: (0, i)),
-        ],
-        scratch_shapes=[pltpu.VMEM((2 * rows, D), BF16), pltpu.VMEM((2 * rows, D), F32)],
-    )
-    return pl.pallas_call(
-        backward_kernel,
-        grid_spec=spec,
-        out_shape=[
-            SHAPE((rows, D), BF16),
-            SHAPE((rows, D), BF16),
-            SHAPE((rows, D), BF16),
-            SHAPE((count, per, half), BF16),
-            SHAPE((count, per, half), BF16),
-            SHAPE((1, half), F32),
-        ],
-        compiler_params=params(),
-        cost_estimate=cost(6.4),
-        name="feed_backward",
-    )(place, g, gg, slope, in_t, in_t, w1, w2, wo)
+    return result[:8], grads
 
 
 def present(slot, y, z):
@@ -424,15 +372,16 @@
 
 
 def whole_kernel(span, depth, place_ref, *refs):
-    even_ref, odd_ref, q_ref, do_ref, out_ref, dq_ref, even_out_ref, odd_out_ref = refs
+    pair_refs, (q_ref, do_ref, tables_ref, out_ref, dq_ref, even_out_ref, odd_out_ref) = refs[:depth], refs[depth:]
     y, z = place_ref[2], place_ref[3]
+    tables = [tables_ref[i] for i in range(3)]
     rows = PAIRS * span
     low = lax.broadcasted_iota(jnp.int32, (1, 128), 1) < HEAD_DIM
 
     def stacked(ref):
         return jnp.concatenate([ref[:, p * 128 : (p + 1) * 128] for p in range(PAIRS)], axis=0)
 
-    blocks = [ref[k] for k in range(depth) for ref in (even_ref, odd_ref)]
+    blocks = [ref[i] for ref in pair_refs for i in range(2)]
     kv = jnp.concatenate(blocks, axis=0)
     swapped = pltpu.roll(kv.astype(F32), HEAD_DIM, 1).astype(BF16)
     zero, one = jnp.zeros_like(kv), jnp.ones_like(kv)
@@ -471,9 +420,9 @@
         dq = dq + dot(dscore, keys[h])
         dk = dk + dot(q_t[head], dscore)
         dv = dv + dot(do_t[head], expd[h])
-    dq = dq * inverse
+    dq = dq * (inverse * SCALE)
     for p in range(PAIRS):
-        dq_ref[:, p * 128 : (p + 1) * 128] = dq[p * span : (p + 1) * span].astype(BF16)
+        dq_ref[:, p * 128 : (p + 1) * 128] = turn(dq[p * span : (p + 1) * span], tables, -1).astype(BF16)
     both = jnp.concatenate([dk, dv], axis=0).T.astype(BF16)
     for k in range(depth):
         even_out_ref[k] = both[2 * k * span : (2 * k + 1) * span]
@@ -481,9 +430,11 @@
 
 
 def loop_kernel(groups, span, block, count, place_ref, *refs):
-    even_ref, odd_ref, q_ref, do_ref, out_ref, dq_ref, even_out_ref, odd_out_ref = refs[:8]
-    kv_scr, e_ref, kv_t_ref, max_ref, acc_ref, ext_ref = refs[8:]
     depth = count // 2
+    pair_refs, refs = refs[:depth], refs[depth:]
+    q_ref, do_ref, tables_ref, out_ref, dq_ref, even_out_ref, odd_out_ref = refs[:7]
+    kv_scr, e_ref, kv_t_ref, max_ref, acc_ref, ext_ref = refs[7:]
+    tables = [tables_ref[i] for i in range(3)]
     rows = groups * span
     per = block // span
     y, z = place_ref[2], place_ref[3]
@@ -498,7 +449,7 @@
     @pl.when(group == 0)
     def _():
         for i in range(count):
-            kv_scr[i * span : (i + 1) * span] = (odd_ref if i % 2 else even_ref)[i // 2]
+            kv_scr[i * span : (i + 1) * span] = pair_refs[i // 2][i % 2]
 
     q = stacked(q_ref)
     do = stacked(do_ref)
@@ -615,9 +566,9 @@
         kv_t_ref[b] = jnp.where(group == 0, both, kv_t_ref[b] + both)
 
     over_blocks(backward)
-    dq = acc_ref[0] * inverse
+    dq = acc_ref[0] * (inverse * SCALE)
     for p in range(groups):
-        dq_ref[:, p * 128 : (p + 1) * 128] = dq[p * span : (p + 1) * span].astype(BF16)
+        dq_ref[:, p * 128 : (p + 1) * 128] = turn(dq[p * span : (p + 1) * span], tables, -1).astype(BF16)
 
     @pl.when(group == group_count - 1)
     def _():
@@ -629,14 +580,15 @@
                 result[slot // 2] = used_block[i * span : (i + 1) * span]
 
 
-def attention(place, evens, odds, q, do):
-    depth = evens.shape[0]
+def attention(place, pairs, q, do, tables):
+    depth = len(pairs)
     count = 2 * depth
     seqs, span, _ = q.shape
     single = count * span <= 1024
     groups = PAIRS if single else 2
     wide_spec = pl.BlockSpec((None, span, groups * 128), lambda s, i: (s, 0, i))
     pieces = pl.BlockSpec((depth, None, span, 128), lambda s, i: (0, s, 0, 0))
+    two = pl.BlockSpec((2, None, span, 128), lambda s, i: (0, s, 0, 0))
     if single:
         kernel, scratch = functools.partial(whole_kernel, span, depth), []
     else:
@@ -655,7 +607,7 @@
     return pl.pallas_call(
         kernel,
         grid=(seqs, PAIRS // groups),
-        in_specs=[SMEM, pieces, pieces, wide_spec, wide_spec],
+        in_specs=[SMEM] + [two] * depth + [wide_spec, wide_spec, pl.BlockSpec(tables.shape, lambda s, i: (0, 0, 0))],
         out_specs=[wide_spec] * 2 + [pieces] * 2,
         out_shape=[SHAPE((seqs, span, D), BF16), SHAPE((seqs, span, D), BF16)]
         + [SHAPE((depth, seqs, span, 128), BF16)] * 2,
@@ -663,60 +615,43 @@
         compiler_params=params(),
         cost_estimate=cost(10),
         name="attention",
-    )(place, evens, odds, q, do)
-
-
-def weights_kernel(
-    copies, place_ref, dq_ref, attn_ref, g_ref, x_ref, gain_ref, bias_ref, tables_ref, send_ref, keep_ref, grad_ref, small_ref
-):
+    )(place, *pairs, q, do, tables)
+
+
+def weights_kernel(place_ref, attn_ref, g_ref, first_in_ref, grad_ref, send_ref, keep_ref, small_ref):
     half = D // 2
     own = place_ref[0] == 0
 
-    def products(left, right):
-        lower, upper = right[:, :half], right[:, half:]
-        send_ref[0] = dot(left, jnp.where(own, upper, lower)).astype(BF16)
-        keep_ref[0] = dot(left, jnp.where(own, lower, upper)).astype(BF16)
+    def products(left, right, line):
+        small_ref[line : line + 1] = jnp.sum(right.astype(F32), axis=0, keepdims=True)
+        result = dot_tn(left, right).astype(BF16)
+        lower, upper = result[:, :half], result[:, half:]
+        send_ref[0] = jnp.where(own, upper, lower)
+        keep_ref[0] = jnp.where(own, lower, upper)
 
     @pl.when(pl.program_id(0) == 0)
     def _():
-        g = g_ref[...]
-        small_ref[1:2] = jnp.sum(g.astype(F32), axis=0, keepdims=True)
-        products(attn_ref[...].astype(F32).T.astype(BF16), g)
+        products(attn_ref[...], g_ref[...], 1)
 
     @pl.when(pl.program_id(0) == 1)
     def _():
-        tables = repeated(tables_ref, copies)
-        for p in range(PAIRS):
-            columns = slice(p * 128, (p + 1) * 128)
-            grad_ref[:, columns] = turn(dq_ref[:, columns].astype(F32) * SCALE, tables, -1).astype(BF16)
-        grad = grad_ref[...]
-        small_ref[0:1] = jnp.sum(grad.astype(F32), axis=0, keepdims=True)
-        normed, _ = normalize(x_ref[...].astype(F32))
-        first_in = normed * wide(gain_ref) + wide(bias_ref)
-        products(first_in.T.astype(BF16), grad)
-
-
-def weights(place, dq, attn, g, x, gain, bias, tables):
-    rows = x.shape[0]
-    whole = lambda a: pl.BlockSpec(a.shape, lambda i: (0,) * a.ndim)
-    fixed = lambda *shape: pl.BlockSpec(shape, lambda i: (0, 0))
+        products(first_in_ref[...], grad_ref[...], 0)
+
+
+def weights(place, attn, g, first_in, grad):
+    rows = attn.shape[0]
+    whole = pl.BlockSpec((rows, D), lambda i: (0, 0))
     part = pl.BlockSpec((1, D, D // 2), lambda i: (i, 0, 0))
-    arrays = (dq, attn, g, x, gain, bias, tables)
     return pl.pallas_call(
-        functools.partial(weights_kernel, rows // tables.shape[1]),
+        weights_kernel,
         grid=(2,),
-        in_specs=[SMEM] + [whole(a) for a in arrays],
-        out_specs=[part, part, fixed(rows, D), fixed(8, D)],
-        out_shape=[
-            SHAPE((2, D, D // 2), BF16),
-            SHAPE((2, D, D // 2), BF16),
-            SHAPE((rows, D), BF16),
-            SHAPE((8, D), F32),
-        ],
+        in_specs=[SMEM] + [whole] * 4,
+        out_specs=[part, part, pl.BlockSpec((8, D), lambda i: (0, 0))],
+        out_shape=[SHAPE((2, D, D // 2), BF16), SHAPE((2, D, D // 2), BF16), SHAPE((8, D), F32)],
         compiler_params=params(),
         cost_estimate=cost(2.4),
         name="weights",
-    )(place, *arrays)
+    )(place, attn, g, first_in, grad)
 
 
 def mix_kernel(x_ref, mlp_ref, mlp2_ref, attn_ref, grad_ref, add_ref, wo_ref, wq_ref, output_ref, first_ref):
@@ -937,35 +872,32 @@
 
     x_other, g_other = over_core(x), over_core(g)
     tables = rotary_tables(own * span, span)
-    q, kv = project(x, ln1_gain, ln1_bias, qkv_weight, qkv_bias, tables)
+    kv, first_in = project_keys(x, ln1_gain, ln1_bias, qkv_weight, qkv_bias, tables)
     kv3 = kv.reshape(seqs, span, 128)
-    evens = [kv3] + [along(kv3, k) for k in range(1, depth)]
-
-    x_fed, g_fed = after((x, g), kv)
-    (mlp, mlp_other, slope, in_t), grads2 = feed_forward(
-        place, depth, x_fed, x_other, g_fed, g_other, ln2_gain, ln2_bias, fc1_weight, fc1_bias.reshape(1, -1), fc2_weight
-    )
-    theirs2, mine2 = grads2
-    come2 = over_z(theirs2, 0)
-    mlp_come = over_core(mlp_other)
-    evens = [kv3] + list(after(evens[1:], slope))
-    evens = jnp.stack(evens)
-    odds = over_y(evens)
-    back, back_other, attn_grad, theirs1, mine1, b1_grad = feed_backward(
-        place, count, g, g_other, slope, in_t, fc1_weight, fc2_weight, out_weight
+    kv_y = over_y(kv3)
+    q = project_queries(first_in, qkv_weight, qkv_bias, tables)
+    (kv_y,) = after((kv_y,), q)
+    two = jnp.stack([kv3, kv_y])
+    pairs = [two] + [along(two, k) for k in range(1, depth)]
+
+    x_fed, g_fed = after((x, g), two)
+    (mlp, mlp_other, back, back_other, attn_grad, b1_grad, theirs1, mine1), (theirs2, mine2) = feed(
+        place, count, x_fed, x_other, g_fed, g_other, ln2_gain, ln2_bias, fc1_weight, fc1_bias.reshape(1, -1),
+        fc2_weight, out_weight,
     )
     come1 = over_x(theirs1)
-    back_come = over_core(back_other)
+    come2 = over_z(theirs2, 0)
+    mlp_come, back_come = over_core(mlp_other), over_core(back_other)
 
     q3, do3 = q.reshape(seqs, span, D), attn_grad.reshape(seqs, span, D)
-    out, dq, even, odd = attention(place, evens, odds, q3, do3)
+    out, q_rows, even, odd = attention(place, pairs, q3, do3, tables)
     odd = over_y(odd)
 
     def halved(a, parts, height):
         return a.reshape(parts, 2, height, a.shape[-1])
 
-    g_weights, x_weights, come1, mlp_come, back_come = after((g, x, come1, mlp_come, back_come), out)
-    send, keep, q_rows, early = weights(place, flat(dq), flat(out), g_weights, x_weights, ln1_gain, ln1_bias, tables)
+    q_rows, come1, mlp_come, back_come = after((flat(q_rows), come1, mlp_come, back_come), out)
+    send, keep, early = weights(place, flat(out), g, first_in, q_rows)
     come3 = over_core(send)
 
     mine2, come2 = after((mine2, come2), send)
@@ -979,9 +911,9 @@
     got = [along(kv_sums[k], -k) for k in range(1, depth)]
 
     mine1, come1 = after((mine1, come1), *kv_sums)
-    view = lambda v: halved(v, depth, per1 // 2)
-    theirs1, mine1 = add_split(place, [(view(mine1), view(come1), 2)])
-    come1 = over_y(theirs1)
+    view = lambda v: halved(v, depth // 2, per1)
+    theirs1, mine1 = add_split(place, [(view(mine1), view(come1), 3)])
+    come1 = over_z(theirs1, 0)
 
     x_mix, mlp_come = after((x, mlp_come), theirs1)
     output, first = mix(x_mix, mlp, mlp_come, flat(out), q_rows, out_bias, out_weight, qkv_weight)
@@ -1004,14 +936,13 @@
     )
     messages = lax.all_to_all(messages, "seq", 0, 0, tiled=True)
 
-    mine3, come3 = after((mine3, come3), tokens_grad)
-    view = lambda v: halved(v, depth, per1)
-    theirs3, mine3 = add_split(place, [(view(mine3), view(come3), 3)])
-    come3 = over_z(theirs3, 0)
-    mine1, come1 = after((mine1, come1), theirs3)
-    view = lambda v: halved(v, depth // 2, per1 // 2)
-    theirs1, mine1 = add_split(place, [(view(mine1), view(come1), 3)])
-    come1 = over_z(theirs1, 0)
+    mine3, come3, mine1, come1 = after((mine3, come3, mine1, come1), tokens_grad)
+    view3 = lambda v: halved(v, depth, per1)
+    view1 = lambda v: halved(v, depth // 2, per1 // 2)
+    theirs3, mine3, theirs1, mine1 = add_split(
+        place, [(view3(mine3), view3(come3), 3), (view1(mine1), view1(come1), 2)]
+    )
+    come3, come1 = over_z(theirs3, 0), over_y(theirs1)
     mine2, come2 = after((mine2, come2), theirs1)
     for bit in range(1, z_bits - 1):
         view = lambda v: halved(v, half_depth >> (bit + 1), height)
@@ -1024,16 +955,15 @@
     message = gather_sums(messages, lines)
     got = [flipped(message, "batch", i) for i in range(1, batches)]
 
-    mine3, come3 = after((mine3, come3), message)
+    mine3, come3, mine1, come1 = after((mine3, come3, mine1, come1), message)
     for bit in range(1, z_bits):
-        view = lambda v: halved(v, 2 * (depth >> (bit + 1)), per1)
-        theirs3, mine3 = add_split(place, [(view(mine3), view(come3), 3 + bit)])
-        come3 = over_z(theirs3, bit)
-    mine1, come1 = after((mine1, come1), theirs3)
-    for bit in range(1, z_bits):
-        view = lambda v: halved(v, depth >> (bit + 1), per1 // 2)
-        theirs1, mine1 = add_split(place, [(view(mine1), view(come1), 3 + bit)])
-        come1 = over_z(theirs1, bit)
+        parts = depth >> (bit + 1)
+        view3 = lambda v: halved(v, 2 * parts, per1)
+        view1 = lambda v: halved(v, parts, per1 // 2)
+        theirs3, mine3, theirs1, mine1 = add_split(
+            place, [(view3(mine3), view3(come3), 3 + bit), (view1(mine1), view1(come1), 3 + bit)]
+        )
+        come3, come1 = over_z(theirs3, bit), over_z(theirs1, bit)
 
     sum2, come2 = after((sum2, come2), theirs1)
     sum2 = summed(sum2, come2)

time: 185 us -> 175 us (0.946)
  Pallas kernels: 107 us -> 95.4 us
  waiting for transfers between devices: 23.6 us -> 28 us
  starting transfers between devices: 37.1 us -> 35.2 us
    pallas_call x5, Pallas kernels: 74 us -> 65.8 us  [the longest x1 28.6 us: feed(): pl.pallas_call(feed_kernel, grid_spec=spec, out_shape=[SHAPE((rows, D), B...]
    ppermute x26, waiting for transfers between devices: 23.6 us -> 27.3 us  [flipped(): lax.ppermute(block, axis, [(i, i ^ bits) for i in range(lax.axis_size(axi...]
    pallas_call x8 -> x6, Pallas kernels: 19 us -> 15.7 us  [add_split(): pl.pallas_call(kernel, in_specs=[SMEM] + [VMEM] * len(arrays), out_specs=...]
    unnamed x60 -> x62, local copies, waits for them, and re-layouts: 7.51 us -> 7.07 us
  transfers between devices with their start and end apart: 34 -> 34, of which waited for: 7 -> 7; matrix products, arithmetic and copies ran while one was open for 4% -> 3% of each run, Pallas kernels for 58% -> 55%
where the time goes in v2:
time: 175 us
  Pallas kernels  95.4 us (55%)
  starting transfers between devices  35.2 us (20%)
  waiting for transfers between devices  28 us (16%)
  local copies, waits for them, and re-layouts  7.82 us (4%)
  other arithmetic  7.29 us (4%)
    pallas_call x1, Pallas kernels, feed(): pl.pallas_call(feed_kernel, grid_spec=spec, out_shape=[SHAPE((rows, D), B...  28.6 us
    ppermute x26, waiting for transfers between devices, flipped(): lax.ppermute(block, axis, [(i, i ^ bits) for i in range(lax.axis_size(axi...  27.3 us
    pallas_call x1, Pallas kernels, attention(): pl.pallas_call(kernel, grid=(seqs, PAIRS // groups), in_specs=[SMEM] + [t...  24.8 us
    ppermute x26, starting transfers between devices, flipped(): lax.ppermute(block, axis, [(i, i ^ bits) for i in range(lax.axis_size(axi...  21.1 us
    pallas_call x6, Pallas kernels, add_split(): pl.pallas_call(kernel, in_specs=[SMEM] + [VMEM] * len(arrays), out_specs=...  15.7 us
    ppermute x6, starting transfers between devices, along(): lax.ppermute(block, 'seq', [(i, (i + 2 * distance) % size) for i in range...  8.49 us
    unnamed x62, local copies, waits for them, and re-layouts  7.07 us
    pallas_call x1, Pallas kernels, finish(): pl.pallas_call(functools.partial(finish_kernel, rows // tables.shape[1],...  5.65 us
  transfers between devices with their start and end apart: 34, of which 7 were waited for; matrix products, arithmetic and copies ran while one was open for 3% of the time, Pallas kernels for 55%

profile of v2, /device:TPU:0, one launch (start us, length us, event | category | flops | bytes accessed | tf_op | source)
XLA Modules:
  0.0 174.8 jit_solution(2570348649805939409)
XLA Ops:
  2.3 2.8 %project_keys.1 = (bf16[512,128]{1,0:T(8,128)(2,1)}, bf16[512,768]{1,0:T(8,128)(2,1)}) custom-call(bf16[512,768]{1,0:T(8,128)(2,1)} %bitcast.60, f32[768]{0:T(1024)} %refs_10_.1, f32[768]{0:T(1024)} %refs_11_.1, bf16[768,896]{1,0:T(8,128)(2,1)} %refs_13_.1, f32[896]{0:T(1024)} %add_ref.4, f32[3,128,128]{2,1,0:T(8,128)} %pad_maximum_fusion.4.tables_ref.refs_6_.refs_14_), custom_call_target="tpu_custom_call" | custom-call | flops 3000000000 | tf_op jit(solution)/shard_map/project_keys/pallas_call | solution.py:171
  5.1 2.9 %collective-permute-start = (bf16[4,128,128]{2,1,0:T(8,128)(2,1)}, bf16[4,128,128]{2,1,0:T(8,128)(2,1)S(1)}, u32[]{:S(2)}, u32[]{:S(2)}) collective-permute-start(bf16[4,128,128]{2,1,0:T(8,128)(2,1)} %bitcast.52), channel_id=1, source_target_pairs={{0,1},{1,0},{2,3},{3,2},{4,5},{5,4},{6,7},{7,6},{8,9},{9,8},{10,11... | collective-permute-start | bytes 393224 | tf_op jit(solution)/shard_map/ppermute | solution.py:41
  8.1 4.1 %project_queries.1 = bf16[512,768]{1,0:T(8,128)(2,1)} custom-call(bf16[512,768]{1,0:T(8,128)(2,1)} %get-tuple-element.114.first_ref.first_in_ref, bf16[768,896]{1,0:T(8,128)(2,1)} %refs_13_.1, f32[896]{0:T(1024)} %add_ref.4, f32[3,128,128]{2,1,0:T(8,128)} %pad_maximum_fusion.4.tables_ref.refs_6_.refs_14_), custom_call_target="tpu_custom_call" | custom-call | flops 6000000000 | tf_op jit(solution)/shard_map/project_queries/pallas_call | solution.py:193
  12.8 3.7 %collective-permute-start.3 = (bf16[2,4,128,128]{3,2,1,0:T(8,128)(2,1)S(1)}, bf16[2,4,128,128]{3,2,1,0:T(8,128)(2,1)S(1)}, u32[]{:S(2)}, u32[]{:S(2)}) collective-permute-start(bf16[2,4,128,128]{3,2,1,0:T(8,128)(2,1)S(1)} %pad_maximum_fusion.3.refs_0_), channel_id=1, source_target_pairs={{0,6},{1,7},{2,0},{3,1},{4,2},{5,3},{6,4},{7,5},{8,14},{9,15},{10,... | collective-permute-start | bytes 786440 | tf_op jit(solution)/shard_map/ppermute | solution.py:46
  16.4 1.0 collective-permute-start.1
  17.5 0.9 copy-done.13
  18.6 28.6 %feed_forward.1 = (bf16[512,768]{1,0:T(8,128)(2,1)}, bf16[512,768]{1,0:T(8,128)(2,1)}, bf16[512,768]{1,0:T(8,128)(2,1)}, bf16[512,768]{1,0:T(8,128)(2,1)}, bf16[...) custom-call(s32[4]{0:T(128)} %pad_add_fusion.place_ref, ...), custom_call_target="tpu_custom_call" | custom-call | flops 35999997952 | tf_op jit(solution)/shard_map/feed_forward/pallas_call | solution.py:351
  47.8 1.5 collective-permute-start.6
  49.3 2.5 %collective-permute-start.10 = (bf16[768,768]{1,0:T(8,128)(2,1)}, bf16[768,768]{1,0:T(8,128)(2,1)S(1)}, u32[]{:S(2)}, u32[]{:S(2)}) collective-permute-start(bf16[768,768]{1,0:T(8,128)(2,1)} %get-tuple-element.130), channel_id=1, source_target_pairs={{0,2},{1,3},{2,0},{3,1},{4,6},{5,7},{6,4},{7,5},{8,10},{9,11},{10,... | collective-permute-start | bytes 3538952 | tf_op jit(solution)/shard_map/ppermute | solution.py:41
  52.5 24.8 %attention.1 = (bf16[4,128,768]{2,1,0:T(8,128)(2,1)}, bf16[4,128,768]{2,1,0:T(8,128)(2,1)}, bf16[4,4,128,128]{3,2,1,0:T(8,128)(2,1)}, bf16[4,4,128,128]{3,2,1,0:T(8,128)(2,1)}) custom-call(s32[4]{0:T(128)} %pad_add_fusion.place_ref, bf16[2,4,128,128]{3,2,1,0:T(8,128)(2,1)} %copy-done.3, bf16[2,4,128,128]{3,2,1,0:T(8,128)(2,1)} %copy-done.24, ...), custom_call_target="tpu_custom_call" | custom-call | flops 30000001024 | tf_op jit(solution)/shard_map/attention/pallas_call | solution.py:607
  77.3 1.1 collective-permute-start.9
  78.4 5.5 %weights.1 = (bf16[2,768,384]{2,1,0:T(8,128)(2,1)}, bf16[2,768,384]{2,1,0:T(8,128)(2,1)}, f32[8,768]{1,0:T(8,128)}) custom-call(s32[4]{0:T(128)} %pad_add_fusion.place_ref, bf16[512,768]{1,0:T(8,128)(2,1)} %bitcast.84, bf16[512,768]{1,0:T(8,128)(2,1)} %bitcast.66, bf16[512,768]{1,0:T(8,128)(2,1)} %get-tuple-element.114.first_ref.first_in_ref, ...), custom_call_target="tpu_custom_call" | custom-call | flops 7200000000 | tf_op jit(solution)/shard_map/weights/pallas_call | solution.py:645
  84.1 1.0 copy-done.10
  85.1 2.9 %add_split.6 = (bf16[2,192,768]{2,1,0:T(8,128)(2,1)}, bf16[2,192,768]{2,1,0:T(8,128)(2,1)}) custom-call(s32[4]{0:T(128)} %pad_add_fusion.place_ref, bf16[2,2,192,768]{3,2,1,0:T(8,128)(2,1)} %bitcast.79, bf16[2,2,192,768]{3,2,1,0:T(8,128)(2,1)} %bitcast.58), custom_call_target="tpu_custom_call" | custom-call | flops 3600000000 | tf_op jit(solution)/shard_map/add_split/pallas_call | solution.py:139
  88.5 2.4 %collective-permute-done.9 = bf16[4,4,128,128]{3,2,1,0:T(8,128)(2,1)S(1)} collective-permute-done((bf16[4,4,128,128]{3,2,1,0:T(8,128)(2,1)}, bf16[4,4,128,128]{3,2,1,0:T(8,128)(2,1)S(1)}, u32[]{:S(2)}, u32[]{:S(2)}) %collective-permute-start.9) | collective-permute-done | bytes 524320 | tf_op jit(solution)/shard_map/ppermute | solution.py:41
  90.9 0.8 add_convert_fusion.5
  92.1 1.1 collective-permute-start.12
  93.2 2.4 %collective-permute-start.11 = (bf16[4,128,128]{2,1,0:T(8,128)(2,1)S(1)}, bf16[4,128,128]{2,1,0:T(8,128)(2,1)S(1)}, u32[]{:S(2)}, u32[]{:S(2)}) collective-permute-start(bf16[4,128,128]{2,1,0:T(8,128)(2,1)S(1)} %get-tuple-element.215), channel_id=1, source_target_pairs={{0,6},{1,7},{2,0},{3,1},{4,2},{5,3},{6,4},{7,5},{8,14},{9,15},{10,... | collective-permute-start | bytes 393224 | tf_op jit(solution)/shard_map/ppermute | solution.py:46
  95.5 2.9 %add_split.7 = (bf16[2,96,1536]{2,1,0:T(8,128)(2,1)}, bf16[2,96,1536]{2,1,0:T(8,128)(2,1)}) custom-call(s32[4]{0:T(128)} %pad_add_fusion.place_ref, bf16[2,2,96,1536]{3,2,1,0:T(8,128)(2,1)} %bitcast.78, bf16[2,2,96,1536]{3,2,1,0:T(8,128)(2,1)} %bitcast.56), custom_call_target="tpu_custom_call" | custom-call | flops 3600000000 | tf_op jit(solution)/shard_map/add_split/pallas_call | solution.py:139
  98.4 5.0 %mix.1 = (bf16[512,768]{1,0:T(8,128)(2,1)}, bf16[512,768]{1,0:T(8,128)(2,1)}) custom-call(bf16[512,768]{1,0:T(8,128)(2,1)} %bitcast.62, bf16[512,768]{1,0:T(8,128)(2,1)} %get-tuple-element.142.mlp_ref, bf16[512,768]{1,0:T(8,128)(2,1)} %copy-done.12, bf16[512,768]{1,0:T(8,128)(2,1)} %bitcast.85, bf16[512,768]{1,0:T(8,128)(2,1)} %bitcast.87, f32[768]{0:T(1024)} %add_ref.5, ...), custom_call_target="tpu_custom_call" | custom-call | flops 7200000000 | tf_op jit(solution)/shard_map/mix/pallas_call | solution.py:668
  104.4 2.9 %add_split.8 = (bf16[8,96,384]{2,1,0:T(8,128)(2,1)}, bf16[8,96,384]{2,1,0:T(8,128)(2,1)}) custom-call(s32[4]{0:T(128)} %pad_add_fusion.place_ref, bf16[8,2,96,384]{3,2,1,0:T(8,128)(2,1)} %bitcast.80, bf16[8,2,96,384]{3,2,1,0:T(8,128)(2,1)} %bitcast.57), custom_call_target="tpu_custom_call" | custom-call | flops 3600000000 | tf_op jit(solution)/shard_map/add_split/pallas_call | solution.py:139
  107.4 1.0 collective-permute-start.17
  108.4 2.2 %add_split.9 = (bf16[1,192,768]{2,1,0:T(8,128)(2,1)}, bf16[1,192,768]{2,1,0:T(8,128)(2,1)}) custom-call(s32[4]{0:T(128)} %pad_add_fusion.place_ref, bf16[1,2,192,768]{3,2,1,0:T(8,128)(2,1)} %bitcast.91, bf16[1,2,192,768]{3,2,1,0:T(8,128)(2,1)} %bitcast.70), custom_call_target="tpu_custom_call" | custom-call | flops 3600000000 | tf_op jit(solution)/shard_map/add_split/pallas_call | solution.py:139
  111.3 5.6 %finish.1 = (bf16[512,768]{1,0:T(8,128)(2,1)}, bf16[8,224,128]{2,1,0:T(8,128)(2,1)}) custom-call(s32[4]{0:T(128)} %pad_add_fusion.place_ref, bf16[512,128]{1,0:T(8,128)(2,1)} %bitcast.51, bf16[512,128]{1,0:T(8,128)(2,1)} %bitcast.76, bf16[512,128]{1,0:T(8,128)(2,1)} %bitcast.75, bf16[512,128]{1,0:T(8,128)(2,1)} %bitcast.74, bf16[512,128]{1,0:T(8,128)(2,1)} %bitcast.73, ...), custom_call_target="tpu_custom_call" | custom-call | flops 7200000000 | tf_op jit(solution)/shard_map/finish/pallas_call | solution.py:762
  117.0 4.3 %all-to-all-start = ((bf16[8,224,128]{2,1,0:T(8,128)(2,1)}), bf16[8,224,128]{2,1,0:T(8,128)(2,1)S(1)}, u32[]{:S(2)}, u32[]{:S(2)}) async-start(bf16[8,224,128]{2,1,0:T(8,128)(2,1)} %get-tuple-element.162), calls=%async_computation | async-start | bytes 917504 | tf_op jit(solution)/shard_map/all_to_all | solution.py:937
  121.2 2.0 %collective-permute-start.16 = (bf16[1,192,768]{2,1,0:T(8,128)(2,1)S(1)}, bf16[1,192,768]{2,1,0:T(8,128)(2,1)S(1)}, u32[]{:S(2)}, u32[]{:S(2)}) collective-permute-start(bf16[1,192,768]{2,1,0:T(8,128)(2,1)S(1)} %copy-done.19), channel_id=1, source_target_pairs={{0,1},{1,0},{2,3},{3,2},{4,5},{5,4},{6,7},{7,6},{8,9},{9,8},{10,11... | collective-permute-start | bytes 884744 | tf_op jit(solution)/shard_map/ppermute | solution.py:41
  123.3 0.8 copy-done.16
  124.3 2.8 %add_split.10 = (bf16[4,96,384]{2,1,0:T(8,128)(2,1)}, bf16[4,96,384]{2,1,0:T(8,128)(2,1)}, bf16[2,48,1536]{2,1,0:T(8,128)(2,1)}, bf16[2,48,1536]{2,1,0:T(8,128)(2,1)}) custom-call(s32[4]{0:T(128)} %pad_add_fusion.place_ref, bf16[4,2,96,384]{3,2,1,0:T(8,128)(2,1)} %bitcast.90, bf16[4,2,96,384]{3,2,1,0:T(8,128)(2,1)} %bitcast.69, ...), custom_call_target="tpu_custom_call" | custom-call | flops 3600000000 | tf_op jit(solution)/shard_map/add_split/pallas_call | solution.py:139
  127.1 7.9 %collective-permute-done.16 = bf16[1,192,768]{2,1,0:T(8,128)(2,1)S(1)} collective-permute-done((bf16[1,192,768]{2,1,0:T(8,128)(2,1)S(1)}, bf16[1,192,768]{2,1,0:T(8,128)(2,1)S(1)}, u32[]{:S(2)}, u32[]{:S(2)}) %collective-permute-start.16) | collective-permute-done | bytes 294944 | tf_op jit(solution)/shard_map/ppermute | solution.py:41
  135.1 0.9 collective-permute-start.23
  136.0 1.3 collective-permute-start.22
  137.3 0.8 copy-done.1
  138.1 1.7 gather_sums.1.refs_0_
  140.5 1.8 %collective-permute-done.23 = bf16[4,96,384]{2,1,0:T(8,128)(2,1)S(1)} collective-permute-done((bf16[4,96,384]{2,1,0:T(8,128)(2,1)}, bf16[4,96,384]{2,1,0:T(8,128)(2,1)S(1)}, u32[]{:S(2)}, u32[]{:S(2)}) %collective-permute-start.23) | collective-permute-done | bytes 294944 | tf_op jit(solution)/shard_map/ppermute | solution.py:41
  143.1 2.1 %add_split.11 = (bf16[2,96,384]{2,1,0:T(8,128)(2,1)}, bf16[2,96,384]{2,1,0:T(8,128)(2,1)}, bf16[1,48,1536]{2,1,0:T(8,128)(2,1)}, bf16[1,48,1536]{2,1,0:T(8,128)(2,1)}) custom-call(s32[4]{0:T(128)} %pad_add_fusion.place_ref, bf16[2,2,96,384]{3,2,1,0:T(8,128)(2,1)} %bitcast.92, bf16[2,2,96,384]{3,2,1,0:T(8,128)(2,1)} %bitcast.72, ...), custom_call_target="tpu_custom_call" | custom-call | flops 3600000000 | tf_op jit(solution)/shard_map/add_split/pallas_call | solution.py:139
  145.2 2.8 %collective-permute-start.28 = (bf16[1,48,1536]{2,1,0:T(8,128)(2,1)}, bf16[1,48,1536]{2,1,0:T(8,128)(2,1)S(1)}, u32[]{:S(2)}, u32[]{:S(2)}) collective-permute-start(bf16[1,48,1536]{2,1,0:T(8,128)(2,1)} %get-tuple-element.181), channel_id=1, source_target_pairs={{0,4},{1,5},{2,6},{3,7},{4,0},{5,1},{6,2},{7,3},{8,12},{9,13},{10,... | collective-permute-start | bytes 442376 | tf_op jit(solution)/shard_map/ppermute | solution.py:41
  148.8 0.7 collective-permute-start.27
  150.2 1.6 last_sums.1
  151.7 1.3 pad_maximum_fusion.5
  153.0 9.0 %collective-permute-done.25 = bf16[2,96,384]{2,1,0:T(8,128)(2,1)S(1)} collective-permute-done((bf16[2,96,384]{2,1,0:T(8,128)(2,1)}, bf16[2,96,384]{2,1,0:T(8,128)(2,1)S(1)}, u32[]{:S(2)}, u32[]{:S(2)}) %collective-permute-start.25) | collective-permute-done | bytes 147488 | tf_op jit(solution)/shard_map/ppermute | solution.py:41
  162.0 0.9 collective-permute-start.26
  162.9 1.3 collective-permute-start.31
  164.4 4.4 %collective-permute-done.26 = bf16[2,96,384]{2,1,0:T(8,128)(2,1)S(1)} collective-permute-done((bf16[2,96,384]{2,1,0:T(8,128)(2,1)S(1)}, bf16[2,96,384]{2,1,0:T(8,128)(2,1)S(1)}, u32[]{:S(2)}, u32[]{:S(2)}) %collective-permute-start.26) | collective-permute-done | bytes 147488 | tf_op jit(solution)/shard_map/ppermute | solution.py:41
  169.0 1.7 collective-permute-done.31
  170.8 1.1 select_convert_fusion
  172.0 0.8 slice_bitcast_fusion
  172.9 0.8 pad_maximum_fusion.1
  173.6 1.1 maximum_convert_fusion
  (122 shorter events, 10.4 us)
Async XLA Ops:
  0.6 16.8 %collective-permute-start.4 = (bf16[512,768]{1,0:T(8,128)(2,1)}, bf16[512,768]{1,0:T(8,128)(2,1)S(1)}, u32[]{:S(2)}, u32[]{:S(2)}) collective-permute-start(bf16[512,768]{1,0:T(8,128)(2,1)} %bitcast.59), channel_id=1, source_target_pairs={{0,8},{8,0},{16,24},{24,16},{1,9},{9,1},{17,25},{25,17},{2,10},{10... | collective-permute-start | bytes 2359304 | tf_op jit(solution)/shard_map/ppermute | solution.py:41
  1.2 16.3 %collective-permute-start.5 = (bf16[512,768]{1,0:T(8,128)(2,1)}, bf16[512,768]{1,0:T(8,128)(2,1)S(1)}, u32[]{:S(2)}, u32[]{:S(2)}) collective-permute-start(bf16[512,768]{1,0:T(8,128)(2,1)} %bitcast.64), channel_id=1, source_target_pairs={{0,8},{8,0},{16,24},{24,16},{1,9},{9,1},{17,25},{25,17},{2,10},{10... | collective-permute-start | bytes 2359304 | tf_op jit(solution)/shard_map/ppermute | solution.py:41
  5.1 7.6 %collective-permute-start = (bf16[4,128,128]{2,1,0:T(8,128)(2,1)}, bf16[4,128,128]{2,1,0:T(8,128)(2,1)S(1)}, u32[]{:S(2)}, u32[]{:S(2)}) collective-permute-start(bf16[4,128,128]{2,1,0:T(8,128)(2,1)} %bitcast.52), channel_id=1, source_target_pairs={{0,1},{1,0},{2,3},{3,2},{4,5},{5,4},{6,7},{7,6},{8,9},{9,8},{10,11... | collective-permute-start | bytes 393224 | tf_op jit(solution)/shard_map/ppermute | solution.py:41
  8.1 4.7 %copy-start.6 = (bf16[512,128]{1,0:T(8,128)(2,1)S(1)}, bf16[512,128]{1,0:T(8,128)(2,1)}, u32[]{:S(2)}) copy-start(bf16[512,128]{1,0:T(8,128)(2,1)} %get-tuple-element.113) | copy-start | bytes 393220
  12.8 34.4 %copy-start.3 = (bf16[2,4,128,128]{3,2,1,0:T(8,128)(2,1)}, bf16[2,4,128,128]{3,2,1,0:T(8,128)(2,1)S(1)}, u32[]{:S(2)}) copy-start(bf16[2,4,128,128]{3,2,1,0:T(8,128)(2,1)S(1)} %pad_maximum_fusion.3.refs_0_) | copy-start | bytes 786436
  12.8 35.0 %collective-permute-start.3 = (bf16[2,4,128,128]{3,2,1,0:T(8,128)(2,1)S(1)}, bf16[2,4,128,128]{3,2,1,0:T(8,128)(2,1)S(1)}, u32[]{:S(2)}, u32[]{:S(2)}) collective-permute-start(bf16[2,4,128,128]{3,2,1,0:T(8,128)(2,1)S(1)} %pad_maximum_fusion.3.refs_0_), channel_id=1, source_target_pairs={{0,6},{1,7},{2,0},{3,1},{4,2},{5,3},{6,4},{7,5},{8,14},{9,15},{10,... | collective-permute-start | bytes 786440 | tf_op jit(solution)/shard_map/ppermute | solution.py:46
  16.4 32.8 %collective-permute-start.2 = (bf16[2,4,128,128]{3,2,1,0:T(8,128)(2,1)S(1)}, bf16[2,4,128,128]{3,2,1,0:T(8,128)(2,1)S(1)}, u32[]{:S(2)}, u32[]{:S(2)}) collective-permute-start(bf16[2,4,128,128]{3,2,1,0:T(8,128)(2,1)S(1)} %pad_maximum_fusion.3.refs_0_), channel_id=1, source_target_pairs={{0,4},{1,5},{2,6},{3,7},{4,0},{5,1},{6,2},{7,3},{8,12},{9,13},{10,... | collective-permute-start | bytes 786440 | tf_op jit(solution)/shard_map/ppermute | solution.py:46
  16.4 35.3 %collective-permute-start.1 = (bf16[2,4,128,128]{3,2,1,0:T(8,128)(2,1)S(1)}, bf16[2,4,128,128]{3,2,1,0:T(8,128)(2,1)S(1)}, u32[]{:S(2)}, u32[]{:S(2)}) collective-permute-start(bf16[2,4,128,128]{3,2,1,0:T(8,128)(2,1)S(1)} %pad_maximum_fusion.3.refs_0_), channel_id=1, source_target_pairs={{0,2},{1,3},{2,4},{3,5},{4,6},{5,7},{6,0},{7,1},{8,10},{9,11},{10,... | collective-permute-start | bytes 786440 | tf_op jit(solution)/shard_map/ppermute | solution.py:46
  17.5 1.1 copy-start.14
  47.2 31.2 %collective-permute-start.7 = (bf16[512,768]{1,0:T(8,128)(2,1)}, bf16[512,768]{1,0:T(8,128)(2,1)S(1)}, u32[]{:S(2)}, u32[]{:S(2)}) collective-permute-start(bf16[512,768]{1,0:T(8,128)(2,1)} %get-tuple-element.121), channel_id=1, source_target_pairs={{0,8},{8,0},{16,24},{24,16},{1,9},{9,1},{17,25},{25,17},{2,10},{10... | collective-permute-start | bytes 2359304 | tf_op jit(solution)/shard_map/ppermute | solution.py:41
  47.3 31.1 %collective-permute-start.8 = (bf16[512,768]{1,0:T(8,128)(2,1)}, bf16[512,768]{1,0:T(8,128)(2,1)S(1)}, u32[]{:S(2)}, u32[]{:S(2)}) collective-permute-start(bf16[512,768]{1,0:T(8,128)(2,1)} %get-tuple-element.122), channel_id=1, source_target_pairs={{0,8},{8,0},{16,24},{24,16},{1,9},{9,1},{17,25},{25,17},{2,10},{10... | collective-permute-start | bytes 2359304 | tf_op jit(solution)/shard_map/ppermute | solution.py:41
  47.8 4.0 %copy-start.22 = (bf16[2,4,128,128]{3,2,1,0:T(8,128)(2,1)}, bf16[2,4,128,128]{3,2,1,0:T(8,128)(2,1)S(1)}, u32[]{:S(2)}) copy-start(bf16[2,4,128,128]{3,2,1,0:T(8,128)(2,1)S(1)} %collective-permute-done.3.refs_3_) | copy-start | bytes 786436
  47.8 30.6 %collective-permute-start.6 = (bf16[8,48,1536]{2,1,0:T(8,128)(2,1)}, bf16[8,48,1536]{2,1,0:T(8,128)(2,1)S(1)}, u32[]{:S(2)}, u32[]{:S(2)}) collective-permute-start(bf16[8,48,1536]{2,1,0:T(8,128)(2,1)} %get-tuple-element.120), channel_id=1, source_target_pairs={{0,16},{8,24},{16,0},{24,8},{1,17},{9,25},{17,1},{25,9},{2,18},{10... | collective-permute-start | bytes 3538952 | tf_op jit(solution)/shard_map/ppermute | solution.py:41
  49.3 2.5 %copy-start.23 = (bf16[2,4,128,128]{3,2,1,0:T(8,128)(2,1)}, bf16[2,4,128,128]{3,2,1,0:T(8,128)(2,1)S(1)}, u32[]{:S(2)}) copy-start(bf16[2,4,128,128]{3,2,1,0:T(8,128)(2,1)S(1)} %collective-permute-done.2.refs_2_) | copy-start | bytes 786436
  49.3 34.8 %collective-permute-start.10 = (bf16[768,768]{1,0:T(8,128)(2,1)}, bf16[768,768]{1,0:T(8,128)(2,1)S(1)}, u32[]{:S(2)}, u32[]{:S(2)}) collective-permute-start(bf16[768,768]{1,0:T(8,128)(2,1)} %get-tuple-element.130), channel_id=1, source_target_pairs={{0,2},{1,3},{2,0},{3,1},{4,6},{5,7},{6,4},{7,5},{8,10},{9,11},{10,... | collective-permute-start | bytes 3538952 | tf_op jit(solution)/shard_map/ppermute | solution.py:41
  77.3 13.6 %collective-permute-start.9 = (bf16[4,4,128,128]{3,2,1,0:T(8,128)(2,1)}, bf16[4,4,128,128]{3,2,1,0:T(8,128)(2,1)S(1)}, u32[]{:S(2)}, u32[]{:S(2)}) collective-permute-start(bf16[4,4,128,128]{3,2,1,0:T(8,128)(2,1)} %get-tuple-element.128), channel_id=1, source_target_pairs={{0,1},{1,0},{2,3},{3,2},{4,5},{5,4},{6,7},{7,6},{8,9},{9,8},{10,11... | collective-permute-start | bytes 1572872 | tf_op jit(solution)/shard_map/ppermute | solution.py:41
  78.4 5.6 %copy-start.12 = (bf16[512,768]{1,0:T(8,128)(2,1)}, bf16[512,768]{1,0:T(8,128)(2,1)S(1)}, u32[]{:S(2)}) copy-start(bf16[512,768]{1,0:T(8,128)(2,1)S(1)} %collective-permute-done.7.mlp2_ref) | copy-start | bytes 2359300
  78.4 5.6 %copy-start.11 = (bf16[512,768]{1,0:T(8,128)(2,1)}, bf16[512,768]{1,0:T(8,128)(2,1)S(1)}, u32[]{:S(2)}) copy-start(bf16[512,768]{1,0:T(8,128)(2,1)S(1)} %collective-permute-done.8.refs_9_) | copy-start | bytes 2359300
  78.4 5.6 %copy-start.8 = (bf16[8,48,1536]{2,1,0:T(8,128)(2,1)}, bf16[8,48,1536]{2,1,0:T(8,128)(2,1)S(1)}, u32[]{:S(2)}) copy-start(bf16[8,48,1536]{2,1,0:T(8,128)(2,1)S(1)} %collective-permute-done.6) | copy-start | bytes 3538948
  84.0 19.5 %collective-permute-start.15 = (bf16[2,768,384]{2,1,0:T(8,128)(2,1)}, bf16[2,768,384]{2,1,0:T(8,128)(2,1)S(1)}, u32[]{:S(2)}, u32[]{:S(2)}) collective-permute-start(bf16[2,768,384]{2,1,0:T(8,128)(2,1)} %get-tuple-element.132), channel_id=1, source_target_pairs={{0,8},{8,0},{16,24},{24,16},{1,9},{9,1},{17,25},{25,17},{2,10},{10... | collective-permute-start | bytes 3538952 | tf_op jit(solution)/shard_map/ppermute | solution.py:41
  85.1 5.8 %copy-start = (bf16[4,4,128,128]{3,2,1,0:T(8,128)(2,1)S(1)}, bf16[4,4,128,128]{3,2,1,0:T(8,128)(2,1)}, u32[]{:S(2)}) copy-start(bf16[4,4,128,128]{3,2,1,0:T(8,128)(2,1)} %get-tuple-element.136) | copy-start | bytes 1572868
  88.0 19.4 %collective-permute-start.14 = (bf16[2,192,768]{2,1,0:T(8,128)(2,1)}, bf16[2,192,768]{2,1,0:T(8,128)(2,1)S(1)}, u32[]{:S(2)}, u32[]{:S(2)}) collective-permute-start(bf16[2,192,768]{2,1,0:T(8,128)(2,1)} %get-tuple-element.135), channel_id=1, source_target_pairs={{0,16},{8,24},{16,0},{24,8},{1,17},{9,25},{17,1},{25,9},{2,18},{10... | collective-permute-start | bytes 1769480 | tf_op jit(solution)/shard_map/ppermute | solution.py:41
  91.7 18.8 %collective-permute-start.13 = (bf16[4,128,128]{2,1,0:T(8,128)(2,1)S(1)}, bf16[4,128,128]{2,1,0:T(8,128)(2,1)S(1)}, u32[]{:S(2)}, u32[]{:S(2)}) collective-permute-start(bf16[4,128,128]{2,1,0:T(8,128)(2,1)S(1)} %get-tuple-element.213), channel_id=1, source_target_pairs={{0,2},{1,3},{2,4},{3,5},{4,6},{5,7},{6,0},{7,1},{8,10},{9,11},{10,... | collective-permute-start | bytes 393224 | tf_op jit(solution)/shard_map/ppermute | solution.py:46
  92.1 18.5 %collective-permute-start.12 = (bf16[4,128,128]{2,1,0:T(8,128)(2,1)S(1)}, bf16[4,128,128]{2,1,0:T(8,128)(2,1)S(1)}, u32[]{:S(2)}, u32[]{:S(2)}) collective-permute-start(bf16[4,128,128]{2,1,0:T(8,128)(2,1)S(1)} %get-tuple-element.214), channel_id=1, source_target_pairs={{0,4},{1,5},{2,6},{3,7},{4,0},{5,1},{6,2},{7,3},{8,12},{9,13},{10,... | collective-permute-start | bytes 393224 | tf_op jit(solution)/shard_map/ppermute | solution.py:46
  93.2 17.4 %collective-permute-start.11 = (bf16[4,128,128]{2,1,0:T(8,128)(2,1)S(1)}, bf16[4,128,128]{2,1,0:T(8,128)(2,1)S(1)}, u32[]{:S(2)}, u32[]{:S(2)}) collective-permute-start(bf16[4,128,128]{2,1,0:T(8,128)(2,1)S(1)} %get-tuple-element.215), channel_id=1, source_target_pairs={{0,6},{1,7},{2,0},{3,1},{4,2},{5,3},{6,4},{7,5},{8,14},{9,15},{10,... | collective-permute-start | bytes 393224 | tf_op jit(solution)/shard_map/ppermute | solution.py:46
  98.4 5.0 %copy-start.15 = (bf16[2,96,1536]{2,1,0:T(8,128)(2,1)S(1)}, bf16[2,96,1536]{2,1,0:T(8,128)(2,1)}, u32[]{:S(2)}) copy-start(bf16[2,96,1536]{2,1,0:T(8,128)(2,1)} %get-tuple-element.140) | copy-start | bytes 1769476
  103.4 19.8 %collective-permute-start.18 = (bf16[2,96,1536]{2,1,0:T(8,128)(2,1)S(1)}, bf16[2,96,1536]{2,1,0:T(8,128)(2,1)S(1)}, u32[]{:S(2)}, u32[]{:S(2)}) collective-permute-start(bf16[2,96,1536]{2,1,0:T(8,128)(2,1)S(1)} %copy-done.15), channel_id=1, source_target_pairs={{0,2},{1,3},{2,0},{3,1},{4,6},{5,7},{6,4},{7,5},{8,10},{9,11},{10,... | collective-permute-start | bytes 1769480 | tf_op jit(solution)/shard_map/ppermute | solution.py:41
  107.4 15.9 %collective-permute-start.17 = (bf16[8,96,384]{2,1,0:T(8,128)(2,1)}, bf16[8,96,384]{2,1,0:T(8,128)(2,1)S(1)}, u32[]{:S(2)}, u32[]{:S(2)}) collective-permute-start(bf16[8,96,384]{2,1,0:T(8,128)(2,1)} %get-tuple-element.150), channel_id=1, source_target_pairs={{0,1},{1,0},{2,3},{3,2},{4,5},{5,4},{6,7},{7,6},{8,9},{9,8},{10,11... | collective-permute-start | bytes 1769480 | tf_op jit(solution)/shard_map/ppermute | solution.py:41
  111.3 9.9 %copy-start.19 = (bf16[1,192,768]{2,1,0:T(8,128)(2,1)S(1)}, bf16[1,192,768]{2,1,0:T(8,128)(2,1)}, u32[]{:S(2)}) copy-start(bf16[1,192,768]{2,1,0:T(8,128)(2,1)} %get-tuple-element.153) | copy-start | bytes 884740
  117.0 20.4 %all-to-all-start = ((bf16[8,224,128]{2,1,0:T(8,128)(2,1)}), bf16[8,224,128]{2,1,0:T(8,128)(2,1)S(1)}, u32[]{:S(2)}, u32[]{:S(2)}) async-start(bf16[8,224,128]{2,1,0:T(8,128)(2,1)} %get-tuple-element.162), calls=%async_computation | async-start | bytes 917504 | tf_op jit(solution)/shard_map/all_to_all | solution.py:937
  121.2 13.8 %collective-permute-start.16 = (bf16[1,192,768]{2,1,0:T(8,128)(2,1)S(1)}, bf16[1,192,768]{2,1,0:T(8,128)(2,1)S(1)}, u32[]{:S(2)}, u32[]{:S(2)}) collective-permute-start(bf16[1,192,768]{2,1,0:T(8,128)(2,1)S(1)} %copy-done.19), channel_id=1, source_target_pairs={{0,1},{1,0},{2,3},{3,2},{4,5},{5,4},{6,7},{7,6},{8,9},{9,8},{10,11... | collective-permute-start | bytes 884744 | tf_op jit(solution)/shard_map/ppermute | solution.py:41
  124.3 11.7 %copy-start.2 = (bf16[1,192,768]{2,1,0:T(8,128)(2,1)S(1)}, bf16[1,192,768]{2,1,0:T(8,128)(2,1)}, u32[]{:S(2)}) copy-start(bf16[1,192,768]{2,1,0:T(8,128)(2,1)} %get-tuple-element.171) | copy-start | bytes 884740
  127.0 15.3 %collective-permute-start.24 = (bf16[2,48,1536]{2,1,0:T(8,128)(2,1)}, bf16[2,48,1536]{2,1,0:T(8,128)(2,1)S(1)}, u32[]{:S(2)}, u32[]{:S(2)}) collective-permute-start(bf16[2,48,1536]{2,1,0:T(8,128)(2,1)} %get-tuple-element.170), channel_id=1, source_target_pairs={{0,1},{1,0},{2,3},{3,2},{4,5},{5,4},{6,7},{7,6},{8,9},{9,8},{10,11... | collective-permute-start | bytes 884744 | tf_op jit(solution)/shard_map/ppermute | solution.py:41
  135.1 7.2 %collective-permute-start.23 = (bf16[4,96,384]{2,1,0:T(8,128)(2,1)}, bf16[4,96,384]{2,1,0:T(8,128)(2,1)S(1)}, u32[]{:S(2)}, u32[]{:S(2)}) collective-permute-start(bf16[4,96,384]{2,1,0:T(8,128)(2,1)} %get-tuple-element.175), channel_id=1, source_target_pairs={{0,2},{1,3},{2,0},{3,1},{4,6},{5,7},{6,4},{7,5},{8,10},{9,11},{10,... | collective-permute-start | bytes 884744 | tf_op jit(solution)/shard_map/ppermute | solution.py:41
  136.0 12.7 %collective-permute-start.22 = (bf16[192,768]{1,0:T(8,128)(2,1)S(1)}, bf16[192,768]{1,0:T(8,128)(2,1)S(1)}, u32[]{:S(2)}, u32[]{:S(2)}) collective-permute-start(bf16[192,768]{1,0:T(8,128)(2,1)S(1)} %fusion), channel_id=1, source_target_pairs={{4,0},{5,1},{6,2},{7,3},{8,12},{9,13},{10,14},{11,15},{20,16},{21,... | collective-permute-start | bytes 884744 | tf_op jit(solution)/shard_map/ppermute | solution.py:57
  139.8 9.7 %collective-permute-start.21 = (bf16[224,128]{1,0:T(8,128)(2,1)}, bf16[224,128]{1,0:T(8,128)(2,1)S(1)}, u32[]{:S(2)}, u32[]{:S(2)}) collective-permute-start(bf16[224,128]{1,0:T(8,128)(2,1)} %gather_sums.1.refs_0_), channel_id=1, source_target_pairs={{0,24},{8,16},{16,8},{24,0},{1,25},{9,17},{17,9},{25,1},{2,26},{10... | collective-permute-start | bytes 172040 | tf_op jit(solution)/shard_map/ppermute | solution.py:41
  139.8 9.7 %collective-permute-start.20 = (bf16[224,128]{1,0:T(8,128)(2,1)}, bf16[224,128]{1,0:T(8,128)(2,1)S(1)}, u32[]{:S(2)}, u32[]{:S(2)}) collective-permute-start(bf16[224,128]{1,0:T(8,128)(2,1)} %gather_sums.1.refs_0_), channel_id=1, source_target_pairs={{0,16},{8,24},{16,0},{24,8},{1,17},{9,25},{17,1},{25,9},{2,18},{10... | collective-permute-start | bytes 172040 | tf_op jit(solution)/shard_map/ppermute | solution.py:41
  142.3 7.2 %collective-permute-start.19 = (bf16[224,128]{1,0:T(8,128)(2,1)}, bf16[224,128]{1,0:T(8,128)(2,1)S(1)}, u32[]{:S(2)}, u32[]{:S(2)}) collective-permute-start(bf16[224,128]{1,0:T(8,128)(2,1)} %gather_sums.1.refs_0_), channel_id=1, source_target_pairs={{0,8},{8,0},{16,24},{24,16},{1,9},{9,1},{17,25},{25,17},{2,10},{10... | collective-permute-start | bytes 172040 | tf_op jit(solution)/shard_map/ppermute | solution.py:41
  145.2 17.7 %collective-permute-start.28 = (bf16[1,48,1536]{2,1,0:T(8,128)(2,1)}, bf16[1,48,1536]{2,1,0:T(8,128)(2,1)S(1)}, u32[]{:S(2)}, u32[]{:S(2)}) collective-permute-start(bf16[1,48,1536]{2,1,0:T(8,128)(2,1)} %get-tuple-element.181), channel_id=1, source_target_pairs={{0,4},{1,5},{2,6},{3,7},{4,0},{5,1},{6,2},{7,3},{8,12},{9,13},{10,... | collective-permute-start | bytes 442376 | tf_op jit(solution)/shard_map/ppermute | solution.py:41
  148.8 15.5 %collective-permute-start.27 = (bf16[192,768]{1,0:T(8,128)(2,1)S(1)}, bf16[192,768]{1,0:T(8,128)(2,1)S(1)}, u32[]{:S(2)}, u32[]{:S(2)}) collective-permute-start(bf16[192,768]{1,0:T(8,128)(2,1)S(1)} %add_convert_fusion), channel_id=1, source_target_pairs={{0,16},{8,24},{16,0},{24,8},{1,17},{9,25},{17,1},{25,9},{2,18},{10... | collective-permute-start | bytes 884744 | tf_op jit(solution)/shard_map/ppermute | solution.py:41
  149.5 12.4 %copy-start.5 = (bf16[2,96,384]{2,1,0:T(8,128)(2,1)S(1)}, bf16[2,96,384]{2,1,0:T(8,128)(2,1)}, u32[]{:S(2)}) copy-start(bf16[2,96,384]{2,1,0:T(8,128)(2,1)} %get-tuple-element.192) | copy-start | bytes 442372
  149.5 13.4 %copy-start.4 = (bf16[1,48,1536]{2,1,0:T(8,128)(2,1)S(1)}, bf16[1,48,1536]{2,1,0:T(8,128)(2,1)}, u32[]{:S(2)}) copy-start(bf16[1,48,1536]{2,1,0:T(8,128)(2,1)} %get-tuple-element.195) | copy-start | bytes 442372
  149.6 12.4 %collective-permute-start.25 = (bf16[2,96,384]{2,1,0:T(8,128)(2,1)}, bf16[2,96,384]{2,1,0:T(8,128)(2,1)S(1)}, u32[]{:S(2)}, u32[]{:S(2)}) collective-permute-start(bf16[2,96,384]{2,1,0:T(8,128)(2,1)} %get-tuple-element.190), channel_id=1, source_target_pairs={{0,4},{1,5},{2,6},{3,7},{4,0},{5,1},{6,2},{7,3},{8,12},{9,13},{10,... | collective-permute-start | bytes 442376 | tf_op jit(solution)/shard_map/ppermute | solution.py:41
  162.0 6.8 %collective-permute-start.26 = (bf16[2,96,384]{2,1,0:T(8,128)(2,1)S(1)}, bf16[2,96,384]{2,1,0:T(8,128)(2,1)S(1)}, u32[]{:S(2)}, u32[]{:S(2)}) collective-permute-start(bf16[2,96,384]{2,1,0:T(8,128)(2,1)S(1)} %add_convert_fusion.4), channel_id=1, source_target_pairs={{0,16},{8,24},{16,0},{24,8},{1,17},{9,25},{17,1},{25,9},{2,18},{10... | collective-permute-start | bytes 442376 | tf_op jit(solution)/shard_map/ppermute | solution.py:41
  162.9 7.7 %collective-permute-start.31 = (bf16[48,1536]{1,0:T(8,128)(2,1)S(1)}, bf16[48,1536]{1,0:T(8,128)(2,1)S(1)}, u32[]{:S(2)}, u32[]{:S(2)}) collective-permute-start(bf16[48,1536]{1,0:T(8,128)(2,1)S(1)} %fusion.1), channel_id=1, source_target_pairs={{0,16},{8,24},{16,0},{24,8},{1,17},{9,25},{17,1},{25,9},{2,18},{10... | collective-permute-start | bytes 442376 | tf_op jit(solution)/shard_map/ppermute | solution.py:41
  164.3 6.5 %collective-permute-start.30 = (bf16[384,768]{1,0:T(8,128)(2,1)S(1)}, bf16[384,768]{1,0:T(8,128)(2,1)S(1)}, u32[]{:S(2)}, u32[]{:S(2)}) collective-permute-start(bf16[384,768]{1,0:T(8,128)(2,1)S(1)} %pad_maximum_fusion), channel_id=1, source_target_pairs={{0,8},{8,0},{16,24},{24,16},{1,9},{9,1},{17,25},{25,17},{2,10},{10... | collective-permute-start | bytes 1769480 | tf_op jit(solution)/shard_map/ppermute | solution.py:41
  168.9 3.0 %collective-permute-start.29 = (bf16[2,96,384]{2,1,0:T(8,128)(2,1)S(1)}, bf16[2,96,384]{2,1,0:T(8,128)(2,1)S(1)}, u32[]{:S(2)}, u32[]{:S(2)}) collective-permute-start(bf16[2,96,384]{2,1,0:T(8,128)(2,1)S(1)} %add_convert_fusion.2), channel_id=1, source_target_pairs={{0,8},{8,0},{16,24},{24,16},{1,9},{9,1},{17,25},{25,17},{2,10},{10... | collective-permute-start | bytes 442376 | tf_op jit(solution)/shard_map/ppermute | solution.py:41
  170.7 2.1 %collective-permute-start.32 = (bf16[96,1536]{1,0:T(8,128)(2,1)S(1)}, bf16[96,1536]{1,0:T(8,128)(2,1)S(1)}, u32[]{:S(2)}, u32[]{:S(2)}) collective-permute-start(bf16[96,1536]{1,0:T(8,128)(2,1)S(1)} %pad_maximum_fusion.2), channel_id=1, source_target_pairs={{0,8},{8,0},{16,24},{24,16},{1,9},{9,1},{17,25},{25,17},{2,10},{10... | collective-permute-start | bytes 884744 | tf_op jit(solution)/shard_map/ppermute | solution.py:41
  (17 other events, 13.6 us)

commit v3 on v2

--- a/solution.py
+++ b/solution.py
@@ -618,63 +618,70 @@
     )(place, *pairs, q, do, tables)
 
 
-def weights_kernel(place_ref, attn_ref, g_ref, first_in_ref, grad_ref, send_ref, keep_ref, small_ref):
+def weights_kernel(place_ref, attn_ref, attn2_ref, g_ref, g2_ref, in_ref, in2_ref, q_ref, q2_ref, theirs_ref, mine_ref, small_ref, scr):
     half = D // 2
-    own = place_ref[0] == 0
+    y = place_ref[2]
 
     def products(left, right, line):
-        small_ref[line : line + 1] = jnp.sum(right.astype(F32), axis=0, keepdims=True)
-        result = dot_tn(left, right).astype(BF16)
-        lower, upper = result[:, :half], result[:, half:]
-        send_ref[0] = jnp.where(own, upper, lower)
-        keep_ref[0] = jnp.where(own, lower, upper)
+        at = pl.ds(pl.multiple_of(place_ref[0] * half, 128), half)
+        small_ref[line : line + 1] = jnp.zeros_like(small_ref[line : line + 1])
+        small_ref[line : line + 1, at] = jnp.sum(right.astype(F32), axis=0, keepdims=True)
+        scr[...] = dot_tn(left, right).reshape(scr.shape)
+        theirs_ref[0] = scr[:, pl.ds(1 - y, 1)].reshape(theirs_ref.shape[1:]).astype(BF16)
+        mine_ref[0] = scr[:, pl.ds(y, 1)].reshape(mine_ref.shape[1:]).astype(BF16)
+
+    both = lambda a, b: jnp.concatenate([a[...], b[...]], axis=0)
 
     @pl.when(pl.program_id(0) == 0)
     def _():
-        products(attn_ref[...], g_ref[...], 1)
+        products(both(attn_ref, attn2_ref), both(g_ref, g2_ref), 1)
 
     @pl.when(pl.program_id(0) == 1)
     def _():
-        products(first_in_ref[...], grad_ref[...], 0)
-
-
-def weights(place, attn, g, first_in, grad):
+        products(both(in_ref, in2_ref), both(q_ref, q2_ref), 0)
+
+
+def weights(place, count, attn, attn2, g, g2, first_in, first_in2, grad, grad2):
     rows = attn.shape[0]
-    whole = pl.BlockSpec((rows, D), lambda i: (0, 0))
-    part = pl.BlockSpec((1, D, D // 2), lambda i: (i, 0, 0))
+    depth, per, half = count // 2, D // count, D // 2
+    whole = pl.BlockSpec((rows, D), lambda i, place: (0, 0), pipeline_mode=pl.Buffered(1))
+    part = pl.BlockSpec((rows, half), lambda i, place: (0, place[0]), pipeline_mode=pl.Buffered(1))
+    result = pl.BlockSpec((1, depth, per, half), lambda i, place: (i, 0, 0, 0))
     return pl.pallas_call(
         weights_kernel,
-        grid=(2,),
-        in_specs=[SMEM] + [whole] * 4,
-        out_specs=[part, part, pl.BlockSpec((8, D), lambda i: (0, 0))],
-        out_shape=[SHAPE((2, D, D // 2), BF16), SHAPE((2, D, D // 2), BF16), SHAPE((8, D), F32)],
+        grid_spec=pltpu.PrefetchScalarGridSpec(
+            num_scalar_prefetch=1,
+            grid=(2,),
+            in_specs=[whole, whole, part, part, whole, whole, part, part],
+            out_specs=[result, result, pl.BlockSpec((8, D), lambda i, place: (0, 0))],
+            scratch_shapes=[pltpu.VMEM((depth, 2, per, half), F32)],
+        ),
+        out_shape=[SHAPE((2, depth, per, half), BF16), SHAPE((2, depth, per, half), BF16), SHAPE((8, D), F32)],
         compiler_params=params(),
         cost_estimate=cost(2.4),
         name="weights",
-    )(place, attn, g, first_in, grad)
-
-
-def mix_kernel(x_ref, mlp_ref, mlp2_ref, attn_ref, grad_ref, add_ref, wo_ref, wq_ref, output_ref, first_ref):
-    first_ref[...] = dot_nt(grad_ref[...], wq_ref[...]).astype(BF16)
+    )(place, attn, attn2, g, g2, first_in, first_in2, grad, grad2)
+
+
+def mix_kernel(x_ref, mlp_ref, mlp2_ref, attn_ref, add_ref, wo_ref, output_ref):
     mlp = mlp_ref[...].astype(F32) + mlp2_ref[...].astype(F32)
     x = x_ref[...].astype(F32)
     output_ref[...] = (x + (mlp + dot(attn_ref[...], wo_ref[...])) + wide(add_ref)).astype(BF16)
 
 
-def mix(x, mlp, mlp2, attn, grad, add, wo, wqkv):
+def mix(x, mlp, mlp2, attn, add, wo):
     rows = x.shape[0]
     row = pl.BlockSpec((rows // 2, D), lambda i: (i, 0))
-    square = pl.BlockSpec((D, D), lambda i: (0, 0))
     return pl.pallas_call(
         mix_kernel,
         grid=(2,),
-        in_specs=[row] * 5 + [pl.BlockSpec((D,), lambda i: (0,)), square, square],
-        out_specs=[row] * 2,
-        out_shape=[SHAPE((rows, D), BF16)] * 2,
+        in_specs=[row] * 4 + [pl.BlockSpec((D,), lambda i: (0,)), pl.BlockSpec((D, D), lambda i: (0, 0))],
+        out_specs=row,
+        out_shape=SHAPE((rows, D), BF16),
         compiler_params=params(),
-        cost_estimate=cost(2.4),
+        cost_estimate=cost(1.2),
         name="mix",
-    )(x, mlp, mlp2, attn, grad, add, wo, wqkv)
+    )(x, mlp, mlp2, attn, add, wo)
 
 
 def two_terms(values):
@@ -698,19 +705,21 @@
         extra_ref,
         x_ref,
         g_ref,
-        first_ref,
+        q_ref,
         back_ref,
         back2_ref,
         gain_ref,
         bias_ref,
         gain2_ref,
-        wkv_ref,
+        wqkv_ref,
         tables_ref,
         b1_ref,
         early_ref,
         tokens_ref,
-        message_ref,
+        theirs_ref,
+        mine_ref,
         vector_scr,
+        weight_scr,
     ) = refs
     total = extra_ref[...].astype(F32)
     for ref in kv_refs:
@@ -721,7 +730,7 @@
     normed, inverse = normalize(x)
     gain = wide(gain_ref)
     first_in = normed * gain + wide(bias_ref)
-    first_grad = first_ref[...].astype(F32) + dot_nt(grad, wkv_ref[...])
+    first_grad = dot_nt(jnp.concatenate([q_ref[...], grad], axis=1), wqkv_ref[...])
     second_grad = back_ref[...].astype(F32) + back2_ref[...].astype(F32)
 
     vector_scr[...] = jnp.zeros_like(vector_scr)
@@ -739,13 +748,12 @@
             vector_scr[at : at + 1] = row[:, i * 128 : (i + 1) * 128]
             at += 1
     high, rest = two_terms(vector_scr[...])
-    weight = dot(first_in.T.astype(BF16), grad).astype(BF16)
-    places = message_ref.shape[0]
-    per = weight.shape[0] // places
-    for i in range(places):
-        message_ref[i, :lines] = high
-        message_ref[i, lines : 2 * lines] = rest
-        message_ref[i, 2 * lines :] = weight[i * per : (i + 1) * per]
+    weight_scr[...] = dot(first_in.T.astype(BF16), grad).reshape(weight_scr.shape)
+    y = place_ref[2]
+    for message, at in ((theirs_ref, 1 - y), (mine_ref, y)):
+        message[:lines] = high
+        message[lines : 2 * lines] = rest
+        message[2 * lines :] = weight_scr[:, pl.ds(at, 1)].reshape(-1, 128).astype(BF16)
 
     normed_grad = first_grad * gain + second_grad * wide(gain2_ref)
     mean = jnp.mean(normed_grad, axis=-1, keepdims=True)
@@ -753,50 +761,57 @@
     tokens_ref[...] = (g_ref[...].astype(F32) + inverse * (normed_grad - mean - normed * along_rows)).astype(BF16)
 
 
-def finish(place, places, ff, kv_parts, extra, x, g, first, back, back2, gain, bias, gain2, wqkv, tables, b1, early):
+def finish(place, places, ff, kv_parts, extra, x, g, q_rows, back, back2, gain, bias, gain2, wqkv, tables, b1, early):
     rows = x.shape[0]
     lines = message_lines(ff)
     whole = lambda a: pl.BlockSpec(a.shape, lambda i: (0,) * a.ndim)
-    before = (*kv_parts, extra, x, g, first, back, back2, gain, bias, gain2)
-    after_it = (tables, b1, early)
+    arrays = (*kv_parts, extra, x, g, q_rows, back, back2, gain, bias, gain2, wqkv, tables, b1, early)
     return pl.pallas_call(
         functools.partial(finish_kernel, rows // tables.shape[1], len(kv_parts), lines),
         grid=(1,),
-        in_specs=[SMEM]
-        + [whole(a) for a in before]
-        + [pl.BlockSpec((D, 128), lambda i: (0, D // 128))]
-        + [whole(a) for a in after_it],
+        in_specs=[SMEM] + [whole(a) for a in arrays],
         out_specs=[
             pl.BlockSpec((rows, D), lambda i: (0, 0)),
-            pl.BlockSpec((places, 2 * lines + D // places, 128), lambda i: (0, 0, 0)),
+            pl.BlockSpec((2 * lines + D // 2, 128), lambda i: (0, 0)),
+            pl.BlockSpec((2 * lines + D // 2, 128), lambda i: (0, 0)),
         ],
-        out_shape=[SHAPE((rows, D), BF16), SHAPE((places, 2 * lines + D // places, 128), BF16)],
-        scratch_shapes=[pltpu.VMEM((lines, 128), F32)],
+        out_shape=[SHAPE((rows, D), BF16)] + [SHAPE((2 * lines + D // 2, 128), BF16)] * 2,
+        scratch_shapes=[pltpu.VMEM((lines, 128), F32), pltpu.VMEM((places // 2, 2, D // places, 128), F32)],
         compiler_params=params(),
         cost_estimate=cost(2.4),
         name="finish",
-    )(place, *before, wqkv, *after_it)
-
-
-def gather_sums(messages, lines):
-    rows = messages.shape[1]
-
-    def kernel(refs, result):
-        total = tree_sum([refs[i] for i in range(messages.shape[0])])
-        high, rest = two_terms(total[:lines] + total[lines : 2 * lines])
-        result[:lines] = high
-        result[lines : 2 * lines] = rest
-        result[2 * lines :] = total[2 * lines :].astype(BF16)
-
+    )(place, *arrays)
+
+
+def message_step(place, mine, come, lines, per, bit):
+    count = (mine.shape[0] - 2 * lines) // per
+    last = count == 1
+
+    def kernel(place_ref, a_ref, b_ref, *refs):
+        vector = tree_sum([ref[at : at + lines] for ref in (a_ref, b_ref) for at in (0, lines)])
+        high, rest = two_terms(vector)
+        weight = a_ref[2 * lines :].astype(F32) + b_ref[2 * lines :].astype(F32)
+        own = (place_ref[3] >> bit) & 1
+        if not last:
+            refs[-1][...] = weight.reshape(count // 2, 2, per, 128)
+        for result, at in zip(refs[: 1 if last else 2], (1 - own, own)):
+            result[:lines] = high
+            result[lines : 2 * lines] = rest
+            rows = weight if last else refs[-1][:, pl.ds(at, 1)].reshape(-1, 128)
+            result[2 * lines :] = rows.astype(BF16)
+
+    results = 1 if last else 2
+    scratch = [] if last else [pltpu.VMEM((count // 2, 2, per, 128), F32)]
     return pl.pallas_call(
         kernel,
-        in_specs=[VMEM],
-        out_specs=VMEM,
-        out_shape=SHAPE((rows, 128), BF16),
+        in_specs=[SMEM, VMEM, VMEM],
+        out_specs=[VMEM] * results,
+        out_shape=[SHAPE((2 * lines + count * per // results, 128), BF16)] * results,
+        scratch_shapes=scratch,
         compiler_params=params(),
         cost_estimate=cost(0.6),
-        name="gather_sums",
-    )(messages)
+        name="message_step",
+    )(place, mine, come)
 
 
 def last_sums(messages, lines, widths):
@@ -875,14 +890,15 @@
     kv, first_in = project_keys(x, ln1_gain, ln1_bias, qkv_weight, qkv_bias, tables)
     kv3 = kv.reshape(seqs, span, 128)
     kv_y = over_y(kv3)
+    first_other = over_core(first_in)
     q = project_queries(first_in, qkv_weight, qkv_bias, tables)
     (kv_y,) = after((kv_y,), q)
     two = jnp.stack([kv3, kv_y])
     pairs = [two] + [along(two, k) for k in range(1, depth)]
 
-    x_fed, g_fed = after((x, g), two)
+    x_fed, g_fed, first_other = after((x, g, first_other), two)
     (mlp, mlp_other, back, back_other, attn_grad, b1_grad, theirs1, mine1), (theirs2, mine2) = feed(
-        place, count, x_fed, x_other, g_fed, g_other, ln2_gain, ln2_bias, fc1_weight, fc1_bias.reshape(1, -1),
+        place, count, *after((x_fed, x_other, g_fed, g_other), first_other), ln2_gain, ln2_bias, fc1_weight, fc1_bias.reshape(1, -1),
         fc2_weight, out_weight,
     )
     come1 = over_x(theirs1)
@@ -896,66 +912,55 @@
     def halved(a, parts, height):
         return a.reshape(parts, 2, height, a.shape[-1])
 
-    q_rows, come1, mlp_come, back_come = after((flat(q_rows), come1, mlp_come, back_come), out)
-    send, keep, early = weights(place, flat(out), g, first_in, q_rows)
-    come3 = over_core(send)
-
-    mine2, come2 = after((mine2, come2), send)
+    out, q_rows = flat(out), flat(q_rows)
+    out_other, q_other = over_core(out), over_core(q_rows)
+    mine1, come1, come2, mlp_come, back_come = after((mine1, come1, come2, mlp_come, back_come), out)
+    view = lambda v: halved(v, depth // 2, per1)
+    theirs1, mine1 = add_split(place, [(view(mine1), view(come1), 3)])
+    come1 = over_z(theirs1, 0)
+
+    out_other, q_other = after((out_other, q_other), theirs1)
+    theirs3, mine3, early = weights(place, count, out, out_other, g, g_other, first_in, first_other, q_rows, q_other)
+    come3 = over_y(theirs3)
+
+    even, odd = after((even, odd), theirs3)
+    kv_sums = [summed(even[k], odd[k]) for k in range(depth)]
+    got = [along(kv_sums[k], -k) for k in range(1, depth)]
+
+    mine2, come2 = after((mine2, come2), *kv_sums)
     height = per2 // 2
     view = lambda v: halved(v, half_depth, height)
     theirs2, mine2 = add_split(place, [(view(mine2), view(come2), 1)])
     come2 = over_x(theirs2)
 
-    even, odd = after((even, odd), theirs2)
-    kv_sums = [summed(even[k], odd[k]) for k in range(depth)]
-    got = [along(kv_sums[k], -k) for k in range(1, depth)]
-
-    mine1, come1 = after((mine1, come1), *kv_sums)
-    view = lambda v: halved(v, depth // 2, per1)
-    theirs1, mine1 = add_split(place, [(view(mine1), view(come1), 3)])
-    come1 = over_z(theirs1, 0)
-
-    x_mix, mlp_come = after((x, mlp_come), theirs1)
-    output, first = mix(x_mix, mlp, mlp_come, flat(out), q_rows, out_bias, out_weight, qkv_weight)
-
-    keep, come3 = after((keep, come3), first)
-    view = lambda v: halved(v, 2 * depth, per1)
-    theirs3, mine3 = add_split(place, [(view(keep), view(come3), 2)])
-    come3 = over_y(theirs3)
-
-    mine2, come2 = after((mine2, come2), theirs3)
+    (x_mix,) = after((x,), theirs2)
+    output = mix(x_mix, mlp, mlp_come, out, out_bias, out_weight)
+
+    mine1, come1 = after((mine1, come1), output)
+    view = lambda v: halved(v, depth // 2, per1 // 2)
+    theirs1, mine1 = add_split(place, [(view(mine1), view(come1), 2)])
+    come1 = over_y(theirs1)
+    mine3, come3 = after((mine3, come3), theirs1)
+    view3 = lambda v: halved(v, depth, per1)
+    theirs3, mine3 = add_split(place, [(view3(mine3), view3(come3), 3)])
+    come3 = over_z(theirs3, 0)
+
+    got = after(got, theirs3)
+    lines = message_lines(ff)
+    tokens_grad, theirs4, mine4 = finish(
+        place, count, ff, [flat(v) for v in (kv_sums[0], *got)], flat(key_value_grad), x, g, q_rows, back, back_come,
+        ln1_gain, ln1_bias, ln2_gain, qkv_weight, tables, b1_grad, early,
+    )
+    come4 = over_y(theirs4)
+
+    mine2, come2 = after((mine2, come2), tokens_grad)
     view = lambda v: halved(v, half_depth // 2, height)
     theirs2, mine2 = add_split(place, [(view(mine2), view(come2), 2)])
     come2 = over_y(theirs2)
-
-    got = after(got, theirs2)
-    lines = message_lines(ff)
-    tokens_grad, messages = finish(
-        place, count, ff, [flat(v) for v in (kv_sums[0], *got)], flat(key_value_grad), x, g, first, back, back_come,
-        ln1_gain, ln1_bias, ln2_gain, qkv_weight, tables, b1_grad, early,
-    )
-    messages = lax.all_to_all(messages, "seq", 0, 0, tiled=True)
-
-    mine3, come3, mine1, come1 = after((mine3, come3, mine1, come1), tokens_grad)
-    view3 = lambda v: halved(v, depth, per1)
-    view1 = lambda v: halved(v, depth // 2, per1 // 2)
-    theirs3, mine3, theirs1, mine1 = add_split(
-        place, [(view3(mine3), view3(come3), 3), (view1(mine1), view1(come1), 2)]
-    )
-    come3, come1 = over_z(theirs3, 0), over_y(theirs1)
-    mine2, come2 = after((mine2, come2), theirs1)
-    for bit in range(1, z_bits - 1):
-        view = lambda v: halved(v, half_depth >> (bit + 1), height)
-        theirs2, mine2 = add_split(place, [(view(mine2), view(come2), 3 + bit)])
-        come2 = over_z(theirs2, bit)
-    sum2 = summed(mine2, come2).reshape(height, D)
-    come2 = to_owner(sum2)
-
-    (messages,) = after((messages,), sum2)
-    message = gather_sums(messages, lines)
-    got = [flipped(message, "batch", i) for i in range(1, batches)]
-
-    mine3, come3, mine1, come1 = after((mine3, come3, mine1, come1), message)
+    mine4, come4 = after((mine4, come4), theirs2)
+    theirs4, mine4 = message_step(place, mine4, come4, lines, per1, 0)
+    come4 = over_z(theirs4, 0)
+    mine1, come1, mine3, come3 = after((mine1, come1, mine3, come3), theirs4)
     for bit in range(1, z_bits):
         parts = depth >> (bit + 1)
         view3 = lambda v: halved(v, 2 * parts, per1)
@@ -964,37 +969,51 @@
             place, [(view3(mine3), view3(come3), 3 + bit), (view1(mine1), view1(come1), 3 + bit)]
         )
         come3, come1 = over_z(theirs3, bit), over_z(theirs1, bit)
-
-    sum2, come2 = after((sum2, come2), theirs1)
+    mine4, come4 = after((mine4, come4), theirs3)
+    for bit in range(1, z_bits):
+        theirs4, mine4 = message_step(place, mine4, come4, lines, per1, bit)
+        come4 = over_z(theirs4, bit)
+    mine2, come2 = after((mine2, come2), theirs4)
+    for bit in range(1, z_bits - 1):
+        view = lambda v: halved(v, half_depth >> (bit + 1), height)
+        theirs2, mine2 = add_split(place, [(view(mine2), view(come2), 3 + bit)])
+        come2 = over_z(theirs2, bit)
+    sum2 = summed(mine2, come2).reshape(height, D)
+    come2 = to_owner(sum2)
+
+    mine3, come3 = after((mine3, come3), sum2)
+    sum3 = summed(mine3, come3)
+    other3 = over_x(sum3)
+    mine4, come4 = after((mine4, come4), sum3)
+    (message,) = message_step(place, mine4, come4, lines, per1, 0)
+    got = [flipped(message, "batch", i) for i in range(1, batches)]
+    mine1, come1 = after((mine1, come1), message)
+    sum1 = summed(mine1, come1).reshape(per1 // 2, -1)
+    other1 = over_x(sum1)
+    sum2, come2 = after((sum2, come2), sum1)
     sum2 = summed(sum2, come2)
     other2 = over_x(sum2)
-    got = after(got, sum2)
-    widths = (ff,) + (D,) * 6 + (128,)
-    b1_sum, q_sum, out_sum, gain1, bias1, gain2, bias2, kv_bias, kv_sum = last_sums([message, *got], lines, widths)
-    mine3, come3 = after((mine3, come3), kv_sum)
-    sum3 = summed(mine3, come3)
-    other3 = over_x(sum3)
-    mine1, come1 = after((mine1, come1), sum3)
-    sum1 = summed(mine1, come1).reshape(per1 // 2, -1)
-    other1 = over_x(sum1)
-
-    sum2, other2 = after((sum2, other2), sum1)
-    sum2 = pair(sum2, other2, xs, 0)
-    other2 = over_core(sum2)
+
     sum3, other3 = after((sum3, other3), sum2)
     sum3 = summed(sum3, other3)
     other3 = over_core(sum3)
     sum1, other1 = after((sum1, other1), sum3)
     sum1 = pair(sum1, other1, xs, 0)
     other1 = over_core(sum1)
+    got = after(got, sum1)
+    widths = (ff,) + (D,) * 6 + (128,)
+    b1_sum, q_sum, out_sum, gain1, bias1, gain2, bias2, kv_bias, kv_sum = last_sums([message, *got], lines, widths)
 
     owner = (z >> (z_bits - 1)) == core
-    (other2,) = after((other2,), sum1)
-    fc2_grad = jnp.where(owner, sum2, other2).astype(F32)
-    (other3,) = after((other3,), fc2_grad)
+    sum2, other2 = after((sum2, other2), kv_sum)
+    sum2 = pair(sum2, other2, xs, 0)
+    other2 = over_core(sum2)
+    (other3,) = after((other3,), sum2)
     both3 = pair(sum3, other3, core, 2).astype(F32)
     (other1,) = after((other1,), both3)
     fc1_grad = pair(sum1, other1, core, 1).astype(F32)
+    (other2,) = after((other2,), fc1_grad)
+    fc2_grad = jnp.where(owner, sum2, other2).astype(F32)
     return (
         output.reshape(tokens.shape),
         kv3,

time: 175 us -> 168 us (0.960)
  waiting for transfers between devices: 28 us -> 17.8 us
  Pallas kernels: 95.4 us -> 97.3 us
    ppermute x26 -> x31, waiting for transfers between devices: 27.3 us -> 14.7 us  [flipped(): lax.ppermute(block, axis, [(i, i ^ bits) for i in range(lax.axis_size(axi...]
    ppermute x26 -> x31, starting transfers between devices: 21.1 us -> 27.4 us  [flipped(): lax.ppermute(block, axis, [(i, i ^ bits) for i in range(lax.axis_size(axi...]
    all_to_all x1 -> x0, starting transfers between devices: 4.26 us -> none  [local(): messages = lax.all_to_all(messages, 'seq', 0, 0, tiled=True)]
    pallas_call x3 -> x5, Pallas kernels: 12.2 us -> 15 us  [the longest x1 6.17 us: weights(): pl.pallas_call(weights_kernel, grid_spec=pltpu.PrefetchScalarGridSpec(num...]
    ppermute x1, waiting for transfers between devices: 0.66 us -> 3.11 us  [to_owner(): return lax.ppermute(block, ('batch', 'seq'), route)]
    ppermute x6, starting transfers between devices: 8.49 us -> 6.69 us  [along(): lax.ppermute(block, 'seq', [(i, (i + 2 * distance) % size) for i in range...]
    unnamed x62 -> x64, local copies, waits for them, and re-layouts: 7.07 us -> 7.54 us
  transfers between devices with their start and end apart: 34 -> 38, of which waited for: 7 -> 8; matrix products, arithmetic and copies ran while one was open for 3% -> 4% of each run, Pallas kernels for 55% -> 58%
where the time goes in v3:
time: 168 us; the launch traced here: 167 us
  Pallas kernels  97.3 us (58%)
  starting transfers between devices  35.4 us (21%)
  waiting for transfers between devices  17.8 us (11%)
  local copies, waits for them, and re-layouts  8.29 us (5%)
  other arithmetic  7.28 us (4%)
    pallas_call x1, Pallas kernels, feed(): pl.pallas_call(feed_kernel, grid_spec=spec, out_shape=[SHAPE((rows, D), B...  28.6 us
    ppermute x31, starting transfers between devices, flipped(): lax.ppermute(block, axis, [(i, i ^ bits) for i in range(lax.axis_size(axi...  27.4 us
    pallas_call x1, Pallas kernels, attention(): pl.pallas_call(kernel, grid=(seqs, PAIRS // groups), in_specs=[SMEM] + [t...  24.9 us
    ppermute x31, waiting for transfers between devices, flipped(): lax.ppermute(block, axis, [(i, i ^ bits) for i in range(lax.axis_size(axi...  14.7 us
    pallas_call x6, Pallas kernels, add_split(): pl.pallas_call(kernel, in_specs=[SMEM] + [VMEM] * len(arrays), out_specs=...  14.4 us
    unnamed x64, local copies, waits for them, and re-layouts  7.54 us
    ppermute x6, starting transfers between devices, along(): lax.ppermute(block, 'seq', [(i, (i + 2 * distance) % size) for i in range...  6.69 us
    pallas_call x1, Pallas kernels, weights(): pl.pallas_call(weights_kernel, grid_spec=pltpu.PrefetchScalarGridSpec(num...  6.17 us
  transfers between devices with their start and end apart: 38, of which 8 were waited for; matrix products, arithmetic and copies ran while one was open for 4% of the time, Pallas kernels for 58%

profile of v3, /device:TPU:0, one launch (start us, length us, event | category | flops | bytes accessed | tf_op | source)
XLA Modules:
  0.0 166.9 jit_solution(14517445733245646348)
XLA Ops:
  2.2 2.9 %project_keys.1 = (bf16[512,128]{1,0:T(8,128)(2,1)}, bf16[512,768]{1,0:T(8,128)(2,1)}) custom-call(bf16[512,768]{1,0:T(8,128)(2,1)} %bitcast.57, f32[768]{0:T(1024)} %refs_10_.1, f32[768]{0:T(1024)} %refs_11_.1, bf16[768,896]{1,0:T(8,128)(2,1)} %refs_13_.1, f32[896]{0:T(1024)} %add_ref.4, f32[3,128,128]{2,1,0:T(8,128)} %pad_maximum_fusion.4.tables_ref.refs_6_.refs_14_), custom_call_target="tpu_custom_call" | custom-call | flops 3000000000 | tf_op jit(solution)/shard_map/project_keys/pallas_call | solution.py:171
  5.1 2.5 %collective-permute-start.1 = (bf16[4,128,128]{2,1,0:T(8,128)(2,1)}, bf16[4,128,128]{2,1,0:T(8,128)(2,1)S(1)}, u32[]{:S(2)}, u32[]{:S(2)}) collective-permute-start(bf16[4,128,128]{2,1,0:T(8,128)(2,1)} %bitcast.50), channel_id=1, source_target_pairs={{0,1},{1,0},{2,3},{3,2},{4,5},{5,4},{6,7},{7,6},{8,9},{9,8},{10,11... | collective-permute-start | bytes 393224 | tf_op jit(solution)/shard_map/ppermute | solution.py:41
  8.2 4.0 %project_queries.1 = bf16[512,768]{1,0:T(8,128)(2,1)} custom-call(bf16[512,768]{1,0:T(8,128)(2,1)} %get-tuple-element.122.first_ref.in_ref, bf16[768,896]{1,0:T(8,128)(2,1)} %refs_13_.1, f32[896]{0:T(1024)} %add_ref.4, f32[3,128,128]{2,1,0:T(8,128)} %pad_maximum_fusion.4.tables_ref.refs_6_.refs_14_), custom_call_target="tpu_custom_call" | custom-call | flops 6000000000 | tf_op jit(solution)/shard_map/project_queries/pallas_call | solution.py:193
  12.8 3.7 %collective-permute-start.10 = (bf16[2,4,128,128]{3,2,1,0:T(8,128)(2,1)S(1)}, bf16[2,4,128,128]{3,2,1,0:T(8,128)(2,1)S(1)}, u32[]{:S(2)}, u32[]{:S(2)}) collective-permute-start(bf16[2,4,128,128]{3,2,1,0:T(8,128)(2,1)S(1)} %pad_maximum_fusion.3.refs_0_), channel_id=1, source_target_pairs={{0,6},{1,7},{2,0},{3,1},{4,2},{5,3},{6,4},{7,5},{8,14},{9,15},{10,... | collective-permute-start | bytes 786440 | tf_op jit(solution)/shard_map/ppermute | solution.py:46
  16.5 1.0 collective-permute-start.9
  17.5 0.9 copy-done.12
  18.4 28.6 %feed_forward.1 = (bf16[512,768]{1,0:T(8,128)(2,1)}, bf16[512,768]{1,0:T(8,128)(2,1)}, bf16[512,768]{1,0:T(8,128)(2,1)}, bf16[512,768]{1,0:T(8,128)(2,1)}, bf16[...) custom-call(s32[4]{0:T(128)} %pad_add_fusion.place_ref, ...), custom_call_target="tpu_custom_call" | custom-call | flops 35999997952 | tf_op jit(solution)/shard_map/feed_forward/pallas_call | solution.py:351
  47.0 1.6 collective-permute-start.4
  48.5 3.4 %collective-permute-start.5 = (bf16[768,768]{1,0:T(8,128)(2,1)}, bf16[768,768]{1,0:T(8,128)(2,1)S(1)}, u32[]{:S(2)}, u32[]{:S(2)}) collective-permute-start(bf16[768,768]{1,0:T(8,128)(2,1)} %get-tuple-element.135), channel_id=1, source_target_pairs={{0,2},{1,3},{2,0},{3,1},{4,6},{5,7},{6,4},{7,5},{8,10},{9,11},{10,... | collective-permute-start | bytes 3538952 | tf_op jit(solution)/shard_map/ppermute | solution.py:41
  53.1 24.9 %attention.1 = (bf16[4,128,768]{2,1,0:T(8,128)(2,1)}, bf16[4,128,768]{2,1,0:T(8,128)(2,1)}, bf16[4,4,128,128]{3,2,1,0:T(8,128)(2,1)}, bf16[4,4,128,128]{3,2,1,0:T(8,128)(2,1)}) custom-call(s32[4]{0:T(128)} %pad_add_fusion.place_ref, bf16[2,4,128,128]{3,2,1,0:T(8,128)(2,1)} %copy-done.2, bf16[2,4,128,128]{3,2,1,0:T(8,128)(2,1)} %copy-done.20, ...), custom_call_target="tpu_custom_call" | custom-call | flops 30000001024 | tf_op jit(solution)/shard_map/attention/pallas_call | solution.py:607
  78.7 0.9 collective-permute-start.11
  79.6 1.0 copy-done.8
  80.6 2.9 %add_split.6 = (bf16[2,96,1536]{2,1,0:T(8,128)(2,1)}, bf16[2,96,1536]{2,1,0:T(8,128)(2,1)}) custom-call(s32[4]{0:T(128)} %pad_add_fusion.place_ref, bf16[2,2,96,1536]{3,2,1,0:T(8,128)(2,1)} %bitcast.82, bf16[2,2,96,1536]{3,2,1,0:T(8,128)(2,1)} %bitcast.55), custom_call_target="tpu_custom_call" | custom-call | flops 3600000000 | tf_op jit(solution)/shard_map/add_split/pallas_call | solution.py:139
  83.7 6.2 %weights.1 = (bf16[2,4,96,384]{3,2,1,0:T(8,128)(2,1)}, bf16[2,4,96,384]{3,2,1,0:T(8,128)(2,1)}, f32[8,768]{1,0:T(8,128)}) custom-call(s32[4]{0:T(128)} %pad_add_fusion.place_ref, bf16[512,768]{1,0:T(8,128)(2,1)} %bitcast.69, bf16[512,768]{1,0:T(8,128)(2,1)} %collective-permute-done.12.attn2_ref, bf16[512,768]{1,0:T(8,128)(2,1)} %bitcast.62, ...), custom_call_target="tpu_custom_call" | custom-call | flops 7200000000 | tf_op jit(solution)/shard_map/weights/pallas_call | solution.py:650
  89.8 1.2 collective-permute-start.17
  91.0 2.0 %collective-permute-done.11 = bf16[4,4,128,128]{3,2,1,0:T(8,128)(2,1)S(1)} collective-permute-done((bf16[4,4,128,128]{3,2,1,0:T(8,128)(2,1)}, bf16[4,4,128,128]{3,2,1,0:T(8,128)(2,1)S(1)}, u32[]{:S(2)}, u32[]{:S(2)}) %collective-permute-start.11) | collective-permute-done | bytes 524320 | tf_op jit(solution)/shard_map/ppermute | solution.py:41
  93.0 0.8 add_convert_fusion.5
  93.8 1.3 collective-permute-start.15
  95.9 2.8 %add_split.7 = (bf16[2,192,768]{2,1,0:T(8,128)(2,1)}, bf16[2,192,768]{2,1,0:T(8,128)(2,1)}) custom-call(s32[4]{0:T(128)} %pad_add_fusion.place_ref, bf16[2,2,192,768]{3,2,1,0:T(8,128)(2,1)} %bitcast.81, bf16[2,2,192,768]{3,2,1,0:T(8,128)(2,1)} %bitcast.54), custom_call_target="tpu_custom_call" | custom-call | flops 3600000000 | tf_op jit(solution)/shard_map/add_split/pallas_call | solution.py:139
  98.7 3.9 %mix.1 = bf16[512,768]{1,0:T(8,128)(2,1)} custom-call(bf16[512,768]{1,0:T(8,128)(2,1)} %bitcast.59, bf16[512,768]{1,0:T(8,128)(2,1)} %get-tuple-element.156.mlp_ref, bf16[512,768]{1,0:T(8,128)(2,1)} %collective-permute-done.6.mlp2_ref, bf16[512,768]{1,0:T(8,128)(2,1)} %bitcast.70, f32[768]{0:T(1024)} %add_ref.5, bf16[768,768]{1,0:T(8,128)(2,1)} %wo_ref.3), custom_call_target="tpu_custom_call" | custom-call | flops 3600000000 | tf_op jit(solution)/shard_map/mix/pallas_call | solution.py:675
  103.7 2.2 %add_split.8 = (bf16[2,48,1536]{2,1,0:T(8,128)(2,1)}, bf16[2,48,1536]{2,1,0:T(8,128)(2,1)}) custom-call(s32[4]{0:T(128)} %pad_add_fusion.place_ref, bf16[2,2,48,1536]{3,2,1,0:T(8,128)(2,1)} %bitcast.88, bf16[2,2,48,1536]{3,2,1,0:T(8,128)(2,1)} %bitcast.71), custom_call_target="tpu_custom_call" | custom-call | flops 3600000000 | tf_op jit(solution)/shard_map/add_split/pallas_call | solution.py:139
  105.9 1.1 collective-permute-start.22
  107.0 2.2 %add_split.9 = (bf16[4,96,384]{2,1,0:T(8,128)(2,1)}, bf16[4,96,384]{2,1,0:T(8,128)(2,1)}) custom-call(s32[4]{0:T(128)} %pad_add_fusion.place_ref, bf16[4,2,96,384]{3,2,1,0:T(8,128)(2,1)} %bitcast.89, bf16[4,2,96,384]{3,2,1,0:T(8,128)(2,1)} %bitcast.73), custom_call_target="tpu_custom_call" | custom-call | flops 3600000000 | tf_op jit(solution)/shard_map/add_split/pallas_call | solution.py:139
  109.2 1.0 collective-permute-start.23
  110.9 5.9 %finish.1 = (bf16[512,768]{1,0:T(8,128)(2,1)}, bf16[512,128]{1,0:T(8,128)(2,1)}, bf16[512,128]{1,0:T(8,128)(2,1)}) custom-call(s32[4]{0:T(128)} %pad_add_fusion.place_ref, bf16[512,128]{1,0:T(8,128)(2,1)} %bitcast.49, bf16[512,128]{1,0:T(8,128)(2,1)} %bitcast.77, bf16[512,128]{1,0:T(8,128)(2,1)} %bitcast.78, bf16[512,128]{1,0:T(8,128)(2,1)} %bitcast.79, ...), custom_call_target="tpu_custom_call" | custom-call | flops 7200000000 | tf_op jit(solution)/shard_map/finish/pallas_call | solution.py:769
  116.8 1.3 collective-permute-start.19
  118.1 2.1 %add_split.10 = (bf16[1,192,768]{2,1,0:T(8,128)(2,1)}, bf16[1,192,768]{2,1,0:T(8,128)(2,1)}) custom-call(s32[4]{0:T(128)} %pad_add_fusion.place_ref, bf16[1,2,192,768]{3,2,1,0:T(8,128)(2,1)} %bitcast.87, bf16[1,2,192,768]{3,2,1,0:T(8,128)(2,1)} %bitcast.72), custom_call_target="tpu_custom_call" | custom-call | flops 3600000000 | tf_op jit(solution)/shard_map/add_split/pallas_call | solution.py:139
  120.3 0.8 collective-permute-start.26
  121.1 2.3 %collective-permute-done.19.b_ref = bf16[512,128]{1,0:T(8,128)(2,1)S(1)} collective-permute-done((bf16[512,128]{1,0:T(8,128)(2,1)}, bf16[512,128]{1,0:T(8,128)(2,1)S(1)}, u32[]{:S(2)}, u32[]{:S(2)}) %collective-permute-start.19) | collective-permute-done | bytes 131104 | tf_op jit(solution)/shard_map/ppermute | solution.py:41
  124.1 1.7 %message_step.3 = (bf16[320,128]{1,0:T(8,128)(2,1)}, bf16[320,128]{1,0:T(8,128)(2,1)}) custom-call(s32[4]{0:T(128)} %pad_add_fusion.place_ref, bf16[512,128]{1,0:T(8,128)(2,1)} %get-tuple-element.180.a_ref, bf16[512,128]{1,0:T(8,128)(2,1)} %copy-done.26), custom_call_target="tpu_custom_call" | custom-call | flops 1800000000 | tf_op jit(solution)/shard_map/message_step/pallas_call | solution.py:805
  125.7 1.1 collective-permute-start.21
  127.6 2.1 %add_split.11 = (bf16[2,96,384]{2,1,0:T(8,128)(2,1)}, bf16[2,96,384]{2,1,0:T(8,128)(2,1)}, bf16[1,48,1536]{2,1,0:T(8,128)(2,1)}, bf16[1,48,1536]{2,1,0:T(8,128)(2,1)}) custom-call(s32[4]{0:T(128)} %pad_add_fusion.place_ref, bf16[2,2,96,384]{3,2,1,0:T(8,128)(2,1)} %bitcast.91, bf16[2,2,96,384]{3,2,1,0:T(8,128)(2,1)} %bitcast.75, ...), custom_call_target="tpu_custom_call" | custom-call | flops 3600000000 | tf_op jit(solution)/shard_map/add_split/pallas_call | solution.py:139
  129.7 2.5 %collective-permute-start.25 = (bf16[2,96,384]{2,1,0:T(8,128)(2,1)}, bf16[2,96,384]{2,1,0:T(8,128)(2,1)S(1)}, u32[]{:S(2)}, u32[]{:S(2)}) collective-permute-start(bf16[2,96,384]{2,1,0:T(8,128)(2,1)} %get-tuple-element.190), channel_id=1, source_target_pairs={{0,4},{1,5},{2,6},{3,7},{4,0},{5,1},{6,2},{7,3},{8,12},{9,13},{10,... | collective-permute-start | bytes 442376 | tf_op jit(solution)/shard_map/ppermute | solution.py:41
  132.9 1.7 %message_step.4 = (bf16[224,128]{1,0:T(8,128)(2,1)}, bf16[224,128]{1,0:T(8,128)(2,1)}) custom-call(s32[4]{0:T(128)} %pad_add_fusion.place_ref, bf16[320,128]{1,0:T(8,128)(2,1)} %get-tuple-element.191.a_ref, bf16[320,128]{1,0:T(8,128)(2,1)} %copy-done.27), custom_call_target="tpu_custom_call" | custom-call | flops 1800000000 | tf_op jit(solution)/shard_map/message_step/pallas_call | solution.py:805
  135.1 2.3 %collective-permute-start.30 = (bf16[1,48,1536]{2,1,0:T(8,128)(2,1)S(1)}, bf16[1,48,1536]{2,1,0:T(8,128)(2,1)S(1)}, u32[]{:S(2)}, u32[]{:S(2)}) collective-permute-start(bf16[1,48,1536]{2,1,0:T(8,128)(2,1)S(1)} %copy-done.22), channel_id=1, source_target_pairs={{0,4},{1,5},{2,6},{3,7},{4,0},{5,1},{6,2},{7,3},{8,12},{9,13},{10,... | collective-permute-start | bytes 442376 | tf_op jit(solution)/shard_map/ppermute | solution.py:41
  137.5 1.3 collective-permute-start.33
  138.8 3.9 %collective-permute-done.25 = bf16[2,96,384]{2,1,0:T(8,128)(2,1)S(1)} collective-permute-done((bf16[2,96,384]{2,1,0:T(8,128)(2,1)}, bf16[2,96,384]{2,1,0:T(8,128)(2,1)S(1)}, u32[]{:S(2)}, u32[]{:S(2)}) %collective-permute-start.25) | collective-permute-done | bytes 147488 | tf_op jit(solution)/shard_map/ppermute | solution.py:41
  144.0 1.5 message_step.5.refs_0_
  145.5 1.5 collective-permute-start.28
  147.0 1.1 collective-permute-done.30
  148.1 3.1 %collective-permute-done.33 = bf16[192,768]{1,0:T(8,128)(2,1)S(1)} collective-permute-done((bf16[192,768]{1,0:T(8,128)(2,1)S(1)}, bf16[192,768]{1,0:T(8,128)(2,1)S(1)}, u32[]{:S(2)}, u32[]{:S(2)}) %collective-permute-start.33) | collective-permute-done | bytes 294944 | tf_op jit(solution)/shard_map/ppermute | solution.py:57
  151.2 1.0 collective-permute-start.31
  152.3 1.1 collective-permute-start.35
  153.5 4.6 %collective-permute-done.31 = bf16[48,1536]{1,0:T(8,128)(2,1)S(1)} collective-permute-done((bf16[48,1536]{1,0:T(8,128)(2,1)S(1)}, bf16[48,1536]{1,0:T(8,128)(2,1)S(1)}, u32[]{:S(2)}, u32[]{:S(2)}) %collective-permute-start.31) | collective-permute-done | bytes 147488 | tf_op jit(solution)/shard_map/ppermute | solution.py:41
  159.9 1.6 last_sums.1
  161.5 1.3 pad_maximum_fusion.5
  164.7 1.1 maximum_convert_fusion
  165.8 1.1 select_convert_fusion
  (134 shorter events, 15.0 us)
Async XLA Ops:
  0.6 16.9 %collective-permute-start.2 = (bf16[512,768]{1,0:T(8,128)(2,1)}, bf16[512,768]{1,0:T(8,128)(2,1)}, u32[]{:S(2)}, u32[]{:S(2)}) collective-permute-start(bf16[512,768]{1,0:T(8,128)(2,1)} %bitcast.56), channel_id=1, source_target_pairs={{0,8},{8,0},{16,24},{24,16},{1,9},{9,1},{17,25},{25,17},{2,10},{10... | collective-permute-start | bytes 2359304 | tf_op jit(solution)/shard_map/ppermute | solution.py:41
  2.2 5.6 %copy-start.9 = (bf16[4,128,768]{2,1,0:T(8,128)(2,1)S(1)}, bf16[4,128,768]{2,1,0:T(8,128)(2,1)}, u32[]{:S(2)}) copy-start(bf16[4,128,768]{2,1,0:T(8,128)(2,1)} %param.26) | copy-start | bytes 2359300
  5.1 7.7 %collective-permute-start.1 = (bf16[4,128,128]{2,1,0:T(8,128)(2,1)}, bf16[4,128,128]{2,1,0:T(8,128)(2,1)S(1)}, u32[]{:S(2)}, u32[]{:S(2)}) collective-permute-start(bf16[4,128,128]{2,1,0:T(8,128)(2,1)} %bitcast.50), channel_id=1, source_target_pairs={{0,1},{1,0},{2,3},{3,2},{4,5},{5,4},{6,7},{7,6},{8,9},{9,8},{10,11... | collective-permute-start | bytes 393224 | tf_op jit(solution)/shard_map/ppermute | solution.py:41
  7.6 8.8 %collective-permute-start = (bf16[512,768]{1,0:T(8,128)(2,1)}, bf16[512,768]{1,0:T(8,128)(2,1)S(1)}, u32[]{:S(2)}, u32[]{:S(2)}) collective-permute-start(bf16[512,768]{1,0:T(8,128)(2,1)} %get-tuple-element.122.first_ref.in_ref), channel_id=1, source_target_pairs={{0,8},{8,0},{16,24},{24,16},{1,9},{9,1},{17,25},{25,17},{2,10},{10... | collective-permute-start | bytes 2359304 | tf_op jit(solution)/shard_map/ppermute | solution.py:41
  7.8 4.9 %copy-start.5 = (bf16[512,128]{1,0:T(8,128)(2,1)S(1)}, bf16[512,128]{1,0:T(8,128)(2,1)}, u32[]{:S(2)}) copy-start(bf16[512,128]{1,0:T(8,128)(2,1)} %get-tuple-element.123) | copy-start | bytes 393220
  7.8 9.7 %collective-permute-start.3 = (bf16[512,768]{1,0:T(8,128)(2,1)S(1)}, bf16[512,768]{1,0:T(8,128)(2,1)S(1)}, u32[]{:S(2)}, u32[]{:S(2)}) collective-permute-start(bf16[512,768]{1,0:T(8,128)(2,1)S(1)} %bitcast.64), channel_id=1, source_target_pairs={{0,8},{8,0},{16,24},{24,16},{1,9},{9,1},{17,25},{25,17},{2,10},{10... | collective-permute-start | bytes 2359304 | tf_op jit(solution)/shard_map/ppermute | solution.py:41
  12.8 34.1 %copy-start.2 = (bf16[2,4,128,128]{3,2,1,0:T(8,128)(2,1)}, bf16[2,4,128,128]{3,2,1,0:T(8,128)(2,1)S(1)}, u32[]{:S(2)}) copy-start(bf16[2,4,128,128]{3,2,1,0:T(8,128)(2,1)S(1)} %pad_maximum_fusion.3.refs_0_) | copy-start | bytes 786436
  12.8 39.1 %collective-permute-start.10 = (bf16[2,4,128,128]{3,2,1,0:T(8,128)(2,1)S(1)}, bf16[2,4,128,128]{3,2,1,0:T(8,128)(2,1)S(1)}, u32[]{:S(2)}, u32[]{:S(2)}) collective-permute-start(bf16[2,4,128,128]{3,2,1,0:T(8,128)(2,1)S(1)} %pad_maximum_fusion.3.refs_0_), channel_id=1, source_target_pairs={{0,6},{1,7},{2,0},{3,1},{4,2},{5,3},{6,4},{7,5},{8,14},{9,15},{10,... | collective-permute-start | bytes 786440 | tf_op jit(solution)/shard_map/ppermute | solution.py:46
  16.5 35.4 %collective-permute-start.8 = (bf16[2,4,128,128]{3,2,1,0:T(8,128)(2,1)S(1)}, bf16[2,4,128,128]{3,2,1,0:T(8,128)(2,1)S(1)}, u32[]{:S(2)}, u32[]{:S(2)}) collective-permute-start(bf16[2,4,128,128]{3,2,1,0:T(8,128)(2,1)S(1)} %pad_maximum_fusion.3.refs_0_), channel_id=1, source_target_pairs={{0,2},{1,3},{2,4},{3,5},{4,6},{5,7},{6,0},{7,1},{8,10},{9,11},{10,... | collective-permute-start | bytes 786440 | tf_op jit(solution)/shard_map/ppermute | solution.py:46
  16.5 30.5 %copy-start.11 = (bf16[512,768]{1,0:T(8,128)(2,1)}, bf16[512,768]{1,0:T(8,128)(2,1)S(1)}, u32[]{:S(2)}) copy-start(bf16[512,768]{1,0:T(8,128)(2,1)S(1)} %collective-permute-done.in2_ref) | copy-start | bytes 2359300
  16.5 35.9 %collective-permute-start.9 = (bf16[2,4,128,128]{3,2,1,0:T(8,128)(2,1)S(1)}, bf16[2,4,128,128]{3,2,1,0:T(8,128)(2,1)S(1)}, u32[]{:S(2)}, u32[]{:S(2)}) collective-permute-start(bf16[2,4,128,128]{3,2,1,0:T(8,128)(2,1)S(1)} %pad_maximum_fusion.3.refs_0_), channel_id=1, source_target_pairs={{0,4},{1,5},{2,6},{3,7},{4,0},{5,1},{6,2},{7,3},{8,12},{9,13},{10,... | collective-permute-start | bytes 786440 | tf_op jit(solution)/shard_map/ppermute | solution.py:46
  47.0 32.6 %collective-permute-start.4 = (bf16[8,48,1536]{2,1,0:T(8,128)(2,1)}, bf16[8,48,1536]{2,1,0:T(8,128)(2,1)S(1)}, u32[]{:S(2)}, u32[]{:S(2)}) collective-permute-start(bf16[8,48,1536]{2,1,0:T(8,128)(2,1)} %get-tuple-element.134), channel_id=1, source_target_pairs={{0,16},{8,24},{16,0},{24,8},{1,17},{9,25},{17,1},{25,9},{2,18},{10... | collective-permute-start | bytes 3538952 | tf_op jit(solution)/shard_map/ppermute | solution.py:41
  48.5 31.1 %collective-permute-start.5 = (bf16[768,768]{1,0:T(8,128)(2,1)}, bf16[768,768]{1,0:T(8,128)(2,1)S(1)}, u32[]{:S(2)}, u32[]{:S(2)}) collective-permute-start(bf16[768,768]{1,0:T(8,128)(2,1)} %get-tuple-element.135), channel_id=1, source_target_pairs={{0,2},{1,3},{2,0},{3,1},{4,6},{5,7},{6,4},{7,5},{8,10},{9,11},{10,... | collective-permute-start | bytes 3538952 | tf_op jit(solution)/shard_map/ppermute | solution.py:41
  51.9 26.3 %collective-permute-start.6 = (bf16[512,768]{1,0:T(8,128)(2,1)}, bf16[512,768]{1,0:T(8,128)(2,1)}, u32[]{:S(2)}, u32[]{:S(2)}) collective-permute-start(bf16[512,768]{1,0:T(8,128)(2,1)} %get-tuple-element.136), channel_id=1, source_target_pairs={{0,8},{8,0},{16,24},{24,16},{1,9},{9,1},{17,25},{25,17},{2,10},{10... | collective-permute-start | bytes 2359304 | tf_op jit(solution)/shard_map/ppermute | solution.py:41
  52.0 26.7 %collective-permute-start.7 = (bf16[512,768]{1,0:T(8,128)(2,1)}, bf16[512,768]{1,0:T(8,128)(2,1)S(1)}, u32[]{:S(2)}, u32[]{:S(2)}) collective-permute-start(bf16[512,768]{1,0:T(8,128)(2,1)} %get-tuple-element.137), channel_id=1, source_target_pairs={{0,8},{8,0},{16,24},{24,16},{1,9},{9,1},{17,25},{25,17},{2,10},{10... | collective-permute-start | bytes 2359304 | tf_op jit(solution)/shard_map/ppermute | solution.py:41
  78.1 5.6 %collective-permute-start.12 = (bf16[512,768]{1,0:T(8,128)(2,1)}, bf16[512,768]{1,0:T(8,128)(2,1)}, u32[]{:S(2)}, u32[]{:S(2)}) collective-permute-start(bf16[512,768]{1,0:T(8,128)(2,1)} %bitcast.68), channel_id=1, source_target_pairs={{0,8},{8,0},{16,24},{24,16},{1,9},{9,1},{17,25},{25,17},{2,10},{10... | collective-permute-start | bytes 2359304 | tf_op jit(solution)/shard_map/ppermute | solution.py:41
  78.2 5.4 %collective-permute-start.13 = (bf16[512,768]{1,0:T(8,128)(2,1)}, bf16[512,768]{1,0:T(8,128)(2,1)}, u32[]{:S(2)}, u32[]{:S(2)}) collective-permute-start(bf16[512,768]{1,0:T(8,128)(2,1)} %bitcast.65), channel_id=1, source_target_pairs={{0,8},{8,0},{16,24},{24,16},{1,9},{9,1},{17,25},{25,17},{2,10},{10... | collective-permute-start | bytes 2359304 | tf_op jit(solution)/shard_map/ppermute | solution.py:41
  78.6 4.9 %copy-start.10 = (bf16[512,768]{1,0:T(8,128)(2,1)}, bf16[512,768]{1,0:T(8,128)(2,1)S(1)}, u32[]{:S(2)}) copy-start(bf16[512,768]{1,0:T(8,128)(2,1)S(1)} %collective-permute-done.7.refs_9_) | copy-start | bytes 2359300
  78.7 14.4 %collective-permute-start.11 = (bf16[4,4,128,128]{3,2,1,0:T(8,128)(2,1)}, bf16[4,4,128,128]{3,2,1,0:T(8,128)(2,1)S(1)}, u32[]{:S(2)}, u32[]{:S(2)}) collective-permute-start(bf16[4,4,128,128]{3,2,1,0:T(8,128)(2,1)} %get-tuple-element.142), channel_id=1, source_target_pairs={{0,1},{1,0},{2,3},{3,2},{4,5},{5,4},{6,7},{7,6},{8,9},{9,8},{10,11... | collective-permute-start | bytes 1572872 | tf_op jit(solution)/shard_map/ppermute | solution.py:41
  83.5 9.5 %copy-start = (bf16[4,4,128,128]{3,2,1,0:T(8,128)(2,1)S(1)}, bf16[4,4,128,128]{3,2,1,0:T(8,128)(2,1)}, u32[]{:S(2)}) copy-start(bf16[4,4,128,128]{3,2,1,0:T(8,128)(2,1)} %get-tuple-element.150) | copy-start | bytes 1572868
  83.5 19.3 %collective-permute-start.18 = (bf16[2,96,1536]{2,1,0:T(8,128)(2,1)}, bf16[2,96,1536]{2,1,0:T(8,128)(2,1)S(1)}, u32[]{:S(2)}, u32[]{:S(2)}) collective-permute-start(bf16[2,96,1536]{2,1,0:T(8,128)(2,1)} %get-tuple-element.146), channel_id=1, source_target_pairs={{0,2},{1,3},{2,0},{3,1},{4,6},{5,7},{6,4},{7,5},{8,10},{9,11},{10,... | collective-permute-start | bytes 1769480 | tf_op jit(solution)/shard_map/ppermute | solution.py:41
  89.8 16.0 %collective-permute-start.17 = (bf16[2,4,96,384]{3,2,1,0:T(8,128)(2,1)}, bf16[2,4,96,384]{3,2,1,0:T(8,128)(2,1)S(1)}, u32[]{:S(2)}, u32[]{:S(2)}) collective-permute-start(bf16[2,4,96,384]{3,2,1,0:T(8,128)(2,1)} %get-tuple-element.149), channel_id=1, source_target_pairs={{0,1},{1,0},{2,3},{3,2},{4,5},{5,4},{6,7},{7,6},{8,9},{9,8},{10,11... | collective-permute-start | bytes 1769480 | tf_op jit(solution)/shard_map/ppermute | solution.py:41
  93.8 15.4 %collective-permute-start.14 = (bf16[4,128,128]{2,1,0:T(8,128)(2,1)S(1)}, bf16[4,128,128]{2,1,0:T(8,128)(2,1)S(1)}, u32[]{:S(2)}, u32[]{:S(2)}) collective-permute-start(bf16[4,128,128]{2,1,0:T(8,128)(2,1)S(1)} %get-tuple-element.233), channel_id=1, source_target_pairs={{0,6},{1,7},{2,0},{3,1},{4,2},{5,3},{6,4},{7,5},{8,14},{9,15},{10,... | collective-permute-start | bytes 393224 | tf_op jit(solution)/shard_map/ppermute | solution.py:46
  93.8 16.4 %collective-permute-start.15 = (bf16[4,128,128]{2,1,0:T(8,128)(2,1)S(1)}, bf16[4,128,128]{2,1,0:T(8,128)(2,1)S(1)}, u32[]{:S(2)}, u32[]{:S(2)}) collective-permute-start(bf16[4,128,128]{2,1,0:T(8,128)(2,1)S(1)} %get-tuple-element.232), channel_id=1, source_target_pairs={{0,4},{1,5},{2,6},{3,7},{4,0},{5,1},{6,2},{7,3},{8,12},{9,13},{10,... | collective-permute-start | bytes 393224 | tf_op jit(solution)/shard_map/ppermute | solution.py:46
  95.1 15.1 %collective-permute-start.16 = (bf16[4,128,128]{2,1,0:T(8,128)(2,1)S(1)}, bf16[4,128,128]{2,1,0:T(8,128)(2,1)S(1)}, u32[]{:S(2)}, u32[]{:S(2)}) collective-permute-start(bf16[4,128,128]{2,1,0:T(8,128)(2,1)S(1)} %get-tuple-element.231), channel_id=1, source_target_pairs={{0,2},{1,3},{2,4},{3,5},{4,6},{5,7},{6,0},{7,1},{8,10},{9,11},{10,... | collective-permute-start | bytes 393224 | tf_op jit(solution)/shard_map/ppermute | solution.py:46
  98.7 4.2 %copy-start.13 = (bf16[2,192,768]{2,1,0:T(8,128)(2,1)S(1)}, bf16[2,192,768]{2,1,0:T(8,128)(2,1)}, u32[]{:S(2)}) copy-start(bf16[2,192,768]{2,1,0:T(8,128)(2,1)} %get-tuple-element.154) | copy-start | bytes 1769476
  102.9 14.0 %collective-permute-start.20 = (bf16[2,192,768]{2,1,0:T(8,128)(2,1)S(1)}, bf16[2,192,768]{2,1,0:T(8,128)(2,1)S(1)}, u32[]{:S(2)}, u32[]{:S(2)}) collective-permute-start(bf16[2,192,768]{2,1,0:T(8,128)(2,1)S(1)} %copy-done.13), channel_id=1, source_target_pairs={{0,16},{8,24},{16,0},{24,8},{1,17},{9,25},{17,1},{25,9},{2,18},{10... | collective-permute-start | bytes 1769480 | tf_op jit(solution)/shard_map/ppermute | solution.py:41
  105.9 21.0 %collective-permute-start.22 = (bf16[2,48,1536]{2,1,0:T(8,128)(2,1)}, bf16[2,48,1536]{2,1,0:T(8,128)(2,1)S(1)}, u32[]{:S(2)}, u32[]{:S(2)}) collective-permute-start(bf16[2,48,1536]{2,1,0:T(8,128)(2,1)} %get-tuple-element.162), channel_id=1, source_target_pairs={{0,1},{1,0},{2,3},{3,2},{4,5},{5,4},{6,7},{7,6},{8,9},{9,8},{10,11... | collective-permute-start | bytes 884744 | tf_op jit(solution)/shard_map/ppermute | solution.py:41
  109.2 17.6 %collective-permute-start.23 = (bf16[4,96,384]{2,1,0:T(8,128)(2,1)}, bf16[4,96,384]{2,1,0:T(8,128)(2,1)S(1)}, u32[]{:S(2)}, u32[]{:S(2)}) collective-permute-start(bf16[4,96,384]{2,1,0:T(8,128)(2,1)} %get-tuple-element.165), channel_id=1, source_target_pairs={{0,2},{1,3},{2,0},{3,1},{4,6},{5,7},{6,4},{7,5},{8,10},{9,11},{10,... | collective-permute-start | bytes 884744 | tf_op jit(solution)/shard_map/ppermute | solution.py:41
  116.8 6.6 %collective-permute-start.19 = (bf16[512,128]{1,0:T(8,128)(2,1)}, bf16[512,128]{1,0:T(8,128)(2,1)S(1)}, u32[]{:S(2)}, u32[]{:S(2)}) collective-permute-start(bf16[512,128]{1,0:T(8,128)(2,1)} %get-tuple-element.175), channel_id=1, source_target_pairs={{0,1},{1,0},{2,3},{3,2},{4,5},{5,4},{6,7},{7,6},{8,9},{9,8},{10,11... | collective-permute-start | bytes 393224 | tf_op jit(solution)/shard_map/ppermute | solution.py:41
  120.3 14.9 %collective-permute-start.26 = (bf16[1,192,768]{2,1,0:T(8,128)(2,1)}, bf16[1,192,768]{2,1,0:T(8,128)(2,1)S(1)}, u32[]{:S(2)}, u32[]{:S(2)}) collective-permute-start(bf16[1,192,768]{2,1,0:T(8,128)(2,1)} %get-tuple-element.179), channel_id=1, source_target_pairs={{0,1},{1,0},{2,3},{3,2},{4,5},{5,4},{6,7},{7,6},{8,9},{9,8},{10,11... | collective-permute-start | bytes 884744 | tf_op jit(solution)/shard_map/ppermute | solution.py:41
  125.7 6.5 %collective-permute-start.21 = (bf16[320,128]{1,0:T(8,128)(2,1)}, bf16[320,128]{1,0:T(8,128)(2,1)S(1)}, u32[]{:S(2)}, u32[]{:S(2)}) collective-permute-start(bf16[320,128]{1,0:T(8,128)(2,1)} %get-tuple-element.183), channel_id=1, source_target_pairs={{0,2},{1,3},{2,0},{3,1},{4,6},{5,7},{6,4},{7,5},{8,10},{9,11},{10,... | collective-permute-start | bytes 245768 | tf_op jit(solution)/shard_map/ppermute | solution.py:41
  129.7 13.0 %collective-permute-start.25 = (bf16[2,96,384]{2,1,0:T(8,128)(2,1)}, bf16[2,96,384]{2,1,0:T(8,128)(2,1)S(1)}, u32[]{:S(2)}, u32[]{:S(2)}) collective-permute-start(bf16[2,96,384]{2,1,0:T(8,128)(2,1)} %get-tuple-element.190), channel_id=1, source_target_pairs={{0,4},{1,5},{2,6},{3,7},{4,0},{5,1},{6,2},{7,3},{8,12},{9,13},{10,... | collective-permute-start | bytes 442376 | tf_op jit(solution)/shard_map/ppermute | solution.py:41
  132.8 4.6 %copy-start.1 = (bf16[1,192,768]{2,1,0:T(8,128)(2,1)S(1)}, bf16[1,192,768]{2,1,0:T(8,128)(2,1)}, u32[]{:S(2)}) copy-start(bf16[1,192,768]{2,1,0:T(8,128)(2,1)} %get-tuple-element.197) | copy-start | bytes 884740
  132.9 9.9 %copy-start.4 = (bf16[2,96,384]{2,1,0:T(8,128)(2,1)S(1)}, bf16[2,96,384]{2,1,0:T(8,128)(2,1)}, u32[]{:S(2)}) copy-start(bf16[2,96,384]{2,1,0:T(8,128)(2,1)} %get-tuple-element.199) | copy-start | bytes 442372
  134.5 8.8 %collective-permute-start.24 = (bf16[224,128]{1,0:T(8,128)(2,1)}, bf16[224,128]{1,0:T(8,128)(2,1)S(1)}, u32[]{:S(2)}, u32[]{:S(2)}) collective-permute-start(bf16[224,128]{1,0:T(8,128)(2,1)} %get-tuple-element.194), channel_id=1, source_target_pairs={{0,4},{1,5},{2,6},{3,7},{4,0},{5,1},{6,2},{7,3},{8,12},{9,13},{10,... | collective-permute-start | bytes 172040 | tf_op jit(solution)/shard_map/ppermute | solution.py:41
  135.1 13.0 %collective-permute-start.30 = (bf16[1,48,1536]{2,1,0:T(8,128)(2,1)S(1)}, bf16[1,48,1536]{2,1,0:T(8,128)(2,1)S(1)}, u32[]{:S(2)}, u32[]{:S(2)}) collective-permute-start(bf16[1,48,1536]{2,1,0:T(8,128)(2,1)S(1)} %copy-done.22), channel_id=1, source_target_pairs={{0,4},{1,5},{2,6},{3,7},{4,0},{5,1},{6,2},{7,3},{8,12},{9,13},{10,... | collective-permute-start | bytes 442376 | tf_op jit(solution)/shard_map/ppermute | solution.py:41
  137.5 13.7 %collective-permute-start.33 = (bf16[192,768]{1,0:T(8,128)(2,1)S(1)}, bf16[192,768]{1,0:T(8,128)(2,1)S(1)}, u32[]{:S(2)}, u32[]{:S(2)}) collective-permute-start(bf16[192,768]{1,0:T(8,128)(2,1)S(1)} %fusion), channel_id=1, source_target_pairs={{4,0},{5,1},{6,2},{7,3},{8,12},{9,13},{10,14},{11,15},{20,16},{21,... | collective-permute-start | bytes 884744 | tf_op jit(solution)/shard_map/ppermute | solution.py:57
  142.7 9.6 %collective-permute-start.32 = (bf16[2,96,384]{2,1,0:T(8,128)(2,1)S(1)}, bf16[2,96,384]{2,1,0:T(8,128)(2,1)S(1)}, u32[]{:S(2)}, u32[]{:S(2)}) collective-permute-start(bf16[2,96,384]{2,1,0:T(8,128)(2,1)S(1)} %add_convert_fusion.4), channel_id=1, source_target_pairs={{0,16},{8,24},{16,0},{24,8},{1,17},{9,25},{17,1},{25,9},{2,18},{10... | collective-permute-start | bytes 442376 | tf_op jit(solution)/shard_map/ppermute | solution.py:41
  144.0 4.1 %copy-start.3 = (bf16[1,48,1536]{2,1,0:T(8,128)(2,1)S(1)}, bf16[1,48,1536]{2,1,0:T(8,128)(2,1)}, u32[]{:S(2)}) copy-start(bf16[1,48,1536]{2,1,0:T(8,128)(2,1)} %get-tuple-element.205) | copy-start | bytes 442372
  145.5 12.6 %collective-permute-start.27 = (bf16[224,128]{1,0:T(8,128)(2,1)}, bf16[224,128]{1,0:T(8,128)(2,1)S(1)}, u32[]{:S(2)}, u32[]{:S(2)}) collective-permute-start(bf16[224,128]{1,0:T(8,128)(2,1)} %message_step.5.refs_0_), channel_id=1, source_target_pairs={{0,8},{8,0},{16,24},{24,16},{1,9},{9,1},{17,25},{25,17},{2,10},{10... | collective-permute-start | bytes 172040 | tf_op jit(solution)/shard_map/ppermute | solution.py:41
  145.5 13.2 %collective-permute-start.28 = (bf16[224,128]{1,0:T(8,128)(2,1)}, bf16[224,128]{1,0:T(8,128)(2,1)S(1)}, u32[]{:S(2)}, u32[]{:S(2)}) collective-permute-start(bf16[224,128]{1,0:T(8,128)(2,1)} %message_step.5.refs_0_), channel_id=1, source_target_pairs={{0,16},{8,24},{16,0},{24,8},{1,17},{9,25},{17,1},{25,9},{2,18},{10... | collective-permute-start | bytes 172040 | tf_op jit(solution)/shard_map/ppermute | solution.py:41
  148.1 10.6 %collective-permute-start.29 = (bf16[224,128]{1,0:T(8,128)(2,1)}, bf16[224,128]{1,0:T(8,128)(2,1)S(1)}, u32[]{:S(2)}, u32[]{:S(2)}) collective-permute-start(bf16[224,128]{1,0:T(8,128)(2,1)} %message_step.5.refs_0_), channel_id=1, source_target_pairs={{0,24},{8,16},{16,8},{24,0},{1,25},{9,17},{17,9},{25,1},{2,26},{10... | collective-permute-start | bytes 172040 | tf_op jit(solution)/shard_map/ppermute | solution.py:41
  151.2 6.8 %collective-permute-start.31 = (bf16[48,1536]{1,0:T(8,128)(2,1)S(1)}, bf16[48,1536]{1,0:T(8,128)(2,1)S(1)}, u32[]{:S(2)}, u32[]{:S(2)}) collective-permute-start(bf16[48,1536]{1,0:T(8,128)(2,1)S(1)} %fusion.1), channel_id=1, source_target_pairs={{0,16},{8,24},{16,0},{24,8},{1,17},{9,25},{17,1},{25,9},{2,18},{10... | collective-permute-start | bytes 442376 | tf_op jit(solution)/shard_map/ppermute | solution.py:41
  152.3 10.4 %collective-permute-start.35 = (bf16[192,768]{1,0:T(8,128)(2,1)S(1)}, bf16[192,768]{1,0:T(8,128)(2,1)S(1)}, u32[]{:S(2)}, u32[]{:S(2)}) collective-permute-start(bf16[192,768]{1,0:T(8,128)(2,1)S(1)} %add_convert_fusion), channel_id=1, source_target_pairs={{0,16},{8,24},{16,0},{24,8},{1,17},{9,25},{17,1},{25,9},{2,18},{10... | collective-permute-start | bytes 884744 | tf_op jit(solution)/shard_map/ppermute | solution.py:41
  158.0 4.9 %collective-permute-start.34 = (bf16[2,96,384]{2,1,0:T(8,128)(2,1)S(1)}, bf16[2,96,384]{2,1,0:T(8,128)(2,1)S(1)}, u32[]{:S(2)}, u32[]{:S(2)}) collective-permute-start(bf16[2,96,384]{2,1,0:T(8,128)(2,1)S(1)} %add_convert_fusion.2), channel_id=1, source_target_pairs={{0,8},{8,0},{16,24},{24,16},{1,9},{9,1},{17,25},{25,17},{2,10},{10... | collective-permute-start | bytes 442376 | tf_op jit(solution)/shard_map/ppermute | solution.py:41
  158.1 6.5 %collective-permute-start.36 = (bf16[96,1536]{1,0:T(8,128)(2,1)S(1)}, bf16[96,1536]{1,0:T(8,128)(2,1)S(1)}, u32[]{:S(2)}, u32[]{:S(2)}) collective-permute-start(bf16[96,1536]{1,0:T(8,128)(2,1)S(1)} %pad_maximum_fusion.2), channel_id=1, source_target_pairs={{0,8},{8,0},{16,24},{24,16},{1,9},{9,1},{17,25},{25,17},{2,10},{10... | collective-permute-start | bytes 884744 | tf_op jit(solution)/shard_map/ppermute | solution.py:41
  162.9 2.9 %collective-permute-start.37 = (bf16[384,768]{1,0:T(8,128)(2,1)S(1)}, bf16[384,768]{1,0:T(8,128)(2,1)S(1)}, u32[]{:S(2)}, u32[]{:S(2)}) collective-permute-start(bf16[384,768]{1,0:T(8,128)(2,1)S(1)} %pad_maximum_fusion), channel_id=1, source_target_pairs={{0,8},{8,0},{16,24},{24,16},{1,9},{9,1},{17,25},{25,17},{2,10},{10... | collective-permute-start | bytes 1769480 | tf_op jit(solution)/shard_map/ppermute | solution.py:41
  (22 other events, 22.0 us)

commit v4 on v3

--- a/solution.py
+++ b/solution.py
@@ -122,7 +122,7 @@
     return ref[...].reshape(1, -1)
 
 
-def add_split(place, items):
+def add_split(place, items, share=1.2):
     def kernel(place_ref, *refs):
         sources, results = refs[: 2 * len(items)], refs[2 * len(items) :]
         for n, (_, _, which) in enumerate(items):
@@ -142,9 +142,88 @@
         out_specs=[VMEM] * len(shapes),
         out_shape=shapes,
         compiler_params=params(),
-        cost_estimate=cost(1.2),
+        cost_estimate=cost(share),
         name="add_split",
     )(place, *arrays)
+
+
+def exchange_split(place, mine1, come1, mine2, come2):
+    def kernel(place_ref, a1, b1, a2, b2, theirs, keep1, keep2):
+        y = place_ref[2]
+        row = 0
+        for a, b, keep in ((a1, b1, keep1), (a2, b2, keep2)):
+            m, _, r, c = a.shape
+            part = a[:, pl.ds(1 - y, 1)].astype(F32) + b[:, pl.ds(1 - y, 1)].astype(F32)
+            part = part.reshape(m * r, c).astype(BF16)
+            for at in range(0, c, D // 2):
+                theirs[row : row + m * r] = part[:, at : at + D // 2]
+                row += m * r
+            part = a[:, pl.ds(y, 1)].astype(F32) + b[:, pl.ds(y, 1)].astype(F32)
+            keep[...] = part.reshape(m, r, c).astype(BF16)
+
+    shapes = [(a.shape[0],) + a.shape[2:] for a in (mine1, mine2)]
+    size = sum(math.prod(s) for s in shapes)
+    return pl.pallas_call(
+        kernel,
+        in_specs=[SMEM] + [VMEM] * 4,
+        out_specs=[VMEM] * 3,
+        out_shape=[SHAPE((size // (D // 2), D // 2), BF16)] + [SHAPE(s, BF16) for s in shapes],
+        compiler_params=params(),
+        cost_estimate=cost(1.2),
+        name="exchange_split",
+    )(place, mine1, come1, mine2, come2)
+
+
+def exchange_add(place, mine1, mine2, come, bit):
+    def kernel(place_ref, a1, a2, b, theirs, keep, total):
+        row = 0
+        parts = []
+        for a in (a1, a2):
+            m, r, c = a.shape
+            columns = []
+            for _ in range(0, c, D // 2):
+                columns.append(b[row : row + m * r])
+                row += m * r
+            parts.append(jnp.concatenate(columns, axis=1).astype(F32).reshape(m, r, c))
+        own = (place_ref[3] >> bit) & 1
+        total[...] = (a2[...].astype(F32) + parts[1]).astype(BF16)
+        both = (a1[...].astype(F32) + parts[0]).astype(BF16)
+        m, r, c = a1.shape
+        both = both.reshape(m // 2, 2, r, c)
+        lower, upper = both[:, 0], both[:, 1]
+        theirs[...] = jnp.where(own == 0, upper, lower)
+        keep[...] = jnp.where(own == 0, lower, upper)
+
+    half = SHAPE((mine1.shape[0] // 2,) + mine1.shape[1:], BF16)
+    return pl.pallas_call(
+        kernel,
+        in_specs=[SMEM] + [VMEM] * 3,
+        out_specs=[VMEM] * 3,
+        out_shape=[half, half, SHAPE(mine2.shape, BF16)],
+        compiler_params=params(),
+        cost_estimate=cost(0.01),
+        name="exchange_add",
+    )(place, mine1, mine2, come)
+
+
+def add_cut(place, a, b):
+    parts = a.shape[1]
+
+    def kernel(place_ref, a_ref, b_ref, *results):
+        for i in range(parts):
+            at = place_ref[3] ^ i
+            for k in range(a.shape[0]):
+                results[i][k] = (a_ref[k, at].astype(F32) + b_ref[k, at].astype(F32)).astype(BF16)
+
+    return pl.pallas_call(
+        kernel,
+        in_specs=[SMEM, VMEM, VMEM],
+        out_specs=[VMEM] * parts,
+        out_shape=[SHAPE((a.shape[0],) + a.shape[2:], BF16)] * parts,
+        compiler_params=params(),
+        cost_estimate=cost(1.2),
+        name="add_cut",
+    )(place, a, b)
 
 
 def keys_kernel(copies, x_ref, gain_ref, bias_ref, weight_ref, add_ref, tables_ref, kv_ref, first_ref):
@@ -231,9 +310,8 @@
     w2_ref,
     wo_ref,
     mlp_ref,
-    mlp2_ref,
     back_ref,
-    back2_ref,
+    other_ref,
     attn_grad_ref,
     b1_grad_ref,
     theirs1_ref,
@@ -291,10 +369,10 @@
 
     @pl.when(step == steps - 1)
     def _():
-        for scr, last, own_ref, other_ref in ((mlp_scr, mlp, mlp_ref, mlp2_ref), (back_scr, back, back_ref, back2_ref)):
+        for i, (scr, last, own_ref) in enumerate(((mlp_scr, mlp, mlp_ref), (back_scr, back, back_ref))):
             total = (scr[...] + last).astype(BF16)
             own_ref[...] = total[:rows]
-            other_ref[...] = total[rows:]
+            other_ref[i] = total[rows:]
 
 
 CHUNK = 512
@@ -337,7 +415,12 @@
             pl.BlockSpec((chunk, D), lambda i, place: (at(i, place), 0)),
             whole(wo),
         ],
-        out_specs=[fixed(rows, D)] * 5
+        out_specs=[
+            fixed(rows, D),
+            fixed(rows, D),
+            pl.BlockSpec((2, rows, D), lambda i, place: (0, 0, 0)),
+            fixed(rows, D),
+        ]
         + [pl.BlockSpec((1, chunk), lambda i, place: (0, piece(i, place))), cut, cut]
         + grad_specs,
         scratch_shapes=[
@@ -351,19 +434,19 @@
     result = pl.pallas_call(
         feed_kernel,
         grid_spec=spec,
-        out_shape=[SHAPE((rows, D), BF16)] * 5
+        out_shape=[SHAPE((rows, D), BF16), SHAPE((rows, D), BF16), SHAPE((2, rows, D), BF16), SHAPE((rows, D), BF16)]
         + [SHAPE((1, half), F32), SHAPE((count, per, half), BF16), SHAPE((count, per, half), BF16)]
         + grad_shapes,
         compiler_params=params(),
         cost_estimate=cost(12),
         name="feed_forward",
     )(place, x, xx, g, gg, gain, bias, w1, b1, w2, wo)
-    grads = result[8:]
+    grads = result[7:]
     if not aligned:
         cut = grads[0].reshape(pieces // 2, 2, -1, D)
         low = place[3] & 1
         grads = [take(cut, 1 - low, 1), take(cut, low, 1)]
-    return result[:8], grads
+    return result[:7], grads
 
 
 def present(slot, y, z):
@@ -372,7 +455,8 @@
 
 
 def whole_kernel(span, depth, place_ref, *refs):
-    pair_refs, (q_ref, do_ref, tables_ref, out_ref, dq_ref, even_out_ref, odd_out_ref) = refs[:depth], refs[depth:]
+    pair_refs, (q_ref, do_ref, tables_ref, rows_ref, even_out_ref, odd_out_ref) = refs[:depth], refs[depth:]
+    out_ref, dq_ref = rows_ref.at[0], rows_ref.at[1]
     y, z = place_ref[2], place_ref[3]
     tables = [tables_ref[i] for i in range(3)]
     rows = PAIRS * span
@@ -432,8 +516,9 @@
 def loop_kernel(groups, span, block, count, place_ref, *refs):
     depth = count // 2
     pair_refs, refs = refs[:depth], refs[depth:]
-    q_ref, do_ref, tables_ref, out_ref, dq_ref, even_out_ref, odd_out_ref = refs[:7]
-    kv_scr, e_ref, kv_t_ref, max_ref, acc_ref, ext_ref = refs[7:]
+    q_ref, do_ref, tables_ref, rows_ref, even_out_ref, odd_out_ref = refs[:6]
+    out_ref, dq_ref = rows_ref.at[0], rows_ref.at[1]
+    kv_scr, e_ref, kv_t_ref, max_ref, acc_ref, ext_ref = refs[6:]
     tables = [tables_ref[i] for i in range(3)]
     rows = groups * span
     per = block // span
@@ -608,8 +693,8 @@
         kernel,
         grid=(seqs, PAIRS // groups),
         in_specs=[SMEM] + [two] * depth + [wide_spec, wide_spec, pl.BlockSpec(tables.shape, lambda s, i: (0, 0, 0))],
-        out_specs=[wide_spec] * 2 + [pieces] * 2,
-        out_shape=[SHAPE((seqs, span, D), BF16), SHAPE((seqs, span, D), BF16)]
+        out_specs=[pl.BlockSpec((2, None, span, groups * 128), lambda s, i: (0, s, 0, i))] + [pieces] * 2,
+        out_shape=[SHAPE((2, seqs, span, D), BF16)]
         + [SHAPE((depth, seqs, span, 128), BF16)] * 2,
         scratch_shapes=scratch,
         compiler_params=params(),
@@ -641,18 +726,20 @@
         products(both(in_ref, in2_ref), both(q_ref, q2_ref), 0)
 
 
-def weights(place, count, attn, attn2, g, g2, first_in, first_in2, grad, grad2):
-    rows = attn.shape[0]
+def weights(place, count, both, both2, g, g2, first_in, first_in2):
+    rows = g.shape[0]
     depth, per, half = count // 2, D // count, D // 2
     whole = pl.BlockSpec((rows, D), lambda i, place: (0, 0), pipeline_mode=pl.Buffered(1))
     part = pl.BlockSpec((rows, half), lambda i, place: (0, place[0]), pipeline_mode=pl.Buffered(1))
+    attn_part = pl.BlockSpec((None, rows, D), lambda i, place: (0, 0, 0), pipeline_mode=pl.Buffered(1))
+    q_part = pl.BlockSpec((None, rows, half), lambda i, place: (1, 0, place[0]), pipeline_mode=pl.Buffered(1))
     result = pl.BlockSpec((1, depth, per, half), lambda i, place: (i, 0, 0, 0))
     return pl.pallas_call(
         weights_kernel,
         grid_spec=pltpu.PrefetchScalarGridSpec(
             num_scalar_prefetch=1,
             grid=(2,),
-            in_specs=[whole, whole, part, part, whole, whole, part, part],
+            in_specs=[attn_part, attn_part, part, part, whole, whole, q_part, q_part],
             out_specs=[result, result, pl.BlockSpec((8, D), lambda i, place: (0, 0))],
             scratch_shapes=[pltpu.VMEM((depth, 2, per, half), F32)],
         ),
@@ -660,7 +747,7 @@
         compiler_params=params(),
         cost_estimate=cost(2.4),
         name="weights",
-    )(place, attn, attn2, g, g2, first_in, first_in2, grad, grad2)
+    )(place, both, both2, g, g2, first_in, first_in2, both, both2)
 
 
 def mix_kernel(x_ref, mlp_ref, mlp2_ref, attn_ref, add_ref, wo_ref, output_ref):
@@ -669,19 +756,20 @@
     output_ref[...] = (x + (mlp + dot(attn_ref[...], wo_ref[...])) + wide(add_ref)).astype(BF16)
 
 
-def mix(x, mlp, mlp2, attn, add, wo):
+def mix(x, mlp, other, both, add, wo):
     rows = x.shape[0]
     row = pl.BlockSpec((rows // 2, D), lambda i: (i, 0))
+    first = pl.BlockSpec((None, rows // 2, D), lambda i: (0, i, 0))
     return pl.pallas_call(
         mix_kernel,
         grid=(2,),
-        in_specs=[row] * 4 + [pl.BlockSpec((D,), lambda i: (0,)), pl.BlockSpec((D, D), lambda i: (0, 0))],
+        in_specs=[row, row, first, first, pl.BlockSpec((D,), lambda i: (0,)), pl.BlockSpec((D, D), lambda i: (0, 0))],
         out_specs=row,
         out_shape=SHAPE((rows, D), BF16),
         compiler_params=params(),
         cost_estimate=cost(1.2),
         name="mix",
-    )(x, mlp, mlp2, attn, add, wo)
+    )(x, mlp, other, both, add, wo)
 
 
 def two_terms(values):
@@ -739,10 +827,9 @@
     for i in range(b1_lines):
         vector_scr[pl.ds(place_ref[0] * b1_lines + i, 1)] = b1[:, i * 128 : (i + 1) * 128]
     at = 2 * b1_lines
-    sums = [early_ref[0:1], early_ref[1:2]]
+    sums = [early_ref[0:1], jnp.sum(grad.astype(F32), axis=0, keepdims=True), early_ref[1:2]]
     for rows in (first_grad * normed, first_grad, second_grad * normed, second_grad):
         sums.append(jnp.sum(rows, axis=0, keepdims=True))
-    sums.append(jnp.sum(grad.astype(F32), axis=0, keepdims=True))
     for row in sums:
         for i in range(row.shape[1] // 128):
             vector_scr[at : at + 1] = row[:, i * 128 : (i + 1) * 128]
@@ -761,15 +848,21 @@
     tokens_ref[...] = (g_ref[...].astype(F32) + inverse * (normed_grad - mean - normed * along_rows)).astype(BF16)
 
 
-def finish(place, places, ff, kv_parts, extra, x, g, q_rows, back, back2, gain, bias, gain2, wqkv, tables, b1, early):
+def finish(place, places, ff, kv_parts, extra, x, g, both, back, other, gain, bias, gain2, wqkv, tables, b1, early):
     rows = x.shape[0]
     lines = message_lines(ff)
     whole = lambda a: pl.BlockSpec(a.shape, lambda i: (0,) * a.ndim)
-    arrays = (*kv_parts, extra, x, g, q_rows, back, back2, gain, bias, gain2, wqkv, tables, b1, early)
+    second = pl.BlockSpec((None, rows, D), lambda i: (1, 0, 0))
+    before, between, behind = (*kv_parts, extra, x, g), (back,), (gain, bias, gain2, wqkv, tables, b1, early)
     return pl.pallas_call(
         functools.partial(finish_kernel, rows // tables.shape[1], len(kv_parts), lines),
         grid=(1,),
-        in_specs=[SMEM] + [whole(a) for a in arrays],
+        in_specs=[SMEM]
+        + [whole(a) for a in before]
+        + [second]
+        + [whole(a) for a in between]
+        + [second]
+        + [whole(a) for a in behind],
         out_specs=[
             pl.BlockSpec((rows, D), lambda i: (0, 0)),
             pl.BlockSpec((2 * lines + D // 2, 128), lambda i: (0, 0)),
@@ -780,38 +873,51 @@
         compiler_params=params(),
         cost_estimate=cost(2.4),
         name="finish",
-    )(place, *arrays)
-
-
-def message_step(place, mine, come, lines, per, bit):
+    )(place, *before, both, *between, other, *behind)
+
+
+def message_cut(place, mine, come, lines, per):
     count = (mine.shape[0] - 2 * lines) // per
-    last = count == 1
 
     def kernel(place_ref, a_ref, b_ref, *refs):
-        vector = tree_sum([ref[at : at + lines] for ref in (a_ref, b_ref) for at in (0, lines)])
-        high, rest = two_terms(vector)
-        weight = a_ref[2 * lines :].astype(F32) + b_ref[2 * lines :].astype(F32)
-        own = (place_ref[3] >> bit) & 1
-        if not last:
-            refs[-1][...] = weight.reshape(count // 2, 2, per, 128)
-        for result, at in zip(refs[: 1 if last else 2], (1 - own, own)):
+        results, scr = refs[:-1], refs[-1]
+        high, rest = two_terms(tree_sum([ref[at : at + lines] for ref in (a_ref, b_ref) for at in (0, lines)]))
+        scr[...] = (a_ref[2 * lines :].astype(F32) + b_ref[2 * lines :].astype(F32)).reshape(scr.shape)
+        for i, result in enumerate(results):
             result[:lines] = high
             result[lines : 2 * lines] = rest
-            rows = weight if last else refs[-1][:, pl.ds(at, 1)].reshape(-1, 128)
-            result[2 * lines :] = rows.astype(BF16)
-
-    results = 1 if last else 2
-    scratch = [] if last else [pltpu.VMEM((count // 2, 2, per, 128), F32)]
+            result[2 * lines :] = scr[place_ref[3] ^ i].astype(BF16)
+
     return pl.pallas_call(
         kernel,
         in_specs=[SMEM, VMEM, VMEM],
-        out_specs=[VMEM] * results,
-        out_shape=[SHAPE((2 * lines + count * per // results, 128), BF16)] * results,
-        scratch_shapes=scratch,
+        out_specs=[VMEM] * count,
+        out_shape=[SHAPE((2 * lines + per, 128), BF16)] * count,
+        scratch_shapes=[pltpu.VMEM((count, per, 128), F32)],
         compiler_params=params(),
         cost_estimate=cost(0.6),
-        name="message_step",
+        name="message_cut",
     )(place, mine, come)
+
+
+def message_sum(messages, lines):
+    def kernel(*refs):
+        result = refs[-1]
+        total = tree_sum([ref[...] for ref in refs[:-1]])
+        high, rest = two_terms(total[:lines] + total[lines : 2 * lines])
+        result[:lines] = high
+        result[lines : 2 * lines] = rest
+        result[2 * lines :] = total[2 * lines :].astype(BF16)
+
+    return pl.pallas_call(
+        kernel,
+        in_specs=[VMEM] * len(messages),
+        out_specs=VMEM,
+        out_shape=SHAPE(messages[0].shape, BF16),
+        compiler_params=params(),
+        cost_estimate=cost(0.6),
+        name="message_sum",
+    )(*messages)
 
 
 def last_sums(messages, lines, widths):
@@ -897,118 +1003,105 @@
     pairs = [two] + [along(two, k) for k in range(1, depth)]
 
     x_fed, g_fed, first_other = after((x, g, first_other), two)
-    (mlp, mlp_other, back, back_other, attn_grad, b1_grad, theirs1, mine1), (theirs2, mine2) = feed(
+    (mlp, back, feed_other, attn_grad, b1_grad, theirs1, mine1), (theirs2, mine2) = feed(
         place, count, *after((x_fed, x_other, g_fed, g_other), first_other), ln2_gain, ln2_bias, fc1_weight, fc1_bias.reshape(1, -1),
         fc2_weight, out_weight,
     )
     come1 = over_x(theirs1)
     come2 = over_z(theirs2, 0)
-    mlp_come, back_come = over_core(mlp_other), over_core(back_other)
+    feed_come = over_core(feed_other)
 
     q3, do3 = q.reshape(seqs, span, D), attn_grad.reshape(seqs, span, D)
-    out, q_rows, even, odd = attention(place, pairs, q3, do3, tables)
+    both, even, odd = attention(place, pairs, q3, do3, tables)
     odd = over_y(odd)
 
     def halved(a, parts, height):
         return a.reshape(parts, 2, height, a.shape[-1])
 
-    out, q_rows = flat(out), flat(q_rows)
-    out_other, q_other = over_core(out), over_core(q_rows)
-    mine1, come1, come2, mlp_come, back_come = after((mine1, come1, come2, mlp_come, back_come), out)
-    view = lambda v: halved(v, depth // 2, per1)
-    theirs1, mine1 = add_split(place, [(view(mine1), view(come1), 3)])
-    come1 = over_z(theirs1, 0)
-
-    out_other, q_other = after((out_other, q_other), theirs1)
-    theirs3, mine3, early = weights(place, count, out, out_other, g, g_other, first_in, first_other, q_rows, q_other)
+    both = both.reshape(2, rows, D)
+    both_other = over_core(both)
+    mine1, come1, mine2, come2, feed_come = after((mine1, come1, mine2, come2, feed_come), both)
+    height = per2 // 2
+    view1 = lambda v: halved(v, depth // 2, per1)
+    view2 = lambda v: halved(v, half_depth, height)
+    theirs1, mine1, theirs2, mine2 = add_split(
+        place, [(view1(mine1), view1(come1), 3), (view2(mine2), view2(come2), 1)], 6
+    )
+    come1, come2 = over_z(theirs1, 0), over_x(theirs2)
+
+    (both_other,) = after((both_other,), theirs1)
+    theirs3, mine3, early = weights(place, count, both, both_other, g, g_other, first_in, first_other)
     come3 = over_y(theirs3)
 
     even, odd = after((even, odd), theirs3)
     kv_sums = [summed(even[k], odd[k]) for k in range(depth)]
-    got = [along(kv_sums[k], -k) for k in range(1, depth)]
-
-    mine2, come2 = after((mine2, come2), *kv_sums)
-    height = per2 // 2
-    view = lambda v: halved(v, half_depth, height)
-    theirs2, mine2 = add_split(place, [(view(mine2), view(come2), 1)])
-    come2 = over_x(theirs2)
-
-    (x_mix,) = after((x,), theirs2)
-    output = mix(x_mix, mlp, mlp_come, out, out_bias, out_weight)
-
-    mine1, come1 = after((mine1, come1), output)
-    view = lambda v: halved(v, depth // 2, per1 // 2)
-    theirs1, mine1 = add_split(place, [(view(mine1), view(come1), 2)])
-    come1 = over_y(theirs1)
-    mine3, come3 = after((mine3, come3), theirs1)
-    view3 = lambda v: halved(v, depth, per1)
-    theirs3, mine3 = add_split(place, [(view3(mine3), view3(come3), 3)])
-    come3 = over_z(theirs3, 0)
-
-    got = after(got, theirs3)
+    (x_mix,) = after((x,), *kv_sums)
+    output = mix(x_mix, mlp, feed_come, both, out_bias, out_weight)
+    (kv_next,) = after((kv_sums[1],), output)
+    got = [along(kv_next, -1)] + [along(kv_sums[k], -k) for k in range(2, depth)]
+
+    mine1, come1, mine2, come2 = after((mine1, come1, mine2, come2), output)
+    view1 = lambda v: halved(v, depth // 2, per1 // 2)
+    view2 = lambda v: halved(v, half_depth // 2, height)
+    theirs12, mine1, mine2 = exchange_split(place, view1(mine1), view1(come1), view2(mine2), view2(come2))
+    come12 = over_y(theirs12)
+    mine3, come3 = after((mine3, come3), theirs12)
+    parts3 = add_cut(place, mine3, come3)
+    come3 = [flipped(parts3[i], "seq", 2 * i) for i in range(1, depth)]
+
+    got = after(got, parts3[0])
     lines = message_lines(ff)
     tokens_grad, theirs4, mine4 = finish(
-        place, count, ff, [flat(v) for v in (kv_sums[0], *got)], flat(key_value_grad), x, g, q_rows, back, back_come,
+        place, count, ff, [flat(v) for v in (kv_sums[0], *got)], flat(key_value_grad), x, g, both, back, feed_come,
         ln1_gain, ln1_bias, ln2_gain, qkv_weight, tables, b1_grad, early,
     )
     come4 = over_y(theirs4)
 
-    mine2, come2 = after((mine2, come2), tokens_grad)
-    view = lambda v: halved(v, half_depth // 2, height)
-    theirs2, mine2 = add_split(place, [(view(mine2), view(come2), 2)])
-    come2 = over_y(theirs2)
-    mine4, come4 = after((mine4, come4), theirs2)
-    theirs4, mine4 = message_step(place, mine4, come4, lines, per1, 0)
-    come4 = over_z(theirs4, 0)
-    mine1, come1, mine3, come3 = after((mine1, come1, mine3, come3), theirs4)
-    for bit in range(1, z_bits):
-        parts = depth >> (bit + 1)
-        view3 = lambda v: halved(v, 2 * parts, per1)
-        view1 = lambda v: halved(v, parts, per1 // 2)
-        theirs3, mine3, theirs1, mine1 = add_split(
-            place, [(view3(mine3), view3(come3), 3 + bit), (view1(mine1), view1(come1), 3 + bit)]
-        )
-        come3, come1 = over_z(theirs3, bit), over_z(theirs1, bit)
-    mine4, come4 = after((mine4, come4), theirs3)
-    for bit in range(1, z_bits):
-        theirs4, mine4 = message_step(place, mine4, come4, lines, per1, bit)
-        come4 = over_z(theirs4, bit)
-    mine2, come2 = after((mine2, come2), theirs4)
+    mine1, mine2, come12 = after((mine1, mine2, come12), tokens_grad)
+    theirs1, mine1, sum2 = exchange_add(place, mine1, mine2, come12, 1)
+    come1 = over_z(theirs1, 1)
+    for bit in range(2, z_bits):
+        view1 = lambda v: halved(v, depth >> (bit + 1), per1 // 2)
+        theirs1, mine1 = add_split(place, [(view1(mine1), view1(come1), 3 + bit)], 0.01)
+        come1 = over_z(theirs1, bit)
     for bit in range(1, z_bits - 1):
-        view = lambda v: halved(v, half_depth >> (bit + 1), height)
-        theirs2, mine2 = add_split(place, [(view(mine2), view(come2), 3 + bit)])
-        come2 = over_z(theirs2, bit)
-    sum2 = summed(mine2, come2).reshape(height, D)
+        sum2 = halved(sum2, half_depth >> (bit + 1), height)
+        own_bit = (z >> bit) & 1
+        sum2 = summed(take(sum2, own_bit, 1), over_z(take(sum2, 1 - own_bit, 1), bit))
+    sum2 = sum2.reshape(height, D)
     come2 = to_owner(sum2)
 
-    mine3, come3 = after((mine3, come3), sum2)
-    sum3 = summed(mine3, come3)
+    come3 = after(come3, theirs1, sum2)
+    sum3 = summed(parts3[0], *come3)
     other3 = over_x(sum3)
     mine4, come4 = after((mine4, come4), sum3)
-    (message,) = message_step(place, mine4, come4, lines, per1, 0)
-    got = [flipped(message, "batch", i) for i in range(1, batches)]
-    mine1, come1 = after((mine1, come1), message)
+    parts4 = message_cut(place, mine4, come4, lines, per1)
+    come4 = [flipped(parts4[i], "seq", 2 * i) for i in range(1, depth)]
+    mine1, come1 = after((mine1, come1), parts4[0])
     sum1 = summed(mine1, come1).reshape(per1 // 2, -1)
     other1 = over_x(sum1)
-    sum2, come2 = after((sum2, come2), sum1)
+    sum3, other3 = after((sum3, other3), sum1)
+    sum3 = summed(sum3, other3)
+    other3 = over_core(sum3)
+    sum2, come2 = after((sum2, come2), sum3)
     sum2 = summed(sum2, come2)
     other2 = over_x(sum2)
-
-    sum3, other3 = after((sum3, other3), sum2)
-    sum3 = summed(sum3, other3)
-    other3 = over_core(sum3)
-    sum1, other1 = after((sum1, other1), sum3)
+    come4 = after(come4, sum2)
+    message = message_sum([parts4[0], *come4], lines)
+    got = [flipped(message, "batch", i) for i in range(1, batches)]
+    sum1, other1 = after((sum1, other1), message)
+
     sum1 = pair(sum1, other1, xs, 0)
     other1 = over_core(sum1)
-    got = after(got, sum1)
-    widths = (ff,) + (D,) * 6 + (128,)
-    b1_sum, q_sum, out_sum, gain1, bias1, gain2, bias2, kv_bias, kv_sum = last_sums([message, *got], lines, widths)
-
-    owner = (z >> (z_bits - 1)) == core
-    sum2, other2 = after((sum2, other2), kv_sum)
+    sum2, other2 = after((sum2, other2), sum1)
     sum2 = pair(sum2, other2, xs, 0)
     other2 = over_core(sum2)
-    (other3,) = after((other3,), sum2)
+    got = after(got, sum2)
+    widths = (ff, D + 128) + (D,) * 5
+    b1_sum, qkv_sum, out_sum, gain1, bias1, gain2, bias2, kv_sum = last_sums([message, *got], lines, widths)
+
+    owner = (z >> (z_bits - 1)) == core
+    (other3,) = after((other3,), kv_sum)
     both3 = pair(sum3, other3, core, 2).astype(F32)
     (other1,) = after((other1,), both3)
     fc1_grad = pair(sum1, other1, core, 1).astype(F32)
@@ -1021,7 +1114,7 @@
         gain1,
         bias1,
         jnp.concatenate([both3[1], kv_sum], axis=1),
-        jnp.concatenate([q_sum, kv_bias]),
+        qkv_sum,
         both3[0],
         gain2,
         bias2,

time: 168 us -> 160 us (0.952)
  waiting for transfers between devices: 17.8 us -> 7.92 us
  starting transfers between devices: 35.4 us -> 42.9 us
  Pallas kernels: 97.3 us -> 92.4 us
    pallas_call x6 -> x1, Pallas kernels: 14.4 us -> 4.2 us  [add_split(): pl.pallas_call(kernel, in_specs=[SMEM] + [VMEM] * len(arrays), out_specs=...]
    ppermute x31 -> x30, waiting for transfers between devices: 14.7 us -> 7.3 us  [flipped(): lax.ppermute(block, axis, [(i, i ^ bits) for i in range(lax.axis_size(axi...]
    pallas_call x4 -> x6, Pallas kernels: 8.84 us -> 14 us  [the longest x1 3.67 us: mix(): pl.pallas_call(mix_kernel, grid=(2,), in_specs=[row, row, first, first, p...]
    ppermute x31 -> x30, starting transfers between devices: 27.4 us -> 32 us  [flipped(): lax.ppermute(block, axis, [(i, i ^ bits) for i in range(lax.axis_size(axi...]
    ppermute x6, starting transfers between devices: 6.69 us -> 9.58 us  [along(): lax.ppermute(block, 'seq', [(i, (i + 2 * distance) % size) for i in range...]
    ppermute x1, waiting for transfers between devices: 3.11 us -> 0.6 us  [to_owner(): return lax.ppermute(block, ('batch', 'seq'), route)]
    unnamed x64 -> x62, local copies, waits for them, and re-layouts: 7.54 us -> 8.27 us
  transfers between devices with their start and end apart: 38 -> 37, of which waited for: 8 -> 5; matrix products, arithmetic and copies ran while one was open for 4% -> 4% of each run, Pallas kernels for 58% -> 58%
where the time goes in v4:
time: 160 us; the launch traced here: 159 us
  Pallas kernels  92.4 us (58%)
  starting transfers between devices  42.9 us (27%)
  local copies, waits for them, and re-layouts  9.03 us (6%)
  waiting for transfers between devices  7.92 us (5%)
  other arithmetic  6 us (4%)
    ppermute x30, starting transfers between devices, flipped(): lax.ppermute(block, axis, [(i, i ^ bits) for i in range(lax.axis_size(axi...  32 us
    pallas_call x1, Pallas kernels, feed(): pl.pallas_call(feed_kernel, grid_spec=spec, out_shape=[SHAPE((rows, D), B...  28.6 us
    pallas_call x1, Pallas kernels, attention(): pl.pallas_call(kernel, grid=(seqs, PAIRS // groups), in_specs=[SMEM] + [t...  24.9 us
    ppermute x6, starting transfers between devices, along(): lax.ppermute(block, 'seq', [(i, (i + 2 * distance) % size) for i in range...  9.58 us
    unnamed x62, local copies, waits for them, and re-layouts  8.27 us
    ppermute x30, waiting for transfers between devices, flipped(): lax.ppermute(block, axis, [(i, i ^ bits) for i in range(lax.axis_size(axi...  7.3 us
    pallas_call x1, Pallas kernels, weights(): pl.pallas_call(weights_kernel, grid_spec=pltpu.PrefetchScalarGridSpec(num...  6.11 us
    pallas_call x1, Pallas kernels, finish(): pl.pallas_call(functools.partial(finish_kernel, rows // tables.shape[1],...  5.96 us
  transfers between devices with their start and end apart: 37, of which 5 were waited for; matrix products, arithmetic and copies ran while one was open for 4% of the time, Pallas kernels for 58%

profile of v4, /device:TPU:0, one launch (start us, length us, event | category | flops | bytes accessed | tf_op | source)
XLA Modules:
  0.0 159.2 jit_solution(10926087082966026246)
XLA Ops:
  2.2 2.9 %project_keys.1 = (bf16[512,128]{1,0:T(8,128)(2,1)}, bf16[512,768]{1,0:T(8,128)(2,1)}) custom-call(bf16[512,768]{1,0:T(8,128)(2,1)} %bitcast.56, f32[768]{0:T(1024)} %refs_10_.1, f32[768]{0:T(1024)} %refs_11_.1, bf16[768,896]{1,0:T(8,128)(2,1)} %refs_13_.1, f32[896]{0:T(1024)} %add_ref.4, f32[3,128,128]{2,1,0:T(8,128)} %pad_maximum_fusion.4.tables_ref.refs_6_.refs_14_), custom_call_target="tpu_custom_call" | custom-call | flops 3000000000 | tf_op jit(solution)/shard_map/project_keys/pallas_call | solution.py:250
  5.1 2.5 %collective-permute-start = (bf16[4,128,128]{2,1,0:T(8,128)(2,1)}, bf16[4,128,128]{2,1,0:T(8,128)(2,1)S(1)}, u32[]{:S(2)}, u32[]{:S(2)}) collective-permute-start(bf16[4,128,128]{2,1,0:T(8,128)(2,1)} %bitcast.44), channel_id=1, source_target_pairs={{0,1},{1,0},{2,3},{3,2},{4,5},{5,4},{6,7},{7,6},{8,9},{9,8},{10,11... | collective-permute-start | bytes 393224 | tf_op jit(solution)/shard_map/ppermute | solution.py:41
  8.2 4.0 %project_queries.1 = bf16[512,768]{1,0:T(8,128)(2,1)} custom-call(bf16[512,768]{1,0:T(8,128)(2,1)} %get-tuple-element.115.first_ref.in_ref, bf16[768,896]{1,0:T(8,128)(2,1)} %refs_13_.1, f32[896]{0:T(1024)} %add_ref.4, f32[3,128,128]{2,1,0:T(8,128)} %pad_maximum_fusion.4.tables_ref.refs_6_.refs_14_), custom_call_target="tpu_custom_call" | custom-call | flops 6000000000 | tf_op jit(solution)/shard_map/project_queries/pallas_call | solution.py:272
  12.9 1.6 %collective-permute-start.1 = (bf16[2,4,128,128]{3,2,1,0:T(8,128)(2,1)S(1)}, bf16[2,4,128,128]{3,2,1,0:T(8,128)(2,1)S(1)}, u32[]{:S(2)}, u32[]{:S(2)}) collective-permute-start(bf16[2,4,128,128]{3,2,1,0:T(8,128)(2,1)S(1)} %pad_maximum_fusion.3.refs_0_), channel_id=1, source_target_pairs={{0,2},{1,3},{2,4},{3,5},{4,6},{5,7},{6,0},{7,1},{8,10},{9,11},{10,... | collective-permute-start | bytes 786440 | tf_op jit(solution)/shard_map/ppermute | solution.py:46
  14.5 2.6 %collective-permute-start.2 = (bf16[2,4,128,128]{3,2,1,0:T(8,128)(2,1)S(1)}, bf16[2,4,128,128]{3,2,1,0:T(8,128)(2,1)S(1)}, u32[]{:S(2)}, u32[]{:S(2)}) collective-permute-start(bf16[2,4,128,128]{3,2,1,0:T(8,128)(2,1)S(1)} %pad_maximum_fusion.3.refs_0_), channel_id=1, source_target_pairs={{0,4},{1,5},{2,6},{3,7},{4,0},{5,1},{6,2},{7,3},{8,12},{9,13},{10,... | collective-permute-start | bytes 786440 | tf_op jit(solution)/shard_map/ppermute | solution.py:46
  17.1 1.3 collective-permute-start.3
  18.5 0.9 copy-done.14
  19.3 28.6 %feed_forward.1 = (bf16[512,768]{1,0:T(8,128)(2,1)}, bf16[512,768]{1,0:T(8,128)(2,1)}, bf16[2,512,768]{2,1,0:T(8,128)(2,1)}, bf16[512,768]{1,0:T(8,128)(2,1)}, f...) custom-call(s32[4]{0:T(128)} %pad_add_fusion.place_ref, ...), custom_call_target="tpu_custom_call" | custom-call | flops 35999997952 | tf_op jit(solution)/shard_map/feed_forward/pallas_call | solution.py:434
  48.8 1.5 collective-permute-start.9
  51.1 24.9 %attention.1 = (bf16[2,4,128,768]{3,2,1,0:T(8,128)(2,1)}, bf16[4,4,128,128]{3,2,1,0:T(8,128)(2,1)}, bf16[4,4,128,128]{3,2,1,0:T(8,128)(2,1)}) custom-call(s32[4]{0:T(128)} %pad_add_fusion.place_ref, bf16[2,4,128,128]{3,2,1,0:T(8,128)(2,1)} %copy-done.3, bf16[2,4,128,128]{3,2,1,0:T(8,128)(2,1)} %copy-done.18, bf16[2,4,128,128]{3,2,1,0:T(8,128)(2,1)} %copy-done.19, ...), custom_call_target="tpu_custom_call" | custom-call | flops 30000001024 | tf_op jit(solution)/shard_map/attention/pallas_call | solution.py:692
  76.1 1.0 collective-permute-start.7
  77.1 1.0 copy-done.10
  78.5 4.2 %add_split.1 = (bf16[2,96,1536]{2,1,0:T(8,128)(2,1)}, bf16[2,96,1536]{2,1,0:T(8,128)(2,1)}, bf16[2,192,768]{2,1,0:T(8,128)(2,1)}, bf16[2,192,768]{2,1,0:T(8,128)(2,1)}) custom-call(s32[4]{0:T(128)} %pad_add_fusion.place_ref, bf16[2,2,96,1536]{3,2,1,0:T(8,128)(2,1)} %bitcast.71, bf16[2,2,96,1536]{3,2,1,0:T(8,128)(2,1)} %bitcast.54, ...), custom_call_target="tpu_custom_call" | custom-call | flops 17999998976 | tf_op jit(solution)/shard_map/add_split/pallas_call | solution.py:139
  82.7 1.4 collective-permute-start.16
  84.1 1.0 collective-permute-start.17
  85.3 6.1 %weights.1 = (bf16[2,4,96,384]{3,2,1,0:T(8,128)(2,1)}, bf16[2,4,96,384]{3,2,1,0:T(8,128)(2,1)}, f32[8,768]{1,0:T(8,128)}) custom-call(s32[4]{0:T(128)} %pad_add_fusion.place_ref, bf16[2,512,768]{2,1,0:T(8,128)(2,1)} %bitcast.49, bf16[2,512,768]{2,1,0:T(8,128)(2,1)} %copy-done.9, bf16[512,768]{1,0:T(8,128)(2,1)} %bitcast.61, bf16[512,768]{1,0:T(8,128)(2,1)} %copy-done.14, ...), custom_call_target="tpu_custom_call" | custom-call | flops 7200000000 | tf_op jit(solution)/shard_map/weights/pallas_call | solution.py:737
  91.4 1.1 collective-permute-start.15
  92.5 0.8 add_convert_fusion.4
  94.3 3.7 %mix.1 = bf16[512,768]{1,0:T(8,128)(2,1)} custom-call(bf16[512,768]{1,0:T(8,128)(2,1)} %bitcast.58, bf16[512,768]{1,0:T(8,128)(2,1)} %get-tuple-element.143.mlp_ref, bf16[2,512,768]{2,1,0:T(8,128)(2,1)} %copy-done.8, bf16[2,512,768]{2,1,0:T(8,128)(2,1)} %bitcast.51, f32[768]{0:T(1024)} %add_ref.5, bf16[768,768]{1,0:T(8,128)(2,1)} %wo_ref.3), custom_call_target="tpu_custom_call" | custom-call | flops 3600000000 | tf_op jit(solution)/shard_map/mix/pallas_call | solution.py:763
  98.0 2.0 %collective-permute-done.16 = bf16[2,96,1536]{2,1,0:T(8,128)(2,1)S(1)} collective-permute-done((bf16[2,96,1536]{2,1,0:T(8,128)(2,1)}, bf16[2,96,1536]{2,1,0:T(8,128)(2,1)S(1)}, u32[]{:S(2)}, u32[]{:S(2)}) %collective-permute-start.16) | collective-permute-done | bytes 589856 | tf_op jit(solution)/shard_map/ppermute | solution.py:41
  100.0 3.0 %collective-permute-start.12 = (bf16[4,128,128]{2,1,0:T(8,128)(2,1)S(1)}, bf16[4,128,128]{2,1,0:T(8,128)(2,1)S(1)}, u32[]{:S(2)}, u32[]{:S(2)}) collective-permute-start(bf16[4,128,128]{2,1,0:T(8,128)(2,1)S(1)} %get-tuple-element.145), channel_id=1, source_target_pairs={{0,6},{1,7},{2,0},{3,1},{4,2},{5,3},{6,4},{7,5},{8,14},{9,15},{10,... | collective-permute-start | bytes 393224 | tf_op jit(solution)/shard_map/ppermute | solution.py:46
  103.1 0.8 copy-done.17
  103.9 2.7 %exchange_split.1 = (bf16[768,384]{1,0:T(8,128)(2,1)}, bf16[2,48,1536]{2,1,0:T(8,128)(2,1)}, bf16[1,192,768]{2,1,0:T(8,128)(2,1)}) custom-call(s32[4]{0:T(128)} %pad_add_fusion.place_ref, bf16[2,2,48,1536]{3,2,1,0:T(8,128)(2,1)} %bitcast.77, bf16[2,2,48,1536]{3,2,1,0:T(8,128)(2,1)} %bitcast.64, bf16[1,2,192,768]{3,2,1,0:T(8,128)(2,1)} %bitcast.78, ...), custom_call_target="tpu_custom_call" | custom-call | flops 3600000000 | tf_op jit(solution)/shard_map/exchange_split/pallas_call | solution.py:166
  106.6 1.1 collective-permute-start.22
  107.7 0.8 copy-done.16
  108.5 2.1 %add_cut.1 = (bf16[2,96,384]{2,1,0:T(8,128)(2,1)}, bf16[2,96,384]{2,1,0:T(8,128)(2,1)}, bf16[2,96,384]{2,1,0:T(8,128)(2,1)}, bf16[2,96,384]{2,1,0:T(8,128)(2,1)}) custom-call(s32[4]{0:T(128)} %pad_add_fusion.place_ref, bf16[2,4,96,384]{3,2,1,0:T(8,128)(2,1)} %get-tuple-element.155.a_ref, bf16[2,4,96,384]{3,2,1,0:T(8,128)(2,1)} %copy-done.16), custom_call_target="tpu_custom_call" | custom-call | flops 3600000000 | tf_op jit(solution)/shard_map/add_cut/pallas_call | solution.py:218
  110.8 0.7 collective-permute-start.20
  111.5 3.6 %collective-permute-start.21 = (bf16[2,96,384]{2,1,0:T(8,128)(2,1)}, bf16[2,96,384]{2,1,0:T(8,128)(2,1)S(1)}, u32[]{:S(2)}, u32[]{:S(2)}) collective-permute-start(bf16[2,96,384]{2,1,0:T(8,128)(2,1)} %get-tuple-element.169), channel_id=1, source_target_pairs={{0,6},{1,7},{2,4},{3,5},{4,2},{5,3},{6,0},{7,1},{8,14},{9,15},{10,... | collective-permute-start | bytes 442376 | tf_op jit(solution)/shard_map/ppermute | solution.py:41
  115.1 6.0 %finish.1 = (bf16[512,768]{1,0:T(8,128)(2,1)}, bf16[512,128]{1,0:T(8,128)(2,1)}, bf16[512,128]{1,0:T(8,128)(2,1)}) custom-call(s32[4]{0:T(128)} %pad_add_fusion.place_ref, bf16[512,128]{1,0:T(8,128)(2,1)} %bitcast.43, bf16[512,128]{1,0:T(8,128)(2,1)} %bitcast.69, bf16[512,128]{1,0:T(8,128)(2,1)} %bitcast.67, bf16[512,128]{1,0:T(8,128)(2,1)} %bitcast.68, ...), custom_call_target="tpu_custom_call" | custom-call | flops 7200000000 | tf_op jit(solution)/shard_map/finish/pallas_call | solution.py:857
  121.1 1.0 collective-permute-start.18
  122.1 0.8 copy-done
  122.9 2.2 %exchange_add.1 = (bf16[1,48,1536]{2,1,0:T(8,128)(2,1)}, bf16[1,48,1536]{2,1,0:T(8,128)(2,1)}, bf16[1,192,768]{2,1,0:T(8,128)(2,1)}) custom-call(s32[4]{0:T(128)} %pad_add_fusion.place_ref, bf16[2,48,1536]{2,1,0:T(8,128)(2,1)} %get-tuple-element.172.a1, bf16[1,192,768]{2,1,0:T(8,128)(2,1)} %get-tuple-element.173.a2, bf16[768,384]{1,0:T(8,128)(2,1)} %copy-done), custom_call_target="tpu_custom_call" | custom-call | flops 30000000 | tf_op jit(solution)/shard_map/exchange_add/pallas_call | solution.py:198
  125.1 1.3 collective-permute-start.26
  126.5 1.2 collective-permute-start.27
  128.4 1.7 %message_cut.1 = (bf16[224,128]{1,0:T(8,128)(2,1)}, bf16[224,128]{1,0:T(8,128)(2,1)}, bf16[224,128]{1,0:T(8,128)(2,1)}, bf16[224,128]{1,0:T(8,128)(2,1)}) custom-call(s32[4]{0:T(128)} %pad_add_fusion.place_ref, bf16[512,128]{1,0:T(8,128)(2,1)} %get-tuple-element.180.a_ref, bf16[512,128]{1,0:T(8,128)(2,1)} %copy-done.24), custom_call_target="tpu_custom_call" | custom-call | flops 1800000000 | tf_op jit(solution)/shard_map/message_cut/pallas_call | solution.py:891
  130.1 0.7 collective-permute-start.23
  130.9 3.6 %collective-permute-start.24 = (bf16[224,128]{1,0:T(8,128)(2,1)}, bf16[224,128]{1,0:T(8,128)(2,1)S(1)}, u32[]{:S(2)}, u32[]{:S(2)}) collective-permute-start(bf16[224,128]{1,0:T(8,128)(2,1)} %get-tuple-element.184), channel_id=1, source_target_pairs={{0,4},{1,5},{2,6},{3,7},{4,0},{5,1},{6,2},{7,3},{8,12},{9,13},{10,... | collective-permute-start | bytes 172040 | tf_op jit(solution)/shard_map/ppermute | solution.py:41
  134.4 4.9 %collective-permute-start.25 = (bf16[224,128]{1,0:T(8,128)(2,1)}, bf16[224,128]{1,0:T(8,128)(2,1)S(1)}, u32[]{:S(2)}, u32[]{:S(2)}) collective-permute-start(bf16[224,128]{1,0:T(8,128)(2,1)} %get-tuple-element.185), channel_id=1, source_target_pairs={{0,6},{1,7},{2,4},{3,5},{4,2},{5,3},{6,0},{7,1},{8,14},{9,15},{10,... | collective-permute-start | bytes 172040 | tf_op jit(solution)/shard_map/ppermute | solution.py:41
  139.3 1.2 collective-permute-start.33
  141.2 1.1 collective-permute-start.32
  143.6 1.6 message_sum.1.refs_0_
  145.4 1.0 collective-permute-start.30
  147.1 4.1 %collective-permute-done.32 = bf16[192,768]{1,0:T(8,128)(2,1)S(1)} collective-permute-done((bf16[192,768]{1,0:T(8,128)(2,1)S(1)}, bf16[192,768]{1,0:T(8,128)(2,1)S(1)}, u32[]{:S(2)}, u32[]{:S(2)}) %collective-permute-start.32) | collective-permute-done | bytes 294944 | tf_op jit(solution)/shard_map/ppermute | solution.py:41
  153.7 1.6 last_sums.1
  155.4 0.8 slice_bitcast_fusion
  156.2 0.8 pad_maximum_fusion.1
  157.0 1.1 maximum_convert_fusion
  158.1 1.1 select_convert_fusion
  (125 shorter events, 12.3 us)
Async XLA Ops:
  0.6 17.8 %collective-permute-start.5 = (bf16[512,768]{1,0:T(8,128)(2,1)}, bf16[512,768]{1,0:T(8,128)(2,1)}, u32[]{:S(2)}, u32[]{:S(2)}) collective-permute-start(bf16[512,768]{1,0:T(8,128)(2,1)} %bitcast.55), channel_id=1, source_target_pairs={{0,8},{8,0},{16,24},{24,16},{1,9},{9,1},{17,25},{25,17},{2,10},{10... | collective-permute-start | bytes 2359304 | tf_op jit(solution)/shard_map/ppermute | solution.py:41
  2.2 5.7 %copy-start.12 = (bf16[4,128,768]{2,1,0:T(8,128)(2,1)S(1)}, bf16[4,128,768]{2,1,0:T(8,128)(2,1)}, u32[]{:S(2)}) copy-start(bf16[4,128,768]{2,1,0:T(8,128)(2,1)} %param.26) | copy-start | bytes 2359300
  5.1 7.7 %collective-permute-start = (bf16[4,128,128]{2,1,0:T(8,128)(2,1)}, bf16[4,128,128]{2,1,0:T(8,128)(2,1)S(1)}, u32[]{:S(2)}, u32[]{:S(2)}) collective-permute-start(bf16[4,128,128]{2,1,0:T(8,128)(2,1)} %bitcast.44), channel_id=1, source_target_pairs={{0,1},{1,0},{2,3},{3,2},{4,5},{5,4},{6,7},{7,6},{8,9},{9,8},{10,11... | collective-permute-start | bytes 393224 | tf_op jit(solution)/shard_map/ppermute | solution.py:41
  7.7 9.4 %collective-permute-start.4 = (bf16[512,768]{1,0:T(8,128)(2,1)}, bf16[512,768]{1,0:T(8,128)(2,1)S(1)}, u32[]{:S(2)}, u32[]{:S(2)}) collective-permute-start(bf16[512,768]{1,0:T(8,128)(2,1)} %get-tuple-element.115.first_ref.in_ref), channel_id=1, source_target_pairs={{0,8},{8,0},{16,24},{24,16},{1,9},{9,1},{17,25},{25,17},{2,10},{10... | collective-permute-start | bytes 2359304 | tf_op jit(solution)/shard_map/ppermute | solution.py:41
  7.9 4.9 %copy-start.6 = (bf16[512,128]{1,0:T(8,128)(2,1)S(1)}, bf16[512,128]{1,0:T(8,128)(2,1)}, u32[]{:S(2)}) copy-start(bf16[512,128]{1,0:T(8,128)(2,1)} %get-tuple-element.114) | copy-start | bytes 393220
  7.9 10.6 %collective-permute-start.6 = (bf16[512,768]{1,0:T(8,128)(2,1)S(1)}, bf16[512,768]{1,0:T(8,128)(2,1)S(1)}, u32[]{:S(2)}, u32[]{:S(2)}) collective-permute-start(bf16[512,768]{1,0:T(8,128)(2,1)S(1)} %bitcast.63), channel_id=1, source_target_pairs={{0,8},{8,0},{16,24},{24,16},{1,9},{9,1},{17,25},{25,17},{2,10},{10... | collective-permute-start | bytes 2359304 | tf_op jit(solution)/shard_map/ppermute | solution.py:41
  12.9 35.1 %copy-start.3 = (bf16[2,4,128,128]{3,2,1,0:T(8,128)(2,1)}, bf16[2,4,128,128]{3,2,1,0:T(8,128)(2,1)S(1)}, u32[]{:S(2)}) copy-start(bf16[2,4,128,128]{3,2,1,0:T(8,128)(2,1)S(1)} %pad_maximum_fusion.3.refs_0_) | copy-start | bytes 786436
  12.9 35.9 %collective-permute-start.1 = (bf16[2,4,128,128]{3,2,1,0:T(8,128)(2,1)S(1)}, bf16[2,4,128,128]{3,2,1,0:T(8,128)(2,1)S(1)}, u32[]{:S(2)}, u32[]{:S(2)}) collective-permute-start(bf16[2,4,128,128]{3,2,1,0:T(8,128)(2,1)S(1)} %pad_maximum_fusion.3.refs_0_), channel_id=1, source_target_pairs={{0,2},{1,3},{2,4},{3,5},{4,6},{5,7},{6,0},{7,1},{8,10},{9,11},{10,... | collective-permute-start | bytes 786440 | tf_op jit(solution)/shard_map/ppermute | solution.py:46
  14.5 35.8 %collective-permute-start.2 = (bf16[2,4,128,128]{3,2,1,0:T(8,128)(2,1)S(1)}, bf16[2,4,128,128]{3,2,1,0:T(8,128)(2,1)S(1)}, u32[]{:S(2)}, u32[]{:S(2)}) collective-permute-start(bf16[2,4,128,128]{3,2,1,0:T(8,128)(2,1)S(1)} %pad_maximum_fusion.3.refs_0_), channel_id=1, source_target_pairs={{0,4},{1,5},{2,6},{3,7},{4,0},{5,1},{6,2},{7,3},{8,12},{9,13},{10,... | collective-permute-start | bytes 786440 | tf_op jit(solution)/shard_map/ppermute | solution.py:46
  17.1 30.9 %copy-start.13 = (bf16[512,768]{1,0:T(8,128)(2,1)}, bf16[512,768]{1,0:T(8,128)(2,1)S(1)}, u32[]{:S(2)}) copy-start(bf16[512,768]{1,0:T(8,128)(2,1)S(1)} %collective-permute-done.4.in2_ref) | copy-start | bytes 2359300
  17.1 33.2 %collective-permute-start.3 = (bf16[2,4,128,128]{3,2,1,0:T(8,128)(2,1)S(1)}, bf16[2,4,128,128]{3,2,1,0:T(8,128)(2,1)S(1)}, u32[]{:S(2)}, u32[]{:S(2)}) collective-permute-start(bf16[2,4,128,128]{3,2,1,0:T(8,128)(2,1)S(1)} %pad_maximum_fusion.3.refs_0_), channel_id=1, source_target_pairs={{0,6},{1,7},{2,0},{3,1},{4,2},{5,3},{6,4},{7,5},{8,14},{9,15},{10,... | collective-permute-start | bytes 786440 | tf_op jit(solution)/shard_map/ppermute | solution.py:46
  48.0 29.2 %collective-permute-start.11 = (bf16[2,512,768]{2,1,0:T(8,128)(2,1)}, bf16[2,512,768]{2,1,0:T(8,128)(2,1)S(1)}, u32[]{:S(2)}, u32[]{:S(2)}) collective-permute-start(bf16[2,512,768]{2,1,0:T(8,128)(2,1)} %get-tuple-element.132), channel_id=1, source_target_pairs={{0,8},{8,0},{16,24},{24,16},{1,9},{9,1},{17,25},{25,17},{2,10},{10... | collective-permute-start | bytes 4718600 | tf_op jit(solution)/shard_map/ppermute | solution.py:41
  48.1 29.1 %collective-permute-start.10 = (bf16[768,768]{1,0:T(8,128)(2,1)}, bf16[768,768]{1,0:T(8,128)(2,1)S(1)}, u32[]{:S(2)}, u32[]{:S(2)}) collective-permute-start(bf16[768,768]{1,0:T(8,128)(2,1)} %get-tuple-element.131), channel_id=1, source_target_pairs={{0,2},{1,3},{2,0},{3,1},{4,6},{5,7},{6,4},{7,5},{8,10},{9,11},{10,... | collective-permute-start | bytes 3538952 | tf_op jit(solution)/shard_map/ppermute | solution.py:41
  48.8 28.3 %collective-permute-start.9 = (bf16[8,48,1536]{2,1,0:T(8,128)(2,1)}, bf16[8,48,1536]{2,1,0:T(8,128)(2,1)S(1)}, u32[]{:S(2)}, u32[]{:S(2)}) collective-permute-start(bf16[8,48,1536]{2,1,0:T(8,128)(2,1)} %get-tuple-element.129), channel_id=1, source_target_pairs={{0,16},{8,24},{16,0},{24,8},{1,17},{9,25},{17,1},{25,9},{2,18},{10... | collective-permute-start | bytes 3538952 | tf_op jit(solution)/shard_map/ppermute | solution.py:41
  76.0 8.1 %collective-permute-start.8 = (bf16[2,512,768]{2,1,0:T(8,128)(2,1)}, bf16[2,512,768]{2,1,0:T(8,128)(2,1)S(1)}, u32[]{:S(2)}, u32[]{:S(2)}) collective-permute-start(bf16[2,512,768]{2,1,0:T(8,128)(2,1)} %bitcast.48), channel_id=1, source_target_pairs={{0,8},{8,0},{16,24},{24,16},{1,9},{9,1},{17,25},{25,17},{2,10},{10... | collective-permute-start | bytes 4718600 | tf_op jit(solution)/shard_map/ppermute | solution.py:41
  76.1 16.4 %collective-permute-start.7 = (bf16[4,4,128,128]{3,2,1,0:T(8,128)(2,1)}, bf16[4,4,128,128]{3,2,1,0:T(8,128)(2,1)S(1)}, u32[]{:S(2)}, u32[]{:S(2)}) collective-permute-start(bf16[4,4,128,128]{3,2,1,0:T(8,128)(2,1)} %get-tuple-element.126), channel_id=1, source_target_pairs={{0,1},{1,0},{2,3},{3,2},{4,5},{5,4},{6,7},{7,6},{8,9},{9,8},{10,11... | collective-permute-start | bytes 1572872 | tf_op jit(solution)/shard_map/ppermute | solution.py:41
  77.1 5.6 %copy-start.8 = (bf16[2,512,768]{2,1,0:T(8,128)(2,1)}, bf16[2,512,768]{2,1,0:T(8,128)(2,1)S(1)}, u32[]{:S(2)}) copy-start(bf16[2,512,768]{2,1,0:T(8,128)(2,1)S(1)} %collective-permute-done.11.mlp2_ref.refs_9_) | copy-start | bytes 4718596
  82.7 17.3 %collective-permute-start.16 = (bf16[2,96,1536]{2,1,0:T(8,128)(2,1)}, bf16[2,96,1536]{2,1,0:T(8,128)(2,1)S(1)}, u32[]{:S(2)}, u32[]{:S(2)}) collective-permute-start(bf16[2,96,1536]{2,1,0:T(8,128)(2,1)} %get-tuple-element.137), channel_id=1, source_target_pairs={{0,2},{1,3},{2,0},{3,1},{4,6},{5,7},{6,4},{7,5},{8,10},{9,11},{10,... | collective-permute-start | bytes 1769480 | tf_op jit(solution)/shard_map/ppermute | solution.py:41
  84.1 8.4 %copy-start.1 = (bf16[4,4,128,128]{3,2,1,0:T(8,128)(2,1)S(1)}, bf16[4,4,128,128]{3,2,1,0:T(8,128)(2,1)}, u32[]{:S(2)}) copy-start(bf16[4,4,128,128]{3,2,1,0:T(8,128)(2,1)} %get-tuple-element.140) | copy-start | bytes 1572868
  84.1 19.0 %collective-permute-start.17 = (bf16[2,192,768]{2,1,0:T(8,128)(2,1)}, bf16[2,192,768]{2,1,0:T(8,128)(2,1)S(1)}, u32[]{:S(2)}, u32[]{:S(2)}) collective-permute-start(bf16[2,192,768]{2,1,0:T(8,128)(2,1)} %get-tuple-element.149), channel_id=1, source_target_pairs={{0,16},{8,24},{16,0},{24,8},{1,17},{9,25},{17,1},{25,9},{2,18},{10... | collective-permute-start | bytes 1769480 | tf_op jit(solution)/shard_map/ppermute | solution.py:41
  91.4 16.3 %collective-permute-start.15 = (bf16[2,4,96,384]{3,2,1,0:T(8,128)(2,1)}, bf16[2,4,96,384]{3,2,1,0:T(8,128)(2,1)S(1)}, u32[]{:S(2)}, u32[]{:S(2)}) collective-permute-start(bf16[2,4,96,384]{3,2,1,0:T(8,128)(2,1)} %get-tuple-element.139), channel_id=1, source_target_pairs={{0,1},{1,0},{2,3},{3,2},{4,5},{5,4},{6,7},{7,6},{8,9},{9,8},{10,11... | collective-permute-start | bytes 1769480 | tf_op jit(solution)/shard_map/ppermute | solution.py:41
  93.3 17.3 %collective-permute-start.13 = (bf16[4,128,128]{2,1,0:T(8,128)(2,1)S(1)}, bf16[4,128,128]{2,1,0:T(8,128)(2,1)S(1)}, u32[]{:S(2)}, u32[]{:S(2)}) collective-permute-start(bf16[4,128,128]{2,1,0:T(8,128)(2,1)S(1)} %get-tuple-element.216), channel_id=1, source_target_pairs={{0,4},{1,5},{2,6},{3,7},{4,0},{5,1},{6,2},{7,3},{8,12},{9,13},{10,... | collective-permute-start | bytes 393224 | tf_op jit(solution)/shard_map/ppermute | solution.py:46
  93.7 17.0 %collective-permute-start.14 = (bf16[4,128,128]{2,1,0:T(8,128)(2,1)S(1)}, bf16[4,128,128]{2,1,0:T(8,128)(2,1)S(1)}, u32[]{:S(2)}, u32[]{:S(2)}) collective-permute-start(bf16[4,128,128]{2,1,0:T(8,128)(2,1)S(1)} %get-tuple-element.215), channel_id=1, source_target_pairs={{0,2},{1,3},{2,4},{3,5},{4,6},{5,7},{6,0},{7,1},{8,10},{9,11},{10,... | collective-permute-start | bytes 393224 | tf_op jit(solution)/shard_map/ppermute | solution.py:46
  100.0 10.6 %collective-permute-start.12 = (bf16[4,128,128]{2,1,0:T(8,128)(2,1)S(1)}, bf16[4,128,128]{2,1,0:T(8,128)(2,1)S(1)}, u32[]{:S(2)}, u32[]{:S(2)}) collective-permute-start(bf16[4,128,128]{2,1,0:T(8,128)(2,1)S(1)} %get-tuple-element.145), channel_id=1, source_target_pairs={{0,6},{1,7},{2,0},{3,1},{4,2},{5,3},{6,4},{7,5},{8,14},{9,15},{10,... | collective-permute-start | bytes 393224 | tf_op jit(solution)/shard_map/ppermute | solution.py:46
  106.6 15.5 %collective-permute-start.22 = (bf16[768,384]{1,0:T(8,128)(2,1)}, bf16[768,384]{1,0:T(8,128)(2,1)S(1)}, u32[]{:S(2)}, u32[]{:S(2)}) collective-permute-start(bf16[768,384]{1,0:T(8,128)(2,1)} %get-tuple-element.154), channel_id=1, source_target_pairs={{0,1},{1,0},{2,3},{3,2},{4,5},{5,4},{6,7},{7,6},{8,9},{9,8},{10,11... | collective-permute-start | bytes 1769480 | tf_op jit(solution)/shard_map/ppermute | solution.py:41
  110.6 4.5 %copy-start.23 = (bf16[4,128,128]{2,1,0:T(8,128)(2,1)}, bf16[4,128,128]{2,1,0:T(8,128)(2,1)S(1)}, u32[]{:S(2)}) copy-start(bf16[4,128,128]{2,1,0:T(8,128)(2,1)S(1)} %collective-permute-done.12) | copy-start | bytes 393220
  110.7 4.5 %copy-start.21 = (bf16[4,128,128]{2,1,0:T(8,128)(2,1)}, bf16[4,128,128]{2,1,0:T(8,128)(2,1)S(1)}, u32[]{:S(2)}) copy-start(bf16[4,128,128]{2,1,0:T(8,128)(2,1)S(1)} %collective-permute-done.13) | copy-start | bytes 393220
  110.7 14.4 %collective-permute-start.19 = (bf16[2,96,384]{2,1,0:T(8,128)(2,1)}, bf16[2,96,384]{2,1,0:T(8,128)(2,1)S(1)}, u32[]{:S(2)}, u32[]{:S(2)}) collective-permute-start(bf16[2,96,384]{2,1,0:T(8,128)(2,1)} %get-tuple-element.167), channel_id=1, source_target_pairs={{0,2},{1,3},{2,0},{3,1},{4,6},{5,7},{6,4},{7,5},{8,10},{9,11},{10,... | collective-permute-start | bytes 442376 | tf_op jit(solution)/shard_map/ppermute | solution.py:41
  110.8 15.7 %collective-permute-start.20 = (bf16[2,96,384]{2,1,0:T(8,128)(2,1)}, bf16[2,96,384]{2,1,0:T(8,128)(2,1)S(1)}, u32[]{:S(2)}, u32[]{:S(2)}) collective-permute-start(bf16[2,96,384]{2,1,0:T(8,128)(2,1)} %get-tuple-element.168), channel_id=1, source_target_pairs={{0,4},{1,5},{2,6},{3,7},{4,0},{5,1},{6,2},{7,3},{8,12},{9,13},{10,... | collective-permute-start | bytes 442376 | tf_op jit(solution)/shard_map/ppermute | solution.py:41
  111.5 14.9 %collective-permute-start.21 = (bf16[2,96,384]{2,1,0:T(8,128)(2,1)}, bf16[2,96,384]{2,1,0:T(8,128)(2,1)S(1)}, u32[]{:S(2)}, u32[]{:S(2)}) collective-permute-start(bf16[2,96,384]{2,1,0:T(8,128)(2,1)} %get-tuple-element.169), channel_id=1, source_target_pairs={{0,6},{1,7},{2,4},{3,5},{4,2},{5,3},{6,0},{7,1},{8,14},{9,15},{10,... | collective-permute-start | bytes 442376 | tf_op jit(solution)/shard_map/ppermute | solution.py:41
  121.1 5.3 %copy-start.5 = (bf16[2,96,384]{2,1,0:T(8,128)(2,1)S(1)}, bf16[2,96,384]{2,1,0:T(8,128)(2,1)}, u32[]{:S(2)}) copy-start(bf16[2,96,384]{2,1,0:T(8,128)(2,1)} %get-tuple-element.157) | copy-start | bytes 442372
  121.1 6.6 %collective-permute-start.18 = (bf16[512,128]{1,0:T(8,128)(2,1)}, bf16[512,128]{1,0:T(8,128)(2,1)S(1)}, u32[]{:S(2)}, u32[]{:S(2)}) collective-permute-start(bf16[512,128]{1,0:T(8,128)(2,1)} %get-tuple-element.166), channel_id=1, source_target_pairs={{0,1},{1,0},{2,3},{3,2},{4,5},{5,4},{6,7},{7,6},{8,9},{9,8},{10,11... | collective-permute-start | bytes 393224 | tf_op jit(solution)/shard_map/ppermute | solution.py:41
  125.1 9.3 %collective-permute-start.28 = (bf16[1,48,1536]{2,1,0:T(8,128)(2,1)}, bf16[1,48,1536]{2,1,0:T(8,128)(2,1)S(1)}, u32[]{:S(2)}, u32[]{:S(2)}) collective-permute-start(bf16[1,48,1536]{2,1,0:T(8,128)(2,1)} %get-tuple-element.175), channel_id=1, source_target_pairs={{0,4},{1,5},{2,6},{3,7},{4,0},{5,1},{6,2},{7,3},{8,12},{9,13},{10,... | collective-permute-start | bytes 442376 | tf_op jit(solution)/shard_map/ppermute | solution.py:41
  125.1 16.0 %collective-permute-start.26 = (bf16[192,768]{1,0:T(8,128)(2,1)}, bf16[192,768]{1,0:T(8,128)(2,1)S(1)}, u32[]{:S(2)}, u32[]{:S(2)}) collective-permute-start(bf16[192,768]{1,0:T(8,128)(2,1)} %bitcast.41), channel_id=1, source_target_pairs={{4,0},{5,1},{6,2},{7,3},{8,12},{9,13},{10,14},{11,15},{20,16},{21,... | collective-permute-start | bytes 884744 | tf_op jit(solution)/shard_map/ppermute | solution.py:57
  126.5 12.8 %collective-permute-start.27 = (bf16[2,96,384]{2,1,0:T(8,128)(2,1)S(1)}, bf16[2,96,384]{2,1,0:T(8,128)(2,1)S(1)}, u32[]{:S(2)}, u32[]{:S(2)}) collective-permute-start(bf16[2,96,384]{2,1,0:T(8,128)(2,1)S(1)} %add_convert_fusion.3), channel_id=1, source_target_pairs={{0,16},{8,24},{16,0},{24,8},{1,17},{9,25},{17,1},{25,9},{2,18},{10... | collective-permute-start | bytes 442376 | tf_op jit(solution)/shard_map/ppermute | solution.py:41
  128.4 10.9 %copy-start.4 = (bf16[1,48,1536]{2,1,0:T(8,128)(2,1)S(1)}, bf16[1,48,1536]{2,1,0:T(8,128)(2,1)}, u32[]{:S(2)}) copy-start(bf16[1,48,1536]{2,1,0:T(8,128)(2,1)} %get-tuple-element.187) | copy-start | bytes 442372
  128.4 12.8 %copy-start.2 = (bf16[1,192,768]{2,1,0:T(8,128)(2,1)S(1)}, bf16[1,192,768]{2,1,0:T(8,128)(2,1)}, u32[]{:S(2)}) copy-start(bf16[1,192,768]{2,1,0:T(8,128)(2,1)} %get-tuple-element.176) | copy-start | bytes 884740
  130.1 11.1 %collective-permute-start.23 = (bf16[224,128]{1,0:T(8,128)(2,1)}, bf16[224,128]{1,0:T(8,128)(2,1)S(1)}, u32[]{:S(2)}, u32[]{:S(2)}) collective-permute-start(bf16[224,128]{1,0:T(8,128)(2,1)} %get-tuple-element.183), channel_id=1, source_target_pairs={{0,2},{1,3},{2,0},{3,1},{4,6},{5,7},{6,4},{7,5},{8,10},{9,11},{10,... | collective-permute-start | bytes 172040 | tf_op jit(solution)/shard_map/ppermute | solution.py:41
  130.9 11.5 %collective-permute-start.24 = (bf16[224,128]{1,0:T(8,128)(2,1)}, bf16[224,128]{1,0:T(8,128)(2,1)S(1)}, u32[]{:S(2)}, u32[]{:S(2)}) collective-permute-start(bf16[224,128]{1,0:T(8,128)(2,1)} %get-tuple-element.184), channel_id=1, source_target_pairs={{0,4},{1,5},{2,6},{3,7},{4,0},{5,1},{6,2},{7,3},{8,12},{9,13},{10,... | collective-permute-start | bytes 172040 | tf_op jit(solution)/shard_map/ppermute | solution.py:41
  134.4 8.0 %collective-permute-start.25 = (bf16[224,128]{1,0:T(8,128)(2,1)}, bf16[224,128]{1,0:T(8,128)(2,1)S(1)}, u32[]{:S(2)}, u32[]{:S(2)}) collective-permute-start(bf16[224,128]{1,0:T(8,128)(2,1)} %get-tuple-element.185), channel_id=1, source_target_pairs={{0,6},{1,7},{2,4},{3,5},{4,2},{5,3},{6,0},{7,1},{8,14},{9,15},{10,... | collective-permute-start | bytes 172040 | tf_op jit(solution)/shard_map/ppermute | solution.py:41
  139.3 7.0 %collective-permute-start.33 = (bf16[48,1536]{1,0:T(8,128)(2,1)S(1)}, bf16[48,1536]{1,0:T(8,128)(2,1)S(1)}, u32[]{:S(2)}, u32[]{:S(2)}) collective-permute-start(bf16[48,1536]{1,0:T(8,128)(2,1)S(1)} %fusion), channel_id=1, source_target_pairs={{0,16},{8,24},{16,0},{24,8},{1,17},{9,25},{17,1},{25,9},{2,18},{10... | collective-permute-start | bytes 442376 | tf_op jit(solution)/shard_map/ppermute | solution.py:41
  141.1 14.1 %collective-permute-start.34 = (bf16[2,96,384]{2,1,0:T(8,128)(2,1)S(1)}, bf16[2,96,384]{2,1,0:T(8,128)(2,1)S(1)}, u32[]{:S(2)}, u32[]{:S(2)}) collective-permute-start(bf16[2,96,384]{2,1,0:T(8,128)(2,1)S(1)} %add_convert_fusion.1), channel_id=1, source_target_pairs={{0,8},{8,0},{16,24},{24,16},{1,9},{9,1},{17,25},{25,17},{2,10},{10... | collective-permute-start | bytes 442376 | tf_op jit(solution)/shard_map/ppermute | solution.py:41
  141.2 9.9 %collective-permute-start.32 = (bf16[192,768]{1,0:T(8,128)(2,1)S(1)}, bf16[192,768]{1,0:T(8,128)(2,1)S(1)}, u32[]{:S(2)}, u32[]{:S(2)}) collective-permute-start(bf16[192,768]{1,0:T(8,128)(2,1)S(1)} %add_convert_fusion), channel_id=1, source_target_pairs={{0,16},{8,24},{16,0},{24,8},{1,17},{9,25},{17,1},{25,9},{2,18},{10... | collective-permute-start | bytes 884744 | tf_op jit(solution)/shard_map/ppermute | solution.py:41
  145.2 6.1 %collective-permute-start.29 = (bf16[224,128]{1,0:T(8,128)(2,1)}, bf16[224,128]{1,0:T(8,128)(2,1)S(1)}, u32[]{:S(2)}, u32[]{:S(2)}) collective-permute-start(bf16[224,128]{1,0:T(8,128)(2,1)} %message_sum.1.refs_0_), channel_id=1, source_target_pairs={{0,8},{8,0},{16,24},{24,16},{1,9},{9,1},{17,25},{25,17},{2,10},{10... | collective-permute-start | bytes 172040 | tf_op jit(solution)/shard_map/ppermute | solution.py:41
  145.4 7.0 %collective-permute-start.30 = (bf16[224,128]{1,0:T(8,128)(2,1)}, bf16[224,128]{1,0:T(8,128)(2,1)S(1)}, u32[]{:S(2)}, u32[]{:S(2)}) collective-permute-start(bf16[224,128]{1,0:T(8,128)(2,1)} %message_sum.1.refs_0_), channel_id=1, source_target_pairs={{0,16},{8,24},{16,0},{24,8},{1,17},{9,25},{17,1},{25,9},{2,18},{10... | collective-permute-start | bytes 172040 | tf_op jit(solution)/shard_map/ppermute | solution.py:41
  146.4 6.6 %collective-permute-start.31 = (bf16[224,128]{1,0:T(8,128)(2,1)}, bf16[224,128]{1,0:T(8,128)(2,1)S(1)}, u32[]{:S(2)}, u32[]{:S(2)}) collective-permute-start(bf16[224,128]{1,0:T(8,128)(2,1)} %message_sum.1.refs_0_), channel_id=1, source_target_pairs={{0,24},{8,16},{16,8},{24,0},{1,25},{9,17},{17,9},{25,1},{2,26},{10... | collective-permute-start | bytes 172040 | tf_op jit(solution)/shard_map/ppermute | solution.py:41
  151.2 4.2 %collective-permute-start.35 = (bf16[96,1536]{1,0:T(8,128)(2,1)S(1)}, bf16[96,1536]{1,0:T(8,128)(2,1)S(1)}, u32[]{:S(2)}, u32[]{:S(2)}) collective-permute-start(bf16[96,1536]{1,0:T(8,128)(2,1)S(1)} %pad_maximum_fusion.2), channel_id=1, source_target_pairs={{0,8},{8,0},{16,24},{24,16},{1,9},{9,1},{17,25},{25,17},{2,10},{10... | collective-permute-start | bytes 884744 | tf_op jit(solution)/shard_map/ppermute | solution.py:41
  151.3 6.8 %collective-permute-start.36 = (bf16[384,768]{1,0:T(8,128)(2,1)S(1)}, bf16[384,768]{1,0:T(8,128)(2,1)S(1)}, u32[]{:S(2)}, u32[]{:S(2)}) collective-permute-start(bf16[384,768]{1,0:T(8,128)(2,1)S(1)} %pad_maximum_fusion), channel_id=1, source_target_pairs={{0,8},{8,0},{16,24},{24,16},{1,9},{9,1},{17,25},{25,17},{2,10},{10... | collective-permute-start | bytes 1769480 | tf_op jit(solution)/shard_map/ppermute | solution.py:41
  (20 other events, 24.3 us)

commit v5 on v4

--- a/solution.py
+++ b/solution.py
@@ -19,6 +19,7 @@
 F32 = jnp.float32
 BF16 = jnp.bfloat16
 VMEM_BYTES = 56 * 1024 * 1024
+FULL_BYTES = 63 * 1024 * 1024
 
 
 def dot(a, b):
@@ -33,8 +34,8 @@
     return lax.dot_general(a, b, (((0,), (0,)), ((), ())), preferred_element_type=F32)
 
 
-def params():
-    return pltpu.CompilerParams(vmem_limit_bytes=VMEM_BYTES)
+def params(limit=VMEM_BYTES):
+    return pltpu.CompilerParams(vmem_limit_bytes=limit)
 
 
 def flipped(block, axis, bits):
@@ -46,14 +47,19 @@
     return lax.ppermute(block, "seq", [(i, (i + 2 * distance) % size) for i in range(size)])
 
 
+def owners(size):
+    return [(b, i) for b in range(lax.axis_size("batch")) for i in range(size) if i // (size // 2) == b % 2]
+
+
 def to_owner(block):
     size = lax.axis_size("seq")
-    route = []
-    for b in range(lax.axis_size("batch")):
-        for i in range(size):
-            j = i ^ (size // 2)
-            if j // (size // 2) == b % 2:
-                route.append((b * size + i, b * size + j))
+    route = [(b * size + (i ^ (size // 2)), b * size + i) for b, i in owners(size)]
+    return lax.ppermute(block, ("batch", "seq"), route)
+
+
+def between_owners(block):
+    size = lax.axis_size("seq")
+    route = [(b * size + i, (b ^ 2) * size + i) for b, i in owners(size)]
     return lax.ppermute(block, ("batch", "seq"), route)
 
 
@@ -81,19 +87,17 @@
 
 
 def rotary_tables(first, count):
-    lane = jnp.arange(128) % HEAD_DIM
+    kind = lax.broadcasted_iota(jnp.int32, (3, count, 128), 0)
+    place = lax.broadcasted_iota(jnp.int32, (3, count, 128), 1)
+    lane = lax.broadcasted_iota(jnp.int32, (3, count, 128), 2) % HEAD_DIM
     half = ROT // 2
     freqs = 10000.0 ** (-(lane % half).astype(F32) / half)
-    places = (first + jnp.arange(count)).astype(F32) * 0.25
-    angles = places[:, None] * freqs[None, :]
-    cosine, sine = jnp.cos(angles), jnp.sin(angles)
-    return jnp.stack(
-        [
-            jnp.where(lane < ROT, cosine, 1.0),
-            jnp.where((lane >= half) & (lane < ROT), sine, 0.0),
-            jnp.where(lane < half, -sine, 0.0),
-        ]
-    )
+    angles = (first + place).astype(F32) * 0.25 * freqs
+    cosine = jnp.where(lane < ROT, jnp.cos(angles), 1.0)
+    sine = jnp.sin(angles)
+    below = jnp.where((lane >= half) & (lane < ROT), sine, 0.0)
+    above = jnp.where(lane < half, -sine, 0.0)
+    return jnp.where(kind == 0, cosine, jnp.where(kind == 1, below, above))
 
 
 def turn(values, tables, sign):
@@ -168,7 +172,7 @@
         in_specs=[SMEM] + [VMEM] * 4,
         out_specs=[VMEM] * 3,
         out_shape=[SHAPE((size // (D // 2), D // 2), BF16)] + [SHAPE(s, BF16) for s in shapes],
-        compiler_params=params(),
+        compiler_params=params(FULL_BYTES),
         cost_estimate=cost(1.2),
         name="exchange_split",
     )(place, mine1, come1, mine2, come2)
@@ -220,7 +224,7 @@
         in_specs=[SMEM, VMEM, VMEM],
         out_specs=[VMEM] * parts,
         out_shape=[SHAPE((a.shape[0],) + a.shape[2:], BF16)] * parts,
-        compiler_params=params(),
+        compiler_params=params(FULL_BYTES),
         cost_estimate=cost(1.2),
         name="add_cut",
     )(place, a, b)
@@ -437,7 +441,7 @@
         out_shape=[SHAPE((rows, D), BF16), SHAPE((rows, D), BF16), SHAPE((2, rows, D), BF16), SHAPE((rows, D), BF16)]
         + [SHAPE((1, half), F32), SHAPE((count, per, half), BF16), SHAPE((count, per, half), BF16)]
         + grad_shapes,
-        compiler_params=params(),
+        compiler_params=params(FULL_BYTES),
         cost_estimate=cost(12),
         name="feed_forward",
     )(place, x, xx, g, gg, gain, bias, w1, b1, w2, wo)
@@ -697,7 +701,7 @@
         out_shape=[SHAPE((2, seqs, span, D), BF16)]
         + [SHAPE((depth, seqs, span, 128), BF16)] * 2,
         scratch_shapes=scratch,
-        compiler_params=params(),
+        compiler_params=params(FULL_BYTES),
         cost_estimate=cost(10),
         name="attention",
     )(place, *pairs, q, do, tables)
@@ -920,29 +924,40 @@
     )(*messages)
 
 
-def last_sums(messages, lines, widths):
-    rows = messages[0].shape[0] - 2 * lines
-
-    def kernel(*refs):
-        sources, results = refs[: len(messages)], refs[len(messages) :]
+def last_sums(place, messages, lines, widths, top, mine2, other2, mine3, other3):
+    count = len(messages)
+    half = D // 2
+    per = mine3.shape[1]
+
+    def kernel(place_ref, *refs):
+        sources, (a2, b2, a3, b3) = refs[:count], refs[count : count + 4]
+        vectors, (second, out, qkv) = refs[count + 4 : -3], refs[-3:]
+        core = place_ref[0]
         total = tree_sum([ref[...] for ref in sources])
         vector = total[:lines] + total[lines : 2 * lines]
         at = 0
-        for result, width in zip(results[:-1], widths):
+        for result, width in zip(vectors, widths):
             for i in range(width // 128):
                 result[i * 128 : (i + 1) * 128] = vector[at + i]
             at += width // 128
-        results[-1][...] = total[2 * lines :]
+        owner = (place_ref[3] >> top) == core
+        second[...] = jnp.where(owner, a2[...].astype(F32), b2[...].astype(F32))
+        for i, result in ((0, out), (1, qkv)):
+            own, other = a3[i].astype(F32), b3[i].astype(F32)
+            result[:, :half] = jnp.where(core == 0, own, other)
+            result[:, half:D] = jnp.where(core == 0, other, own)
+        qkv[:, D:] = total[2 * lines :]
 
     return pl.pallas_call(
         kernel,
-        in_specs=[VMEM] * len(messages),
-        out_specs=[VMEM] * (len(widths) + 1),
-        out_shape=[SHAPE((width,), F32) for width in widths] + [SHAPE((rows, 128), F32)],
+        in_specs=[SMEM] + [VMEM] * (count + 4),
+        out_specs=[VMEM] * (len(widths) + 3),
+        out_shape=[SHAPE((width,), F32) for width in widths]
+        + [SHAPE(mine2.shape, F32), SHAPE((per, D), F32), SHAPE((per, D + 128), F32)],
         compiler_params=params(),
         cost_estimate=cost(0.6),
         name="last_sums",
-    )(*messages)
+    )(place, *messages, mine2, other2, mine3, other3)
 
 
 def local(
@@ -1072,50 +1087,48 @@
     come2 = to_owner(sum2)
 
     come3 = after(come3, theirs1, sum2)
-    sum3 = summed(parts3[0], *come3)
-    other3 = over_x(sum3)
-    mine4, come4 = after((mine4, come4), sum3)
+    mine4, come4 = after((mine4, come4), *come3)
     parts4 = message_cut(place, mine4, come4, lines, per1)
     come4 = [flipped(parts4[i], "seq", 2 * i) for i in range(1, depth)]
     mine1, come1 = after((mine1, come1), parts4[0])
     sum1 = summed(mine1, come1).reshape(per1 // 2, -1)
     other1 = over_x(sum1)
+    come3 = after(come3, sum1)
+    sum3 = summed(parts3[0], *come3)
+    other3 = over_x(sum3)
+    sum2, come2 = after((sum2, come2), sum3)
+    sum2 = summed(sum2, come2)
+    other2 = between_owners(sum2)
+    come4 = after(come4, sum2)
+    message = message_sum([parts4[0], *come4], lines)
+    got = [flipped(message, "batch", i) for i in range(1, batches)]
+
+    sum1, other1 = after((sum1, other1), message)
+    sum1 = pair(sum1, other1, xs, 0)
+    other1 = over_core(sum1)
     sum3, other3 = after((sum3, other3), sum1)
     sum3 = summed(sum3, other3)
     other3 = over_core(sum3)
-    sum2, come2 = after((sum2, come2), sum3)
-    sum2 = summed(sum2, come2)
-    other2 = over_x(sum2)
-    come4 = after(come4, sum2)
-    message = message_sum([parts4[0], *come4], lines)
-    got = [flipped(message, "batch", i) for i in range(1, batches)]
-    sum1, other1 = after((sum1, other1), message)
-
-    sum1 = pair(sum1, other1, xs, 0)
-    other1 = over_core(sum1)
-    sum2, other2 = after((sum2, other2), sum1)
+    sum2, other2 = after((sum2, other2), sum3)
     sum2 = pair(sum2, other2, xs, 0)
     other2 = over_core(sum2)
-    got = after(got, sum2)
+
+    (other1,) = after((other1,), sum2)
+    fc1_grad = pair(sum1, other1, core, 1).astype(F32)
+    got = after(got, fc1_grad)
     widths = (ff, D + 128) + (D,) * 5
-    b1_sum, qkv_sum, out_sum, gain1, bias1, gain2, bias2, kv_sum = last_sums([message, *got], lines, widths)
-
-    owner = (z >> (z_bits - 1)) == core
-    (other3,) = after((other3,), kv_sum)
-    both3 = pair(sum3, other3, core, 2).astype(F32)
-    (other1,) = after((other1,), both3)
-    fc1_grad = pair(sum1, other1, core, 1).astype(F32)
-    (other2,) = after((other2,), fc1_grad)
-    fc2_grad = jnp.where(owner, sum2, other2).astype(F32)
+    b1_sum, qkv_sum, out_sum, gain1, bias1, gain2, bias2, fc2_grad, out_grad, qkv_grad = last_sums(
+        place, [message, *got], lines, widths, z_bits - 1, sum2, other2, sum3, other3
+    )
     return (
         output.reshape(tokens.shape),
         kv3,
         tokens_grad.reshape(tokens.shape),
         gain1,
         bias1,
-        jnp.concatenate([both3[1], kv_sum], axis=1),
+        qkv_grad,
         qkv_sum,
-        both3[0],
+        out_grad,
         gain2,
         bias2,
         fc1_grad,

time: 160 us -> 156 us (0.975)
  local copies, waits for them, and re-layouts: 9.03 us -> 4.7 us
  starting transfers between devices: 42.9 us -> 45.4 us
  other arithmetic: 6 us -> 4.02 us
    ppermute x30 -> x29, waiting for transfers between devices: 7.3 us -> 3.27 us  [flipped(): lax.ppermute(block, axis, [(i, i ^ bits) for i in range(lax.axis_size(axi...]
    unnamed x62 -> x48, local copies, waits for them, and re-layouts: 8.27 us -> 4.7 us
    ppermute x0 -> x1, starting transfers between devices: none -> 2.15 us  [between_owners(): return lax.ppermute(block, ('batch', 'seq'), route)]
    ppermute x30 -> x29, starting transfers between devices: 32 us -> 32.2 us  [flipped(): lax.ppermute(block, axis, [(i, i ^ bits) for i in range(lax.axis_size(axi...]
  transfers between devices with their start and end apart: 37 -> 37, of which waited for: 5 -> 8; matrix products, arithmetic and copies ran while one was open for 4% -> 3% of each run, Pallas kernels for 58% -> 58%
where the time goes in v5:
time: 156 us; the launch traced here: 155 us
  Pallas kernels  93.4 us (60%)
  starting transfers between devices  45.4 us (29%)
  waiting for transfers between devices  6.93 us (4%)
  local copies, waits for them, and re-layouts  4.7 us (3%)
  other arithmetic  4.02 us (3%)
    ppermute x29, starting transfers between devices, flipped(): lax.ppermute(block, axis, [(i, i ^ bits) for i in range(lax.axis_size(axi...  32.2 us
    pallas_call x1, Pallas kernels, feed(): pl.pallas_call(feed_kernel, grid_spec=spec, out_shape=[SHAPE((rows, D), B...  28.6 us
    pallas_call x1, Pallas kernels, attention(): pl.pallas_call(kernel, grid=(seqs, PAIRS // groups), in_specs=[SMEM] + [t...  24.8 us
    ppermute x6, starting transfers between devices, along(): lax.ppermute(block, 'seq', [(i, (i + 2 * distance) % size) for i in range...  9.76 us
    pallas_call x1, Pallas kernels, weights(): pl.pallas_call(weights_kernel, grid_spec=pltpu.PrefetchScalarGridSpec(num...  6.04 us
    pallas_call x1, Pallas kernels, finish(): pl.pallas_call(functools.partial(finish_kernel, rows // tables.shape[1],...  5.9 us
    unnamed x48, local copies, waits for them, and re-layouts  4.7 us
    pallas_call x1, Pallas kernels, add_split(): pl.pallas_call(kernel, in_specs=[SMEM] + [VMEM] * len(arrays), out_specs=...  4.3 us
  transfers between devices with their start and end apart: 37, of which 8 were waited for; matrix products, arithmetic and copies ran while one was open for 3% of the time, Pallas kernels for 58%

profile of v5, /device:TPU:0, one launch (start us, length us, event | category | flops | bytes accessed | tf_op | source)
XLA Modules:
  0.0 155.5 jit_solution(15135983934269898110)
XLA Ops:
  1.2 1.0 fusion.2.tables_ref.refs_6_.refs_14_
  2.2 2.9 %project_keys.1 = (bf16[512,128]{1,0:T(8,128)(2,1)}, bf16[512,768]{1,0:T(8,128)(2,1)}) custom-call(bf16[512,768]{1,0:T(8,128)(2,1)} %bitcast.50, f32[768]{0:T(1024)} %refs_10_.1, f32[768]{0:T(1024)} %refs_11_.1, bf16[768,896]{1,0:T(8,128)(2,1)} %refs_13_.1, f32[896]{0:T(1024)} %add_ref.4, f32[3,128,128]{2,1,0:T(8,128)} %fusion.2.tables_ref.refs_6_.refs_14_), custom_call_target="tpu_custom_call" | custom-call | flops 3000000000 | tf_op jit(solution)/shard_map/project_keys/pallas_call | solution.py:254
  5.1 2.6 %collective-permute-start = (bf16[4,128,128]{2,1,0:T(8,128)(2,1)}, bf16[4,128,128]{2,1,0:T(8,128)(2,1)S(1)}, u32[]{:S(2)}, u32[]{:S(2)}) collective-permute-start(bf16[4,128,128]{2,1,0:T(8,128)(2,1)} %bitcast.40), channel_id=1, source_target_pairs={{0,1},{1,0},{2,3},{3,2},{4,5},{5,4},{6,7},{7,6},{8,9},{9,8},{10,11... | collective-permute-start | bytes 393224 | tf_op jit(solution)/shard_map/ppermute | solution.py:42
  8.2 4.1 %project_queries.1 = bf16[512,768]{1,0:T(8,128)(2,1)} custom-call(bf16[512,768]{1,0:T(8,128)(2,1)} %get-tuple-element.118.first_ref.in_ref, bf16[768,896]{1,0:T(8,128)(2,1)} %refs_13_.1, f32[896]{0:T(1024)} %add_ref.4, f32[3,128,128]{2,1,0:T(8,128)} %fusion.2.tables_ref.refs_6_.refs_14_), custom_call_target="tpu_custom_call" | custom-call | flops 6000000000 | tf_op jit(solution)/shard_map/project_queries/pallas_call | solution.py:276
  12.9 1.6 %collective-permute-start.1 = (bf16[2,4,128,128]{3,2,1,0:T(8,128)(2,1)S(1)}, bf16[2,4,128,128]{3,2,1,0:T(8,128)(2,1)S(1)}, u32[]{:S(2)}, u32[]{:S(2)}) collective-permute-start(bf16[2,4,128,128]{3,2,1,0:T(8,128)(2,1)S(1)} %pad_maximum_fusion.2.refs_0_), channel_id=1, source_target_pairs={{0,2},{1,3},{2,4},{3,5},{4,6},{5,7},{6,0},{7,1},{8,10},{9,11},{10,... | collective-permute-start | bytes 786440 | tf_op jit(solution)/shard_map/ppermute | solution.py:47
  14.6 2.6 %collective-permute-start.2 = (bf16[2,4,128,128]{3,2,1,0:T(8,128)(2,1)S(1)}, bf16[2,4,128,128]{3,2,1,0:T(8,128)(2,1)S(1)}, u32[]{:S(2)}, u32[]{:S(2)}) collective-permute-start(bf16[2,4,128,128]{3,2,1,0:T(8,128)(2,1)S(1)} %pad_maximum_fusion.2.refs_0_), channel_id=1, source_target_pairs={{0,4},{1,5},{2,6},{3,7},{4,0},{5,1},{6,2},{7,3},{8,12},{9,13},{10,... | collective-permute-start | bytes 786440 | tf_op jit(solution)/shard_map/ppermute | solution.py:47
  17.1 1.3 collective-permute-start.3
  18.5 28.6 %feed_forward.1 = (bf16[512,768]{1,0:T(8,128)(2,1)}, bf16[512,768]{1,0:T(8,128)(2,1)}, bf16[2,512,768]{2,1,0:T(8,128)(2,1)}, bf16[512,768]{1,0:T(8,128)(2,1)}, f...) custom-call(s32[4]{0:T(128)} %pad_add_fusion.place_ref, ...), custom_call_target="tpu_custom_call" | custom-call | flops 35999997952 | tf_op jit(solution)/shard_map/feed_forward/pallas_call | solution.py:438
  47.2 0.7 collective-permute-start.10
  47.9 1.5 collective-permute-start.9
  49.4 0.7 copy-done.15
  50.2 24.8 %attention.1 = (bf16[2,4,128,768]{3,2,1,0:T(8,128)(2,1)}, bf16[4,4,128,128]{3,2,1,0:T(8,128)(2,1)}, bf16[4,4,128,128]{3,2,1,0:T(8,128)(2,1)}) custom-call(s32[4]{0:T(128)} %pad_add_fusion.place_ref, bf16[2,4,128,128]{3,2,1,0:T(8,128)(2,1)} %copy-done.4, bf16[2,4,128,128]{3,2,1,0:T(8,128)(2,1)} %copy-done.14, bf16[2,4,128,128]{3,2,1,0:T(8,128)(2,1)} %copy-done.15, ...), custom_call_target="tpu_custom_call" | custom-call | flops 30000001024 | tf_op jit(solution)/shard_map/attention/pallas_call | solution.py:696
  75.0 0.9 collective-permute-start.7
  76.3 4.3 %add_split.1 = (bf16[2,96,1536]{2,1,0:T(8,128)(2,1)}, bf16[2,96,1536]{2,1,0:T(8,128)(2,1)}, bf16[2,192,768]{2,1,0:T(8,128)(2,1)}, bf16[2,192,768]{2,1,0:T(8,128)(2,1)}) custom-call(s32[4]{0:T(128)} %pad_add_fusion.place_ref, bf16[2,2,96,1536]{3,2,1,0:T(8,128)(2,1)} %bitcast.61, bf16[2,2,96,1536]{3,2,1,0:T(8,128)(2,1)} %bitcast.14.refs_1_, ...), custom_call_target="tpu_custom_call" | custom-call | flops 17999998976 | tf_op jit(solution)/shard_map/add_split/pallas_call | solution.py:143
  80.6 1.3 collective-permute-start.16
  81.9 1.5 collective-permute-start.17
  83.4 6.0 %weights.1 = (bf16[2,4,96,384]{3,2,1,0:T(8,128)(2,1)}, bf16[2,4,96,384]{3,2,1,0:T(8,128)(2,1)}, f32[8,768]{1,0:T(8,128)}) custom-call(s32[4]{0:T(128)} %pad_add_fusion.place_ref, bf16[2,512,768]{2,1,0:T(8,128)(2,1)} %bitcast.45, bf16[2,512,768]{2,1,0:T(8,128)(2,1)} %copy-done.9, bf16[512,768]{1,0:T(8,128)(2,1)} %bitcast.55, ...), custom_call_target="tpu_custom_call" | custom-call | flops 7200000000 | tf_op jit(solution)/shard_map/weights/pallas_call | solution.py:741
  89.5 0.9 collective-permute-start.15
  90.4 0.8 add_convert_fusion.4
  91.5 1.1 collective-permute-start.14
  92.6 3.7 %mix.1 = bf16[512,768]{1,0:T(8,128)(2,1)} custom-call(bf16[512,768]{1,0:T(8,128)(2,1)} %bitcast.52, bf16[512,768]{1,0:T(8,128)(2,1)} %get-tuple-element.146.mlp_ref, bf16[2,512,768]{2,1,0:T(8,128)(2,1)} %collective-permute-done.11.mlp2_ref.refs_9_, bf16[2,512,768]{2,1,0:T(8,128)(2,1)} %bitcast.47, f32[768]{0:T(1024)} %add_ref.5, bf16[768,768]{1,0:T(8,128)(2,1)} %wo_ref.3), custom_call_target="tpu_custom_call" | custom-call | flops 3600000000 | tf_op jit(solution)/shard_map/mix/pallas_call | solution.py:767
  96.3 1.8 %collective-permute-done.16 = bf16[2,96,1536]{2,1,0:T(8,128)(2,1)S(1)} collective-permute-done((bf16[2,96,1536]{2,1,0:T(8,128)(2,1)}, bf16[2,96,1536]{2,1,0:T(8,128)(2,1)S(1)}, u32[]{:S(2)}, u32[]{:S(2)}) %collective-permute-start.16) | collective-permute-done | bytes 589856 | tf_op jit(solution)/shard_map/ppermute | solution.py:42
  98.1 2.8 %collective-permute-start.12 = (bf16[4,128,128]{2,1,0:T(8,128)(2,1)S(1)}, bf16[4,128,128]{2,1,0:T(8,128)(2,1)}, u32[]{:S(2)}, u32[]{:S(2)}) collective-permute-start(bf16[4,128,128]{2,1,0:T(8,128)(2,1)S(1)} %get-tuple-element.148), channel_id=1, source_target_pairs={{0,6},{1,7},{2,0},{3,1},{4,2},{5,3},{6,4},{7,5},{8,14},{9,15},{10,... | collective-permute-start | bytes 393224 | tf_op jit(solution)/shard_map/ppermute | solution.py:47
  100.9 2.7 %exchange_split.1 = (bf16[768,384]{1,0:T(8,128)(2,1)}, bf16[2,48,1536]{2,1,0:T(8,128)(2,1)}, bf16[1,192,768]{2,1,0:T(8,128)(2,1)}) custom-call(s32[4]{0:T(128)} %pad_add_fusion.place_ref, bf16[2,2,48,1536]{3,2,1,0:T(8,128)(2,1)} %bitcast.67, bf16[2,2,48,1536]{3,2,1,0:T(8,128)(2,1)} %bitcast.58, bf16[1,2,192,768]{3,2,1,0:T(8,128)(2,1)} %bitcast.68, ...), custom_call_target="tpu_custom_call" | custom-call | flops 3600000000 | tf_op jit(solution)/shard_map/exchange_split/pallas_call | solution.py:170
  103.7 0.8 collective-permute-start.22
  105.0 2.1 %add_cut.1 = (bf16[2,96,384]{2,1,0:T(8,128)(2,1)}, bf16[2,96,384]{2,1,0:T(8,128)(2,1)}, bf16[2,96,384]{2,1,0:T(8,128)(2,1)}, bf16[2,96,384]{2,1,0:T(8,128)(2,1)}) custom-call(s32[4]{0:T(128)} %pad_add_fusion.place_ref, bf16[2,4,96,384]{3,2,1,0:T(8,128)(2,1)} %get-tuple-element.158.a_ref, bf16[2,4,96,384]{3,2,1,0:T(8,128)(2,1)} %collective-permute-done.15.b_ref), custom_call_target="tpu_custom_call" | custom-call | flops 3600000000 | tf_op jit(solution)/shard_map/add_cut/pallas_call | solution.py:222
  107.2 1.0 collective-permute-start.19
  108.4 3.2 %collective-permute-start.21 = (bf16[2,96,384]{2,1,0:T(8,128)(2,1)}, bf16[2,96,384]{2,1,0:T(8,128)(2,1)S(1)}, u32[]{:S(2)}, u32[]{:S(2)}) collective-permute-start(bf16[2,96,384]{2,1,0:T(8,128)(2,1)} %get-tuple-element.172), channel_id=1, source_target_pairs={{0,6},{1,7},{2,4},{3,5},{4,2},{5,3},{6,0},{7,1},{8,14},{9,15},{10,... | collective-permute-start | bytes 442376 | tf_op jit(solution)/shard_map/ppermute | solution.py:42
  111.6 5.9 %finish.1 = (bf16[512,768]{1,0:T(8,128)(2,1)}, bf16[512,128]{1,0:T(8,128)(2,1)}, bf16[512,128]{1,0:T(8,128)(2,1)}) custom-call(s32[4]{0:T(128)} %pad_add_fusion.place_ref, bf16[512,128]{1,0:T(8,128)(2,1)} %bitcast.39, bf16[512,128]{1,0:T(8,128)(2,1)} %bitcast.26.refs_1_, bf16[512,128]{1,0:T(8,128)(2,1)} %bitcast.27.refs_2_, ...), custom_call_target="tpu_custom_call" | custom-call | flops 7200000000 | tf_op jit(solution)/shard_map/finish/pallas_call | solution.py:861
  117.5 0.7 collective-permute-start.18
  118.3 0.8 copy-done
  119.1 2.2 %exchange_add.1 = (bf16[1,48,1536]{2,1,0:T(8,128)(2,1)}, bf16[1,48,1536]{2,1,0:T(8,128)(2,1)}, bf16[1,192,768]{2,1,0:T(8,128)(2,1)}) custom-call(s32[4]{0:T(128)} %pad_add_fusion.place_ref, bf16[2,48,1536]{2,1,0:T(8,128)(2,1)} %get-tuple-element.175.a1, bf16[1,192,768]{2,1,0:T(8,128)(2,1)} %get-tuple-element.176.a2, bf16[768,384]{1,0:T(8,128)(2,1)} %copy-done), custom_call_target="tpu_custom_call" | custom-call | flops 30000000 | tf_op jit(solution)/shard_map/exchange_add/pallas_call | solution.py:202
  121.3 1.3 collective-permute-start.26
  122.7 0.7 copy-done.17
  123.4 1.7 %message_cut.1 = (bf16[224,128]{1,0:T(8,128)(2,1)}, bf16[224,128]{1,0:T(8,128)(2,1)}, bf16[224,128]{1,0:T(8,128)(2,1)}, bf16[224,128]{1,0:T(8,128)(2,1)}) custom-call(s32[4]{0:T(128)} %pad_add_fusion.place_ref, bf16[512,128]{1,0:T(8,128)(2,1)} %get-tuple-element.183.a_ref, bf16[512,128]{1,0:T(8,128)(2,1)} %copy-done.17), custom_call_target="tpu_custom_call" | custom-call | flops 1800000000 | tf_op jit(solution)/shard_map/message_cut/pallas_call | solution.py:895
  125.1 1.3 collective-permute-start.23
  126.4 3.6 %collective-permute-start.24 = (bf16[224,128]{1,0:T(8,128)(2,1)}, bf16[224,128]{1,0:T(8,128)(2,1)S(1)}, u32[]{:S(2)}, u32[]{:S(2)}) collective-permute-start(bf16[224,128]{1,0:T(8,128)(2,1)} %get-tuple-element.187), channel_id=1, source_target_pairs={{0,4},{1,5},{2,6},{3,7},{4,0},{5,1},{6,2},{7,3},{8,12},{9,13},{10,... | collective-permute-start | bytes 172040 | tf_op jit(solution)/shard_map/ppermute | solution.py:42
  130.1 6.2 %collective-permute-start.31 = (bf16[48,1536]{1,0:T(8,128)(2,1)S(1)}, bf16[48,1536]{1,0:T(8,128)(2,1)S(1)}, u32[]{:S(2)}, u32[]{:S(2)}) collective-permute-start(bf16[48,1536]{1,0:T(8,128)(2,1)S(1)} %fusion.9), channel_id=1, source_target_pairs={{0,16},{8,24},{16,0},{24,8},{1,17},{9,25},{17,1},{25,9},{2,18},{10... | collective-permute-start | bytes 442376 | tf_op jit(solution)/shard_map/ppermute | solution.py:42
  136.3 2.1 %collective-permute-done.26 = bf16[192,768]{1,0:T(8,128)(2,1)S(1)} collective-permute-done((bf16[192,768]{1,0:T(8,128)(2,1)}, bf16[192,768]{1,0:T(8,128)(2,1)S(1)}, u32[]{:S(2)}, u32[]{:S(2)}) %collective-permute-start.26) | collective-permute-done | bytes 294944 | tf_op jit(solution)/shard_map/ppermute | solution.py:57
  138.4 1.8 %collective-permute-start.34 = (bf16[2,96,384]{2,1,0:T(8,128)(2,1)S(1)}, bf16[2,96,384]{2,1,0:T(8,128)(2,1)S(1)}, u32[]{:S(2)}, u32[]{:S(2)}) collective-permute-start(bf16[2,96,384]{2,1,0:T(8,128)(2,1)S(1)} %add_convert_fusion.2), channel_id=1, source_target_pairs={{0,16},{8,24},{16,0},{24,8},{1,17},{9,25},{17,1},{25,9},{2,18},{10... | collective-permute-start | bytes 442376 | tf_op jit(solution)/shard_map/ppermute | solution.py:42
  140.3 2.2 %collective-permute-start.33 = (bf16[192,768]{1,0:T(8,128)(2,1)S(1)}, bf16[192,768]{1,0:T(8,128)(2,1)S(1)}, u32[]{:S(2)}, u32[]{:S(2)}) collective-permute-start(bf16[192,768]{1,0:T(8,128)(2,1)S(1)} %add_convert_fusion), channel_id=1, source_target_pairs={{0,16},{1,17},{2,18},{3,19},{12,28},{13,29},{14,30},{15,31},{16,0}... | collective-permute-start | bytes 884744 | tf_op jit(solution)/shard_map/ppermute | solution.py:63
  143.1 0.6 copy-done.23
  143.7 1.6 %message_sum.1.refs_0_ = bf16[224,128]{1,0:T(8,128)(2,1)} custom-call(bf16[224,128]{1,0:T(8,128)(2,1)} %get-tuple-element.185.refs_0_, bf16[224,128]{1,0:T(8,128)(2,1)} %copy-done.21, bf16[224,128]{1,0:T(8,128)(2,1)} %copy-done.22, bf16[224,128]{1,0:T(8,128)(2,1)} %copy-done.23), custom_call_target="tpu_custom_call" | custom-call | flops 1800000000 | tf_op jit(solution)/shard_map/message_sum/pallas_call | solution.py:916
  145.3 1.8 %collective-permute-start.29 = (bf16[224,128]{1,0:T(8,128)(2,1)}, bf16[224,128]{1,0:T(8,128)(2,1)S(1)}, u32[]{:S(2)}, u32[]{:S(2)}) collective-permute-start(bf16[224,128]{1,0:T(8,128)(2,1)} %message_sum.1.refs_0_), channel_id=1, source_target_pairs={{0,16},{8,24},{16,0},{24,8},{1,17},{9,25},{17,1},{25,9},{2,18},{10... | collective-permute-start | bytes 172040 | tf_op jit(solution)/shard_map/ppermute | solution.py:42
  147.6 1.5 collective-permute-done.33
  149.9 1.1 maximum_convert_fusion
  151.9 0.8 copy-done.13
  152.7 2.8 %last_sums.1 = (f32[3072]{0:T(1024)}, f32[896]{0:T(1024)}, f32[768]{0:T(1024)}, f32[768]{0:T(1024)}, f32[768]{0:T(1024)}, /*index=5*/f32[768]{0:T(1024)}, f32[76...) custom-call(s32[4]{0:T(128)} %pad_add_fusion.place_ref, bf16[224,128]{1,0:T(8,128)(2,1)} %message_sum.1.refs_0_, ...), custom_call_target="tpu_custom_call" | custom-call | flops 1800000000 | tf_op jit(solution)/shard_map/last_sums/pallas_call | solution.py:951
  (106 shorter events, 6.4 us)
Async XLA Ops:
  0.6 17.9 %collective-permute-start.5 = (bf16[512,768]{1,0:T(8,128)(2,1)}, bf16[512,768]{1,0:T(8,128)(2,1)}, u32[]{:S(2)}, u32[]{:S(2)}) collective-permute-start(bf16[512,768]{1,0:T(8,128)(2,1)} %bitcast.49), channel_id=1, source_target_pairs={{0,8},{8,0},{16,24},{24,16},{1,9},{9,1},{17,25},{25,17},{2,10},{10... | collective-permute-start | bytes 2359304 | tf_op jit(solution)/shard_map/ppermute | solution.py:42
  2.2 5.6 %copy-start.10 = (bf16[4,128,768]{2,1,0:T(8,128)(2,1)S(1)}, bf16[4,128,768]{2,1,0:T(8,128)(2,1)}, u32[]{:S(2)}) copy-start(bf16[4,128,768]{2,1,0:T(8,128)(2,1)} %param.26) | copy-start | bytes 2359300
  5.1 7.8 %collective-permute-start = (bf16[4,128,128]{2,1,0:T(8,128)(2,1)}, bf16[4,128,128]{2,1,0:T(8,128)(2,1)S(1)}, u32[]{:S(2)}, u32[]{:S(2)}) collective-permute-start(bf16[4,128,128]{2,1,0:T(8,128)(2,1)} %bitcast.40), channel_id=1, source_target_pairs={{0,1},{1,0},{2,3},{3,2},{4,5},{5,4},{6,7},{7,6},{8,9},{9,8},{10,11... | collective-permute-start | bytes 393224 | tf_op jit(solution)/shard_map/ppermute | solution.py:42
  7.7 9.5 %collective-permute-start.4 = (bf16[512,768]{1,0:T(8,128)(2,1)}, bf16[512,768]{1,0:T(8,128)(2,1)S(1)}, u32[]{:S(2)}, u32[]{:S(2)}) collective-permute-start(bf16[512,768]{1,0:T(8,128)(2,1)} %get-tuple-element.118.first_ref.in_ref), channel_id=1, source_target_pairs={{0,8},{8,0},{16,24},{24,16},{1,9},{9,1},{17,25},{25,17},{2,10},{10... | collective-permute-start | bytes 2359304 | tf_op jit(solution)/shard_map/ppermute | solution.py:42
  7.9 5.0 %copy-start.8 = (bf16[512,128]{1,0:T(8,128)(2,1)S(1)}, bf16[512,128]{1,0:T(8,128)(2,1)}, u32[]{:S(2)}) copy-start(bf16[512,128]{1,0:T(8,128)(2,1)} %get-tuple-element.117) | copy-start | bytes 393220
  7.9 10.6 %collective-permute-start.6 = (bf16[512,768]{1,0:T(8,128)(2,1)S(1)}, bf16[512,768]{1,0:T(8,128)(2,1)}, u32[]{:S(2)}, u32[]{:S(2)}) collective-permute-start(bf16[512,768]{1,0:T(8,128)(2,1)S(1)} %bitcast.57), channel_id=1, source_target_pairs={{0,8},{8,0},{16,24},{24,16},{1,9},{9,1},{17,25},{25,17},{2,10},{10... | collective-permute-start | bytes 2359304 | tf_op jit(solution)/shard_map/ppermute | solution.py:42
  12.9 34.2 %copy-start.4 = (bf16[2,4,128,128]{3,2,1,0:T(8,128)(2,1)}, bf16[2,4,128,128]{3,2,1,0:T(8,128)(2,1)S(1)}, u32[]{:S(2)}) copy-start(bf16[2,4,128,128]{3,2,1,0:T(8,128)(2,1)S(1)} %pad_maximum_fusion.2.refs_0_) | copy-start | bytes 786436
  12.9 35.0 %collective-permute-start.1 = (bf16[2,4,128,128]{3,2,1,0:T(8,128)(2,1)S(1)}, bf16[2,4,128,128]{3,2,1,0:T(8,128)(2,1)S(1)}, u32[]{:S(2)}, u32[]{:S(2)}) collective-permute-start(bf16[2,4,128,128]{3,2,1,0:T(8,128)(2,1)S(1)} %pad_maximum_fusion.2.refs_0_), channel_id=1, source_target_pairs={{0,2},{1,3},{2,4},{3,5},{4,6},{5,7},{6,0},{7,1},{8,10},{9,11},{10,... | collective-permute-start | bytes 786440 | tf_op jit(solution)/shard_map/ppermute | solution.py:47
  14.6 34.9 %collective-permute-start.2 = (bf16[2,4,128,128]{3,2,1,0:T(8,128)(2,1)S(1)}, bf16[2,4,128,128]{3,2,1,0:T(8,128)(2,1)S(1)}, u32[]{:S(2)}, u32[]{:S(2)}) collective-permute-start(bf16[2,4,128,128]{3,2,1,0:T(8,128)(2,1)S(1)} %pad_maximum_fusion.2.refs_0_), channel_id=1, source_target_pairs={{0,4},{1,5},{2,6},{3,7},{4,0},{5,1},{6,2},{7,3},{8,12},{9,13},{10,... | collective-permute-start | bytes 786440 | tf_op jit(solution)/shard_map/ppermute | solution.py:47
  17.1 32.3 %collective-permute-start.3 = (bf16[2,4,128,128]{3,2,1,0:T(8,128)(2,1)S(1)}, bf16[2,4,128,128]{3,2,1,0:T(8,128)(2,1)}, u32[]{:S(2)}, u32[]{:S(2)}) collective-permute-start(bf16[2,4,128,128]{3,2,1,0:T(8,128)(2,1)S(1)} %pad_maximum_fusion.2.refs_0_), channel_id=1, source_target_pairs={{0,6},{1,7},{2,0},{3,1},{4,2},{5,3},{6,4},{7,5},{8,14},{9,15},{10,... | collective-permute-start | bytes 786440 | tf_op jit(solution)/shard_map/ppermute | solution.py:47
  47.1 29.2 %collective-permute-start.11 = (bf16[2,512,768]{2,1,0:T(8,128)(2,1)}, bf16[2,512,768]{2,1,0:T(8,128)(2,1)}, u32[]{:S(2)}, u32[]{:S(2)}) collective-permute-start(bf16[2,512,768]{2,1,0:T(8,128)(2,1)} %get-tuple-element.135), channel_id=1, source_target_pairs={{0,8},{8,0},{16,24},{24,16},{1,9},{9,1},{17,25},{25,17},{2,10},{10... | collective-permute-start | bytes 4718600 | tf_op jit(solution)/shard_map/ppermute | solution.py:42
  47.2 28.8 %collective-permute-start.10 = (bf16[768,768]{1,0:T(8,128)(2,1)}, bf16[768,768]{1,0:T(8,128)(2,1)}, u32[]{:S(2)}, u32[]{:S(2)}) collective-permute-start(bf16[768,768]{1,0:T(8,128)(2,1)} %get-tuple-element.134), channel_id=1, source_target_pairs={{0,2},{1,3},{2,0},{3,1},{4,6},{5,7},{6,4},{7,5},{8,10},{9,11},{10,... | collective-permute-start | bytes 3538952 | tf_op jit(solution)/shard_map/ppermute | solution.py:42
  47.9 28.4 %collective-permute-start.9 = (bf16[8,48,1536]{2,1,0:T(8,128)(2,1)}, bf16[8,48,1536]{2,1,0:T(8,128)(2,1)}, u32[]{:S(2)}, u32[]{:S(2)}) collective-permute-start(bf16[8,48,1536]{2,1,0:T(8,128)(2,1)} %get-tuple-element.132), channel_id=1, source_target_pairs={{0,16},{8,24},{16,0},{24,8},{1,17},{9,25},{17,1},{25,9},{2,18},{10... | collective-permute-start | bytes 3538952 | tf_op jit(solution)/shard_map/ppermute | solution.py:42
  75.0 6.9 %collective-permute-start.8 = (bf16[2,512,768]{2,1,0:T(8,128)(2,1)}, bf16[2,512,768]{2,1,0:T(8,128)(2,1)S(1)}, u32[]{:S(2)}, u32[]{:S(2)}) collective-permute-start(bf16[2,512,768]{2,1,0:T(8,128)(2,1)} %bitcast.44), channel_id=1, source_target_pairs={{0,8},{8,0},{16,24},{24,16},{1,9},{9,1},{17,25},{25,17},{2,10},{10... | collective-permute-start | bytes 4718600 | tf_op jit(solution)/shard_map/ppermute | solution.py:42
  75.0 15.4 %collective-permute-start.7 = (bf16[4,4,128,128]{3,2,1,0:T(8,128)(2,1)}, bf16[4,4,128,128]{3,2,1,0:T(8,128)(2,1)S(1)}, u32[]{:S(2)}, u32[]{:S(2)}) collective-permute-start(bf16[4,4,128,128]{3,2,1,0:T(8,128)(2,1)} %get-tuple-element.129), channel_id=1, source_target_pairs={{0,1},{1,0},{2,3},{3,2},{4,5},{5,4},{6,7},{7,6},{8,9},{9,8},{10,11... | collective-permute-start | bytes 1572872 | tf_op jit(solution)/shard_map/ppermute | solution.py:42
  80.6 17.6 %collective-permute-start.16 = (bf16[2,96,1536]{2,1,0:T(8,128)(2,1)}, bf16[2,96,1536]{2,1,0:T(8,128)(2,1)S(1)}, u32[]{:S(2)}, u32[]{:S(2)}) collective-permute-start(bf16[2,96,1536]{2,1,0:T(8,128)(2,1)} %get-tuple-element.140), channel_id=1, source_target_pairs={{0,2},{1,3},{2,0},{3,1},{4,6},{5,7},{6,4},{7,5},{8,10},{9,11},{10,... | collective-permute-start | bytes 1769480 | tf_op jit(solution)/shard_map/ppermute | solution.py:42
  81.9 8.5 %copy-start.2 = (bf16[4,4,128,128]{3,2,1,0:T(8,128)(2,1)S(1)}, bf16[4,4,128,128]{3,2,1,0:T(8,128)(2,1)}, u32[]{:S(2)}) copy-start(bf16[4,4,128,128]{3,2,1,0:T(8,128)(2,1)} %get-tuple-element.143) | copy-start | bytes 1572868
  81.9 19.0 %collective-permute-start.17 = (bf16[2,192,768]{2,1,0:T(8,128)(2,1)}, bf16[2,192,768]{2,1,0:T(8,128)(2,1)}, u32[]{:S(2)}, u32[]{:S(2)}) collective-permute-start(bf16[2,192,768]{2,1,0:T(8,128)(2,1)} %get-tuple-element.152), channel_id=1, source_target_pairs={{0,16},{8,24},{16,0},{24,8},{1,17},{9,25},{17,1},{25,9},{2,18},{10... | collective-permute-start | bytes 1769480 | tf_op jit(solution)/shard_map/ppermute | solution.py:42
  89.5 15.5 %collective-permute-start.15 = (bf16[2,4,96,384]{3,2,1,0:T(8,128)(2,1)}, bf16[2,4,96,384]{3,2,1,0:T(8,128)(2,1)}, u32[]{:S(2)}, u32[]{:S(2)}) collective-permute-start(bf16[2,4,96,384]{3,2,1,0:T(8,128)(2,1)} %get-tuple-element.142), channel_id=1, source_target_pairs={{0,1},{1,0},{2,3},{3,2},{4,5},{5,4},{6,7},{7,6},{8,9},{9,8},{10,11... | collective-permute-start | bytes 1769480 | tf_op jit(solution)/shard_map/ppermute | solution.py:42
  91.2 15.9 %collective-permute-start.13 = (bf16[4,128,128]{2,1,0:T(8,128)(2,1)S(1)}, bf16[4,128,128]{2,1,0:T(8,128)(2,1)}, u32[]{:S(2)}, u32[]{:S(2)}) collective-permute-start(bf16[4,128,128]{2,1,0:T(8,128)(2,1)S(1)} %get-tuple-element.222), channel_id=1, source_target_pairs={{0,4},{1,5},{2,6},{3,7},{4,0},{5,1},{6,2},{7,3},{8,12},{9,13},{10,... | collective-permute-start | bytes 393224 | tf_op jit(solution)/shard_map/ppermute | solution.py:47
  91.5 15.6 %collective-permute-start.14 = (bf16[4,128,128]{2,1,0:T(8,128)(2,1)S(1)}, bf16[4,128,128]{2,1,0:T(8,128)(2,1)}, u32[]{:S(2)}, u32[]{:S(2)}) collective-permute-start(bf16[4,128,128]{2,1,0:T(8,128)(2,1)S(1)} %get-tuple-element.221), channel_id=1, source_target_pairs={{0,2},{1,3},{2,4},{3,5},{4,6},{5,7},{6,0},{7,1},{8,10},{9,11},{10,... | collective-permute-start | bytes 393224 | tf_op jit(solution)/shard_map/ppermute | solution.py:47
  98.1 2.8 %copy-start.12 = (bf16[2,96,1536]{2,1,0:T(8,128)(2,1)}, bf16[2,96,1536]{2,1,0:T(8,128)(2,1)S(1)}, u32[]{:S(2)}) copy-start(bf16[2,96,1536]{2,1,0:T(8,128)(2,1)S(1)} %collective-permute-done.16) | copy-start | bytes 1769476
  98.1 9.0 %collective-permute-start.12 = (bf16[4,128,128]{2,1,0:T(8,128)(2,1)S(1)}, bf16[4,128,128]{2,1,0:T(8,128)(2,1)}, u32[]{:S(2)}, u32[]{:S(2)}) collective-permute-start(bf16[4,128,128]{2,1,0:T(8,128)(2,1)S(1)} %get-tuple-element.148), channel_id=1, source_target_pairs={{0,6},{1,7},{2,0},{3,1},{4,2},{5,3},{6,4},{7,5},{8,14},{9,15},{10,... | collective-permute-start | bytes 393224 | tf_op jit(solution)/shard_map/ppermute | solution.py:47
  103.7 14.6 %collective-permute-start.22 = (bf16[768,384]{1,0:T(8,128)(2,1)}, bf16[768,384]{1,0:T(8,128)(2,1)S(1)}, u32[]{:S(2)}, u32[]{:S(2)}) collective-permute-start(bf16[768,384]{1,0:T(8,128)(2,1)} %get-tuple-element.157), channel_id=1, source_target_pairs={{0,1},{1,0},{2,3},{3,2},{4,5},{5,4},{6,7},{7,6},{8,9},{9,8},{10,11... | collective-permute-start | bytes 1769480 | tf_op jit(solution)/shard_map/ppermute | solution.py:42
  107.2 14.1 %collective-permute-start.19 = (bf16[2,96,384]{2,1,0:T(8,128)(2,1)}, bf16[2,96,384]{2,1,0:T(8,128)(2,1)S(1)}, u32[]{:S(2)}, u32[]{:S(2)}) collective-permute-start(bf16[2,96,384]{2,1,0:T(8,128)(2,1)} %get-tuple-element.170), channel_id=1, source_target_pairs={{0,2},{1,3},{2,0},{3,1},{4,6},{5,7},{6,4},{7,5},{8,10},{9,11},{10,... | collective-permute-start | bytes 442376 | tf_op jit(solution)/shard_map/ppermute | solution.py:42
  108.1 14.4 %collective-permute-start.20 = (bf16[2,96,384]{2,1,0:T(8,128)(2,1)}, bf16[2,96,384]{2,1,0:T(8,128)(2,1)S(1)}, u32[]{:S(2)}, u32[]{:S(2)}) collective-permute-start(bf16[2,96,384]{2,1,0:T(8,128)(2,1)} %get-tuple-element.171), channel_id=1, source_target_pairs={{0,4},{1,5},{2,6},{3,7},{4,0},{5,1},{6,2},{7,3},{8,12},{9,13},{10,... | collective-permute-start | bytes 442376 | tf_op jit(solution)/shard_map/ppermute | solution.py:42
  108.4 14.2 %collective-permute-start.21 = (bf16[2,96,384]{2,1,0:T(8,128)(2,1)}, bf16[2,96,384]{2,1,0:T(8,128)(2,1)S(1)}, u32[]{:S(2)}, u32[]{:S(2)}) collective-permute-start(bf16[2,96,384]{2,1,0:T(8,128)(2,1)} %get-tuple-element.172), channel_id=1, source_target_pairs={{0,6},{1,7},{2,4},{3,5},{4,2},{5,3},{6,0},{7,1},{8,14},{9,15},{10,... | collective-permute-start | bytes 442376 | tf_op jit(solution)/shard_map/ppermute | solution.py:42
  117.5 5.2 %collective-permute-start.18 = (bf16[512,128]{1,0:T(8,128)(2,1)}, bf16[512,128]{1,0:T(8,128)(2,1)S(1)}, u32[]{:S(2)}, u32[]{:S(2)}) collective-permute-start(bf16[512,128]{1,0:T(8,128)(2,1)} %get-tuple-element.169), channel_id=1, source_target_pairs={{0,1},{1,0},{2,3},{3,2},{4,5},{5,4},{6,7},{7,6},{8,9},{9,8},{10,11... | collective-permute-start | bytes 393224 | tf_op jit(solution)/shard_map/ppermute | solution.py:42
  121.2 8.8 %collective-permute-start.27 = (bf16[1,48,1536]{2,1,0:T(8,128)(2,1)}, bf16[1,48,1536]{2,1,0:T(8,128)(2,1)S(1)}, u32[]{:S(2)}, u32[]{:S(2)}) collective-permute-start(bf16[1,48,1536]{2,1,0:T(8,128)(2,1)} %get-tuple-element.178), channel_id=1, source_target_pairs={{0,4},{1,5},{2,6},{3,7},{4,0},{5,1},{6,2},{7,3},{8,12},{9,13},{10,... | collective-permute-start | bytes 442376 | tf_op jit(solution)/shard_map/ppermute | solution.py:42
  121.3 17.2 %collective-permute-start.26 = (bf16[192,768]{1,0:T(8,128)(2,1)}, bf16[192,768]{1,0:T(8,128)(2,1)S(1)}, u32[]{:S(2)}, u32[]{:S(2)}) collective-permute-start(bf16[192,768]{1,0:T(8,128)(2,1)} %bitcast.37), channel_id=1, source_target_pairs={{4,0},{5,1},{6,2},{7,3},{8,12},{9,13},{10,14},{11,15},{20,16},{21,... | collective-permute-start | bytes 884744 | tf_op jit(solution)/shard_map/ppermute | solution.py:57
  123.3 6.7 %copy-start.6 = (bf16[1,48,1536]{2,1,0:T(8,128)(2,1)S(1)}, bf16[1,48,1536]{2,1,0:T(8,128)(2,1)}, u32[]{:S(2)}) copy-start(bf16[1,48,1536]{2,1,0:T(8,128)(2,1)} %get-tuple-element.190) | copy-start | bytes 442372
  123.4 12.9 %copy-start.7 = (bf16[2,96,384]{2,1,0:T(8,128)(2,1)S(1)}, bf16[2,96,384]{2,1,0:T(8,128)(2,1)}, u32[]{:S(2)}) copy-start(bf16[2,96,384]{2,1,0:T(8,128)(2,1)} %get-tuple-element.160) | copy-start | bytes 442372
  125.1 15.1 %copy-start.3 = (bf16[1,192,768]{2,1,0:T(8,128)(2,1)S(1)}, bf16[1,192,768]{2,1,0:T(8,128)(2,1)}, u32[]{:S(2)}) copy-start(bf16[1,192,768]{2,1,0:T(8,128)(2,1)} %get-tuple-element.179) | copy-start | bytes 884740
  125.1 15.2 %collective-permute-start.23 = (bf16[224,128]{1,0:T(8,128)(2,1)}, bf16[224,128]{1,0:T(8,128)(2,1)S(1)}, u32[]{:S(2)}, u32[]{:S(2)}) collective-permute-start(bf16[224,128]{1,0:T(8,128)(2,1)} %get-tuple-element.186), channel_id=1, source_target_pairs={{0,2},{1,3},{2,0},{3,1},{4,6},{5,7},{6,4},{7,5},{8,10},{9,11},{10,... | collective-permute-start | bytes 172040 | tf_op jit(solution)/shard_map/ppermute | solution.py:42
  126.4 16.1 %collective-permute-start.24 = (bf16[224,128]{1,0:T(8,128)(2,1)}, bf16[224,128]{1,0:T(8,128)(2,1)S(1)}, u32[]{:S(2)}, u32[]{:S(2)}) collective-permute-start(bf16[224,128]{1,0:T(8,128)(2,1)} %get-tuple-element.187), channel_id=1, source_target_pairs={{0,4},{1,5},{2,6},{3,7},{4,0},{5,1},{6,2},{7,3},{8,12},{9,13},{10,... | collective-permute-start | bytes 172040 | tf_op jit(solution)/shard_map/ppermute | solution.py:42
  129.9 12.6 %collective-permute-start.25 = (bf16[224,128]{1,0:T(8,128)(2,1)}, bf16[224,128]{1,0:T(8,128)(2,1)S(1)}, u32[]{:S(2)}, u32[]{:S(2)}) collective-permute-start(bf16[224,128]{1,0:T(8,128)(2,1)} %get-tuple-element.188), channel_id=1, source_target_pairs={{0,6},{1,7},{2,4},{3,5},{4,2},{5,3},{6,0},{7,1},{8,14},{9,15},{10,... | collective-permute-start | bytes 172040 | tf_op jit(solution)/shard_map/ppermute | solution.py:42
  130.1 17.0 %collective-permute-start.31 = (bf16[48,1536]{1,0:T(8,128)(2,1)S(1)}, bf16[48,1536]{1,0:T(8,128)(2,1)S(1)}, u32[]{:S(2)}, u32[]{:S(2)}) collective-permute-start(bf16[48,1536]{1,0:T(8,128)(2,1)S(1)} %fusion.9), channel_id=1, source_target_pairs={{0,16},{8,24},{16,0},{24,8},{1,17},{9,25},{17,1},{25,9},{2,18},{10... | collective-permute-start | bytes 442376 | tf_op jit(solution)/shard_map/ppermute | solution.py:42
  138.4 8.9 %collective-permute-start.34 = (bf16[2,96,384]{2,1,0:T(8,128)(2,1)S(1)}, bf16[2,96,384]{2,1,0:T(8,128)(2,1)S(1)}, u32[]{:S(2)}, u32[]{:S(2)}) collective-permute-start(bf16[2,96,384]{2,1,0:T(8,128)(2,1)S(1)} %add_convert_fusion.2), channel_id=1, source_target_pairs={{0,16},{8,24},{16,0},{24,8},{1,17},{9,25},{17,1},{25,9},{2,18},{10... | collective-permute-start | bytes 442376 | tf_op jit(solution)/shard_map/ppermute | solution.py:42
  140.3 2.2 %copy-start.21 = (bf16[224,128]{1,0:T(8,128)(2,1)}, bf16[224,128]{1,0:T(8,128)(2,1)S(1)}, u32[]{:S(2)}) copy-start(bf16[224,128]{1,0:T(8,128)(2,1)S(1)} %collective-permute-done.23.refs_1_) | copy-start | bytes 172036
  140.3 8.8 %collective-permute-start.33 = (bf16[192,768]{1,0:T(8,128)(2,1)S(1)}, bf16[192,768]{1,0:T(8,128)(2,1)S(1)}, u32[]{:S(2)}, u32[]{:S(2)}) collective-permute-start(bf16[192,768]{1,0:T(8,128)(2,1)S(1)} %add_convert_fusion), channel_id=1, source_target_pairs={{0,16},{1,17},{2,18},{3,19},{12,28},{13,29},{14,30},{15,31},{16,0}... | collective-permute-start | bytes 884744 | tf_op jit(solution)/shard_map/ppermute | solution.py:63
  145.3 5.8 %collective-permute-start.28 = (bf16[224,128]{1,0:T(8,128)(2,1)}, bf16[224,128]{1,0:T(8,128)(2,1)S(1)}, u32[]{:S(2)}, u32[]{:S(2)}) collective-permute-start(bf16[224,128]{1,0:T(8,128)(2,1)} %message_sum.1.refs_0_), channel_id=1, source_target_pairs={{0,8},{8,0},{16,24},{24,16},{1,9},{9,1},{17,25},{25,17},{2,10},{10... | collective-permute-start | bytes 172040 | tf_op jit(solution)/shard_map/ppermute | solution.py:42
  145.3 5.8 %collective-permute-start.29 = (bf16[224,128]{1,0:T(8,128)(2,1)}, bf16[224,128]{1,0:T(8,128)(2,1)S(1)}, u32[]{:S(2)}, u32[]{:S(2)}) collective-permute-start(bf16[224,128]{1,0:T(8,128)(2,1)} %message_sum.1.refs_0_), channel_id=1, source_target_pairs={{0,16},{8,24},{16,0},{24,8},{1,17},{9,25},{17,1},{25,9},{2,18},{10... | collective-permute-start | bytes 172040 | tf_op jit(solution)/shard_map/ppermute | solution.py:42
  147.1 4.1 %collective-permute-start.30 = (bf16[224,128]{1,0:T(8,128)(2,1)}, bf16[224,128]{1,0:T(8,128)(2,1)S(1)}, u32[]{:S(2)}, u32[]{:S(2)}) collective-permute-start(bf16[224,128]{1,0:T(8,128)(2,1)} %message_sum.1.refs_0_), channel_id=1, source_target_pairs={{0,24},{8,16},{16,8},{24,0},{1,25},{9,17},{17,9},{25,1},{2,26},{10... | collective-permute-start | bytes 172040 | tf_op jit(solution)/shard_map/ppermute | solution.py:42
  147.3 2.0 %collective-permute-start.32 = (bf16[96,1536]{1,0:T(8,128)(2,1)S(1)}, bf16[96,1536]{1,0:T(8,128)(2,1)S(1)}, u32[]{:S(2)}, u32[]{:S(2)}) collective-permute-start(bf16[96,1536]{1,0:T(8,128)(2,1)S(1)} %pad_maximum_fusion.1), channel_id=1, source_target_pairs={{0,8},{8,0},{16,24},{24,16},{1,9},{9,1},{17,25},{25,17},{2,10},{10... | collective-permute-start | bytes 884744 | tf_op jit(solution)/shard_map/ppermute | solution.py:42
  147.6 1.6 %copy-start.5 = (bf16[2,96,384]{2,1,0:T(8,128)(2,1)}, bf16[2,96,384]{2,1,0:T(8,128)(2,1)S(1)}, u32[]{:S(2)}) copy-start(bf16[2,96,384]{2,1,0:T(8,128)(2,1)S(1)} %add_convert_fusion.1.refs_6_) | copy-start | bytes 442372
  149.1 2.1 %collective-permute-start.36 = (bf16[2,96,384]{2,1,0:T(8,128)(2,1)S(1)}, bf16[2,96,384]{2,1,0:T(8,128)(2,1)S(1)}, u32[]{:S(2)}, u32[]{:S(2)}) collective-permute-start(bf16[2,96,384]{2,1,0:T(8,128)(2,1)S(1)} %add_convert_fusion.1.refs_6_), channel_id=1, source_target_pairs={{0,8},{8,0},{16,24},{24,16},{1,9},{9,1},{17,25},{25,17},{2,10},{10... | collective-permute-start | bytes 442376 | tf_op jit(solution)/shard_map/ppermute | solution.py:42
  149.3 1.8 %copy-start.1 = (bf16[384,768]{1,0:T(8,128)(2,1)}, bf16[384,768]{1,0:T(8,128)(2,1)S(1)}, u32[]{:S(2)}) copy-start(bf16[384,768]{1,0:T(8,128)(2,1)S(1)} %pad_maximum_fusion.refs_4_) | copy-start | bytes 1769476
  149.3 2.2 %collective-permute-start.35 = (bf16[384,768]{1,0:T(8,128)(2,1)S(1)}, bf16[384,768]{1,0:T(8,128)(2,1)S(1)}, u32[]{:S(2)}, u32[]{:S(2)}) collective-permute-start(bf16[384,768]{1,0:T(8,128)(2,1)S(1)} %pad_maximum_fusion.refs_4_), channel_id=1, source_target_pairs={{0,8},{8,0},{16,24},{24,16},{1,9},{9,1},{17,25},{25,17},{2,10},{10... | collective-permute-start | bytes 1769480 | tf_op jit(solution)/shard_map/ppermute | solution.py:42
  (13 other events, 11.2 us)

commit v6 on v5

--- a/solution.py
+++ b/solution.py
@@ -145,7 +145,7 @@
         in_specs=[SMEM] + [VMEM] * len(arrays),
         out_specs=[VMEM] * len(shapes),
         out_shape=shapes,
-        compiler_params=params(),
+        compiler_params=params(FULL_BYTES),
         cost_estimate=cost(share),
         name="add_split",
     )(place, *arrays)
@@ -241,11 +241,10 @@
 def queries_kernel(copies, first_ref, weight_ref, add_ref, tables_ref, q_ref):
     first_in = first_ref[...]
     tables = repeated(tables_ref, copies)
-    bias = wide(add_ref)
+    rows = dot(first_in, weight_ref[...]) + wide(add_ref)[:, :D]
     for p in range(PAIRS):
         columns = slice(p * 128, (p + 1) * 128)
-        part = dot(first_in, weight_ref[:, columns]) + bias[:, columns]
-        q_ref[:, columns] = (turn(part, tables, 1) * SCALE).astype(BF16)
+        q_ref[:, columns] = (turn(rows[:, columns], tables, 1) * SCALE).astype(BF16)
 
 
 def project_keys(x, gain, bias, weight, add, tables):
@@ -748,7 +747,7 @@
             scratch_shapes=[pltpu.VMEM((depth, 2, per, half), F32)],
         ),
         out_shape=[SHAPE((2, depth, per, half), BF16), SHAPE((2, depth, per, half), BF16), SHAPE((8, D), F32)],
-        compiler_params=params(),
+        compiler_params=params(FULL_BYTES),
         cost_estimate=cost(2.4),
         name="weights",
     )(place, both, both2, g, g2, first_in, first_in2, both, both2)
@@ -762,11 +761,11 @@
 
 def mix(x, mlp, other, both, add, wo):
     rows = x.shape[0]
-    row = pl.BlockSpec((rows // 2, D), lambda i: (i, 0))
-    first = pl.BlockSpec((None, rows // 2, D), lambda i: (0, i, 0))
+    row = pl.BlockSpec((rows, D), lambda i: (i, 0))
+    first = pl.BlockSpec((None, rows, D), lambda i: (0, i, 0))
     return pl.pallas_call(
         mix_kernel,
-        grid=(2,),
+        grid=(1,),
         in_specs=[row, row, first, first, pl.BlockSpec((D,), lambda i: (0,)), pl.BlockSpec((D, D), lambda i: (0, 0))],
         out_specs=row,
         out_shape=SHAPE((rows, D), BF16),

time: 156 us -> 155 us (level)
  starting transfers between devices: 45.4 us -> 42 us
    ppermute x1, waiting for transfers between devices: 2.13 us -> 6.86 us  [to_owner(): return lax.ppermute(block, ('batch', 'seq'), route)]
    ppermute x29, starting transfers between devices: 32.2 us -> 27.9 us  [flipped(): lax.ppermute(block, axis, [(i, i ^ bits) for i in range(lax.axis_size(axi...]
    ppermute x29, waiting for transfers between devices: 3.27 us -> 1.14 us  [flipped(): lax.ppermute(block, axis, [(i, i ^ bits) for i in range(lax.axis_size(axi...]
    unnamed x48 -> x44, local copies, waits for them, and re-layouts: 4.7 us -> 4.87 us
  transfers between devices with their start and end apart: 37 -> 37, of which waited for: 8 -> 5; matrix products, arithmetic and copies ran while one was open for 3% -> 3% of each run, Pallas kernels for 58% -> 59%
where the time goes in v6:
time: 155 us
  Pallas kernels  93.3 us (60%)
  starting transfers between devices  42 us (27%)
  waiting for transfers between devices  8.43 us (5%)
  other arithmetic  5.14 us (3%)
  local copies, waits for them, and re-layouts  4.87 us (3%)
    pallas_call x1, Pallas kernels, feed(): pl.pallas_call(feed_kernel, grid_spec=spec, out_shape=[SHAPE((rows, D), B...  28.7 us
    ppermute x29, starting transfers between devices, flipped(): lax.ppermute(block, axis, [(i, i ^ bits) for i in range(lax.axis_size(axi...  27.9 us
    pallas_call x1, Pallas kernels, attention(): pl.pallas_call(kernel, grid=(seqs, PAIRS // groups), in_specs=[SMEM] + [t...  24.8 us
    ppermute x6, starting transfers between devices, along(): lax.ppermute(block, 'seq', [(i, (i + 2 * distance) % size) for i in range...  9.73 us
    ppermute x1, waiting for transfers between devices, to_owner(): return lax.ppermute(block, ('batch', 'seq'), route)  6.86 us
    pallas_call x1, Pallas kernels, weights(): pl.pallas_call(weights_kernel, grid_spec=pltpu.PrefetchScalarGridSpec(num...  6.04 us
    pallas_call x1, Pallas kernels, finish(): pl.pallas_call(functools.partial(finish_kernel, rows // tables.shape[1],...  5.93 us
    unnamed x44, local copies, waits for them, and re-layouts  4.87 us
  transfers between devices with their start and end apart: 37, of which 5 were waited for; matrix products, arithmetic and copies ran while one was open for 3% of the time, Pallas kernels for 59%

profile of v6, /device:TPU:0, one launch (start us, length us, event | category | flops | bytes accessed | tf_op | source)
XLA Modules:
  0.0 154.7 jit_solution(14935070646444627362)
XLA Ops:
  1.2 1.0 fusion.2.tables_ref.refs_6_.refs_14_
  2.2 2.9 %project_keys.1 = (bf16[512,128]{1,0:T(8,128)(2,1)}, bf16[512,768]{1,0:T(8,128)(2,1)}) custom-call(bf16[512,768]{1,0:T(8,128)(2,1)} %bitcast.50, f32[768]{0:T(1024)} %refs_10_.1, f32[768]{0:T(1024)} %refs_11_.1, bf16[768,896]{1,0:T(8,128)(2,1)} %refs_13_.1, f32[896]{0:T(1024)} %add_ref.4, f32[3,128,128]{2,1,0:T(8,128)} %fusion.2.tables_ref.refs_6_.refs_14_), custom_call_target="tpu_custom_call" | custom-call | flops 3000000000 | tf_op jit(solution)/shard_map/project_keys/pallas_call | solution.py:253
  5.1 2.6 %collective-permute-start = (bf16[4,128,128]{2,1,0:T(8,128)(2,1)}, bf16[4,128,128]{2,1,0:T(8,128)(2,1)S(1)}, u32[]{:S(2)}, u32[]{:S(2)}) collective-permute-start(bf16[4,128,128]{2,1,0:T(8,128)(2,1)} %bitcast.40), channel_id=1, source_target_pairs={{0,1},{1,0},{2,3},{3,2},{4,5},{5,4},{6,7},{7,6},{8,9},{9,8},{10,11... | collective-permute-start | bytes 393224 | tf_op jit(solution)/shard_map/ppermute | solution.py:42
  8.2 3.7 %project_queries.1 = bf16[512,768]{1,0:T(8,128)(2,1)} custom-call(bf16[512,768]{1,0:T(8,128)(2,1)} %get-tuple-element.118.first_ref.in_ref, bf16[768,896]{1,0:T(8,128)(2,1)} %refs_13_.1, f32[896]{0:T(1024)} %add_ref.4, f32[3,128,128]{2,1,0:T(8,128)} %fusion.2.tables_ref.refs_6_.refs_14_), custom_call_target="tpu_custom_call" | custom-call | flops 6000000000 | tf_op jit(solution)/shard_map/project_queries/pallas_call | solution.py:275
  11.9 0.6 pad_add_fusion.place_ref
  12.5 1.6 %collective-permute-start.1 = (bf16[2,4,128,128]{3,2,1,0:T(8,128)(2,1)S(1)}, bf16[2,4,128,128]{3,2,1,0:T(8,128)(2,1)S(1)}, u32[]{:S(2)}, u32[]{:S(2)}) collective-permute-start(bf16[2,4,128,128]{3,2,1,0:T(8,128)(2,1)S(1)} %pad_maximum_fusion.2.refs_0_), channel_id=1, source_target_pairs={{0,2},{1,3},{2,4},{3,5},{4,6},{5,7},{6,0},{7,1},{8,10},{9,11},{10,... | collective-permute-start | bytes 786440 | tf_op jit(solution)/shard_map/ppermute | solution.py:47
  14.2 2.6 %collective-permute-start.2 = (bf16[2,4,128,128]{3,2,1,0:T(8,128)(2,1)S(1)}, bf16[2,4,128,128]{3,2,1,0:T(8,128)(2,1)S(1)}, u32[]{:S(2)}, u32[]{:S(2)}) collective-permute-start(bf16[2,4,128,128]{3,2,1,0:T(8,128)(2,1)S(1)} %pad_maximum_fusion.2.refs_0_), channel_id=1, source_target_pairs={{0,4},{1,5},{2,6},{3,7},{4,0},{5,1},{6,2},{7,3},{8,12},{9,13},{10,... | collective-permute-start | bytes 786440 | tf_op jit(solution)/shard_map/ppermute | solution.py:47
  16.8 1.3 collective-permute-start.3
  18.1 28.7 %feed_forward.1 = (bf16[512,768]{1,0:T(8,128)(2,1)}, bf16[512,768]{1,0:T(8,128)(2,1)}, bf16[2,512,768]{2,1,0:T(8,128)(2,1)}, bf16[512,768]{1,0:T(8,128)(2,1)}, f...) custom-call(s32[4]{0:T(128)} %pad_add_fusion.place_ref, ...), custom_call_target="tpu_custom_call" | custom-call | flops 35999997952 | tf_op jit(solution)/shard_map/feed_forward/pallas_call | solution.py:437
  46.9 0.7 collective-permute-start.10
  47.6 1.5 collective-permute-start.9
  49.1 0.7 copy-done.13
  49.8 24.8 %attention.1 = (bf16[2,4,128,768]{3,2,1,0:T(8,128)(2,1)}, bf16[4,4,128,128]{3,2,1,0:T(8,128)(2,1)}, bf16[4,4,128,128]{3,2,1,0:T(8,128)(2,1)}) custom-call(s32[4]{0:T(128)} %pad_add_fusion.place_ref, bf16[2,4,128,128]{3,2,1,0:T(8,128)(2,1)} %copy-done.4, bf16[2,4,128,128]{3,2,1,0:T(8,128)(2,1)} %copy-done.12, bf16[2,4,128,128]{3,2,1,0:T(8,128)(2,1)} %copy-done.13, ...), custom_call_target="tpu_custom_call" | custom-call | flops 30000001024 | tf_op jit(solution)/shard_map/attention/pallas_call | solution.py:695
  74.7 1.3 collective-permute-start.7
  76.0 4.3 %add_split.1 = (bf16[2,96,1536]{2,1,0:T(8,128)(2,1)}, bf16[2,96,1536]{2,1,0:T(8,128)(2,1)}, bf16[2,192,768]{2,1,0:T(8,128)(2,1)}, bf16[2,192,768]{2,1,0:T(8,128)(2,1)}) custom-call(s32[4]{0:T(128)} %pad_add_fusion.place_ref, bf16[2,2,96,1536]{3,2,1,0:T(8,128)(2,1)} %bitcast.60, bf16[2,2,96,1536]{3,2,1,0:T(8,128)(2,1)} %bitcast.14.refs_1_, ...), custom_call_target="tpu_custom_call" | custom-call | flops 17999998976 | tf_op jit(solution)/shard_map/add_split/pallas_call | solution.py:143
  80.3 1.4 collective-permute-start.16
  81.6 1.5 collective-permute-start.17
  83.1 6.0 %weights.1 = (bf16[2,4,96,384]{3,2,1,0:T(8,128)(2,1)}, bf16[2,4,96,384]{3,2,1,0:T(8,128)(2,1)}, f32[8,768]{1,0:T(8,128)}) custom-call(s32[4]{0:T(128)} %pad_add_fusion.place_ref, bf16[2,512,768]{2,1,0:T(8,128)(2,1)} %bitcast.45, bf16[2,512,768]{2,1,0:T(8,128)(2,1)} %collective-permute-done.8.attn2_ref.q2_ref, bf16[512,768]{1,0:T(8,128)(2,1)} %bitcast.55, ...), custom_call_target="tpu_custom_call" | custom-call | flops 7200000000 | tf_op jit(solution)/shard_map/weights/pallas_call | solution.py:740
  89.1 1.3 collective-permute-start.15
  90.4 1.9 %add_convert_fusion.4 = (bf16[1,4,128,128]{3,2,1,0:T(8,128)(2,1)}, bf16[4,128,128]{2,1,0:T(8,128)(2,1)S(1)}, bf16[4,128,128]{2,1,0:T(8,128)(2,1)S(1)}, bf16[4,128,128]{2,1,0:T(8,128)(2,1)S(1)}) fusion(bf16[4,4,128,128]{3,2,1,0:T(8,128)(2,1)} %collective-permute-done.7, bf16[4,4,128,128]{3,2,1,0:T(8,128)(2,1)S(1)} %copy-done.2), kind=kLoop, calls=%fused_computation.20 | loop fusion | flops 1048576 | bytes 1572864 | tf_op jit(solution)/shard_map/convert_element_type | solution.py:1006
  92.7 1.1 collective-permute-start.14
  93.7 4.0 %mix.1 = bf16[512,768]{1,0:T(8,128)(2,1)} custom-call(bf16[512,768]{1,0:T(8,128)(2,1)} %bitcast.52, bf16[512,768]{1,0:T(8,128)(2,1)} %get-tuple-element.146.mlp_ref, bf16[2,512,768]{2,1,0:T(8,128)(2,1)} %collective-permute-done.11.mlp2_ref.refs_9_, bf16[2,512,768]{2,1,0:T(8,128)(2,1)} %bitcast.47, f32[768]{0:T(1024)} %add_ref.5, bf16[768,768]{1,0:T(8,128)(2,1)} %wo_ref.3), custom_call_target="tpu_custom_call" | custom-call | flops 3600000000 | tf_op jit(solution)/shard_map/mix/pallas_call | solution.py:766
  97.7 2.8 %collective-permute-start.12 = (bf16[4,128,128]{2,1,0:T(8,128)(2,1)S(1)}, bf16[4,128,128]{2,1,0:T(8,128)(2,1)}, u32[]{:S(2)}, u32[]{:S(2)}) collective-permute-start(bf16[4,128,128]{2,1,0:T(8,128)(2,1)S(1)} %get-tuple-element.148), channel_id=1, source_target_pairs={{0,6},{1,7},{2,0},{3,1},{4,2},{5,3},{6,4},{7,5},{8,14},{9,15},{10,... | collective-permute-start | bytes 393224 | tf_op jit(solution)/shard_map/ppermute | solution.py:47
  100.5 2.7 %exchange_split.1 = (bf16[768,384]{1,0:T(8,128)(2,1)}, bf16[2,48,1536]{2,1,0:T(8,128)(2,1)}, bf16[1,192,768]{2,1,0:T(8,128)(2,1)}) custom-call(s32[4]{0:T(128)} %pad_add_fusion.place_ref, bf16[2,2,48,1536]{3,2,1,0:T(8,128)(2,1)} %bitcast.66, bf16[2,2,48,1536]{3,2,1,0:T(8,128)(2,1)} %bitcast.23.b1, bf16[1,2,192,768]{3,2,1,0:T(8,128)(2,1)} %bitcast.67, ...), custom_call_target="tpu_custom_call" | custom-call | flops 3600000000 | tf_op jit(solution)/shard_map/exchange_split/pallas_call | solution.py:170
  103.2 0.8 collective-permute-start.22
  104.0 2.1 %add_cut.1 = (bf16[2,96,384]{2,1,0:T(8,128)(2,1)}, bf16[2,96,384]{2,1,0:T(8,128)(2,1)}, bf16[2,96,384]{2,1,0:T(8,128)(2,1)}, bf16[2,96,384]{2,1,0:T(8,128)(2,1)}) custom-call(s32[4]{0:T(128)} %pad_add_fusion.place_ref, bf16[2,4,96,384]{3,2,1,0:T(8,128)(2,1)} %get-tuple-element.158.a_ref, bf16[2,4,96,384]{3,2,1,0:T(8,128)(2,1)} %collective-permute-done.15.b_ref), custom_call_target="tpu_custom_call" | custom-call | flops 3600000000 | tf_op jit(solution)/shard_map/add_cut/pallas_call | solution.py:222
  106.6 1.6 %collective-permute-start.20 = (bf16[2,96,384]{2,1,0:T(8,128)(2,1)}, bf16[2,96,384]{2,1,0:T(8,128)(2,1)S(1)}, u32[]{:S(2)}, u32[]{:S(2)}) collective-permute-start(bf16[2,96,384]{2,1,0:T(8,128)(2,1)} %get-tuple-element.171), channel_id=1, source_target_pairs={{0,4},{1,5},{2,6},{3,7},{4,0},{5,1},{6,2},{7,3},{8,12},{9,13},{10,... | collective-permute-start | bytes 442376 | tf_op jit(solution)/shard_map/ppermute | solution.py:42
  108.2 2.4 %collective-permute-start.21 = (bf16[2,96,384]{2,1,0:T(8,128)(2,1)}, bf16[2,96,384]{2,1,0:T(8,128)(2,1)S(1)}, u32[]{:S(2)}, u32[]{:S(2)}) collective-permute-start(bf16[2,96,384]{2,1,0:T(8,128)(2,1)} %get-tuple-element.172), channel_id=1, source_target_pairs={{0,6},{1,7},{2,4},{3,5},{4,2},{5,3},{6,0},{7,1},{8,14},{9,15},{10,... | collective-permute-start | bytes 442376 | tf_op jit(solution)/shard_map/ppermute | solution.py:42
  110.6 5.9 %finish.1 = (bf16[512,768]{1,0:T(8,128)(2,1)}, bf16[512,128]{1,0:T(8,128)(2,1)}, bf16[512,128]{1,0:T(8,128)(2,1)}) custom-call(s32[4]{0:T(128)} %pad_add_fusion.place_ref, bf16[512,128]{1,0:T(8,128)(2,1)} %bitcast.39, bf16[512,128]{1,0:T(8,128)(2,1)} %bitcast.26.refs_1_, bf16[512,128]{1,0:T(8,128)(2,1)} %bitcast.27.refs_2_, ...), custom_call_target="tpu_custom_call" | custom-call | flops 7200000000 | tf_op jit(solution)/shard_map/finish/pallas_call | solution.py:860
  116.5 1.3 collective-permute-start.18
  117.8 0.8 copy-done
  118.6 2.1 %exchange_add.1 = (bf16[1,48,1536]{2,1,0:T(8,128)(2,1)}, bf16[1,48,1536]{2,1,0:T(8,128)(2,1)}, bf16[1,192,768]{2,1,0:T(8,128)(2,1)}) custom-call(s32[4]{0:T(128)} %pad_add_fusion.place_ref, bf16[2,48,1536]{2,1,0:T(8,128)(2,1)} %get-tuple-element.175.a1, bf16[1,192,768]{2,1,0:T(8,128)(2,1)} %get-tuple-element.176.a2, bf16[768,384]{1,0:T(8,128)(2,1)} %copy-done), custom_call_target="tpu_custom_call" | custom-call | flops 30000000 | tf_op jit(solution)/shard_map/exchange_add/pallas_call | solution.py:202
  120.7 1.3 collective-permute-start.26
  122.1 0.6 copy-done.15
  122.7 1.7 %message_cut.1 = (bf16[224,128]{1,0:T(8,128)(2,1)}, bf16[224,128]{1,0:T(8,128)(2,1)}, bf16[224,128]{1,0:T(8,128)(2,1)}, bf16[224,128]{1,0:T(8,128)(2,1)}) custom-call(s32[4]{0:T(128)} %pad_add_fusion.place_ref, bf16[512,128]{1,0:T(8,128)(2,1)} %get-tuple-element.183.a_ref, bf16[512,128]{1,0:T(8,128)(2,1)} %copy-done.15), custom_call_target="tpu_custom_call" | custom-call | flops 1800000000 | tf_op jit(solution)/shard_map/message_cut/pallas_call | solution.py:894
  124.5 2.6 %collective-permute-start.23 = (bf16[224,128]{1,0:T(8,128)(2,1)}, bf16[224,128]{1,0:T(8,128)(2,1)S(1)}, u32[]{:S(2)}, u32[]{:S(2)}) collective-permute-start(bf16[224,128]{1,0:T(8,128)(2,1)} %get-tuple-element.186), channel_id=1, source_target_pairs={{0,2},{1,3},{2,0},{3,1},{4,6},{5,7},{6,4},{7,5},{8,10},{9,11},{10,... | collective-permute-start | bytes 172040 | tf_op jit(solution)/shard_map/ppermute | solution.py:42
  127.0 2.5 %collective-permute-start.24 = (bf16[224,128]{1,0:T(8,128)(2,1)}, bf16[224,128]{1,0:T(8,128)(2,1)S(1)}, u32[]{:S(2)}, u32[]{:S(2)}) collective-permute-start(bf16[224,128]{1,0:T(8,128)(2,1)} %get-tuple-element.187), channel_id=1, source_target_pairs={{0,4},{1,5},{2,6},{3,7},{4,0},{5,1},{6,2},{7,3},{8,12},{9,13},{10,... | collective-permute-start | bytes 172040 | tf_op jit(solution)/shard_map/ppermute | solution.py:42
  129.5 1.6 %collective-permute-start.31 = (bf16[48,1536]{1,0:T(8,128)(2,1)S(1)}, bf16[48,1536]{1,0:T(8,128)(2,1)S(1)}, u32[]{:S(2)}, u32[]{:S(2)}) collective-permute-start(bf16[48,1536]{1,0:T(8,128)(2,1)S(1)} %fusion.9), channel_id=1, source_target_pairs={{0,16},{8,24},{16,0},{24,8},{1,17},{9,25},{17,1},{25,9},{2,18},{10... | collective-permute-start | bytes 442376 | tf_op jit(solution)/shard_map/ppermute | solution.py:42
  131.3 6.9 %collective-permute-done.26 = bf16[192,768]{1,0:T(8,128)(2,1)S(1)} collective-permute-done((bf16[192,768]{1,0:T(8,128)(2,1)}, bf16[192,768]{1,0:T(8,128)(2,1)S(1)}, u32[]{:S(2)}, u32[]{:S(2)}) %collective-permute-start.26) | collective-permute-done | bytes 294944 | tf_op jit(solution)/shard_map/ppermute | solution.py:57
  138.1 0.9 collective-permute-start.34
  139.1 3.0 %collective-permute-start.33 = (bf16[192,768]{1,0:T(8,128)(2,1)S(1)}, bf16[192,768]{1,0:T(8,128)(2,1)S(1)}, u32[]{:S(2)}, u32[]{:S(2)}) collective-permute-start(bf16[192,768]{1,0:T(8,128)(2,1)S(1)} %add_convert_fusion), channel_id=1, source_target_pairs={{0,16},{1,17},{2,18},{3,19},{12,28},{13,29},{14,30},{15,31},{16,0}... | collective-permute-start | bytes 884744 | tf_op jit(solution)/shard_map/ppermute | solution.py:63
  142.8 0.6 copy-done.21
  143.4 1.6 %message_sum.1.refs_0_ = bf16[224,128]{1,0:T(8,128)(2,1)} custom-call(bf16[224,128]{1,0:T(8,128)(2,1)} %get-tuple-element.185.refs_0_, bf16[224,128]{1,0:T(8,128)(2,1)} %copy-done.19, bf16[224,128]{1,0:T(8,128)(2,1)} %copy-done.20, bf16[224,128]{1,0:T(8,128)(2,1)} %copy-done.21), custom_call_target="tpu_custom_call" | custom-call | flops 1800000000 | tf_op jit(solution)/shard_map/message_sum/pallas_call | solution.py:915
  145.0 0.9 collective-permute-start.29
  145.9 1.0 collective-permute-start.30
  148.9 1.1 maximum_convert_fusion
  151.0 0.8 copy-done.11
  151.9 2.8 %last_sums.1 = (f32[3072]{0:T(1024)}, f32[896]{0:T(1024)}, f32[768]{0:T(1024)}, f32[768]{0:T(1024)}, f32[768]{0:T(1024)}, /*index=5*/f32[768]{0:T(1024)}, f32[76...) custom-call(s32[4]{0:T(128)} %pad_add_fusion.place_ref, bf16[224,128]{1,0:T(8,128)(2,1)} %message_sum.1.refs_0_, ...), custom_call_target="tpu_custom_call" | custom-call | flops 1800000000 | tf_op jit(solution)/shard_map/last_sums/pallas_call | solution.py:950
  (102 shorter events, 5.9 us)
Async XLA Ops:
  0.6 17.5 %collective-permute-start.5 = (bf16[512,768]{1,0:T(8,128)(2,1)}, bf16[512,768]{1,0:T(8,128)(2,1)}, u32[]{:S(2)}, u32[]{:S(2)}) collective-permute-start(bf16[512,768]{1,0:T(8,128)(2,1)} %bitcast.49), channel_id=1, source_target_pairs={{0,8},{8,0},{16,24},{24,16},{1,9},{9,1},{17,25},{25,17},{2,10},{10... | collective-permute-start | bytes 2359304 | tf_op jit(solution)/shard_map/ppermute | solution.py:42
  2.2 5.6 %copy-start.9 = (bf16[4,128,768]{2,1,0:T(8,128)(2,1)S(1)}, bf16[4,128,768]{2,1,0:T(8,128)(2,1)}, u32[]{:S(2)}) copy-start(bf16[4,128,768]{2,1,0:T(8,128)(2,1)} %param.26) | copy-start | bytes 2359300
  5.1 7.4 %collective-permute-start = (bf16[4,128,128]{2,1,0:T(8,128)(2,1)}, bf16[4,128,128]{2,1,0:T(8,128)(2,1)S(1)}, u32[]{:S(2)}, u32[]{:S(2)}) collective-permute-start(bf16[4,128,128]{2,1,0:T(8,128)(2,1)} %bitcast.40), channel_id=1, source_target_pairs={{0,1},{1,0},{2,3},{3,2},{4,5},{5,4},{6,7},{7,6},{8,9},{9,8},{10,11... | collective-permute-start | bytes 393224 | tf_op jit(solution)/shard_map/ppermute | solution.py:42
  7.7 9.1 %collective-permute-start.4 = (bf16[512,768]{1,0:T(8,128)(2,1)}, bf16[512,768]{1,0:T(8,128)(2,1)S(1)}, u32[]{:S(2)}, u32[]{:S(2)}) collective-permute-start(bf16[512,768]{1,0:T(8,128)(2,1)} %get-tuple-element.118.first_ref.in_ref), channel_id=1, source_target_pairs={{0,8},{8,0},{16,24},{24,16},{1,9},{9,1},{17,25},{25,17},{2,10},{10... | collective-permute-start | bytes 2359304 | tf_op jit(solution)/shard_map/ppermute | solution.py:42
  7.9 4.6 %copy-start.8 = (bf16[512,128]{1,0:T(8,128)(2,1)S(1)}, bf16[512,128]{1,0:T(8,128)(2,1)}, u32[]{:S(2)}) copy-start(bf16[512,128]{1,0:T(8,128)(2,1)} %get-tuple-element.117) | copy-start | bytes 393220
  7.9 10.2 %collective-permute-start.6 = (bf16[512,768]{1,0:T(8,128)(2,1)S(1)}, bf16[512,768]{1,0:T(8,128)(2,1)}, u32[]{:S(2)}, u32[]{:S(2)}) collective-permute-start(bf16[512,768]{1,0:T(8,128)(2,1)S(1)} %bitcast.57), channel_id=1, source_target_pairs={{0,8},{8,0},{16,24},{24,16},{1,9},{9,1},{17,25},{25,17},{2,10},{10... | collective-permute-start | bytes 2359304 | tf_op jit(solution)/shard_map/ppermute | solution.py:42
  12.5 34.3 %copy-start.4 = (bf16[2,4,128,128]{3,2,1,0:T(8,128)(2,1)}, bf16[2,4,128,128]{3,2,1,0:T(8,128)(2,1)S(1)}, u32[]{:S(2)}) copy-start(bf16[2,4,128,128]{3,2,1,0:T(8,128)(2,1)S(1)} %pad_maximum_fusion.2.refs_0_) | copy-start | bytes 786436
  12.5 35.1 %collective-permute-start.1 = (bf16[2,4,128,128]{3,2,1,0:T(8,128)(2,1)S(1)}, bf16[2,4,128,128]{3,2,1,0:T(8,128)(2,1)S(1)}, u32[]{:S(2)}, u32[]{:S(2)}) collective-permute-start(bf16[2,4,128,128]{3,2,1,0:T(8,128)(2,1)S(1)} %pad_maximum_fusion.2.refs_0_), channel_id=1, source_target_pairs={{0,2},{1,3},{2,4},{3,5},{4,6},{5,7},{6,0},{7,1},{8,10},{9,11},{10,... | collective-permute-start | bytes 786440 | tf_op jit(solution)/shard_map/ppermute | solution.py:47
  14.2 35.0 %collective-permute-start.2 = (bf16[2,4,128,128]{3,2,1,0:T(8,128)(2,1)S(1)}, bf16[2,4,128,128]{3,2,1,0:T(8,128)(2,1)S(1)}, u32[]{:S(2)}, u32[]{:S(2)}) collective-permute-start(bf16[2,4,128,128]{3,2,1,0:T(8,128)(2,1)S(1)} %pad_maximum_fusion.2.refs_0_), channel_id=1, source_target_pairs={{0,4},{1,5},{2,6},{3,7},{4,0},{5,1},{6,2},{7,3},{8,12},{9,13},{10,... | collective-permute-start | bytes 786440 | tf_op jit(solution)/shard_map/ppermute | solution.py:47
  16.7 1.4 copy-start.10
  16.8 32.4 %collective-permute-start.3 = (bf16[2,4,128,128]{3,2,1,0:T(8,128)(2,1)S(1)}, bf16[2,4,128,128]{3,2,1,0:T(8,128)(2,1)}, u32[]{:S(2)}, u32[]{:S(2)}) collective-permute-start(bf16[2,4,128,128]{3,2,1,0:T(8,128)(2,1)S(1)} %pad_maximum_fusion.2.refs_0_), channel_id=1, source_target_pairs={{0,6},{1,7},{2,0},{3,1},{4,2},{5,3},{6,4},{7,5},{8,14},{9,15},{10,... | collective-permute-start | bytes 786440 | tf_op jit(solution)/shard_map/ppermute | solution.py:47
  46.8 29.2 %collective-permute-start.11 = (bf16[2,512,768]{2,1,0:T(8,128)(2,1)}, bf16[2,512,768]{2,1,0:T(8,128)(2,1)}, u32[]{:S(2)}, u32[]{:S(2)}) collective-permute-start(bf16[2,512,768]{2,1,0:T(8,128)(2,1)} %get-tuple-element.135), channel_id=1, source_target_pairs={{0,8},{8,0},{16,24},{24,16},{1,9},{9,1},{17,25},{25,17},{2,10},{10... | collective-permute-start | bytes 4718600 | tf_op jit(solution)/shard_map/ppermute | solution.py:42
  46.9 29.1 %collective-permute-start.10 = (bf16[768,768]{1,0:T(8,128)(2,1)}, bf16[768,768]{1,0:T(8,128)(2,1)}, u32[]{:S(2)}, u32[]{:S(2)}) collective-permute-start(bf16[768,768]{1,0:T(8,128)(2,1)} %get-tuple-element.134), channel_id=1, source_target_pairs={{0,2},{1,3},{2,0},{3,1},{4,6},{5,7},{6,4},{7,5},{8,10},{9,11},{10,... | collective-permute-start | bytes 3538952 | tf_op jit(solution)/shard_map/ppermute | solution.py:42
  47.6 1.5 copy-start.12
  47.6 28.4 %collective-permute-start.9 = (bf16[8,48,1536]{2,1,0:T(8,128)(2,1)}, bf16[8,48,1536]{2,1,0:T(8,128)(2,1)}, u32[]{:S(2)}, u32[]{:S(2)}) collective-permute-start(bf16[8,48,1536]{2,1,0:T(8,128)(2,1)} %get-tuple-element.132), channel_id=1, source_target_pairs={{0,16},{8,24},{16,0},{24,8},{1,17},{9,25},{17,1},{25,9},{2,18},{10... | collective-permute-start | bytes 3538952 | tf_op jit(solution)/shard_map/ppermute | solution.py:42
  74.6 7.0 %collective-permute-start.8 = (bf16[2,512,768]{2,1,0:T(8,128)(2,1)}, bf16[2,512,768]{2,1,0:T(8,128)(2,1)}, u32[]{:S(2)}, u32[]{:S(2)}) collective-permute-start(bf16[2,512,768]{2,1,0:T(8,128)(2,1)} %bitcast.44), channel_id=1, source_target_pairs={{0,8},{8,0},{16,24},{24,16},{1,9},{9,1},{17,25},{25,17},{2,10},{10... | collective-permute-start | bytes 4718600 | tf_op jit(solution)/shard_map/ppermute | solution.py:42
  74.7 15.8 %collective-permute-start.7 = (bf16[4,4,128,128]{3,2,1,0:T(8,128)(2,1)}, bf16[4,4,128,128]{3,2,1,0:T(8,128)(2,1)}, u32[]{:S(2)}, u32[]{:S(2)}) collective-permute-start(bf16[4,4,128,128]{3,2,1,0:T(8,128)(2,1)} %get-tuple-element.129), channel_id=1, source_target_pairs={{0,1},{1,0},{2,3},{3,2},{4,5},{5,4},{6,7},{7,6},{8,9},{9,8},{10,11... | collective-permute-start | bytes 1572872 | tf_op jit(solution)/shard_map/ppermute | solution.py:42
  80.3 17.5 %collective-permute-start.16 = (bf16[2,96,1536]{2,1,0:T(8,128)(2,1)}, bf16[2,96,1536]{2,1,0:T(8,128)(2,1)}, u32[]{:S(2)}, u32[]{:S(2)}) collective-permute-start(bf16[2,96,1536]{2,1,0:T(8,128)(2,1)} %get-tuple-element.140), channel_id=1, source_target_pairs={{0,2},{1,3},{2,0},{3,1},{4,6},{5,7},{6,4},{7,5},{8,10},{9,11},{10,... | collective-permute-start | bytes 1769480 | tf_op jit(solution)/shard_map/ppermute | solution.py:42
  81.6 8.8 %copy-start.2 = (bf16[4,4,128,128]{3,2,1,0:T(8,128)(2,1)S(1)}, bf16[4,4,128,128]{3,2,1,0:T(8,128)(2,1)}, u32[]{:S(2)}) copy-start(bf16[4,4,128,128]{3,2,1,0:T(8,128)(2,1)} %get-tuple-element.143) | copy-start | bytes 1572868
  81.6 18.9 %collective-permute-start.17 = (bf16[2,192,768]{2,1,0:T(8,128)(2,1)}, bf16[2,192,768]{2,1,0:T(8,128)(2,1)}, u32[]{:S(2)}, u32[]{:S(2)}) collective-permute-start(bf16[2,192,768]{2,1,0:T(8,128)(2,1)} %get-tuple-element.152), channel_id=1, source_target_pairs={{0,16},{8,24},{16,0},{24,8},{1,17},{9,25},{17,1},{25,9},{2,18},{10... | collective-permute-start | bytes 1769480 | tf_op jit(solution)/shard_map/ppermute | solution.py:42
  89.1 14.9 %collective-permute-start.15 = (bf16[2,4,96,384]{3,2,1,0:T(8,128)(2,1)}, bf16[2,4,96,384]{3,2,1,0:T(8,128)(2,1)}, u32[]{:S(2)}, u32[]{:S(2)}) collective-permute-start(bf16[2,4,96,384]{3,2,1,0:T(8,128)(2,1)} %get-tuple-element.142), channel_id=1, source_target_pairs={{0,1},{1,0},{2,3},{3,2},{4,5},{5,4},{6,7},{7,6},{8,9},{9,8},{10,11... | collective-permute-start | bytes 1769480 | tf_op jit(solution)/shard_map/ppermute | solution.py:42
  92.3 13.8 %collective-permute-start.13 = (bf16[4,128,128]{2,1,0:T(8,128)(2,1)S(1)}, bf16[4,128,128]{2,1,0:T(8,128)(2,1)}, u32[]{:S(2)}, u32[]{:S(2)}) collective-permute-start(bf16[4,128,128]{2,1,0:T(8,128)(2,1)S(1)} %get-tuple-element.222), channel_id=1, source_target_pairs={{0,4},{1,5},{2,6},{3,7},{4,0},{5,1},{6,2},{7,3},{8,12},{9,13},{10,... | collective-permute-start | bytes 393224 | tf_op jit(solution)/shard_map/ppermute | solution.py:47
  92.7 13.4 %collective-permute-start.14 = (bf16[4,128,128]{2,1,0:T(8,128)(2,1)S(1)}, bf16[4,128,128]{2,1,0:T(8,128)(2,1)}, u32[]{:S(2)}, u32[]{:S(2)}) collective-permute-start(bf16[4,128,128]{2,1,0:T(8,128)(2,1)S(1)} %get-tuple-element.221), channel_id=1, source_target_pairs={{0,2},{1,3},{2,4},{3,5},{4,6},{5,7},{6,0},{7,1},{8,10},{9,11},{10,... | collective-permute-start | bytes 393224 | tf_op jit(solution)/shard_map/ppermute | solution.py:47
  97.7 8.4 %collective-permute-start.12 = (bf16[4,128,128]{2,1,0:T(8,128)(2,1)S(1)}, bf16[4,128,128]{2,1,0:T(8,128)(2,1)}, u32[]{:S(2)}, u32[]{:S(2)}) collective-permute-start(bf16[4,128,128]{2,1,0:T(8,128)(2,1)S(1)} %get-tuple-element.148), channel_id=1, source_target_pairs={{0,6},{1,7},{2,0},{3,1},{4,2},{5,3},{6,4},{7,5},{8,14},{9,15},{10,... | collective-permute-start | bytes 393224 | tf_op jit(solution)/shard_map/ppermute | solution.py:47
  103.2 14.5 %collective-permute-start.22 = (bf16[768,384]{1,0:T(8,128)(2,1)}, bf16[768,384]{1,0:T(8,128)(2,1)S(1)}, u32[]{:S(2)}, u32[]{:S(2)}) collective-permute-start(bf16[768,384]{1,0:T(8,128)(2,1)} %get-tuple-element.157), channel_id=1, source_target_pairs={{0,1},{1,0},{2,3},{3,2},{4,5},{5,4},{6,7},{7,6},{8,9},{9,8},{10,11... | collective-permute-start | bytes 1769480 | tf_op jit(solution)/shard_map/ppermute | solution.py:42
  106.1 14.6 %collective-permute-start.19 = (bf16[2,96,384]{2,1,0:T(8,128)(2,1)}, bf16[2,96,384]{2,1,0:T(8,128)(2,1)S(1)}, u32[]{:S(2)}, u32[]{:S(2)}) collective-permute-start(bf16[2,96,384]{2,1,0:T(8,128)(2,1)} %get-tuple-element.170), channel_id=1, source_target_pairs={{0,2},{1,3},{2,0},{3,1},{4,6},{5,7},{6,4},{7,5},{8,10},{9,11},{10,... | collective-permute-start | bytes 442376 | tf_op jit(solution)/shard_map/ppermute | solution.py:42
  106.6 15.5 %collective-permute-start.20 = (bf16[2,96,384]{2,1,0:T(8,128)(2,1)}, bf16[2,96,384]{2,1,0:T(8,128)(2,1)S(1)}, u32[]{:S(2)}, u32[]{:S(2)}) collective-permute-start(bf16[2,96,384]{2,1,0:T(8,128)(2,1)} %get-tuple-element.171), channel_id=1, source_target_pairs={{0,4},{1,5},{2,6},{3,7},{4,0},{5,1},{6,2},{7,3},{8,12},{9,13},{10,... | collective-permute-start | bytes 442376 | tf_op jit(solution)/shard_map/ppermute | solution.py:42
  108.2 13.9 %collective-permute-start.21 = (bf16[2,96,384]{2,1,0:T(8,128)(2,1)}, bf16[2,96,384]{2,1,0:T(8,128)(2,1)S(1)}, u32[]{:S(2)}, u32[]{:S(2)}) collective-permute-start(bf16[2,96,384]{2,1,0:T(8,128)(2,1)} %get-tuple-element.172), channel_id=1, source_target_pairs={{0,6},{1,7},{2,4},{3,5},{4,2},{5,3},{6,0},{7,1},{8,14},{9,15},{10,... | collective-permute-start | bytes 442376 | tf_op jit(solution)/shard_map/ppermute | solution.py:42
  116.5 5.6 %collective-permute-start.18 = (bf16[512,128]{1,0:T(8,128)(2,1)}, bf16[512,128]{1,0:T(8,128)(2,1)S(1)}, u32[]{:S(2)}, u32[]{:S(2)}) collective-permute-start(bf16[512,128]{1,0:T(8,128)(2,1)} %get-tuple-element.169), channel_id=1, source_target_pairs={{0,1},{1,0},{2,3},{3,2},{4,5},{5,4},{6,7},{7,6},{8,9},{9,8},{10,11... | collective-permute-start | bytes 393224 | tf_op jit(solution)/shard_map/ppermute | solution.py:42
  120.7 8.8 %collective-permute-start.27 = (bf16[1,48,1536]{2,1,0:T(8,128)(2,1)}, bf16[1,48,1536]{2,1,0:T(8,128)(2,1)S(1)}, u32[]{:S(2)}, u32[]{:S(2)}) collective-permute-start(bf16[1,48,1536]{2,1,0:T(8,128)(2,1)} %get-tuple-element.178), channel_id=1, source_target_pairs={{0,4},{1,5},{2,6},{3,7},{4,0},{5,1},{6,2},{7,3},{8,12},{9,13},{10,... | collective-permute-start | bytes 442376 | tf_op jit(solution)/shard_map/ppermute | solution.py:42
  120.7 17.4 %collective-permute-start.26 = (bf16[192,768]{1,0:T(8,128)(2,1)}, bf16[192,768]{1,0:T(8,128)(2,1)S(1)}, u32[]{:S(2)}, u32[]{:S(2)}) collective-permute-start(bf16[192,768]{1,0:T(8,128)(2,1)} %bitcast.37), channel_id=1, source_target_pairs={{4,0},{5,1},{6,2},{7,3},{8,12},{9,13},{10,14},{11,15},{20,16},{21,... | collective-permute-start | bytes 884744 | tf_op jit(solution)/shard_map/ppermute | solution.py:57
  122.7 6.8 %copy-start.6 = (bf16[1,48,1536]{2,1,0:T(8,128)(2,1)S(1)}, bf16[1,48,1536]{2,1,0:T(8,128)(2,1)}, u32[]{:S(2)}) copy-start(bf16[1,48,1536]{2,1,0:T(8,128)(2,1)} %get-tuple-element.190) | copy-start | bytes 442372
  122.7 8.5 %copy-start.7 = (bf16[2,96,384]{2,1,0:T(8,128)(2,1)S(1)}, bf16[2,96,384]{2,1,0:T(8,128)(2,1)}, u32[]{:S(2)}) copy-start(bf16[2,96,384]{2,1,0:T(8,128)(2,1)} %get-tuple-element.160) | copy-start | bytes 442372
  124.5 14.6 %copy-start.3 = (bf16[1,192,768]{2,1,0:T(8,128)(2,1)S(1)}, bf16[1,192,768]{2,1,0:T(8,128)(2,1)}, u32[]{:S(2)}) copy-start(bf16[1,192,768]{2,1,0:T(8,128)(2,1)} %get-tuple-element.179) | copy-start | bytes 884740
  124.5 14.6 %collective-permute-start.23 = (bf16[224,128]{1,0:T(8,128)(2,1)}, bf16[224,128]{1,0:T(8,128)(2,1)S(1)}, u32[]{:S(2)}, u32[]{:S(2)}) collective-permute-start(bf16[224,128]{1,0:T(8,128)(2,1)} %get-tuple-element.186), channel_id=1, source_target_pairs={{0,2},{1,3},{2,0},{3,1},{4,6},{5,7},{6,4},{7,5},{8,10},{9,11},{10,... | collective-permute-start | bytes 172040 | tf_op jit(solution)/shard_map/ppermute | solution.py:42
  127.0 15.1 %collective-permute-start.24 = (bf16[224,128]{1,0:T(8,128)(2,1)}, bf16[224,128]{1,0:T(8,128)(2,1)S(1)}, u32[]{:S(2)}, u32[]{:S(2)}) collective-permute-start(bf16[224,128]{1,0:T(8,128)(2,1)} %get-tuple-element.187), channel_id=1, source_target_pairs={{0,4},{1,5},{2,6},{3,7},{4,0},{5,1},{6,2},{7,3},{8,12},{9,13},{10,... | collective-permute-start | bytes 172040 | tf_op jit(solution)/shard_map/ppermute | solution.py:42
  129.5 12.7 %collective-permute-start.25 = (bf16[224,128]{1,0:T(8,128)(2,1)}, bf16[224,128]{1,0:T(8,128)(2,1)S(1)}, u32[]{:S(2)}, u32[]{:S(2)}) collective-permute-start(bf16[224,128]{1,0:T(8,128)(2,1)} %get-tuple-element.188), channel_id=1, source_target_pairs={{0,6},{1,7},{2,4},{3,5},{4,2},{5,3},{6,0},{7,1},{8,14},{9,15},{10,... | collective-permute-start | bytes 172040 | tf_op jit(solution)/shard_map/ppermute | solution.py:42
  129.5 16.3 %collective-permute-start.31 = (bf16[48,1536]{1,0:T(8,128)(2,1)S(1)}, bf16[48,1536]{1,0:T(8,128)(2,1)S(1)}, u32[]{:S(2)}, u32[]{:S(2)}) collective-permute-start(bf16[48,1536]{1,0:T(8,128)(2,1)S(1)} %fusion.9), channel_id=1, source_target_pairs={{0,16},{8,24},{16,0},{24,8},{1,17},{9,25},{17,1},{25,9},{2,18},{10... | collective-permute-start | bytes 442376 | tf_op jit(solution)/shard_map/ppermute | solution.py:42
  138.1 8.8 %collective-permute-start.34 = (bf16[2,96,384]{2,1,0:T(8,128)(2,1)S(1)}, bf16[2,96,384]{2,1,0:T(8,128)(2,1)S(1)}, u32[]{:S(2)}, u32[]{:S(2)}) collective-permute-start(bf16[2,96,384]{2,1,0:T(8,128)(2,1)S(1)} %add_convert_fusion.2), channel_id=1, source_target_pairs={{0,16},{8,24},{16,0},{24,8},{1,17},{9,25},{17,1},{25,9},{2,18},{10... | collective-permute-start | bytes 442376 | tf_op jit(solution)/shard_map/ppermute | solution.py:42
  139.1 3.1 %copy-start.19 = (bf16[224,128]{1,0:T(8,128)(2,1)}, bf16[224,128]{1,0:T(8,128)(2,1)S(1)}, u32[]{:S(2)}) copy-start(bf16[224,128]{1,0:T(8,128)(2,1)S(1)} %collective-permute-done.23.refs_1_) | copy-start | bytes 172036
  139.1 8.6 %collective-permute-start.33 = (bf16[192,768]{1,0:T(8,128)(2,1)S(1)}, bf16[192,768]{1,0:T(8,128)(2,1)S(1)}, u32[]{:S(2)}, u32[]{:S(2)}) collective-permute-start(bf16[192,768]{1,0:T(8,128)(2,1)S(1)} %add_convert_fusion), channel_id=1, source_target_pairs={{0,16},{1,17},{2,18},{3,19},{12,28},{13,29},{14,30},{15,31},{16,0}... | collective-permute-start | bytes 884744 | tf_op jit(solution)/shard_map/ppermute | solution.py:63
  145.0 5.1 %collective-permute-start.28 = (bf16[224,128]{1,0:T(8,128)(2,1)}, bf16[224,128]{1,0:T(8,128)(2,1)S(1)}, u32[]{:S(2)}, u32[]{:S(2)}) collective-permute-start(bf16[224,128]{1,0:T(8,128)(2,1)} %message_sum.1.refs_0_), channel_id=1, source_target_pairs={{0,8},{8,0},{16,24},{24,16},{1,9},{9,1},{17,25},{25,17},{2,10},{10... | collective-permute-start | bytes 172040 | tf_op jit(solution)/shard_map/ppermute | solution.py:42
  145.0 5.1 %collective-permute-start.29 = (bf16[224,128]{1,0:T(8,128)(2,1)}, bf16[224,128]{1,0:T(8,128)(2,1)S(1)}, u32[]{:S(2)}, u32[]{:S(2)}) collective-permute-start(bf16[224,128]{1,0:T(8,128)(2,1)} %message_sum.1.refs_0_), channel_id=1, source_target_pairs={{0,16},{8,24},{16,0},{24,8},{1,17},{9,25},{17,1},{25,9},{2,18},{10... | collective-permute-start | bytes 172040 | tf_op jit(solution)/shard_map/ppermute | solution.py:42
  145.9 4.5 %collective-permute-start.30 = (bf16[224,128]{1,0:T(8,128)(2,1)}, bf16[224,128]{1,0:T(8,128)(2,1)S(1)}, u32[]{:S(2)}, u32[]{:S(2)}) collective-permute-start(bf16[224,128]{1,0:T(8,128)(2,1)} %message_sum.1.refs_0_), channel_id=1, source_target_pairs={{0,24},{8,16},{16,8},{24,0},{1,25},{9,17},{17,9},{25,1},{2,26},{10... | collective-permute-start | bytes 172040 | tf_op jit(solution)/shard_map/ppermute | solution.py:42
  146.9 1.6 %collective-permute-start.32 = (bf16[96,1536]{1,0:T(8,128)(2,1)S(1)}, bf16[96,1536]{1,0:T(8,128)(2,1)S(1)}, u32[]{:S(2)}, u32[]{:S(2)}) collective-permute-start(bf16[96,1536]{1,0:T(8,128)(2,1)S(1)} %pad_maximum_fusion.1), channel_id=1, source_target_pairs={{0,8},{8,0},{16,24},{24,16},{1,9},{9,1},{17,25},{25,17},{2,10},{10... | collective-permute-start | bytes 884744 | tf_op jit(solution)/shard_map/ppermute | solution.py:42
  147.7 2.6 %collective-permute-start.36 = (bf16[2,96,384]{2,1,0:T(8,128)(2,1)S(1)}, bf16[2,96,384]{2,1,0:T(8,128)(2,1)S(1)}, u32[]{:S(2)}, u32[]{:S(2)}) collective-permute-start(bf16[2,96,384]{2,1,0:T(8,128)(2,1)S(1)} %add_convert_fusion.1.refs_6_), channel_id=1, source_target_pairs={{0,8},{8,0},{16,24},{24,16},{1,9},{9,1},{17,25},{25,17},{2,10},{10... | collective-permute-start | bytes 442376 | tf_op jit(solution)/shard_map/ppermute | solution.py:42
  147.9 2.1 %copy-start.1 = (bf16[384,768]{1,0:T(8,128)(2,1)}, bf16[384,768]{1,0:T(8,128)(2,1)S(1)}, u32[]{:S(2)}) copy-start(bf16[384,768]{1,0:T(8,128)(2,1)S(1)} %pad_maximum_fusion.refs_4_) | copy-start | bytes 1769476
  148.5 2.0 %collective-permute-start.35 = (bf16[384,768]{1,0:T(8,128)(2,1)S(1)}, bf16[384,768]{1,0:T(8,128)(2,1)S(1)}, u32[]{:S(2)}, u32[]{:S(2)}) collective-permute-start(bf16[384,768]{1,0:T(8,128)(2,1)S(1)} %pad_maximum_fusion.refs_4_), channel_id=1, source_target_pairs={{0,8},{8,0},{16,24},{24,16},{1,9},{9,1},{17,25},{25,17},{2,10},{10... | collective-permute-start | bytes 1769480 | tf_op jit(solution)/shard_map/ppermute | solution.py:42
  (11 other events, 7.5 us)

commit v7 on v6

--- a/solution.py
+++ b/solution.py
@@ -483,18 +483,21 @@
     do = stacked(do_ref)
     do32 = do.astype(F32)
 
+    every = [dot_nt(q, keys[h]) for h in range(2)]
     expd, mixed = [], []
     for h in range(2):
-        scores = dot_nt(q, keys[h])
+        scores = every[h]
         scores = jnp.concatenate([jnp.where(seen, scores[:, :span], MASKED), scores[:, span:] + absent], axis=1)
         top = jnp.max(scores, axis=1, keepdims=True)
         expd.append(jnp.exp(scores - top).astype(BF16))
+    for h in range(2):
         mixed.append(dot(expd[h], summing[h]))
     total = jnp.where(low, pltpu.roll(mixed[0], HEAD_DIM, 1), pltpu.roll(mixed[1], HEAD_DIM, 1))
     inverse = 1.0 / total
     out = jnp.where(low, mixed[0], mixed[1]) * inverse
     for p in range(PAIRS):
         out_ref[:, p * 128 : (p + 1) * 128] = out[p * span : (p + 1) * span].astype(BF16)
+    dprobs = [dot_nt(do, values[h]) for h in range(2)]
     product = do32 * out
     do_t = (do32 * inverse).T.astype(BF16)
     q_t = (q.astype(F32) * inverse).T.astype(BF16)
@@ -502,7 +505,7 @@
     for h in range(2):
         head = slice(h * HEAD_DIM, (h + 1) * HEAD_DIM)
         delta = jnp.sum(jnp.where(low == (h == 0), product, 0.0), axis=1, keepdims=True)
-        dprob = dot_nt(do, values[h])
+        dprob = dprobs[h]
         dscore = (expd[h].astype(F32) * (dprob - delta)).astype(BF16)
         dq = dq + dot(dscore, keys[h])
         dk = dk + dot(q_t[head], dscore)

time: 155 us -> 156 us (level)
  waiting for transfers between devices: 8.43 us -> 11.4 us
    ppermute x29, waiting for transfers between devices: 1.14 us -> 7.29 us  [flipped(): lax.ppermute(block, axis, [(i, i ^ bits) for i in range(lax.axis_size(axi...]
    ppermute x1, waiting for transfers between devices: 6.86 us -> 3.96 us  [to_owner(): return lax.ppermute(block, ('batch', 'seq'), route)]
    ppermute x29, starting transfers between devices: 27.9 us -> 26.2 us  [flipped(): lax.ppermute(block, axis, [(i, i ^ bits) for i in range(lax.axis_size(axi...]
  transfers between devices with their start and end apart: 37 -> 37, of which waited for: 5 -> 8; matrix products, arithmetic and copies ran while one was open for 3% -> 3% of each run, Pallas kernels for 59% -> 58%
where the time goes in v7:
time: 156 us; the launch traced here: 155 us
  Pallas kernels  91.9 us (59%)
  starting transfers between devices  40.5 us (26%)
  waiting for transfers between devices  11.4 us (7%)
  other arithmetic  5.14 us (3%)
  local copies, waits for them, and re-layouts  5 us (3%)
    pallas_call x1, Pallas kernels, feed(): pl.pallas_call(feed_kernel, grid_spec=spec, out_shape=[SHAPE((rows, D), B...  28.7 us
    ppermute x29, starting transfers between devices, flipped(): lax.ppermute(block, axis, [(i, i ^ bits) for i in range(lax.axis_size(axi...  26.2 us
    pallas_call x1, Pallas kernels, attention(): pl.pallas_call(kernel, grid=(seqs, PAIRS // groups), in_specs=[SMEM] + [t...  23.5 us
    ppermute x6, starting transfers between devices, along(): lax.ppermute(block, 'seq', [(i, (i + 2 * distance) % size) for i in range...  9.73 us
    ppermute x29, waiting for transfers between devices, flipped(): lax.ppermute(block, axis, [(i, i ^ bits) for i in range(lax.axis_size(axi...  7.29 us
    pallas_call x1, Pallas kernels, weights(): pl.pallas_call(weights_kernel, grid_spec=pltpu.PrefetchScalarGridSpec(num...  6.04 us
    pallas_call x1, Pallas kernels, finish(): pl.pallas_call(functools.partial(finish_kernel, rows // tables.shape[1],...  5.93 us
    unnamed x44, local copies, waits for them, and re-layouts  5 us
  transfers between devices with their start and end apart: 37, of which 8 were waited for; matrix products, arithmetic and copies ran while one was open for 3% of the time, Pallas kernels for 58%

profile of v7, /device:TPU:0, one launch (start us, length us, event | category | flops | bytes accessed | tf_op | source)
XLA Modules:
  0.0 155.0 jit_solution(13186154133905508811)
XLA Ops:
  1.2 1.0 fusion.2.tables_ref.refs_6_.refs_14_
  2.2 2.9 %project_keys.1 = (bf16[512,128]{1,0:T(8,128)(2,1)}, bf16[512,768]{1,0:T(8,128)(2,1)}) custom-call(bf16[512,768]{1,0:T(8,128)(2,1)} %bitcast.50, f32[768]{0:T(1024)} %refs_10_.1, f32[768]{0:T(1024)} %refs_11_.1, bf16[768,896]{1,0:T(8,128)(2,1)} %refs_13_.1, f32[896]{0:T(1024)} %add_ref.4, f32[3,128,128]{2,1,0:T(8,128)} %fusion.2.tables_ref.refs_6_.refs_14_), custom_call_target="tpu_custom_call" | custom-call | flops 3000000000 | tf_op jit(solution)/shard_map/project_keys/pallas_call | solution.py:253
  5.1 2.6 %collective-permute-start = (bf16[4,128,128]{2,1,0:T(8,128)(2,1)}, bf16[4,128,128]{2,1,0:T(8,128)(2,1)S(1)}, u32[]{:S(2)}, u32[]{:S(2)}) collective-permute-start(bf16[4,128,128]{2,1,0:T(8,128)(2,1)} %bitcast.40), channel_id=1, source_target_pairs={{0,1},{1,0},{2,3},{3,2},{4,5},{5,4},{6,7},{7,6},{8,9},{9,8},{10,11... | collective-permute-start | bytes 393224 | tf_op jit(solution)/shard_map/ppermute | solution.py:42
  8.2 3.7 %project_queries.1 = bf16[512,768]{1,0:T(8,128)(2,1)} custom-call(bf16[512,768]{1,0:T(8,128)(2,1)} %get-tuple-element.118.first_ref.in_ref, bf16[768,896]{1,0:T(8,128)(2,1)} %refs_13_.1, f32[896]{0:T(1024)} %add_ref.4, f32[3,128,128]{2,1,0:T(8,128)} %fusion.2.tables_ref.refs_6_.refs_14_), custom_call_target="tpu_custom_call" | custom-call | flops 6000000000 | tf_op jit(solution)/shard_map/project_queries/pallas_call | solution.py:275
  12.5 1.6 %collective-permute-start.1 = (bf16[2,4,128,128]{3,2,1,0:T(8,128)(2,1)S(1)}, bf16[2,4,128,128]{3,2,1,0:T(8,128)(2,1)S(1)}, u32[]{:S(2)}, u32[]{:S(2)}) collective-permute-start(bf16[2,4,128,128]{3,2,1,0:T(8,128)(2,1)S(1)} %pad_maximum_fusion.2.refs_0_), channel_id=1, source_target_pairs={{0,2},{1,3},{2,4},{3,5},{4,6},{5,7},{6,0},{7,1},{8,10},{9,11},{10,... | collective-permute-start | bytes 786440 | tf_op jit(solution)/shard_map/ppermute | solution.py:47
  14.2 2.6 %collective-permute-start.2 = (bf16[2,4,128,128]{3,2,1,0:T(8,128)(2,1)S(1)}, bf16[2,4,128,128]{3,2,1,0:T(8,128)(2,1)S(1)}, u32[]{:S(2)}, u32[]{:S(2)}) collective-permute-start(bf16[2,4,128,128]{3,2,1,0:T(8,128)(2,1)S(1)} %pad_maximum_fusion.2.refs_0_), channel_id=1, source_target_pairs={{0,4},{1,5},{2,6},{3,7},{4,0},{5,1},{6,2},{7,3},{8,12},{9,13},{10,... | collective-permute-start | bytes 786440 | tf_op jit(solution)/shard_map/ppermute | solution.py:47
  16.8 1.3 collective-permute-start.3
  18.1 28.7 %feed_forward.1 = (bf16[512,768]{1,0:T(8,128)(2,1)}, bf16[512,768]{1,0:T(8,128)(2,1)}, bf16[2,512,768]{2,1,0:T(8,128)(2,1)}, bf16[512,768]{1,0:T(8,128)(2,1)}, f...) custom-call(s32[4]{0:T(128)} %pad_add_fusion.place_ref, ...), custom_call_target="tpu_custom_call" | custom-call | flops 35999997952 | tf_op jit(solution)/shard_map/feed_forward/pallas_call | solution.py:437
  46.9 0.7 collective-permute-start.10
  47.6 1.5 collective-permute-start.9
  49.1 0.7 copy-done.13
  49.8 23.5 %attention.1 = (bf16[2,4,128,768]{3,2,1,0:T(8,128)(2,1)}, bf16[4,4,128,128]{3,2,1,0:T(8,128)(2,1)}, bf16[4,4,128,128]{3,2,1,0:T(8,128)(2,1)}) custom-call(s32[4]{0:T(128)} %pad_add_fusion.place_ref, bf16[2,4,128,128]{3,2,1,0:T(8,128)(2,1)} %copy-done.4, bf16[2,4,128,128]{3,2,1,0:T(8,128)(2,1)} %copy-done.12, bf16[2,4,128,128]{3,2,1,0:T(8,128)(2,1)} %copy-done.13, ...), custom_call_target="tpu_custom_call" | custom-call | flops 30000001024 | tf_op jit(solution)/shard_map/attention/pallas_call | solution.py:698
  73.3 1.3 collective-permute-start.7
  74.6 0.9 collective-permute-done.10
  76.0 4.2 %add_split.1 = (bf16[2,96,1536]{2,1,0:T(8,128)(2,1)}, bf16[2,96,1536]{2,1,0:T(8,128)(2,1)}, bf16[2,192,768]{2,1,0:T(8,128)(2,1)}, bf16[2,192,768]{2,1,0:T(8,128)(2,1)}) custom-call(s32[4]{0:T(128)} %pad_add_fusion.place_ref, bf16[2,2,96,1536]{3,2,1,0:T(8,128)(2,1)} %bitcast.60, bf16[2,2,96,1536]{3,2,1,0:T(8,128)(2,1)} %bitcast.14.refs_1_, ...), custom_call_target="tpu_custom_call" | custom-call | flops 17999998976 | tf_op jit(solution)/shard_map/add_split/pallas_call | solution.py:143
  80.2 1.3 collective-permute-start.16
  81.6 1.5 collective-permute-start.17
  83.1 6.0 %weights.1 = (bf16[2,4,96,384]{3,2,1,0:T(8,128)(2,1)}, bf16[2,4,96,384]{3,2,1,0:T(8,128)(2,1)}, f32[8,768]{1,0:T(8,128)}) custom-call(s32[4]{0:T(128)} %pad_add_fusion.place_ref, bf16[2,512,768]{2,1,0:T(8,128)(2,1)} %bitcast.45, bf16[2,512,768]{2,1,0:T(8,128)(2,1)} %collective-permute-done.8.attn2_ref.q2_ref, bf16[512,768]{1,0:T(8,128)(2,1)} %bitcast.55, ...), custom_call_target="tpu_custom_call" | custom-call | flops 7200000000 | tf_op jit(solution)/shard_map/weights/pallas_call | solution.py:743
  89.1 1.3 collective-permute-start.15
  90.4 1.9 %add_convert_fusion.4 = (bf16[1,4,128,128]{3,2,1,0:T(8,128)(2,1)}, bf16[4,128,128]{2,1,0:T(8,128)(2,1)S(1)}, bf16[4,128,128]{2,1,0:T(8,128)(2,1)S(1)}, bf16[4,128,128]{2,1,0:T(8,128)(2,1)S(1)}) fusion(bf16[4,4,128,128]{3,2,1,0:T(8,128)(2,1)} %collective-permute-done.7, bf16[4,4,128,128]{3,2,1,0:T(8,128)(2,1)S(1)} %copy-done.2), kind=kLoop, calls=%fused_computation.20 | loop fusion | flops 1048576 | bytes 1572864 | tf_op jit(solution)/shard_map/convert_element_type | solution.py:1009
  92.7 1.1 collective-permute-start.14
  93.7 4.0 %mix.1 = bf16[512,768]{1,0:T(8,128)(2,1)} custom-call(bf16[512,768]{1,0:T(8,128)(2,1)} %bitcast.52, bf16[512,768]{1,0:T(8,128)(2,1)} %get-tuple-element.146.mlp_ref, bf16[2,512,768]{2,1,0:T(8,128)(2,1)} %collective-permute-done.11.mlp2_ref.refs_9_, bf16[2,512,768]{2,1,0:T(8,128)(2,1)} %bitcast.47, f32[768]{0:T(1024)} %add_ref.5, bf16[768,768]{1,0:T(8,128)(2,1)} %wo_ref.3), custom_call_target="tpu_custom_call" | custom-call | flops 3600000000 | tf_op jit(solution)/shard_map/mix/pallas_call | solution.py:769
  97.7 2.8 %collective-permute-start.12 = (bf16[4,128,128]{2,1,0:T(8,128)(2,1)S(1)}, bf16[4,128,128]{2,1,0:T(8,128)(2,1)}, u32[]{:S(2)}, u32[]{:S(2)}) collective-permute-start(bf16[4,128,128]{2,1,0:T(8,128)(2,1)S(1)} %get-tuple-element.148), channel_id=1, source_target_pairs={{0,6},{1,7},{2,0},{3,1},{4,2},{5,3},{6,4},{7,5},{8,14},{9,15},{10,... | collective-permute-start | bytes 393224 | tf_op jit(solution)/shard_map/ppermute | solution.py:47
  100.5 2.7 %exchange_split.1 = (bf16[768,384]{1,0:T(8,128)(2,1)}, bf16[2,48,1536]{2,1,0:T(8,128)(2,1)}, bf16[1,192,768]{2,1,0:T(8,128)(2,1)}) custom-call(s32[4]{0:T(128)} %pad_add_fusion.place_ref, bf16[2,2,48,1536]{3,2,1,0:T(8,128)(2,1)} %bitcast.66, bf16[2,2,48,1536]{3,2,1,0:T(8,128)(2,1)} %bitcast.23.b1, bf16[1,2,192,768]{3,2,1,0:T(8,128)(2,1)} %bitcast.67, ...), custom_call_target="tpu_custom_call" | custom-call | flops 3600000000 | tf_op jit(solution)/shard_map/exchange_split/pallas_call | solution.py:170
  103.2 0.8 collective-permute-start.22
  104.0 2.1 %add_cut.1 = (bf16[2,96,384]{2,1,0:T(8,128)(2,1)}, bf16[2,96,384]{2,1,0:T(8,128)(2,1)}, bf16[2,96,384]{2,1,0:T(8,128)(2,1)}, bf16[2,96,384]{2,1,0:T(8,128)(2,1)}) custom-call(s32[4]{0:T(128)} %pad_add_fusion.place_ref, bf16[2,4,96,384]{3,2,1,0:T(8,128)(2,1)} %get-tuple-element.158.a_ref, bf16[2,4,96,384]{3,2,1,0:T(8,128)(2,1)} %collective-permute-done.15.b_ref), custom_call_target="tpu_custom_call" | custom-call | flops 3600000000 | tf_op jit(solution)/shard_map/add_cut/pallas_call | solution.py:222
  106.1 1.0 collective-permute-start.19
  107.1 0.9 collective-permute-start.20
  107.9 2.6 %collective-permute-start.21 = (bf16[2,96,384]{2,1,0:T(8,128)(2,1)}, bf16[2,96,384]{2,1,0:T(8,128)(2,1)S(1)}, u32[]{:S(2)}, u32[]{:S(2)}) collective-permute-start(bf16[2,96,384]{2,1,0:T(8,128)(2,1)} %get-tuple-element.172), channel_id=1, source_target_pairs={{0,6},{1,7},{2,4},{3,5},{4,2},{5,3},{6,0},{7,1},{8,14},{9,15},{10,... | collective-permute-start | bytes 442376 | tf_op jit(solution)/shard_map/ppermute | solution.py:42
  110.6 5.9 %finish.1 = (bf16[512,768]{1,0:T(8,128)(2,1)}, bf16[512,128]{1,0:T(8,128)(2,1)}, bf16[512,128]{1,0:T(8,128)(2,1)}) custom-call(s32[4]{0:T(128)} %pad_add_fusion.place_ref, bf16[512,128]{1,0:T(8,128)(2,1)} %bitcast.39, bf16[512,128]{1,0:T(8,128)(2,1)} %bitcast.26.refs_1_, bf16[512,128]{1,0:T(8,128)(2,1)} %bitcast.27.refs_2_, ...), custom_call_target="tpu_custom_call" | custom-call | flops 7200000000 | tf_op jit(solution)/shard_map/finish/pallas_call | solution.py:863
  116.5 1.3 collective-permute-start.18
  117.8 0.8 copy-done
  118.6 2.1 %exchange_add.1 = (bf16[1,48,1536]{2,1,0:T(8,128)(2,1)}, bf16[1,48,1536]{2,1,0:T(8,128)(2,1)}, bf16[1,192,768]{2,1,0:T(8,128)(2,1)}) custom-call(s32[4]{0:T(128)} %pad_add_fusion.place_ref, bf16[2,48,1536]{2,1,0:T(8,128)(2,1)} %get-tuple-element.175.a1, bf16[1,192,768]{2,1,0:T(8,128)(2,1)} %get-tuple-element.176.a2, bf16[768,384]{1,0:T(8,128)(2,1)} %copy-done), custom_call_target="tpu_custom_call" | custom-call | flops 30000000 | tf_op jit(solution)/shard_map/exchange_add/pallas_call | solution.py:202
  120.7 1.3 collective-permute-start.26
  122.1 0.6 copy-done.15
  122.7 1.7 %message_cut.1 = (bf16[224,128]{1,0:T(8,128)(2,1)}, bf16[224,128]{1,0:T(8,128)(2,1)}, bf16[224,128]{1,0:T(8,128)(2,1)}, bf16[224,128]{1,0:T(8,128)(2,1)}) custom-call(s32[4]{0:T(128)} %pad_add_fusion.place_ref, bf16[512,128]{1,0:T(8,128)(2,1)} %get-tuple-element.183.a_ref, bf16[512,128]{1,0:T(8,128)(2,1)} %copy-done.15), custom_call_target="tpu_custom_call" | custom-call | flops 1800000000 | tf_op jit(solution)/shard_map/message_cut/pallas_call | solution.py:897
  124.5 2.3 %collective-permute-start.23 = (bf16[224,128]{1,0:T(8,128)(2,1)}, bf16[224,128]{1,0:T(8,128)(2,1)S(1)}, u32[]{:S(2)}, u32[]{:S(2)}) collective-permute-start(bf16[224,128]{1,0:T(8,128)(2,1)} %get-tuple-element.186), channel_id=1, source_target_pairs={{0,2},{1,3},{2,0},{3,1},{4,6},{5,7},{6,4},{7,5},{8,10},{9,11},{10,... | collective-permute-start | bytes 172040 | tf_op jit(solution)/shard_map/ppermute | solution.py:42
  126.8 2.7 %collective-permute-start.24 = (bf16[224,128]{1,0:T(8,128)(2,1)}, bf16[224,128]{1,0:T(8,128)(2,1)S(1)}, u32[]{:S(2)}, u32[]{:S(2)}) collective-permute-start(bf16[224,128]{1,0:T(8,128)(2,1)} %get-tuple-element.187), channel_id=1, source_target_pairs={{0,4},{1,5},{2,6},{3,7},{4,0},{5,1},{6,2},{7,3},{8,12},{9,13},{10,... | collective-permute-start | bytes 172040 | tf_op jit(solution)/shard_map/ppermute | solution.py:42
  129.5 4.8 %collective-permute-done.27 = bf16[1,48,1536]{2,1,0:T(8,128)(2,1)S(1)} collective-permute-done((bf16[1,48,1536]{2,1,0:T(8,128)(2,1)}, bf16[1,48,1536]{2,1,0:T(8,128)(2,1)S(1)}, u32[]{:S(2)}, u32[]{:S(2)}) %collective-permute-start.27) | collective-permute-done | bytes 147488 | tf_op jit(solution)/shard_map/ppermute | solution.py:42
  134.5 4.0 %collective-permute-done.26 = bf16[192,768]{1,0:T(8,128)(2,1)S(1)} collective-permute-done((bf16[192,768]{1,0:T(8,128)(2,1)}, bf16[192,768]{1,0:T(8,128)(2,1)S(1)}, u32[]{:S(2)}, u32[]{:S(2)}) %collective-permute-start.26) | collective-permute-done | bytes 294944 | tf_op jit(solution)/shard_map/ppermute | solution.py:57
  138.5 0.7 collective-permute-start.34
  139.3 3.3 %collective-permute-start.33 = (bf16[192,768]{1,0:T(8,128)(2,1)S(1)}, bf16[192,768]{1,0:T(8,128)(2,1)S(1)}, u32[]{:S(2)}, u32[]{:S(2)}) collective-permute-start(bf16[192,768]{1,0:T(8,128)(2,1)S(1)} %add_convert_fusion), channel_id=1, source_target_pairs={{0,16},{1,17},{2,18},{3,19},{12,28},{13,29},{14,30},{15,31},{16,0}... | collective-permute-start | bytes 884744 | tf_op jit(solution)/shard_map/ppermute | solution.py:63
  143.8 1.6 %message_sum.1.refs_0_ = bf16[224,128]{1,0:T(8,128)(2,1)} custom-call(bf16[224,128]{1,0:T(8,128)(2,1)} %get-tuple-element.185.refs_0_, bf16[224,128]{1,0:T(8,128)(2,1)} %copy-done.19, bf16[224,128]{1,0:T(8,128)(2,1)} %copy-done.20, bf16[224,128]{1,0:T(8,128)(2,1)} %copy-done.21), custom_call_target="tpu_custom_call" | custom-call | flops 1800000000 | tf_op jit(solution)/shard_map/message_sum/pallas_call | solution.py:918
  145.4 0.7 collective-permute-start.29
  146.0 1.2 collective-permute-start.30
  149.3 1.1 maximum_convert_fusion
  151.4 0.8 copy-done.11
  152.3 2.8 %last_sums.1 = (f32[3072]{0:T(1024)}, f32[896]{0:T(1024)}, f32[768]{0:T(1024)}, f32[768]{0:T(1024)}, f32[768]{0:T(1024)}, /*index=5*/f32[768]{0:T(1024)}, f32[76...) custom-call(s32[4]{0:T(128)} %pad_add_fusion.place_ref, bf16[224,128]{1,0:T(8,128)(2,1)} %message_sum.1.refs_0_, ...), custom_call_target="tpu_custom_call" | custom-call | flops 1800000000 | tf_op jit(solution)/shard_map/last_sums/pallas_call | solution.py:953
  (102 shorter events, 7.2 us)
Async XLA Ops:
  0.6 17.5 %collective-permute-start.5 = (bf16[512,768]{1,0:T(8,128)(2,1)}, bf16[512,768]{1,0:T(8,128)(2,1)}, u32[]{:S(2)}, u32[]{:S(2)}) collective-permute-start(bf16[512,768]{1,0:T(8,128)(2,1)} %bitcast.49), channel_id=1, source_target_pairs={{0,8},{8,0},{16,24},{24,16},{1,9},{9,1},{17,25},{25,17},{2,10},{10... | collective-permute-start | bytes 2359304 | tf_op jit(solution)/shard_map/ppermute | solution.py:42
  2.2 5.6 %copy-start.9 = (bf16[4,128,768]{2,1,0:T(8,128)(2,1)S(1)}, bf16[4,128,768]{2,1,0:T(8,128)(2,1)}, u32[]{:S(2)}) copy-start(bf16[4,128,768]{2,1,0:T(8,128)(2,1)} %param.26) | copy-start | bytes 2359300
  5.1 7.4 %collective-permute-start = (bf16[4,128,128]{2,1,0:T(8,128)(2,1)}, bf16[4,128,128]{2,1,0:T(8,128)(2,1)S(1)}, u32[]{:S(2)}, u32[]{:S(2)}) collective-permute-start(bf16[4,128,128]{2,1,0:T(8,128)(2,1)} %bitcast.40), channel_id=1, source_target_pairs={{0,1},{1,0},{2,3},{3,2},{4,5},{5,4},{6,7},{7,6},{8,9},{9,8},{10,11... | collective-permute-start | bytes 393224 | tf_op jit(solution)/shard_map/ppermute | solution.py:42
  7.7 9.1 %collective-permute-start.4 = (bf16[512,768]{1,0:T(8,128)(2,1)}, bf16[512,768]{1,0:T(8,128)(2,1)S(1)}, u32[]{:S(2)}, u32[]{:S(2)}) collective-permute-start(bf16[512,768]{1,0:T(8,128)(2,1)} %get-tuple-element.118.first_ref.in_ref), channel_id=1, source_target_pairs={{0,8},{8,0},{16,24},{24,16},{1,9},{9,1},{17,25},{25,17},{2,10},{10... | collective-permute-start | bytes 2359304 | tf_op jit(solution)/shard_map/ppermute | solution.py:42
  7.9 4.6 %copy-start.8 = (bf16[512,128]{1,0:T(8,128)(2,1)S(1)}, bf16[512,128]{1,0:T(8,128)(2,1)}, u32[]{:S(2)}) copy-start(bf16[512,128]{1,0:T(8,128)(2,1)} %get-tuple-element.117) | copy-start | bytes 393220
  7.9 10.2 %collective-permute-start.6 = (bf16[512,768]{1,0:T(8,128)(2,1)S(1)}, bf16[512,768]{1,0:T(8,128)(2,1)}, u32[]{:S(2)}, u32[]{:S(2)}) collective-permute-start(bf16[512,768]{1,0:T(8,128)(2,1)S(1)} %bitcast.57), channel_id=1, source_target_pairs={{0,8},{8,0},{16,24},{24,16},{1,9},{9,1},{17,25},{25,17},{2,10},{10... | collective-permute-start | bytes 2359304 | tf_op jit(solution)/shard_map/ppermute | solution.py:42
  12.5 34.3 %copy-start.4 = (bf16[2,4,128,128]{3,2,1,0:T(8,128)(2,1)}, bf16[2,4,128,128]{3,2,1,0:T(8,128)(2,1)S(1)}, u32[]{:S(2)}) copy-start(bf16[2,4,128,128]{3,2,1,0:T(8,128)(2,1)S(1)} %pad_maximum_fusion.2.refs_0_) | copy-start | bytes 786436
  12.5 35.1 %collective-permute-start.1 = (bf16[2,4,128,128]{3,2,1,0:T(8,128)(2,1)S(1)}, bf16[2,4,128,128]{3,2,1,0:T(8,128)(2,1)S(1)}, u32[]{:S(2)}, u32[]{:S(2)}) collective-permute-start(bf16[2,4,128,128]{3,2,1,0:T(8,128)(2,1)S(1)} %pad_maximum_fusion.2.refs_0_), channel_id=1, source_target_pairs={{0,2},{1,3},{2,4},{3,5},{4,6},{5,7},{6,0},{7,1},{8,10},{9,11},{10,... | collective-permute-start | bytes 786440 | tf_op jit(solution)/shard_map/ppermute | solution.py:47
  14.2 35.0 %collective-permute-start.2 = (bf16[2,4,128,128]{3,2,1,0:T(8,128)(2,1)S(1)}, bf16[2,4,128,128]{3,2,1,0:T(8,128)(2,1)S(1)}, u32[]{:S(2)}, u32[]{:S(2)}) collective-permute-start(bf16[2,4,128,128]{3,2,1,0:T(8,128)(2,1)S(1)} %pad_maximum_fusion.2.refs_0_), channel_id=1, source_target_pairs={{0,4},{1,5},{2,6},{3,7},{4,0},{5,1},{6,2},{7,3},{8,12},{9,13},{10,... | collective-permute-start | bytes 786440 | tf_op jit(solution)/shard_map/ppermute | solution.py:47
  16.7 1.4 copy-start.10
  16.8 32.4 %collective-permute-start.3 = (bf16[2,4,128,128]{3,2,1,0:T(8,128)(2,1)S(1)}, bf16[2,4,128,128]{3,2,1,0:T(8,128)(2,1)}, u32[]{:S(2)}, u32[]{:S(2)}) collective-permute-start(bf16[2,4,128,128]{3,2,1,0:T(8,128)(2,1)S(1)} %pad_maximum_fusion.2.refs_0_), channel_id=1, source_target_pairs={{0,6},{1,7},{2,0},{3,1},{4,2},{5,3},{6,4},{7,5},{8,14},{9,15},{10,... | collective-permute-start | bytes 786440 | tf_op jit(solution)/shard_map/ppermute | solution.py:47
  46.8 29.2 %collective-permute-start.11 = (bf16[2,512,768]{2,1,0:T(8,128)(2,1)}, bf16[2,512,768]{2,1,0:T(8,128)(2,1)}, u32[]{:S(2)}, u32[]{:S(2)}) collective-permute-start(bf16[2,512,768]{2,1,0:T(8,128)(2,1)} %get-tuple-element.135), channel_id=1, source_target_pairs={{0,8},{8,0},{16,24},{24,16},{1,9},{9,1},{17,25},{25,17},{2,10},{10... | collective-permute-start | bytes 4718600 | tf_op jit(solution)/shard_map/ppermute | solution.py:42
  46.9 28.7 %collective-permute-start.10 = (bf16[768,768]{1,0:T(8,128)(2,1)}, bf16[768,768]{1,0:T(8,128)(2,1)}, u32[]{:S(2)}, u32[]{:S(2)}) collective-permute-start(bf16[768,768]{1,0:T(8,128)(2,1)} %get-tuple-element.134), channel_id=1, source_target_pairs={{0,2},{1,3},{2,0},{3,1},{4,6},{5,7},{6,4},{7,5},{8,10},{9,11},{10,... | collective-permute-start | bytes 3538952 | tf_op jit(solution)/shard_map/ppermute | solution.py:42
  47.6 1.5 copy-start.12
  47.6 28.4 %collective-permute-start.9 = (bf16[8,48,1536]{2,1,0:T(8,128)(2,1)}, bf16[8,48,1536]{2,1,0:T(8,128)(2,1)}, u32[]{:S(2)}, u32[]{:S(2)}) collective-permute-start(bf16[8,48,1536]{2,1,0:T(8,128)(2,1)} %get-tuple-element.132), channel_id=1, source_target_pairs={{0,16},{8,24},{16,0},{24,8},{1,17},{9,25},{17,1},{25,9},{2,18},{10... | collective-permute-start | bytes 3538952 | tf_op jit(solution)/shard_map/ppermute | solution.py:42
  73.3 8.3 %collective-permute-start.8 = (bf16[2,512,768]{2,1,0:T(8,128)(2,1)}, bf16[2,512,768]{2,1,0:T(8,128)(2,1)}, u32[]{:S(2)}, u32[]{:S(2)}) collective-permute-start(bf16[2,512,768]{2,1,0:T(8,128)(2,1)} %bitcast.44), channel_id=1, source_target_pairs={{0,8},{8,0},{16,24},{24,16},{1,9},{9,1},{17,25},{25,17},{2,10},{10... | collective-permute-start | bytes 4718600 | tf_op jit(solution)/shard_map/ppermute | solution.py:42
  73.3 17.1 %collective-permute-start.7 = (bf16[4,4,128,128]{3,2,1,0:T(8,128)(2,1)}, bf16[4,4,128,128]{3,2,1,0:T(8,128)(2,1)}, u32[]{:S(2)}, u32[]{:S(2)}) collective-permute-start(bf16[4,4,128,128]{3,2,1,0:T(8,128)(2,1)} %get-tuple-element.129), channel_id=1, source_target_pairs={{0,1},{1,0},{2,3},{3,2},{4,5},{5,4},{6,7},{7,6},{8,9},{9,8},{10,11... | collective-permute-start | bytes 1572872 | tf_op jit(solution)/shard_map/ppermute | solution.py:42
  80.2 17.5 %collective-permute-start.16 = (bf16[2,96,1536]{2,1,0:T(8,128)(2,1)}, bf16[2,96,1536]{2,1,0:T(8,128)(2,1)}, u32[]{:S(2)}, u32[]{:S(2)}) collective-permute-start(bf16[2,96,1536]{2,1,0:T(8,128)(2,1)} %get-tuple-element.140), channel_id=1, source_target_pairs={{0,2},{1,3},{2,0},{3,1},{4,6},{5,7},{6,4},{7,5},{8,10},{9,11},{10,... | collective-permute-start | bytes 1769480 | tf_op jit(solution)/shard_map/ppermute | solution.py:42
  81.6 8.9 %copy-start.2 = (bf16[4,4,128,128]{3,2,1,0:T(8,128)(2,1)S(1)}, bf16[4,4,128,128]{3,2,1,0:T(8,128)(2,1)}, u32[]{:S(2)}) copy-start(bf16[4,4,128,128]{3,2,1,0:T(8,128)(2,1)} %get-tuple-element.143) | copy-start | bytes 1572868
  81.6 18.9 %collective-permute-start.17 = (bf16[2,192,768]{2,1,0:T(8,128)(2,1)}, bf16[2,192,768]{2,1,0:T(8,128)(2,1)}, u32[]{:S(2)}, u32[]{:S(2)}) collective-permute-start(bf16[2,192,768]{2,1,0:T(8,128)(2,1)} %get-tuple-element.152), channel_id=1, source_target_pairs={{0,16},{8,24},{16,0},{24,8},{1,17},{9,25},{17,1},{25,9},{2,18},{10... | collective-permute-start | bytes 1769480 | tf_op jit(solution)/shard_map/ppermute | solution.py:42
  89.1 14.9 %collective-permute-start.15 = (bf16[2,4,96,384]{3,2,1,0:T(8,128)(2,1)}, bf16[2,4,96,384]{3,2,1,0:T(8,128)(2,1)}, u32[]{:S(2)}, u32[]{:S(2)}) collective-permute-start(bf16[2,4,96,384]{3,2,1,0:T(8,128)(2,1)} %get-tuple-element.142), channel_id=1, source_target_pairs={{0,1},{1,0},{2,3},{3,2},{4,5},{5,4},{6,7},{7,6},{8,9},{9,8},{10,11... | collective-permute-start | bytes 1769480 | tf_op jit(solution)/shard_map/ppermute | solution.py:42
  92.3 13.8 %collective-permute-start.13 = (bf16[4,128,128]{2,1,0:T(8,128)(2,1)S(1)}, bf16[4,128,128]{2,1,0:T(8,128)(2,1)}, u32[]{:S(2)}, u32[]{:S(2)}) collective-permute-start(bf16[4,128,128]{2,1,0:T(8,128)(2,1)S(1)} %get-tuple-element.222), channel_id=1, source_target_pairs={{0,4},{1,5},{2,6},{3,7},{4,0},{5,1},{6,2},{7,3},{8,12},{9,13},{10,... | collective-permute-start | bytes 393224 | tf_op jit(solution)/shard_map/ppermute | solution.py:47
  92.7 13.4 %collective-permute-start.14 = (bf16[4,128,128]{2,1,0:T(8,128)(2,1)S(1)}, bf16[4,128,128]{2,1,0:T(8,128)(2,1)}, u32[]{:S(2)}, u32[]{:S(2)}) collective-permute-start(bf16[4,128,128]{2,1,0:T(8,128)(2,1)S(1)} %get-tuple-element.221), channel_id=1, source_target_pairs={{0,2},{1,3},{2,4},{3,5},{4,6},{5,7},{6,0},{7,1},{8,10},{9,11},{10,... | collective-permute-start | bytes 393224 | tf_op jit(solution)/shard_map/ppermute | solution.py:47
  97.7 8.4 %collective-permute-start.12 = (bf16[4,128,128]{2,1,0:T(8,128)(2,1)S(1)}, bf16[4,128,128]{2,1,0:T(8,128)(2,1)}, u32[]{:S(2)}, u32[]{:S(2)}) collective-permute-start(bf16[4,128,128]{2,1,0:T(8,128)(2,1)S(1)} %get-tuple-element.148), channel_id=1, source_target_pairs={{0,6},{1,7},{2,0},{3,1},{4,2},{5,3},{6,4},{7,5},{8,14},{9,15},{10,... | collective-permute-start | bytes 393224 | tf_op jit(solution)/shard_map/ppermute | solution.py:47
  103.2 14.5 %collective-permute-start.22 = (bf16[768,384]{1,0:T(8,128)(2,1)}, bf16[768,384]{1,0:T(8,128)(2,1)S(1)}, u32[]{:S(2)}, u32[]{:S(2)}) collective-permute-start(bf16[768,384]{1,0:T(8,128)(2,1)} %get-tuple-element.157), channel_id=1, source_target_pairs={{0,1},{1,0},{2,3},{3,2},{4,5},{5,4},{6,7},{7,6},{8,9},{9,8},{10,11... | collective-permute-start | bytes 1769480 | tf_op jit(solution)/shard_map/ppermute | solution.py:42
  106.1 14.6 %collective-permute-start.19 = (bf16[2,96,384]{2,1,0:T(8,128)(2,1)}, bf16[2,96,384]{2,1,0:T(8,128)(2,1)S(1)}, u32[]{:S(2)}, u32[]{:S(2)}) collective-permute-start(bf16[2,96,384]{2,1,0:T(8,128)(2,1)} %get-tuple-element.170), channel_id=1, source_target_pairs={{0,2},{1,3},{2,0},{3,1},{4,6},{5,7},{6,4},{7,5},{8,10},{9,11},{10,... | collective-permute-start | bytes 442376 | tf_op jit(solution)/shard_map/ppermute | solution.py:42
  107.1 15.0 %collective-permute-start.20 = (bf16[2,96,384]{2,1,0:T(8,128)(2,1)}, bf16[2,96,384]{2,1,0:T(8,128)(2,1)S(1)}, u32[]{:S(2)}, u32[]{:S(2)}) collective-permute-start(bf16[2,96,384]{2,1,0:T(8,128)(2,1)} %get-tuple-element.171), channel_id=1, source_target_pairs={{0,4},{1,5},{2,6},{3,7},{4,0},{5,1},{6,2},{7,3},{8,12},{9,13},{10,... | collective-permute-start | bytes 442376 | tf_op jit(solution)/shard_map/ppermute | solution.py:42
  107.9 14.1 %collective-permute-start.21 = (bf16[2,96,384]{2,1,0:T(8,128)(2,1)}, bf16[2,96,384]{2,1,0:T(8,128)(2,1)S(1)}, u32[]{:S(2)}, u32[]{:S(2)}) collective-permute-start(bf16[2,96,384]{2,1,0:T(8,128)(2,1)} %get-tuple-element.172), channel_id=1, source_target_pairs={{0,6},{1,7},{2,4},{3,5},{4,2},{5,3},{6,0},{7,1},{8,14},{9,15},{10,... | collective-permute-start | bytes 442376 | tf_op jit(solution)/shard_map/ppermute | solution.py:42
  116.5 5.6 %collective-permute-start.18 = (bf16[512,128]{1,0:T(8,128)(2,1)}, bf16[512,128]{1,0:T(8,128)(2,1)S(1)}, u32[]{:S(2)}, u32[]{:S(2)}) collective-permute-start(bf16[512,128]{1,0:T(8,128)(2,1)} %get-tuple-element.169), channel_id=1, source_target_pairs={{0,1},{1,0},{2,3},{3,2},{4,5},{5,4},{6,7},{7,6},{8,9},{9,8},{10,11... | collective-permute-start | bytes 393224 | tf_op jit(solution)/shard_map/ppermute | solution.py:42
  120.7 13.6 %collective-permute-start.27 = (bf16[1,48,1536]{2,1,0:T(8,128)(2,1)}, bf16[1,48,1536]{2,1,0:T(8,128)(2,1)S(1)}, u32[]{:S(2)}, u32[]{:S(2)}) collective-permute-start(bf16[1,48,1536]{2,1,0:T(8,128)(2,1)} %get-tuple-element.178), channel_id=1, source_target_pairs={{0,4},{1,5},{2,6},{3,7},{4,0},{5,1},{6,2},{7,3},{8,12},{9,13},{10,... | collective-permute-start | bytes 442376 | tf_op jit(solution)/shard_map/ppermute | solution.py:42
  120.7 17.8 %collective-permute-start.26 = (bf16[192,768]{1,0:T(8,128)(2,1)}, bf16[192,768]{1,0:T(8,128)(2,1)S(1)}, u32[]{:S(2)}, u32[]{:S(2)}) collective-permute-start(bf16[192,768]{1,0:T(8,128)(2,1)} %bitcast.37), channel_id=1, source_target_pairs={{4,0},{5,1},{6,2},{7,3},{8,12},{9,13},{10,14},{11,15},{20,16},{21,... | collective-permute-start | bytes 884744 | tf_op jit(solution)/shard_map/ppermute | solution.py:57
  122.7 11.6 %copy-start.6 = (bf16[1,48,1536]{2,1,0:T(8,128)(2,1)S(1)}, bf16[1,48,1536]{2,1,0:T(8,128)(2,1)}, u32[]{:S(2)}) copy-start(bf16[1,48,1536]{2,1,0:T(8,128)(2,1)} %get-tuple-element.190) | copy-start | bytes 442372
  122.7 11.7 %copy-start.7 = (bf16[2,96,384]{2,1,0:T(8,128)(2,1)S(1)}, bf16[2,96,384]{2,1,0:T(8,128)(2,1)}, u32[]{:S(2)}) copy-start(bf16[2,96,384]{2,1,0:T(8,128)(2,1)} %get-tuple-element.160) | copy-start | bytes 442372
  124.5 14.7 %copy-start.3 = (bf16[1,192,768]{2,1,0:T(8,128)(2,1)S(1)}, bf16[1,192,768]{2,1,0:T(8,128)(2,1)}, u32[]{:S(2)}) copy-start(bf16[1,192,768]{2,1,0:T(8,128)(2,1)} %get-tuple-element.179) | copy-start | bytes 884740
  124.5 14.8 %collective-permute-start.23 = (bf16[224,128]{1,0:T(8,128)(2,1)}, bf16[224,128]{1,0:T(8,128)(2,1)S(1)}, u32[]{:S(2)}, u32[]{:S(2)}) collective-permute-start(bf16[224,128]{1,0:T(8,128)(2,1)} %get-tuple-element.186), channel_id=1, source_target_pairs={{0,2},{1,3},{2,0},{3,1},{4,6},{5,7},{6,4},{7,5},{8,10},{9,11},{10,... | collective-permute-start | bytes 172040 | tf_op jit(solution)/shard_map/ppermute | solution.py:42
  126.8 15.8 %collective-permute-start.24 = (bf16[224,128]{1,0:T(8,128)(2,1)}, bf16[224,128]{1,0:T(8,128)(2,1)S(1)}, u32[]{:S(2)}, u32[]{:S(2)}) collective-permute-start(bf16[224,128]{1,0:T(8,128)(2,1)} %get-tuple-element.187), channel_id=1, source_target_pairs={{0,4},{1,5},{2,6},{3,7},{4,0},{5,1},{6,2},{7,3},{8,12},{9,13},{10,... | collective-permute-start | bytes 172040 | tf_op jit(solution)/shard_map/ppermute | solution.py:42
  129.5 13.1 %collective-permute-start.25 = (bf16[224,128]{1,0:T(8,128)(2,1)}, bf16[224,128]{1,0:T(8,128)(2,1)S(1)}, u32[]{:S(2)}, u32[]{:S(2)}) collective-permute-start(bf16[224,128]{1,0:T(8,128)(2,1)} %get-tuple-element.188), channel_id=1, source_target_pairs={{0,6},{1,7},{2,4},{3,5},{4,2},{5,3},{6,0},{7,1},{8,14},{9,15},{10,... | collective-permute-start | bytes 172040 | tf_op jit(solution)/shard_map/ppermute | solution.py:42
  134.4 11.6 %collective-permute-start.31 = (bf16[48,1536]{1,0:T(8,128)(2,1)S(1)}, bf16[48,1536]{1,0:T(8,128)(2,1)S(1)}, u32[]{:S(2)}, u32[]{:S(2)}) collective-permute-start(bf16[48,1536]{1,0:T(8,128)(2,1)S(1)} %fusion.9), channel_id=1, source_target_pairs={{0,16},{8,24},{16,0},{24,8},{1,17},{9,25},{17,1},{25,9},{2,18},{10... | collective-permute-start | bytes 442376 | tf_op jit(solution)/shard_map/ppermute | solution.py:42
  138.5 8.8 %collective-permute-start.34 = (bf16[2,96,384]{2,1,0:T(8,128)(2,1)S(1)}, bf16[2,96,384]{2,1,0:T(8,128)(2,1)S(1)}, u32[]{:S(2)}, u32[]{:S(2)}) collective-permute-start(bf16[2,96,384]{2,1,0:T(8,128)(2,1)S(1)} %add_convert_fusion.2), channel_id=1, source_target_pairs={{0,16},{8,24},{16,0},{24,8},{1,17},{9,25},{17,1},{25,9},{2,18},{10... | collective-permute-start | bytes 442376 | tf_op jit(solution)/shard_map/ppermute | solution.py:42
  139.2 3.3 %copy-start.19 = (bf16[224,128]{1,0:T(8,128)(2,1)}, bf16[224,128]{1,0:T(8,128)(2,1)S(1)}, u32[]{:S(2)}) copy-start(bf16[224,128]{1,0:T(8,128)(2,1)S(1)} %collective-permute-done.23.refs_1_) | copy-start | bytes 172036
  139.3 8.6 %collective-permute-start.33 = (bf16[192,768]{1,0:T(8,128)(2,1)S(1)}, bf16[192,768]{1,0:T(8,128)(2,1)S(1)}, u32[]{:S(2)}, u32[]{:S(2)}) collective-permute-start(bf16[192,768]{1,0:T(8,128)(2,1)S(1)} %add_convert_fusion), channel_id=1, source_target_pairs={{0,16},{1,17},{2,18},{3,19},{12,28},{13,29},{14,30},{15,31},{16,0}... | collective-permute-start | bytes 884744 | tf_op jit(solution)/shard_map/ppermute | solution.py:63
  145.4 5.1 %collective-permute-start.28 = (bf16[224,128]{1,0:T(8,128)(2,1)}, bf16[224,128]{1,0:T(8,128)(2,1)S(1)}, u32[]{:S(2)}, u32[]{:S(2)}) collective-permute-start(bf16[224,128]{1,0:T(8,128)(2,1)} %message_sum.1.refs_0_), channel_id=1, source_target_pairs={{0,8},{8,0},{16,24},{24,16},{1,9},{9,1},{17,25},{25,17},{2,10},{10... | collective-permute-start | bytes 172040 | tf_op jit(solution)/shard_map/ppermute | solution.py:42
  145.4 5.1 %collective-permute-start.29 = (bf16[224,128]{1,0:T(8,128)(2,1)}, bf16[224,128]{1,0:T(8,128)(2,1)S(1)}, u32[]{:S(2)}, u32[]{:S(2)}) collective-permute-start(bf16[224,128]{1,0:T(8,128)(2,1)} %message_sum.1.refs_0_), channel_id=1, source_target_pairs={{0,16},{8,24},{16,0},{24,8},{1,17},{9,25},{17,1},{25,9},{2,18},{10... | collective-permute-start | bytes 172040 | tf_op jit(solution)/shard_map/ppermute | solution.py:42
  146.0 4.7 %collective-permute-start.30 = (bf16[224,128]{1,0:T(8,128)(2,1)}, bf16[224,128]{1,0:T(8,128)(2,1)S(1)}, u32[]{:S(2)}, u32[]{:S(2)}) collective-permute-start(bf16[224,128]{1,0:T(8,128)(2,1)} %message_sum.1.refs_0_), channel_id=1, source_target_pairs={{0,24},{8,16},{16,8},{24,0},{1,25},{9,17},{17,9},{25,1},{2,26},{10... | collective-permute-start | bytes 172040 | tf_op jit(solution)/shard_map/ppermute | solution.py:42
  147.3 1.6 %collective-permute-start.32 = (bf16[96,1536]{1,0:T(8,128)(2,1)S(1)}, bf16[96,1536]{1,0:T(8,128)(2,1)S(1)}, u32[]{:S(2)}, u32[]{:S(2)}) collective-permute-start(bf16[96,1536]{1,0:T(8,128)(2,1)S(1)} %pad_maximum_fusion.1), channel_id=1, source_target_pairs={{0,8},{8,0},{16,24},{24,16},{1,9},{9,1},{17,25},{25,17},{2,10},{10... | collective-permute-start | bytes 884744 | tf_op jit(solution)/shard_map/ppermute | solution.py:42
  147.9 2.9 %collective-permute-start.36 = (bf16[2,96,384]{2,1,0:T(8,128)(2,1)S(1)}, bf16[2,96,384]{2,1,0:T(8,128)(2,1)S(1)}, u32[]{:S(2)}, u32[]{:S(2)}) collective-permute-start(bf16[2,96,384]{2,1,0:T(8,128)(2,1)S(1)} %add_convert_fusion.1.refs_6_), channel_id=1, source_target_pairs={{0,8},{8,0},{16,24},{24,16},{1,9},{9,1},{17,25},{25,17},{2,10},{10... | collective-permute-start | bytes 442376 | tf_op jit(solution)/shard_map/ppermute | solution.py:42
  148.3 2.1 %copy-start.1 = (bf16[384,768]{1,0:T(8,128)(2,1)}, bf16[384,768]{1,0:T(8,128)(2,1)S(1)}, u32[]{:S(2)}) copy-start(bf16[384,768]{1,0:T(8,128)(2,1)S(1)} %pad_maximum_fusion.refs_4_) | copy-start | bytes 1769476
  148.9 2.0 %collective-permute-start.35 = (bf16[384,768]{1,0:T(8,128)(2,1)S(1)}, bf16[384,768]{1,0:T(8,128)(2,1)S(1)}, u32[]{:S(2)}, u32[]{:S(2)}) collective-permute-start(bf16[384,768]{1,0:T(8,128)(2,1)S(1)} %pad_maximum_fusion.refs_4_), channel_id=1, source_target_pairs={{0,8},{8,0},{16,24},{24,16},{1,9},{9,1},{17,25},{25,17},{2,10},{10... | collective-permute-start | bytes 1769480 | tf_op jit(solution)/shard_map/ppermute | solution.py:42
  (11 other events, 7.5 us)
